TPU v7x, 32 devices: a whole 2x2x4 slice. The times are simulated.
32 devices in a mesh: groups: 2 (over x), blk: 8 (over z, y), split: 2 (over core).
Axes of the slice: x: 2, y: 2, z: 4, core: 2. Of those that a mesh axis runs over, the one named last changes fastest.
Arguments:
- embeddings: bfloat16 [32768, 768], P(('groups', 'blk', 'split')), parts along dimension 0, may hold values from -6 to 6
- cluster_of: int32 [32768], P(('groups', 'blk', 'split')), parts along dimension 0, may hold values from 0 to 15, as said below
- target_pos: int32 [32768], P(('groups', 'blk', 'split')), parts along dimension 0, may hold values from 0 to 16383, as said below
Outputs:
- best: float32 [32768], P(('groups', 'blk', 'split')), parts along dimension 0
There are 2 independent parts, one for each index of `groups`. A program takes and returns all parts, laid end to end along the dimension named above; each array names one. Nothing has to cross between parts.
Inputs may be any that keep to these rules, and one draw needn't show every extreme that they name: `cluster_of`: ordering the members by target_pos lists cluster 0 first, then cluster 1 and so on, each cluster's members contiguous; every cluster has 2 to 4096 members and one has exactly 4096. `target_pos`: A permutation of the rows. For every aligned block of 1024 positions, each device's 1024 data-order rows hold exactly 64 of its positions.
All inputs are finite; a program needn't handle non-finite values.
Results may differ from a plain program's by a relative error of at most 0.0025.
Values may be sent and summed in bfloat16 or wider, within the bound.
No kernel may reach another device: no remote copies, remote signals or barrier semaphores. Data moves between devices by JAX's collectives and lax.ppermute only.
A program may use at most 64 MiB of HBM per device.

v0:
```python
import jax
import jax.numpy as jnp
from jax import lax
from jax.sharding import PartitionSpec as P

MOST = 4096


FILL = -4.0


def from_behind(block, axis, distance):
    devices = range(lax.axis_size(axis))
    route = [((i - distance) % len(devices), i) for i in devices]
    return lax.ppermute(block, axis, route)


def masked_scores(left, left_ids, right, right_ids):
    sims = lax.dot_general(
        left, right, (((1,), (1,)), ((), ())), preferred_element_type=jnp.float32
    )
    return jnp.where(left_ids[:, None] == right_ids[None, :], sims, FILL)


def body(embeddings, cluster_of, target_pos):
    count = lax.axis_size(("blk", "split"))
    rows, width = embeddings.shape
    piece = rows // count
    me = lax.axis_index(("blk", "split"))
    values = embeddings.astype(jnp.float32)
    unit = (values * lax.rsqrt(jnp.sum(values * values, axis=1, keepdims=True) + 1e-06)).astype(
        jnp.bfloat16
    )
    order = jnp.argsort(target_pos)
    packed = unit[order].reshape(count, piece, width)
    labels = jnp.stack(
        [cluster_of[order].reshape(count, piece), target_pos[order].reshape(count, piece)], axis=1
    )
    received, tags = (
        lax.all_to_all(packed, ("blk", "split"), split_axis=0, concat_axis=0, tiled=True),
        lax.all_to_all(labels, ("blk", "split"), split_axis=0, concat_axis=0, tiled=True),
    )
    unit_in = received.reshape(rows, width)
    ids_in = tags[:, 0, :].reshape(rows)
    local = tags[:, 1, :].reshape(rows) - me * rows
    place = jnp.argsort(local)
    mine = unit_in[place]
    my_ids = ids_in[place]
    reach = (MOST + rows - 2) // rows
    own = masked_scores(mine, my_ids, mine, my_ids)
    diagonal = jnp.arange(rows)[:, None] == jnp.arange(rows)[None, :]
    best = jnp.max(jnp.where(diagonal, FILL, own), axis=1)

    def both_maxima(pair, visit_unit, visit_ids):
        row_best, visit_best = pair
        scores = masked_scores(mine, my_ids, visit_unit, visit_ids)
        return (
            jnp.maximum(row_best, jnp.max(scores, axis=1)),
            jnp.maximum(visit_best, jnp.max(scores, axis=0)),
        )

    def turn(step, carry):
        row_best, visit_unit, visit_ids, visit_best = carry
        visit_unit, visit_ids, visit_best = (
            from_behind(visit_unit, ("blk", "split"), 1),
            from_behind(visit_ids, ("blk", "split"), 1),
            from_behind(visit_best.astype(jnp.bfloat16), ("blk", "split"), 1).astype(
                visit_best.dtype
            ),
        )
        row_best, visit_best = both_maxima((row_best, visit_best), visit_unit, visit_ids)
        return (row_best, visit_unit, visit_ids, visit_best)

    start_best = jnp.full((rows,), FILL, jnp.float32)
    best, visit_unit, visit_ids, visit_best = lax.fori_loop(
        0, reach, turn, (best, mine, my_ids, start_best)
    )
    returned_home = from_behind(visit_best, ("blk", "split"), -reach)
    best = jnp.maximum(best, returned_home)
    back = best[local].reshape(count, piece)
    returned = lax.all_to_all(
        back, ("blk", "split"), split_axis=0, concat_axis=0, tiled=True
    ).reshape(rows)
    return jnp.zeros((rows,), jnp.float32).at[order].set(returned)


def solution(mesh):
    return jax.shard_map(
        body,
        mesh=mesh,
        in_specs=(
            P(("groups", "blk", "split"), None),
            P(("groups", "blk", "split")),
            P(("groups", "blk", "split")),
        ),
        out_specs=P(("groups", "blk", "split")),
        check_vma=False,
    )
```

profile of v0, /device:TPU:0, one launch (start us, length us, event | category | flops | bytes accessed | tf_op | source)
XLA Modules:
  0.0 204.0 jit_solution(9965459332306292172)
XLA Ops:
  0.0 5.1 %sort.31 = (s32[1024]{0:T(1024)}, s32[1024]{0:T(1024)S(1)}) sort(s32[1024]{0:T(1024)} %param.7, s32[1024]{0:T(1024)S(1)} %iota.15), dimensions={0}, to_apply=%region_0.0 | sort | flops 10240 | bytes 16384 | tf_op jit(solution)/shard_map/jit(argsort)/sort | solution.py:34
  5.1 4.5 %gather_fusion.1 = s32[1024]{0:T(1024)S(1)} fusion(s32[1024]{0:T(1024)S(1)} %copy-done.1, s32[1024]{0:T(1024)S(1)} %get-tuple-element.92), kind=kCustom, calls=%fused_computation.1 | custom fusion | bytes 12288 | tf_op jit(solution)/shard_map/gather | solution.py:37
  9.7 0.1 stack_reshape.7
  9.8 4.5 %gather_fusion = s32[1024]{0:T(1024)S(1)} fusion(s32[1024]{0:T(1024)S(1)} %copy-done, s32[1024]{0:T(1024)S(1)} %get-tuple-element.92), kind=kCustom, calls=%fused_computation | custom fusion | bytes 12288 | tf_op jit(solution)/shard_map/gather | solution.py:37
  14.3 0.1 stack_reshape.6
  14.4 0.7 reshape.140
  15.1 7.4 %all-to-all-start = ((s32[16,1,128]{2,1,0:T(1,128)}), s32[16,1,128]{2,1,0:T(1,128)S(1)}, u32[]{:S(2)}, u32[]{:S(2)}) async-start(s32[16,1,128]{2,1,0:T(1,128)} %reshape.140), calls=%async_computation | async-start | bytes 16384 | tf_op jit(solution)/shard_map/all_to_all | solution.py:41
  22.5 0.4 fusion.2
  22.9 0.3 fusion.3
  23.2 5.2 %gather_fusion.3 = bf16[1024,768]{1,0:T(8,128)(2,1)} fusion(bf16[1024,768]{1,0:T(8,128)(2,1)S(1)} %fusion.3, s32[1024]{0:T(1024)S(1)} %get-tuple-element.92), kind=kCustom, calls=%fused_computation.3 | custom fusion | bytes 3149824 | tf_op jit(solution)/shard_map/gather | solution.py:35
  28.4 0.5 all-to-all-done
  28.9 5.6 %all-to-all-start.1 = ((bf16[16,64,768]{2,1,0:T(8,128)(2,1)}), bf16[16,64,768]{2,1,0:T(8,128)(2,1)S(1)}, u32[]{:S(2)}, u32[]{:S(2)}) async-start(bf16[16,64,768]{2,1,0:T(8,128)(2,1)} %bitcast), calls=%async_computation.1 | async-start | bytes 3145728 | tf_op jit(solution)/shard_map/all_to_all | solution.py:40
  34.5 0.5 broadcast.95
  35.0 0.7 reduce.15
  35.6 0.1 reshape.141
  35.7 0.5 broadcast.93
  36.2 0.7 fusion.7
  36.9 0.1 sub.21
  37.0 0.1 sub.22
  37.1 0.1 reshape_squeeze.4
  37.2 4.4 %sort.32 = (s32[1024]{0:T(1024)}, s32[1024]{0:T(1024)S(1)}) sort(s32[1024]{0:T(1024)S(1)} %sub.21, s32[1024]{0:T(1024)S(1)} %iota.16), dimensions={0}, to_apply=%region_1.0 | sort | flops 10240 | bytes 16384 | tf_op jit(solution)/shard_map/jit(argsort)/sort | solution.py:46
  41.5 4.5 %gather_fusion.2 = s32[1024]{0:T(1024)S(1)} fusion(s32[1024]{0:T(1024)S(1)} %reshape_squeeze.4, s32[1024]{0:T(1024)S(1)} %fusion.4), kind=kCustom, calls=%fused_computation.2 | custom fusion | bytes 12288 | tf_op jit(solution)/shard_map/gather | solution.py:48
  46.1 20.3 %all-to-all-done.1 = bf16[16,64,768]{2,1,0:T(8,128)(2,1)S(1)} async-done(((bf16[16,64,768]{2,1,0:T(8,128)(2,1)}), bf16[16,64,768]{2,1,0:T(8,128)(2,1)S(1)}, u32[]{:S(2)}, u32[]{:S(2)}) %all-to-all-start.1) | async-done | bytes 1572896 | tf_op jit(solution)/shard_map/all_to_all | solution.py:40
  66.4 4.0 %gather_fusion.4 = bf16[1024,768]{1,0:T(8,128)(2,1)S(1)} fusion(bf16[1024,768]{1,0:T(8,128)(2,1)S(1)} %bitcast.13, s32[1024]{0:T(1024)S(1)} %fusion.4), kind=kCustom, calls=%fused_computation.4 | custom fusion | bytes 3149824 | tf_op jit(solution)/shard_map/gather | solution.py:47
  70.4 1.8 select_reduce_fusion
  72.2 1.2 copy.6
  73.4 106.9 %while.17 = (s32[]{:T(128)}, f32[1024]{0:T(1024)S(1)}, bf16[1024,768]{1,0:T(8,128)(2,1)}, s32[1024]{0:T(1024)S(1)}, f32[1024]{0:T(1024)S(1)}, /*index=5*/s32[102...) while((s32[]{:T(128)}, f32[1024]{0:T(1024)S(1)}, bf16[1024,768]{1,0:T(8,128)(2,1)}, ...), condition=%wide.region_7.8_spmd.clone, body=%wide.region_4.0_spmd.clone.sunk | while | flops 1614809088 | bytes 12660959 | solution.py:75
  73.4 0.8 collective-permute-start.1
  74.2 2.0 collective-permute-start
  76.2 0.8 collective-permute-start.2
  77.0 22.4 %collective-permute-done = s32[1024]{0:T(1024)S(1)} collective-permute-done((s32[1024]{0:T(1024)S(1)}, s32[1024]{0:T(1024)S(1)}, u32[]{:S(2)}, u32[]{:S(2)}) %collective-permute-start) | collective-permute-done | bytes 4128 | tf_op jit(solution)/shard_map/while/body/eval_jaxpr/ppermute | solution.py:15
  99.4 0.0 collective-permute-done.1
  99.4 1.9 fusion.17
  101.3 1.2 copy.16
  102.5 0.0 collective-permute-done.2
  102.5 0.0 collective-permute-start.1
  102.5 0.1 collective-permute-start
  102.6 0.1 collective-permute-start.2
  102.7 22.6 %collective-permute-done = s32[1024]{0:T(1024)S(1)} collective-permute-done((s32[1024]{0:T(1024)S(1)}, s32[1024]{0:T(1024)S(1)}, u32[]{:S(2)}, u32[]{:S(2)}) %collective-permute-start) | collective-permute-done | bytes 4128 | tf_op jit(solution)/shard_map/while/body/eval_jaxpr/ppermute | solution.py:15
  125.3 0.0 collective-permute-done.1
  125.3 1.9 fusion.17
  127.2 1.2 copy.16
  128.4 0.0 collective-permute-done.2
  128.4 0.0 collective-permute-start.1
  128.4 0.1 collective-permute-start
  128.5 0.1 collective-permute-start.2
  128.6 22.6 %collective-permute-done = s32[1024]{0:T(1024)S(1)} collective-permute-done((s32[1024]{0:T(1024)S(1)}, s32[1024]{0:T(1024)S(1)}, u32[]{:S(2)}, u32[]{:S(2)}) %collective-permute-start) | collective-permute-done | bytes 4128 | tf_op jit(solution)/shard_map/while/body/eval_jaxpr/ppermute | solution.py:15
  151.2 1.9 fusion.17
  153.1 1.2 copy.16
  154.3 0.0 collective-permute-start.1
  154.3 0.1 collective-permute-start
  154.4 0.1 collective-permute-start.2
  154.5 22.7 %collective-permute-done = s32[1024]{0:T(1024)S(1)} collective-permute-done((s32[1024]{0:T(1024)S(1)}, s32[1024]{0:T(1024)S(1)}, u32[]{:S(2)}, u32[]{:S(2)}) %collective-permute-start) | collective-permute-done | bytes 4128 | tf_op jit(solution)/shard_map/while/body/eval_jaxpr/ppermute | solution.py:15
  177.2 1.9 fusion.17
  179.1 1.2 copy.16
  180.3 0.0 collective-permute-done.2
  180.3 3.6 %collective-permute-done.3 = f32[1024]{0:T(1024)S(1)} collective-permute-done((f32[1024]{0:T(1024)S(1)}, f32[1024]{0:T(1024)S(1)}, u32[]{:S(2)}, u32[]{:S(2)}) %collective-permute-start.3) | collective-permute-done | bytes 4128 | tf_op jit(solution)/shard_map/ppermute | solution.py:15
  183.9 4.5 %gather_fusion.5 = f32[1024]{0:T(1024)S(1)} fusion(f32[1024]{0:T(1024)S(1)} %max.9, s32[1024]{0:T(1024)S(1)} %broadcast_clamp_fusion), kind=kCustom, calls=%fused_computation.5 | custom fusion | bytes 12288 | tf_op jit(solution)/shard_map/gather | solution.py:80
  188.4 0.1 all_to_all.14
  188.5 9.4 %all_to_all.19 = f32[16,1,64]{2,1,0:T(1,128)S(1)} all-to-all(f32[16,1,64]{2,1,0:T(1,128)S(1)} %all_to_all.14), channel_id=1, replica_groups=mesh['groups'=2,'blk'=8,'split'=2] {'blk','split'}, dimensions={0} | all-to-all | bytes 8192 | tf_op jit(solution)/shard_map/all_to_all | solution.py:81
  197.9 0.5 broadcast.94
  198.4 0.7 reduce.13
  199.1 0.1 reshape.102
  199.2 4.9 %scatter_custom_fusion = f32[1024]{0:T(1024)} fusion(s32[1024]{0:T(1024)S(1)} %get-tuple-element.93, f32[1024]{0:T(1024)S(1)} %reshape.102, f32[]{:T(128)} %constant.3.clone.1), kind=kCustom, calls=%fused_computation.28 | custom fusion | bytes 4100 | tf_op jit(solution)/shard_map/scatter | solution.py:84
  (37 shorter events, 0.2 us)
Async XLA Ops:
  0.0 9.8 %copy-start = (s32[1024]{0:T(1024)S(1)}, s32[1024]{0:T(1024)}, u32[]{:S(2)}) copy-start(s32[1024]{0:T(1024)} %param.6) | copy-start | bytes 12292
  0.0 5.1 %copy-start.1 = (s32[1024]{0:T(1024)S(1)}, s32[1024]{0:T(1024)}, u32[]{:S(2)}) copy-start(s32[1024]{0:T(1024)} %param.7) | copy-start | bytes 12292
  9.8 12.7 %copy-start.2 = (bf16[1024,768]{1,0:T(8,128)(2,1)S(1)}, bf16[1024,768]{1,0:T(8,128)(2,1)}, u32[]{:S(2)}) copy-start(bf16[1024,768]{1,0:T(8,128)(2,1)} %param.5) | copy-start | bytes 4718596
  15.1 13.8 %all-to-all-start = ((s32[16,1,128]{2,1,0:T(1,128)}), s32[16,1,128]{2,1,0:T(1,128)S(1)}, u32[]{:S(2)}, u32[]{:S(2)}) async-start(s32[16,1,128]{2,1,0:T(1,128)} %reshape.140), calls=%async_computation | async-start | bytes 16384 | tf_op jit(solution)/shard_map/all_to_all | solution.py:41
  28.9 37.5 %all-to-all-start.1 = ((bf16[16,64,768]{2,1,0:T(8,128)(2,1)}), bf16[16,64,768]{2,1,0:T(8,128)(2,1)S(1)}, u32[]{:S(2)}, u32[]{:S(2)}) async-start(bf16[16,64,768]{2,1,0:T(8,128)(2,1)} %bitcast), calls=%async_computation.1 | async-start | bytes 3145728 | tf_op jit(solution)/shard_map/all_to_all | solution.py:40
  73.4 26.0 %collective-permute-start.1 = (bf16[1024,768]{1,0:T(8,128)(2,1)}, bf16[1024,768]{1,0:T(8,128)(2,1)S(1)}, u32[]{:S(2)}, u32[]{:S(2)}) collective-permute-start(bf16[1024,768]{1,0:T(8,128)(2,1)} %get-tuple-element.152), channel_id=1, source_target_pairs={{15,0},{0,1},{1,2},{2,3},{3,4},{4,5},{5,6},{6,7},{7,8},{8,9},{9,10... | collective-permute-start | bytes 4718600 | tf_op jit(solution)/shard_map/while/body/eval_jaxpr/ppermute | solution.py:15
  74.2 25.2 %collective-permute-start = (s32[1024]{0:T(1024)S(1)}, s32[1024]{0:T(1024)S(1)}, u32[]{:S(2)}, u32[]{:S(2)}) collective-permute-start(s32[1024]{0:T(1024)S(1)} %get-tuple-element.153), channel_id=1, source_target_pairs={{15,0},{0,1},{1,2},{2,3},{3,4},{4,5},{5,6},{6,7},{7,8},{8,9},{9,10... | collective-permute-start | bytes 12296 | tf_op jit(solution)/shard_map/while/body/eval_jaxpr/ppermute | solution.py:15
  76.2 26.3 %collective-permute-start.2 = (bf16[1024]{0:T(1024)(128)(2,1)S(1)}, bf16[1024]{0:T(1024)(128)(2,1)S(1)}, u32[]{:S(2)}, u32[]{:S(2)}) collective-permute-start(bf16[1024]{0:T(1024)(128)(2,1)S(1)} %select_convert_fusion.2), channel_id=1, source_target_pairs={{15,0},{0,1},{1,2},{2,3},{3,4},{4,5},{5,6},{6,7},{7,8},{8,9},{9,10... | collective-permute-start | bytes 6152 | tf_op jit(solution)/shard_map/while/body/eval_jaxpr/ppermute | solution.py:15
  102.5 22.8 %collective-permute-start.1 = (bf16[1024,768]{1,0:T(8,128)(2,1)}, bf16[1024,768]{1,0:T(8,128)(2,1)S(1)}, u32[]{:S(2)}, u32[]{:S(2)}) collective-permute-start(bf16[1024,768]{1,0:T(8,128)(2,1)} %get-tuple-element.152), channel_id=1, source_target_pairs={{15,0},{0,1},{1,2},{2,3},{3,4},{4,5},{5,6},{6,7},{7,8},{8,9},{9,10... | collective-permute-start | bytes 4718600 | tf_op jit(solution)/shard_map/while/body/eval_jaxpr/ppermute | solution.py:15
  102.5 22.8 %collective-permute-start = (s32[1024]{0:T(1024)S(1)}, s32[1024]{0:T(1024)S(1)}, u32[]{:S(2)}, u32[]{:S(2)}) collective-permute-start(s32[1024]{0:T(1024)S(1)} %get-tuple-element.153), channel_id=1, source_target_pairs={{15,0},{0,1},{1,2},{2,3},{3,4},{4,5},{5,6},{6,7},{7,8},{8,9},{9,10... | collective-permute-start | bytes 12296 | tf_op jit(solution)/shard_map/while/body/eval_jaxpr/ppermute | solution.py:15
  102.6 25.8 %collective-permute-start.2 = (bf16[1024]{0:T(1024)(128)(2,1)S(1)}, bf16[1024]{0:T(1024)(128)(2,1)S(1)}, u32[]{:S(2)}, u32[]{:S(2)}) collective-permute-start(bf16[1024]{0:T(1024)(128)(2,1)S(1)} %select_convert_fusion.2), channel_id=1, source_target_pairs={{15,0},{0,1},{1,2},{2,3},{3,4},{4,5},{5,6},{6,7},{7,8},{8,9},{9,10... | collective-permute-start | bytes 6152 | tf_op jit(solution)/shard_map/while/body/eval_jaxpr/ppermute | solution.py:15
  128.4 22.8 %collective-permute-start.1 = (bf16[1024,768]{1,0:T(8,128)(2,1)}, bf16[1024,768]{1,0:T(8,128)(2,1)S(1)}, u32[]{:S(2)}, u32[]{:S(2)}) collective-permute-start(bf16[1024,768]{1,0:T(8,128)(2,1)} %get-tuple-element.152), channel_id=1, source_target_pairs={{15,0},{0,1},{1,2},{2,3},{3,4},{4,5},{5,6},{6,7},{7,8},{8,9},{9,10... | collective-permute-start | bytes 4718600 | tf_op jit(solution)/shard_map/while/body/eval_jaxpr/ppermute | solution.py:15
  128.4 22.8 %collective-permute-start = (s32[1024]{0:T(1024)S(1)}, s32[1024]{0:T(1024)S(1)}, u32[]{:S(2)}, u32[]{:S(2)}) collective-permute-start(s32[1024]{0:T(1024)S(1)} %get-tuple-element.153), channel_id=1, source_target_pairs={{15,0},{0,1},{1,2},{2,3},{3,4},{4,5},{5,6},{6,7},{7,8},{8,9},{9,10... | collective-permute-start | bytes 12296 | tf_op jit(solution)/shard_map/while/body/eval_jaxpr/ppermute | solution.py:15
  128.5 25.8 %collective-permute-start.2 = (bf16[1024]{0:T(1024)(128)(2,1)S(1)}, bf16[1024]{0:T(1024)(128)(2,1)S(1)}, u32[]{:S(2)}, u32[]{:S(2)}) collective-permute-start(bf16[1024]{0:T(1024)(128)(2,1)S(1)} %select_convert_fusion.2), channel_id=1, source_target_pairs={{15,0},{0,1},{1,2},{2,3},{3,4},{4,5},{5,6},{6,7},{7,8},{8,9},{9,10... | collective-permute-start | bytes 6152 | tf_op jit(solution)/shard_map/while/body/eval_jaxpr/ppermute | solution.py:15
  154.3 22.9 %collective-permute-start.1 = (bf16[1024,768]{1,0:T(8,128)(2,1)}, bf16[1024,768]{1,0:T(8,128)(2,1)S(1)}, u32[]{:S(2)}, u32[]{:S(2)}) collective-permute-start(bf16[1024,768]{1,0:T(8,128)(2,1)} %get-tuple-element.152), channel_id=1, source_target_pairs={{15,0},{0,1},{1,2},{2,3},{3,4},{4,5},{5,6},{6,7},{7,8},{8,9},{9,10... | collective-permute-start | bytes 4718600 | tf_op jit(solution)/shard_map/while/body/eval_jaxpr/ppermute | solution.py:15
  154.3 22.9 %collective-permute-start = (s32[1024]{0:T(1024)S(1)}, s32[1024]{0:T(1024)S(1)}, u32[]{:S(2)}, u32[]{:S(2)}) collective-permute-start(s32[1024]{0:T(1024)S(1)} %get-tuple-element.153), channel_id=1, source_target_pairs={{15,0},{0,1},{1,2},{2,3},{3,4},{4,5},{5,6},{6,7},{7,8},{8,9},{9,10... | collective-permute-start | bytes 12296 | tf_op jit(solution)/shard_map/while/body/eval_jaxpr/ppermute | solution.py:15
  154.4 25.9 %collective-permute-start.2 = (bf16[1024]{0:T(1024)(128)(2,1)S(1)}, bf16[1024]{0:T(1024)(128)(2,1)S(1)}, u32[]{:S(2)}, u32[]{:S(2)}) collective-permute-start(bf16[1024]{0:T(1024)(128)(2,1)S(1)} %select_convert_fusion.2), channel_id=1, source_target_pairs={{15,0},{0,1},{1,2},{2,3},{3,4},{4,5},{5,6},{6,7},{7,8},{8,9},{9,10... | collective-permute-start | bytes 6152 | tf_op jit(solution)/shard_map/while/body/eval_jaxpr/ppermute | solution.py:15
  180.3 3.6 %collective-permute-start.3 = (f32[1024]{0:T(1024)S(1)}, f32[1024]{0:T(1024)S(1)}, u32[]{:S(2)}, u32[]{:S(2)}) collective-permute-start(f32[1024]{0:T(1024)S(1)} %get-tuple-element.48), channel_id=1, source_target_pairs={{4,0},{5,1},{6,2},{7,3},{8,4},{9,5},{10,6},{11,7},{12,8},{13,9},{1... | collective-permute-start | bytes 12296 | tf_op jit(solution)/shard_map/ppermute | solution.py:15
where the time goes:
time: 204 us
  waiting for transfers between devices  115 us (56%)
  local copies, waits for them, and re-layouts  40.8 us (20%)
  starting transfers between devices  16.9 us (8%)
  other arithmetic  12.3 us (6%)
  matrix products  9.55 us (5%)
  blocking collectives  9.38 us (5%)
    ppermute x13, waiting for transfers between devices, from_behind(): return lax.ppermute(block, axis, route)  94 us
    all_to_all x1, waiting for transfers between devices, body(): lax.all_to_all(packed, ('blk', 'split'), split_axis=0, concat_axis=0, til...  20.3 us
    dot_general x5, matrix products, masked_scores(): lax.dot_general(left, right, (((1,), (1,)), ((), ())), preferred_element_...  9.55 us
    all_to_all x1, blocking collectives, body(): lax.all_to_all(back, ('blk', 'split'), split_axis=0, concat_axis=0, tiled...  9.38 us
    all_to_all x1, starting transfers between devices, body(): lax.all_to_all(labels, ('blk', 'split'), split_axis=0, concat_axis=0, til...  7.39 us
    all_to_all x1, starting transfers between devices, body(): lax.all_to_all(packed, ('blk', 'split'), split_axis=0, concat_axis=0, til...  5.56 us
    gather x1, local copies, waits for them, and re-layouts, body(): packed = unit[order].reshape(count, piece, width)  5.21 us
    sort x1, other arithmetic, body(): order = jnp.argsort(target_pos)  5.12 us
  transfers between devices with their start and end apart: 15, of which 7 were waited for; matrix products, arithmetic and copies ran while one was open for 15% of the time, Pallas kernels for 0%

commit v1 on v0

v1 whole, which is shorter than its diff:
```python
import functools

import jax
import jax.numpy as jnp
from jax import lax
from jax.experimental import pallas as pl
from jax.experimental.pallas import tpu as pltpu
from jax.sharding import PartitionSpec as P

MOST = 4096
FILL = -4.0
TAGS = 8
LANES = 128
VMEM = 48 * 1024 * 1024
WHOLE = pl.BlockSpec(memory_space=pltpu.VMEM)
SCALARS = pl.BlockSpec(memory_space=pltpu.SMEM)


def spread(row):
    return jnp.transpose(jnp.broadcast_to(row, (LANES, row.shape[1])))


def column_fold(scores):
    rows, columns = scores.shape
    return jnp.max(scores.reshape(rows // 8, 8, columns), axis=0)


def lane_fold(scores):
    best = scores[:, :LANES]
    for at in range(LANES, scores.shape[1], LANES):
        best = jnp.maximum(best, scores[:, at : at + LANES])
    return best


def order_kernel(parts, place_ref, rows_ref, ids_ref, pos_ref, *refs):
    outs, rank_ref, unit, pick, placed, tags = refs[:parts], *refs[parts:]
    count, width = rows_ref.shape
    slots = count // parts
    step = 256
    values = rows_ref[...].astype(jnp.float32)
    total = jnp.sum(values * values, axis=1, keepdims=True)
    unit[...] = (values * lax.rsqrt(total + 1e-06)).astype(jnp.bfloat16)
    pos = pos_ref[...].astype(jnp.float32)
    below = jnp.zeros((8, count), jnp.float32)
    for at in range(0, count, step):
        other = spread(pos[:, at : at + step])[:, :1]
        below += jnp.sum(jnp.where(other < pos, 1.0, 0.0).reshape(step // 8, 8, count), axis=0)
    rank = jnp.sum(below, axis=0, keepdims=True).astype(jnp.int32)
    rank_ref[...] = rank
    for at in range(0, count, step):
        slot = lax.broadcasted_iota(jnp.int32, (step, count), 0) + at
        pick[at : at + step, :] = jnp.where(slot == rank, 1.0, 0.0).astype(jnp.bfloat16)
    for at in range(0, count, step):
        placed[at : at + step, :] = jnp.dot(
            pick[at : at + step, :], unit[...], preferred_element_type=jnp.float32
        ).astype(jnp.bfloat16)
    ids = jnp.broadcast_to((ids_ref[...] + 1).astype(jnp.bfloat16), (16, count))
    sorted_ids = lax.dot_general(
        ids, pick[...], (((1,), (1,)), ((), ())), preferred_element_type=jnp.float32
    )
    for part in range(parts):
        tags[part, :, :slots] = sorted_ids[:, part * slots : (part + 1) * slots]
    for shift in range(parts):
        goal = lax.rem(place_ref[0] + shift, parts)
        outs[shift][:slots, :] = placed[pl.ds(pl.multiple_of(goal * slots, slots), slots), :]
        outs[shift][slots:, :slots] = tags[goal, :TAGS, :slots].astype(jnp.bfloat16)


def in_order(place, embeddings, ids, pos, parts):
    count, width = embeddings.shape
    slots = count // parts
    return pl.pallas_call(
        functools.partial(order_kernel, parts),
        out_shape=[jax.ShapeDtypeStruct((slots + TAGS, width), jnp.bfloat16)] * parts
        + [jax.ShapeDtypeStruct((1, count), jnp.int32)],
        in_specs=[SCALARS, WHOLE, WHOLE, WHOLE],
        out_specs=[WHOLE] * (parts + 1),
        scratch_shapes=[
            pltpu.VMEM((count, width), jnp.bfloat16),
            pltpu.VMEM((count, count), jnp.bfloat16),
            pltpu.VMEM((count, width), jnp.bfloat16),
            pltpu.VMEM((parts, 16, max(slots, LANES)), jnp.float32),
        ],
        compiler_params=pltpu.CompilerParams(vmem_limit_bytes=VMEM),
        cost_estimate=pl.CostEstimate(
            flops=2 * count * count * width, bytes_accessed=4 * count * width, transcendentals=count
        ),
        name="order",
    )(place, embeddings, ids.reshape(1, count), pos.reshape(1, count))


def gather_left(parts, buffer, ids):
    at = 0
    for ref, n in parts:
        buffer[at : at + n, :] = ref[:n, :]
        ids[:, at : at + n] = ref[n : n + TAGS, :n].astype(jnp.float32)
        at += n


def gather_right(parts, buffer, ids):
    at = 0
    for ref, n in parts:
        buffer[at : at + n, :] = ref[:n, :]
        ids[at : at + n, :] = spread(ref[n : n + 1, :n].astype(jnp.float32))
        at += n


def masked(left, left_ids, right, right_ids):
    scores = lax.dot_general(
        right, left, (((1,), (1,)), ((), ())), preferred_element_type=jnp.float32
    )
    return jnp.where(right_ids[:, :1] == left_ids[:1, :], scores, FILL)


def quarter_kernel(parts, others, step, *refs):
    own, rest = refs[:parts], refs[parts : parts + others]
    best_ref, left, left_ids, right, right_ids = refs[parts + others :]
    slots = own[0].shape[0] - TAGS
    gather_left([(r, slots) for r in own], left, left_ids)
    gather_right([(r, slots) for r in own] + [(r, slots) for r in rest], right, right_ids)
    count = left.shape[0]

    def turn(index, best, diagonal):
        at = pl.multiple_of(index * step, step)
        scores = masked(
            left[...], left_ids[...], right[pl.ds(at, step), :], right_ids[pl.ds(at, step), :]
        )
        if diagonal:
            down = lax.broadcasted_iota(jnp.int32, (step, count), 0) + at
            across = lax.broadcasted_iota(jnp.int32, (step, count), 1)
            scores = jnp.where(down == across, FILL, scores)
        return jnp.maximum(best, column_fold(scores))

    best = jnp.full((8, count), FILL, jnp.float32)
    best = lax.fori_loop(0, count // step, functools.partial(turn, diagonal=True), best)
    best = lax.fori_loop(
        count // step, right.shape[0] // step, functools.partial(turn, diagonal=False), best
    )
    best_ref[...] = jnp.max(best, axis=0, keepdims=True)


def quarter_best(own, rest):
    slots, width = own[0].shape[0] - TAGS, own[0].shape[1]
    count = slots * len(own)
    total = slots * (len(own) + len(rest))
    return pl.pallas_call(
        functools.partial(quarter_kernel, len(own), len(rest), 256),
        out_shape=jax.ShapeDtypeStruct((1, count), jnp.float32),
        in_specs=[WHOLE] * (len(own) + len(rest)),
        out_specs=WHOLE,
        scratch_shapes=[
            pltpu.VMEM((count, width), jnp.bfloat16),
            pltpu.VMEM((TAGS, count), jnp.float32),
            pltpu.VMEM((total, width), jnp.bfloat16),
            pltpu.VMEM((total, LANES), jnp.float32),
        ],
        compiler_params=pltpu.CompilerParams(vmem_limit_bytes=VMEM),
        cost_estimate=pl.CostEstimate(
            flops=2 * count * total * width, bytes_accessed=2 * total * width, transcendentals=0
        ),
        name="quarter",
    )(*own, *rest)


def border_kernel(parts, members, step, place_ref, *refs):
    quarter, refs = refs[: parts * members], refs[parts * members :]
    tails, own_tail, heads, own_head, best_ref = refs[:5]
    out_ref, left, left_ids, right, right_ids, right_best, left_best = refs[5:]
    slots = quarter[0].shape[0] - TAGS
    half = slots // 2
    around = parts * half
    gather_left([(r, slots) for r in quarter], left, left_ids)
    for base, moved, kept, cut in ((0, tails, own_tail, half), (around, heads, own_head, 0)):
        n = around - half
        gather_right(
            [(moved, n)], right.at[pl.ds(base, n), :], right_ids.at[pl.ds(base, n), :]
        )
        right[base + n : base + around, :] = kept[cut : cut + half, :]
        kept_ids = spread(kept[slots : slots + 1, :slots].astype(jnp.float32))
        right_ids[base + n : base + around, :] = kept_ids[cut : cut + half, :]
    total = 2 * around

    def turn(index, best):
        at = pl.multiple_of(index * step, step)
        scores = masked(
            left[...], left_ids[...], right[pl.ds(at, step), :], right_ids[pl.ds(at, step), :]
        )
        right_best[pl.ds(at, step), :] = lane_fold(scores)
        return jnp.maximum(best, column_fold(scores))

    best = lax.fori_loop(
        0, total // step, turn, jnp.full((8, left.shape[0]), FILL, jnp.float32)
    )
    left_best[...] = jnp.max(best, axis=0, keepdims=True)
    count = parts * slots
    left_best[:, :count] = jnp.maximum(left_best[:, :count], best_ref[...])
    visit = jnp.max(jnp.transpose(right_best[...]), axis=0, keepdims=True)
    mine, me_member, width = place_ref[0], place_ref[1], members
    out_ref[...] = jnp.full(out_ref.shape, FILL, jnp.float32)
    for member in range(members):
        whose = lax.bitwise_xor(me_member, member)
        for k in range(parts):
            source = lax.rem(mine - k + parts, parts)
            at = (member * parts + k) * slots
            out_ref[source * width + whose, :, :slots] = left_best[:, at : at + slots]
    for base, offset, kept in ((0, -1, parts - 1), (around, 1, 1)):
        order = [k for k in range(parts) if k != kept] + [kept]
        for index, k in enumerate(order):
            source = lax.rem(mine + offset - k + 2 * parts, parts)
            at = base + index * half
            lane = slots if base == 0 else slots + half
            out_ref[source * width + me_member, :, lane : lane + half] = visit[:, at : at + half]


def border_best(place, quarter, tails, own_tail, heads, own_head, best, parts):
    members = len(quarter) // parts
    slots, width = quarter[0].shape[0] - TAGS, quarter[0].shape[1]
    total, around = slots * len(quarter), parts * slots
    return pl.pallas_call(
        functools.partial(border_kernel, parts, members, 128),
        out_shape=jax.ShapeDtypeStruct((parts * members, 1, 2 * slots), jnp.float32),
        in_specs=[SCALARS] + [WHOLE] * (len(quarter) + 5),
        out_specs=WHOLE,
        scratch_shapes=[
            pltpu.VMEM((total, width), jnp.bfloat16),
            pltpu.VMEM((TAGS, total), jnp.float32),
            pltpu.VMEM((around, width), jnp.bfloat16),
            pltpu.VMEM((around, LANES), jnp.float32),
            pltpu.VMEM((around, LANES), jnp.float32),
            pltpu.VMEM((1, total), jnp.float32),
        ],
        compiler_params=pltpu.CompilerParams(vmem_limit_bytes=VMEM),
        cost_estimate=pl.CostEstimate(
            flops=2 * around * total * width, bytes_accessed=2 * total * width, transcendentals=0
        ),
        name="border",
    )(place, *quarter, tails, own_tail, heads, own_head, best)


def back_kernel(parts, members, got_ref, rank_ref, out_ref):
    slots = got_ref.shape[2] // 2
    half = slots // 2
    rows = []
    for part in range(parts):
        best = got_ref[part * members]
        for member in range(1, members):
            best = jnp.maximum(best, got_ref[part * members + member])
        rows.append(best)
    rank = rank_ref[...]
    nothing = jnp.full((1, half), FILL, jnp.float32)
    best = jnp.full((8, rank.shape[1]), FILL, jnp.float32)
    for part in range(parts):
        heads = rows[part - 1][:, slots + half :] if part > 0 else nothing
        tails = rows[part + 1][:, slots : slots + half] if part < parts - 1 else nothing
        values = jnp.maximum(rows[part][:, :slots], jnp.concatenate([heads, tails], axis=1))
        slot = lax.broadcasted_iota(jnp.int32, (slots, rank.shape[1]), 0) + part * slots
        found = jnp.where(slot == rank, spread(values)[:, :1], FILL)
        best = jnp.maximum(best, column_fold(found))
    out_ref[...] = jnp.max(best, axis=0, keepdims=True)


def in_data_order(got, rank, parts, members):
    return pl.pallas_call(
        functools.partial(back_kernel, parts, members),
        out_shape=jax.ShapeDtypeStruct(rank.shape, jnp.float32),
        in_specs=[WHOLE, WHOLE],
        out_specs=WHOLE,
        compiler_params=pltpu.CompilerParams(vmem_limit_bytes=VMEM),
        name="back",
    )(got, rank)


def halves(pieces, first, half):
    slots = 2 * half
    start = 0 if first else half
    rows = [p[start : start + half] for p in pieces]
    tags = jnp.concatenate([p[slots:, start : start + half] for p in pieces], axis=1)
    tags = jnp.pad(tags, ((0, 0), (0, pieces[0].shape[1] - tags.shape[1])))
    return jnp.concatenate(rows + [tags], axis=0)


def body(embeddings, cluster_of, target_pos):
    blocks, cores = lax.axis_size("blk"), lax.axis_size("split")
    rows, width = embeddings.shape
    members = MOST // rows
    chips = members // cores
    parts = blocks // chips
    half = rows // parts // 2
    chip, core = lax.axis_index("blk"), lax.axis_index("split")
    place = jnp.stack([chip // chips, (chip % chips) * cores + core]).astype(jnp.int32)

    def along(array, shift, wrap):
        route = []
        for part in range(parts):
            goal = part + shift
            if wrap or 0 <= goal < parts:
                for c in range(chips):
                    route.append((part * chips + c, goal % parts * chips + c))
        return lax.ppermute(array, "blk", route)

    def chip_swap(array):
        return lax.ppermute(array, "blk", [(b, b ^ 1) for b in range(blocks)])

    def core_swap(array):
        return lax.ppermute(array, "split", [(c, c ^ 1) for c in range(cores)])

    *pieces, rank = in_order(place, embeddings, cluster_of, target_pos, parts)
    mine = [pieces[0]] + [along(pieces[k], k, True) for k in range(1, parts)]
    tails = along(halves([mine[k] for k in range(parts) if k != parts - 1], False, half), 1, False)
    heads = along(halves([mine[k] for k in range(parts) if k != 1], True, half), -1, False)
    over = [chip_swap(piece) for piece in mine]
    beside = [core_swap(piece) for piece in mine]
    across = [core_swap(piece) for piece in over]
    best = quarter_best(mine, beside + over + across)
    found = border_best(
        place, mine + beside + over + across, tails, pieces[parts - 1], heads, pieces[1], best, parts
    )
    got = lax.all_to_all(found, ("blk", "split"), split_axis=0, concat_axis=0, tiled=True)
    return in_data_order(got, rank, parts, members).reshape(rows)


def solution(mesh):
    spec = P(("groups", "blk", "split"))
    return jax.shard_map(
        body,
        mesh=mesh,
        in_specs=(P(("groups", "blk", "split"), None), spec, spec),
        out_specs=spec,
        check_vma=False,
    )
```

time: 204 us -> 129 us (0.63)
  waiting for transfers between devices: 115 us -> 53.7 us
  Pallas kernels: 0 us -> 37.3 us
  local copies, waits for them, and re-layouts: 40.8 us -> 4.48 us
  other arithmetic: 12.3 us -> 0.17 us
  matrix products: 9.55 us -> 0 us
  starting transfers between devices: 16.9 us -> 21.8 us
    ppermute x13 -> x17, waiting for transfers between devices: 94 us -> 53.7 us  [the longest x5 28.3 us: along(): return lax.ppermute(array, 'blk', route)]
    pallas_call x0 -> x4, Pallas kernels: none -> 37.3 us  [the longest x1 19.6 us: border_best(): pl.pallas_call(functools.partial(border_kernel, parts, members, 128), out...]
    gather x6 -> x0, local copies, waits for them, and re-layouts: 27.3 us -> none  [the longest x1 5.21 us: body(): packed = unit[order].reshape(count, piece, width)]
    all_to_all x2 -> x0, waiting for transfers between devices: 20.8 us -> none  [the longest x1 20.3 us: body(): lax.all_to_all(packed, ('blk', 'split'), split_axis=0, concat_axis=0, til...]
    ppermute x13 -> x17, starting transfers between devices: 3.92 us -> 21.8 us  [the longest x5 15.5 us: along(): return lax.ppermute(array, 'blk', route)]
    all_to_all x2 -> x0, starting transfers between devices: 12.9 us -> none  [the longest x1 7.39 us: body(): lax.all_to_all(labels, ('blk', 'split'), split_axis=0, concat_axis=0, til...]
    dot_general x5 -> x0, matrix products: 9.55 us -> none  [masked_scores(): lax.dot_general(left, right, (((1,), (1,)), ((), ())), preferred_element_...]
    sort x2 -> x0, other arithmetic: 9.49 us -> none  [the longest x1 5.12 us: body(): order = jnp.argsort(target_pos)]
  transfers between devices with their start and end apart: 15 -> 17, of which waited for: 7 -> 6; matrix products, arithmetic and copies ran while one was open for 15% -> 0% of each run, Pallas kernels for 0% -> 10%
where the time goes in v1:
time: 129 us
  waiting for transfers between devices  53.7 us (42%)
  Pallas kernels  37.3 us (29%)
  starting transfers between devices  21.8 us (17%)
  blocking collectives  11.2 us (9%)
  local copies, waits for them, and re-layouts  4.48 us (3%)
    ppermute x5, waiting for transfers between devices, along(): return lax.ppermute(array, 'blk', route)  28.3 us
    ppermute x4, waiting for transfers between devices, chip_swap(): return lax.ppermute(array, 'blk', [(b, b ^ 1) for b in range(blocks)])  25.3 us
    pallas_call x1, Pallas kernels, border_best(): pl.pallas_call(functools.partial(border_kernel, parts, members, 128), out...  19.6 us
    ppermute x5, starting transfers between devices, along(): return lax.ppermute(array, 'blk', route)  15.5 us
    pallas_call x1, Pallas kernels, quarter_best(): pl.pallas_call(functools.partial(quarter_kernel, len(own), len(rest), 256...  12.5 us
    all_to_all x1, blocking collectives, body(): lax.all_to_all(found, ('blk', 'split'), split_axis=0, concat_axis=0, tile...  11.2 us
    ppermute x4, starting transfers between devices, chip_swap(): return lax.ppermute(array, 'blk', [(b, b ^ 1) for b in range(blocks)])  5.18 us
    unnamed x16, local copies, waits for them, and re-layouts  4.39 us
  transfers between devices with their start and end apart: 17, of which 6 were waited for; matrix products, arithmetic and copies ran while one was open for 0% of the time, Pallas kernels for 10%

profile of v1, /device:TPU:0, one launch (start us, length us, event | category | flops | bytes accessed | tf_op | source)
XLA Modules:
  0.0 128.8 jit_solution(4684596657698608918)
XLA Ops:
  0.0 0.1 pad_add_fusion.place_ref
  0.1 0.0 copy-start
  0.1 1.4 %copy-done = bf16[1024,768]{1,0:T(8,128)(2,1)S(1)} copy-done((bf16[1024,768]{1,0:T(8,128)(2,1)S(1)}, bf16[1024,768]{1,0:T(8,128)(2,1)}, u32[]{:S(2)}) %copy-start) | copy-done | bytes 1572888
  1.5 0.0 copy-start.3
  1.5 0.7 copy-done.3
  2.2 0.0 copy-start.4
  2.2 0.7 copy-done.4
  2.9 3.9 %order.1 = (bf16[264,768]{1,0:T(8,128)(2,1)S(1)}, bf16[264,768]{1,0:T(8,128)(2,1)S(1)}, bf16[264,768]{1,0:T(8,128)(2,1)S(1)}, bf16[264,768]{1,0:T(8,128)(2,1)S(1)}, s32[1,1024]{1,0:T(1,128)S(1)}) custom-call(s32[2]{0:T(128)S(1)} %pad_add_fusion.place_ref, bf16[1024,768]{1,0:T(8,128)(2,1)S(1)} %copy-done, s32[1,1024]{1,0:T(1,128)S(1)} %bitcast.5, ...), custom_call_target="tpu_custom_call" | custom-call | flops 1610612736 | bytes 3145728 | tf_op jit(solution)/shard_map/order/pallas_call | solution.py:72
  6.8 0.0 copy-start.1
  6.8 0.0 copy-start.2
  6.8 0.5 collective-permute-start.3
  7.3 2.6 %collective-permute-start.7 = (bf16[264,768]{1,0:T(8,128)(2,1)S(1)}, bf16[264,768]{1,0:T(8,128)(2,1)S(1)}, u32[]{:S(2)}, u32[]{:S(2)}) collective-permute-start(bf16[264,768]{1,0:T(8,128)(2,1)S(1)} %get-tuple-element.10.refs_0_), channel_id=1, source_target_pairs={{0,2},{2,0},{4,6},{6,4},{8,10},{10,8},{12,14},{14,12},{1,3},{3,1},... | collective-permute-start | bytes 1216520 | tf_op jit(solution)/shard_map/ppermute | solution.py:302
  9.9 1.6 %collective-permute-start = (bf16[264,768]{1,0:T(8,128)(2,1)S(1)}, bf16[264,768]{1,0:T(8,128)(2,1)S(1)}, u32[]{:S(2)}, u32[]{:S(2)}) collective-permute-start(bf16[264,768]{1,0:T(8,128)(2,1)S(1)} %get-tuple-element.11.refs_19_), channel_id=1, source_target_pairs={{0,4},{2,6},{4,8},{6,10},{8,12},{10,14},{12,0},{14,2},{1,5},{3,7},... | collective-permute-start | bytes 1216520 | tf_op jit(solution)/shard_map/ppermute | solution.py:299
  11.5 2.6 %collective-permute-start.1 = (bf16[264,768]{1,0:T(8,128)(2,1)S(1)}, bf16[264,768]{1,0:T(8,128)(2,1)S(1)}, u32[]{:S(2)}, u32[]{:S(2)}) collective-permute-start(bf16[264,768]{1,0:T(8,128)(2,1)S(1)} %get-tuple-element.12), channel_id=1, source_target_pairs={{0,8},{2,10},{4,12},{6,14},{8,0},{10,2},{12,4},{14,6},{1,9},{3,11}... | collective-permute-start | bytes 1216520 | tf_op jit(solution)/shard_map/ppermute | solution.py:299
  14.1 1.3 %collective-permute-start.2 = (bf16[264,768]{1,0:T(8,128)(2,1)S(1)}, bf16[264,768]{1,0:T(8,128)(2,1)S(1)}, u32[]{:S(2)}, u32[]{:S(2)}) collective-permute-start(bf16[264,768]{1,0:T(8,128)(2,1)S(1)} %get-tuple-element.13.refs_17_), channel_id=1, source_target_pairs={{0,12},{2,14},{4,0},{6,2},{8,4},{10,6},{12,8},{14,10},{1,13},{3,15... | collective-permute-start | bytes 1216520 | tf_op jit(solution)/shard_map/ppermute | solution.py:299
  15.4 8.6 %collective-permute-done.refs_1_ = bf16[264,768]{1,0:T(8,128)(2,1)S(1)} collective-permute-done((bf16[264,768]{1,0:T(8,128)(2,1)S(1)}, bf16[264,768]{1,0:T(8,128)(2,1)S(1)}, u32[]{:S(2)}, u32[]{:S(2)}) %collective-permute-start) | collective-permute-done | bytes 405536 | tf_op jit(solution)/shard_map/ppermute | solution.py:299
  24.0 0.0 collective-permute-start.4
  24.0 16.7 %collective-permute-done.1.refs_2_ = bf16[264,768]{1,0:T(8,128)(2,1)S(1)} collective-permute-done((bf16[264,768]{1,0:T(8,128)(2,1)S(1)}, bf16[264,768]{1,0:T(8,128)(2,1)S(1)}, u32[]{:S(2)}, u32[]{:S(2)}) %collective-permute-start.1) | collective-permute-done | bytes 405536 | tf_op jit(solution)/shard_map/ppermute | solution.py:299
  40.7 0.5 collective-permute-start.8
  41.2 0.0 collective-permute-done.2.refs_3_
  41.2 0.0 collective-permute-start.5
  41.2 0.0 collective-permute-done.3.refs_4_
  41.2 1.6 %collective-permute-start.9 = (bf16[264,768]{1,0:T(8,128)(2,1)S(1)}, bf16[264,768]{1,0:T(8,128)(2,1)S(1)}, u32[]{:S(2)}, u32[]{:S(2)}) collective-permute-start(bf16[264,768]{1,0:T(8,128)(2,1)S(1)} %collective-permute-done.1.refs_2_), channel_id=1, source_target_pairs={{0,2},{2,0},{4,6},{6,4},{8,10},{10,8},{12,14},{14,12},{1,3},{3,1},... | collective-permute-start | bytes 1216520 | tf_op jit(solution)/shard_map/ppermute | solution.py:302
  42.8 0.0 collective-permute-done.7.refs_8_
  42.8 0.5 collective-permute-start.10
  43.4 0.0 collective-permute-done.4.refs_5_
  43.4 0.1 collective-permute-start.6
  43.5 0.0 collective-permute-done.5.refs_6_
  43.5 0.5 collective-permute-start.11
  44.0 9.0 %collective-permute-done.8.refs_9_ = bf16[264,768]{1,0:T(8,128)(2,1)S(1)} collective-permute-done((bf16[264,768]{1,0:T(8,128)(2,1)S(1)}, bf16[264,768]{1,0:T(8,128)(2,1)S(1)}, u32[]{:S(2)}, u32[]{:S(2)}) %collective-permute-start.8) | collective-permute-done | bytes 405536 | tf_op jit(solution)/shard_map/ppermute | solution.py:302
  53.0 0.0 collective-permute-start.12
  53.0 8.7 %collective-permute-done.9.refs_10_ = bf16[264,768]{1,0:T(8,128)(2,1)S(1)} collective-permute-done((bf16[264,768]{1,0:T(8,128)(2,1)S(1)}, bf16[264,768]{1,0:T(8,128)(2,1)S(1)}, u32[]{:S(2)}, u32[]{:S(2)}) %collective-permute-start.9) | collective-permute-done | bytes 405536 | tf_op jit(solution)/shard_map/ppermute | solution.py:302
  61.7 0.0 collective-permute-start.13
  61.7 7.6 %collective-permute-done.10.refs_11_ = bf16[264,768]{1,0:T(8,128)(2,1)S(1)} collective-permute-done((bf16[264,768]{1,0:T(8,128)(2,1)S(1)}, bf16[264,768]{1,0:T(8,128)(2,1)S(1)}, u32[]{:S(2)}, u32[]{:S(2)}) %collective-permute-start.10) | collective-permute-done | bytes 405536 | tf_op jit(solution)/shard_map/ppermute | solution.py:302
  69.3 0.0 collective-permute-start.14
  69.4 0.0 copy-done.1
  69.4 0.0 copy-done.2
  69.5 0.0 collective-permute-done.6.refs_7_
  69.5 8.7 %collective-permute-start.15 = (bf16[392,768]{1,0:T(8,128)(2,1)S(1)}, bf16[392,768]{1,0:T(8,128)(2,1)S(1)}, u32[]{:S(2)}, u32[]{:S(2)}) collective-permute-start(bf16[392,768]{1,0:T(8,128)(2,1)S(1)} %pad_maximum_fusion), channel_id=1, source_target_pairs={{0,4},{2,6},{4,8},{6,10},{8,12},{10,14},{1,5},{3,7},{5,9},{7,11},{... | collective-permute-start | bytes 1806344 | tf_op jit(solution)/shard_map/ppermute | solution.py:299
  78.2 0.0 collective-permute-done.11.refs_12_
  78.2 1.3 %collective-permute-start.16 = (bf16[392,768]{1,0:T(8,128)(2,1)S(1)}, bf16[392,768]{1,0:T(8,128)(2,1)S(1)}, u32[]{:S(2)}, u32[]{:S(2)}) collective-permute-start(bf16[392,768]{1,0:T(8,128)(2,1)S(1)} %pad_maximum_fusion.1), channel_id=1, source_target_pairs={{4,0},{6,2},{8,4},{10,6},{12,8},{14,10},{5,1},{7,3},{9,5},{11,7},{... | collective-permute-start | bytes 1806344 | tf_op jit(solution)/shard_map/ppermute | solution.py:299
  79.5 0.0 collective-permute-done.12.refs_13_
  79.6 0.0 collective-permute-done.13.refs_14_
  79.6 0.0 collective-permute-done.14.refs_15_
  79.6 0.0 copy-start.7
  79.6 0.7 copy-done.7
  80.3 12.5 %quarter.1.refs_20_ = f32[1,1024]{1,0:T(1,128)S(1)} custom-call(bf16[264,768]{1,0:T(8,128)(2,1)S(1)} %get-tuple-element.10.refs_0_, bf16[264,768]{1,0:T(8,128)(2,1)S(1)} %collective-permute-done.refs_1_, bf16[264,768]{1,0:T(8,128)(2,1)S(1)} %collective-permute-done.1.refs_2_, bf16[264,768]{1,0:T(8,128)(2,1)S(1)} %collective-permute-done.2.refs_3_, ...), custom_call_target="tpu_custom_call" | custom-call | flops 6442450944 | bytes 6291456 | tf_op jit(solution)/shard_map/quarter/pallas_call | solution.py:146
  92.8 0.0 collective-permute-done.15.refs_16_
  92.8 0.0 copy-start.5
  92.8 3.0 %collective-permute-done.16.refs_18_ = bf16[392,768]{1,0:T(8,128)(2,1)S(1)} collective-permute-done((bf16[392,768]{1,0:T(8,128)(2,1)S(1)}, bf16[392,768]{1,0:T(8,128)(2,1)S(1)}, u32[]{:S(2)}, u32[]{:S(2)}) %collective-permute-start.16) | collective-permute-done | bytes 602144 | tf_op jit(solution)/shard_map/ppermute | solution.py:299
  95.9 0.0 copy-done.5
  95.9 0.0 copy-start.6
  95.9 0.8 copy-done.6
  96.7 19.6 %border.1 = f32[16,1,512]{2,1,0:T(1,128)S(1)} custom-call(s32[2]{0:T(128)S(1)} %pad_add_fusion.place_ref, bf16[264,768]{1,0:T(8,128)(2,1)S(1)} %get-tuple-element.10.refs_0_, bf16[264,768]{1,0:T(8,128)(2,1)S(1)} %collective-permute-done.refs_1_, bf16[264,768]{1,0:T(8,128)(2,1)S(1)} %collective-permute-done.1.refs_2_, ...), custom_call_target="tpu_custom_call" | custom-call | flops 6442450944 | bytes 6291456 | tf_op jit(solution)/shard_map/border/pallas_call | solution.py:219
  116.3 11.2 %all_to_all.5.got_ref = f32[16,1,512]{2,1,0:T(1,128)S(1)} all-to-all(f32[16,1,512]{2,1,0:T(1,128)S(1)} %border.1), channel_id=1, replica_groups=mesh['groups'=2,'blk'=8,'split'=2] {'blk','split'}, dimensions={0} | all-to-all | bytes 65536 | tf_op jit(solution)/shard_map/all_to_all | solution.py:318
  127.5 1.3 %back.1 = f32[1,1024]{1,0:T(1,128)} custom-call(f32[16,1,512]{2,1,0:T(1,128)S(1)} %all_to_all.5.got_ref, s32[1,1024]{1,0:T(1,128)S(1)} %get-tuple-element.14.rank_ref), custom_call_target="tpu_custom_call" | custom-call | tf_op jit(solution)/shard_map/back/pallas_call | solution.py:263
  (12 shorter events, 0.2 us)
Async XLA Ops:
  0.1 1.4 %copy-start = (bf16[1024,768]{1,0:T(8,128)(2,1)S(1)}, bf16[1024,768]{1,0:T(8,128)(2,1)}, u32[]{:S(2)}) copy-start(bf16[1024,768]{1,0:T(8,128)(2,1)} %rows_ref.1) | copy-start | bytes 4718596
  1.5 0.7 copy-start.3
  2.2 0.7 copy-start.4
  6.8 62.6 %copy-start.1 = (bf16[264,768]{1,0:T(8,128)(2,1)}, bf16[264,768]{1,0:T(8,128)(2,1)S(1)}, u32[]{:S(2)}) copy-start(bf16[264,768]{1,0:T(8,128)(2,1)S(1)} %get-tuple-element.11.refs_19_) | copy-start | bytes 1216516
  6.8 62.6 %copy-start.2 = (bf16[264,768]{1,0:T(8,128)(2,1)}, bf16[264,768]{1,0:T(8,128)(2,1)S(1)}, u32[]{:S(2)}) copy-start(bf16[264,768]{1,0:T(8,128)(2,1)S(1)} %get-tuple-element.13.refs_17_) | copy-start | bytes 1216516
  6.8 34.5 %collective-permute-start.3 = (bf16[264,768]{1,0:T(8,128)(2,1)S(1)}, bf16[264,768]{1,0:T(8,128)(2,1)S(1)}, u32[]{:S(2)}, u32[]{:S(2)}) collective-permute-start(bf16[264,768]{1,0:T(8,128)(2,1)S(1)} %get-tuple-element.10.refs_0_), channel_id=1, source_target_pairs={{0,1},{1,0},{2,3},{3,2},{4,5},{5,4},{6,7},{7,6},{8,9},{9,8},{10,11... | collective-permute-start | bytes 1216520 | tf_op jit(solution)/shard_map/ppermute | solution.py:305
  7.3 35.5 %collective-permute-start.7 = (bf16[264,768]{1,0:T(8,128)(2,1)S(1)}, bf16[264,768]{1,0:T(8,128)(2,1)S(1)}, u32[]{:S(2)}, u32[]{:S(2)}) collective-permute-start(bf16[264,768]{1,0:T(8,128)(2,1)S(1)} %get-tuple-element.10.refs_0_), channel_id=1, source_target_pairs={{0,2},{2,0},{4,6},{6,4},{8,10},{10,8},{12,14},{14,12},{1,3},{3,1},... | collective-permute-start | bytes 1216520 | tf_op jit(solution)/shard_map/ppermute | solution.py:302
  9.9 14.2 %collective-permute-start = (bf16[264,768]{1,0:T(8,128)(2,1)S(1)}, bf16[264,768]{1,0:T(8,128)(2,1)S(1)}, u32[]{:S(2)}, u32[]{:S(2)}) collective-permute-start(bf16[264,768]{1,0:T(8,128)(2,1)S(1)} %get-tuple-element.11.refs_19_), channel_id=1, source_target_pairs={{0,4},{2,6},{4,8},{6,10},{8,12},{10,14},{12,0},{14,2},{1,5},{3,7},... | collective-permute-start | bytes 1216520 | tf_op jit(solution)/shard_map/ppermute | solution.py:299
  11.5 29.3 %collective-permute-start.1 = (bf16[264,768]{1,0:T(8,128)(2,1)S(1)}, bf16[264,768]{1,0:T(8,128)(2,1)S(1)}, u32[]{:S(2)}, u32[]{:S(2)}) collective-permute-start(bf16[264,768]{1,0:T(8,128)(2,1)S(1)} %get-tuple-element.12), channel_id=1, source_target_pairs={{0,8},{2,10},{4,12},{6,14},{8,0},{10,2},{12,4},{14,6},{1,9},{3,11}... | collective-permute-start | bytes 1216520 | tf_op jit(solution)/shard_map/ppermute | solution.py:299
  14.1 27.2 %collective-permute-start.2 = (bf16[264,768]{1,0:T(8,128)(2,1)S(1)}, bf16[264,768]{1,0:T(8,128)(2,1)S(1)}, u32[]{:S(2)}, u32[]{:S(2)}) collective-permute-start(bf16[264,768]{1,0:T(8,128)(2,1)S(1)} %get-tuple-element.13.refs_17_), channel_id=1, source_target_pairs={{0,12},{2,14},{4,0},{6,2},{8,4},{10,6},{12,8},{14,10},{1,13},{3,15... | collective-permute-start | bytes 1216520 | tf_op jit(solution)/shard_map/ppermute | solution.py:299
  24.0 19.3 %collective-permute-start.4 = (bf16[264,768]{1,0:T(8,128)(2,1)S(1)}, bf16[264,768]{1,0:T(8,128)(2,1)S(1)}, u32[]{:S(2)}, u32[]{:S(2)}) collective-permute-start(bf16[264,768]{1,0:T(8,128)(2,1)S(1)} %collective-permute-done.refs_1_), channel_id=1, source_target_pairs={{0,1},{1,0},{2,3},{3,2},{4,5},{5,4},{6,7},{7,6},{8,9},{9,8},{10,11... | collective-permute-start | bytes 1216520 | tf_op jit(solution)/shard_map/ppermute | solution.py:305
  40.7 12.3 %collective-permute-start.8 = (bf16[264,768]{1,0:T(8,128)(2,1)S(1)}, bf16[264,768]{1,0:T(8,128)(2,1)S(1)}, u32[]{:S(2)}, u32[]{:S(2)}) collective-permute-start(bf16[264,768]{1,0:T(8,128)(2,1)S(1)} %collective-permute-done.refs_1_), channel_id=1, source_target_pairs={{0,2},{2,0},{4,6},{6,4},{8,10},{10,8},{12,14},{14,12},{1,3},{3,1},... | collective-permute-start | bytes 1216520 | tf_op jit(solution)/shard_map/ppermute | solution.py:302
  41.2 2.2 %collective-permute-start.5 = (bf16[264,768]{1,0:T(8,128)(2,1)S(1)}, bf16[264,768]{1,0:T(8,128)(2,1)S(1)}, u32[]{:S(2)}, u32[]{:S(2)}) collective-permute-start(bf16[264,768]{1,0:T(8,128)(2,1)S(1)} %collective-permute-done.1.refs_2_), channel_id=1, source_target_pairs={{0,1},{1,0},{2,3},{3,2},{4,5},{5,4},{6,7},{7,6},{8,9},{9,8},{10,11... | collective-permute-start | bytes 1216520 | tf_op jit(solution)/shard_map/ppermute | solution.py:305
  41.2 20.4 %collective-permute-start.9 = (bf16[264,768]{1,0:T(8,128)(2,1)S(1)}, bf16[264,768]{1,0:T(8,128)(2,1)S(1)}, u32[]{:S(2)}, u32[]{:S(2)}) collective-permute-start(bf16[264,768]{1,0:T(8,128)(2,1)S(1)} %collective-permute-done.1.refs_2_), channel_id=1, source_target_pairs={{0,2},{2,0},{4,6},{6,4},{8,10},{10,8},{12,14},{14,12},{1,3},{3,1},... | collective-permute-start | bytes 1216520 | tf_op jit(solution)/shard_map/ppermute | solution.py:302
  42.8 26.5 %collective-permute-start.10 = (bf16[264,768]{1,0:T(8,128)(2,1)S(1)}, bf16[264,768]{1,0:T(8,128)(2,1)S(1)}, u32[]{:S(2)}, u32[]{:S(2)}) collective-permute-start(bf16[264,768]{1,0:T(8,128)(2,1)S(1)} %collective-permute-done.2.refs_3_), channel_id=1, source_target_pairs={{0,2},{2,0},{4,6},{6,4},{8,10},{10,8},{12,14},{14,12},{1,3},{3,1},... | collective-permute-start | bytes 1216520 | tf_op jit(solution)/shard_map/ppermute | solution.py:302
  43.4 26.1 %collective-permute-start.6 = (bf16[264,768]{1,0:T(8,128)(2,1)S(1)}, bf16[264,768]{1,0:T(8,128)(2,1)S(1)}, u32[]{:S(2)}, u32[]{:S(2)}) collective-permute-start(bf16[264,768]{1,0:T(8,128)(2,1)S(1)} %collective-permute-done.2.refs_3_), channel_id=1, source_target_pairs={{0,1},{1,0},{2,3},{3,2},{4,5},{5,4},{6,7},{7,6},{8,9},{9,8},{10,11... | collective-permute-start | bytes 1216520 | tf_op jit(solution)/shard_map/ppermute | solution.py:305
  43.5 34.8 %collective-permute-start.11 = (bf16[264,768]{1,0:T(8,128)(2,1)S(1)}, bf16[264,768]{1,0:T(8,128)(2,1)S(1)}, u32[]{:S(2)}, u32[]{:S(2)}) collective-permute-start(bf16[264,768]{1,0:T(8,128)(2,1)S(1)} %collective-permute-done.7.refs_8_), channel_id=1, source_target_pairs={{0,1},{1,0},{2,3},{3,2},{4,5},{5,4},{6,7},{7,6},{8,9},{9,8},{10,11... | collective-permute-start | bytes 1216520 | tf_op jit(solution)/shard_map/ppermute | solution.py:305
  53.0 26.6 %collective-permute-start.12 = (bf16[264,768]{1,0:T(8,128)(2,1)S(1)}, bf16[264,768]{1,0:T(8,128)(2,1)S(1)}, u32[]{:S(2)}, u32[]{:S(2)}) collective-permute-start(bf16[264,768]{1,0:T(8,128)(2,1)S(1)} %collective-permute-done.8.refs_9_), channel_id=1, source_target_pairs={{0,1},{1,0},{2,3},{3,2},{4,5},{5,4},{6,7},{7,6},{8,9},{9,8},{10,11... | collective-permute-start | bytes 1216520 | tf_op jit(solution)/shard_map/ppermute | solution.py:305
  61.7 17.9 %collective-permute-start.13 = (bf16[264,768]{1,0:T(8,128)(2,1)S(1)}, bf16[264,768]{1,0:T(8,128)(2,1)S(1)}, u32[]{:S(2)}, u32[]{:S(2)}) collective-permute-start(bf16[264,768]{1,0:T(8,128)(2,1)S(1)} %collective-permute-done.9.refs_10_), channel_id=1, source_target_pairs={{0,1},{1,0},{2,3},{3,2},{4,5},{5,4},{6,7},{7,6},{8,9},{9,8},{10,11... | collective-permute-start | bytes 1216520 | tf_op jit(solution)/shard_map/ppermute | solution.py:305
  69.3 10.3 %collective-permute-start.14 = (bf16[264,768]{1,0:T(8,128)(2,1)S(1)}, bf16[264,768]{1,0:T(8,128)(2,1)S(1)}, u32[]{:S(2)}, u32[]{:S(2)}) collective-permute-start(bf16[264,768]{1,0:T(8,128)(2,1)S(1)} %collective-permute-done.10.refs_11_), channel_id=1, source_target_pairs={{0,1},{1,0},{2,3},{3,2},{4,5},{5,4},{6,7},{7,6},{8,9},{9,8},{10,11... | collective-permute-start | bytes 1216520 | tf_op jit(solution)/shard_map/ppermute | solution.py:305
  69.5 23.3 %collective-permute-start.15 = (bf16[392,768]{1,0:T(8,128)(2,1)S(1)}, bf16[392,768]{1,0:T(8,128)(2,1)S(1)}, u32[]{:S(2)}, u32[]{:S(2)}) collective-permute-start(bf16[392,768]{1,0:T(8,128)(2,1)S(1)} %pad_maximum_fusion), channel_id=1, source_target_pairs={{0,4},{2,6},{4,8},{6,10},{8,12},{10,14},{1,5},{3,7},{5,9},{7,11},{... | collective-permute-start | bytes 1806344 | tf_op jit(solution)/shard_map/ppermute | solution.py:299
  78.2 17.6 %collective-permute-start.16 = (bf16[392,768]{1,0:T(8,128)(2,1)S(1)}, bf16[392,768]{1,0:T(8,128)(2,1)S(1)}, u32[]{:S(2)}, u32[]{:S(2)}) collective-permute-start(bf16[392,768]{1,0:T(8,128)(2,1)S(1)} %pad_maximum_fusion.1), channel_id=1, source_target_pairs={{4,0},{6,2},{8,4},{10,6},{12,8},{14,10},{5,1},{7,3},{9,5},{11,7},{... | collective-permute-start | bytes 1806344 | tf_op jit(solution)/shard_map/ppermute | solution.py:299
  79.6 0.8 copy-start.7
  92.8 3.0 %copy-start.5 = (bf16[392,768]{1,0:T(8,128)(2,1)}, bf16[392,768]{1,0:T(8,128)(2,1)S(1)}, u32[]{:S(2)}) copy-start(bf16[392,768]{1,0:T(8,128)(2,1)S(1)} %collective-permute-done.15.refs_16_) | copy-start | bytes 1806340
  95.9 0.8 copy-start.6

commit v2 on v1

v2 whole, which is shorter than its diff:
```python
import functools

import jax
import jax.numpy as jnp
from jax import lax
from jax.experimental import pallas as pl
from jax.experimental.pallas import tpu as pltpu
from jax.sharding import PartitionSpec as P

MOST = 4096
FILL = -4.0
TAGS = 8
LANES = 128
MIB = 1024 * 1024
WHOLE = pl.BlockSpec(memory_space=pltpu.VMEM)
ANYWHERE = pl.BlockSpec(memory_space=pl.ANY)
SCALARS = pl.BlockSpec(memory_space=pltpu.SMEM)


def grant(mib):
    return pltpu.CompilerParams(vmem_limit_bytes=mib * MIB)


def spread(row):
    return jnp.transpose(jnp.broadcast_to(row, (LANES, row.shape[1])))


def column_fold(scores):
    rows, columns = scores.shape
    return jnp.max(scores.reshape(rows // 8, 8, columns), axis=0)


def lane_fold(scores):
    best = scores[:, :LANES]
    for at in range(LANES, scores.shape[1], LANES):
        best = jnp.maximum(best, scores[:, at : at + LANES])
    return best


def order_kernel(parts, place_ref, rows_ref, ids_ref, pos_ref, *refs):
    first, own, rank_ref = refs[:3]
    facing, turned = refs[3 : 1 + parts], refs[1 + parts : 2 * parts - 1]
    unit, pick, placed, tags = refs[2 * parts - 1 :]
    count, width = rows_ref.shape
    half = count // parts // 2
    step = 256
    values = rows_ref[...].astype(jnp.float32)
    total = jnp.sum(values * values, axis=1, keepdims=True)
    unit[...] = (values * lax.rsqrt(total + 1e-06)).astype(jnp.bfloat16)
    pos = pos_ref[...].astype(jnp.float32)
    below = jnp.zeros((8, count), jnp.float32)
    for at in range(0, count, step):
        other = spread(pos[:, at : at + step])[:, :1]
        below += jnp.sum(jnp.where(other < pos, 1.0, 0.0).reshape(step // 8, 8, count), axis=0)
    rank = jnp.sum(below, axis=0, keepdims=True).astype(jnp.int32)
    rank_ref[...] = rank
    for at in range(0, count, step):
        slot = lax.broadcasted_iota(jnp.int32, (step, count), 0) + at
        pick[at : at + step, :] = jnp.where(slot == rank, 1.0, 0.0).astype(jnp.bfloat16)
    for at in range(0, count, step):
        placed[at : at + step, :] = jnp.dot(
            pick[at : at + step, :], unit[...], preferred_element_type=jnp.float32
        ).astype(jnp.bfloat16)
    ids = jnp.broadcast_to((ids_ref[...] + 1).astype(jnp.bfloat16), (16, count))
    sorted_ids = lax.dot_general(
        ids, pick[...], (((1,), (1,)), ((), ())), preferred_element_type=jnp.float32
    )
    for at in range(2 * parts):
        tags[at, :, :half] = sorted_ids[:, at * half : (at + 1) * half]

    def put(out, at, quarter, faces):
        side = lax.rem(quarter, 2)
        which = 2 * quarter + (1 - side if faces else side)
        out[at : at + half, :] = placed[pl.ds(pl.multiple_of(which * half, half), half), :]
        out[out.shape[0] - TAGS :, at : at + half] = tags[which, :TAGS, :half].astype(jnp.bfloat16)

    part = place_ref[0]
    for out, quarter in ((first, lax.bitwise_xor(part, 1)), (own, part)):
        put(out, 0, quarter, True)
        put(out, half, quarter, False)
    put(first, 2 * half, part, True)
    for k in range(2, parts):
        put(facing[k - 2], 0, lax.bitwise_xor(part, k), True)
        put(turned[k - 2], 0, lax.bitwise_xor(part, k), False)


def in_order(place, embeddings, ids, pos, parts):
    count, width = embeddings.shape
    half = count // parts // 2

    def block(rows):
        return jax.ShapeDtypeStruct((rows + TAGS, width), jnp.bfloat16)

    outs = [block(3 * half), block(2 * half), jax.ShapeDtypeStruct((1, count), jnp.int32)]
    outs += [block(half)] * (2 * (parts - 2))
    first, own, rank, *rest = pl.pallas_call(
        functools.partial(order_kernel, parts),
        out_shape=outs,
        in_specs=[SCALARS, WHOLE, WHOLE, WHOLE],
        out_specs=[WHOLE] * len(outs),
        scratch_shapes=[
            pltpu.VMEM((count, width), jnp.bfloat16),
            pltpu.VMEM((count, count), jnp.bfloat16),
            pltpu.VMEM((count, width), jnp.bfloat16),
            pltpu.VMEM((2 * parts, 16, max(half, LANES)), jnp.float32),
        ],
        compiler_params=grant(24),
        name="order",
    )(place, embeddings, ids.reshape(1, count), pos.reshape(1, count))
    return first, own, rank, rest[: parts - 2], rest[parts - 2 :]


def pack_kernel(plan, inputs, *refs):
    given, outs = refs[:inputs], refs[-len(plan) :]
    for out, pieces in zip(outs, plan):
        at = 0
        for index, start, rows in pieces:
            ref = given[index]
            out[at : at + rows, :] = ref[start : start + rows, :]
            out[out.shape[0] - TAGS :, at : at + rows] = ref[
                ref.shape[0] - TAGS :, start : start + rows
            ]
            at += rows


def pack(blocks, plan, held=()):
    width = blocks[0].shape[1]
    plan = [list(pieces) for pieces in plan]
    outs = [
        jax.ShapeDtypeStruct((sum(p[2] for p in pieces) + TAGS, width), jnp.bfloat16)
        for pieces in plan
    ]
    kept = [jax.ShapeDtypeStruct(h.shape, h.dtype) for h in held]

    def kernel(*refs):
        given = refs[: len(blocks)]
        made = refs[len(blocks) + 2 * len(held) :]
        pack_kernel(plan, len(given), *given, *made)

    return pl.pallas_call(
        kernel,
        out_shape=kept + outs,
        in_specs=[WHOLE] * len(blocks) + [ANYWHERE] * len(held),
        out_specs=[ANYWHERE] * len(held) + [WHOLE] * len(outs),
        input_output_aliases={len(blocks) + i: i for i in range(len(held))},
        compiler_params=grant(8),
        name="pack",
    )(*blocks, *held)


def after(held, earlier):
    return pl.pallas_call(
        lambda *refs: None,
        out_shape=[jax.ShapeDtypeStruct(h.shape, h.dtype) for h in held],
        in_specs=[ANYWHERE] * (len(held) + len(earlier)),
        out_specs=[ANYWHERE] * len(held),
        input_output_aliases={i: i for i in range(len(held))},
        compiler_params=grant(1),
        name="after",
    )(*held, *earlier)


def meet_kernel(plan_left, plan_right, inputs, step, own, visits, *refs):
    given = refs[:inputs]
    left_out = refs[inputs]
    right_out = refs[inputs + 1] if visits else None
    left, left_ids, right, right_ids = refs[inputs + 1 + visits : inputs + 5 + visits]
    at = 0
    for index, start, rows in plan_left:
        ref = given[index]
        left[at : at + rows, :] = ref[start : start + rows, :]
        tags = ref[ref.shape[0] - TAGS :, start : start + rows]
        left_ids[:, at : at + rows] = tags.astype(jnp.float32)
        at += rows
    at = 0
    for index, start, rows in plan_right:
        ref = given[index]
        right[at : at + rows, :] = ref[start : start + rows, :]
        tags = ref[ref.shape[0] - TAGS : ref.shape[0] - TAGS + 1, start : start + rows]
        right_ids[at : at + rows, :] = spread(tags.astype(jnp.float32))
        at += rows
    count, total = left.shape[0], right.shape[0]

    def turn(index, best, diagonal):
        at = pl.multiple_of(index * step, step)
        scores = lax.dot_general(
            right[pl.ds(at, step), :],
            left[...],
            (((1,), (1,)), ((), ())),
            preferred_element_type=jnp.float32,
        )
        scores = jnp.where(right_ids[pl.ds(at, step), :1] == left_ids[:1, :], scores, FILL)
        if diagonal:
            down = lax.broadcasted_iota(jnp.int32, (step, count), 0) + at
            across = lax.broadcasted_iota(jnp.int32, (step, count), 1)
            scores = jnp.where(down == across, FILL, scores)
        if visits:
            refs[-1][pl.ds(at, step), :] = lane_fold(scores)
        return jnp.maximum(best, column_fold(scores))

    best = jnp.full((8, count), FILL, jnp.float32)
    split = count // step if own else 0
    if own:
        best = lax.fori_loop(0, split, functools.partial(turn, diagonal=True), best)
    best = lax.fori_loop(split, total // step, functools.partial(turn, diagonal=False), best)
    left_out[...] = jnp.max(best, axis=0, keepdims=True)
    if visits:
        right_out[...] = jnp.max(jnp.transpose(refs[-1][...]), axis=0, keepdims=True)


def meet(left, right, own=False, visits=False):
    blocks = []

    def plan(pieces):
        out = []
        for block, start, rows in pieces:
            known = [i for i, b in enumerate(blocks) if b is block]
            if not known:
                blocks.append(block)
            out.append((known[0] if known else len(blocks) - 1, start, rows))
        return out

    plan_left, plan_right = plan(left), plan(right)
    width = blocks[0].shape[1]
    count, total = sum(p[2] for p in left), sum(p[2] for p in right)
    step = 8
    while step < 512 and total % (2 * step) == 0 and (count % (2 * step) == 0 or not own):
        if 2 * step * count * 4 > 4 * MIB:
            break
        step *= 2
    scratch = [
        pltpu.VMEM((count, width), jnp.bfloat16),
        pltpu.VMEM((TAGS, count), jnp.float32),
        pltpu.VMEM((total, width), jnp.bfloat16),
        pltpu.VMEM((total, LANES), jnp.float32),
    ]
    outs = [jax.ShapeDtypeStruct((1, count), jnp.float32)]
    if visits:
        scratch.append(pltpu.VMEM((total, LANES), jnp.float32))
        outs.append(jax.ShapeDtypeStruct((1, total), jnp.float32))
    return pl.pallas_call(
        functools.partial(
            meet_kernel, plan_left, plan_right, len(blocks), step, own, visits
        ),
        out_shape=outs,
        in_specs=[WHOLE] * len(blocks),
        out_specs=[WHOLE] * len(outs),
        scratch_shapes=scratch,
        compiler_params=grant(32),
        cost_estimate=pl.CostEstimate(
            flops=2 * count * total * width, bytes_accessed=0, transcendentals=0
        ),
        name="meet",
    )(*blocks)


def route_kernel(parts, members, half, near, place_ref, *refs):
    own_a, own_b, before_u, before_v, last, u_before, v_before, visit_last, out_ref = refs
    part, me = place_ref[0], place_ref[1]
    slots = 2 * half
    rest = (parts - 2) * half
    early = 2 * slots + rest
    out_ref[...] = jnp.full(out_ref.shape, FILL, jnp.float32)
    quarter = jnp.maximum(before_u[...], before_v[...])
    final = last[...]
    own = jnp.maximum(own_a[...], own_b[...])
    for member in range(members):
        whose = lax.bitwise_xor(me, member)
        block = quarter[:, member * early : (member + 1) * early]
        tail = final[:, member * rest : (member + 1) * rest]
        if member == 0:
            block = jnp.maximum(block, own[:, :early])
            tail = jnp.maximum(tail, own[:, early:])
        for k in range(parts):
            source = lax.bitwise_xor(part, k) * members + whose
            if k < 2:
                out_ref[source, :, :slots] = block[:, k * slots : (k + 1) * slots]
            else:
                at = (k - 2) * half
                out_ref[source, :, :half] = block[:, 2 * slots + at : 2 * slots + at + half]
                out_ref[source, :, half:slots] = tail[:, at : at + half]
    size = parts * half
    visit_u = jnp.maximum(u_before[...], visit_last[:, :size])
    visit_v = jnp.maximum(v_before[...], visit_last[:, size:])
    beyond = lax.rem(part + parts - 1 + 2 * lax.rem(part, 2), parts)
    if near:
        beyond = lax.bitwise_xor(part, 3)
    next_to = lax.bitwise_xor(part, 1)
    from_u = [next_to] + [lax.bitwise_xor(next_to, k) for k in range(2, parts)] + [part]
    from_v = [beyond, lax.bitwise_xor(beyond, 1)]
    from_v += [next_to, part] if near else [lax.bitwise_xor(beyond, k) for k in range(2, parts)]
    for visit, sources, lane in ((visit_u, from_u, slots), (visit_v, from_v, slots + half)):
        for index, source in enumerate(sources):
            at = index * half
            out_ref[source * members + me, :, lane : lane + half] = visit[:, at : at + half]


def back_kernel(parts, members, got_ref, rank_ref, out_ref):
    slots = got_ref.shape[2] // 2
    half = slots // 2
    rows = []
    for part in range(parts):
        best = got_ref[part * members]
        for member in range(1, members):
            best = jnp.maximum(best, got_ref[part * members + member])
        rows.append(best)
    rank = rank_ref[...]
    nothing = jnp.full((1, half), FILL, jnp.float32)
    best = jnp.full((8, rank.shape[1]), FILL, jnp.float32)
    for part in range(parts):
        beyond = part + 1 if part % 2 else part - 1
        there = 0 <= beyond < parts
        faces = jnp.maximum(rows[part][:, :half], rows[part ^ 1][:, slots : slots + half])
        turned = jnp.maximum(
            rows[part][:, half:slots], rows[beyond][:, slots + half :] if there else nothing
        )
        pair = [faces, turned] if part % 2 else [turned, faces]
        values = spread(jnp.concatenate(pair, axis=1))[:, :1]
        slot = lax.broadcasted_iota(jnp.int32, (slots, rank.shape[1]), 0) + part * slots
        best = jnp.maximum(best, column_fold(jnp.where(slot == rank, values, FILL)))
    out_ref[...] = jnp.max(best, axis=0, keepdims=True)


def in_data_order(got, rank, parts, members):
    return pl.pallas_call(
        functools.partial(back_kernel, parts, members),
        out_shape=jax.ShapeDtypeStruct(rank.shape, jnp.float32),
        in_specs=[WHOLE, WHOLE],
        out_specs=WHOLE,
        compiler_params=grant(16),
        name="back",
    )(got, rank)


def body(embeddings, cluster_of, target_pos):
    blocks, cores = lax.axis_size("blk"), lax.axis_size("split")
    rows, width = embeddings.shape
    members = MOST // rows
    chips = members // cores
    parts = blocks // chips
    half = rows // parts // 2
    slots = 2 * half
    rest = (parts - 2) * half
    chip, core = lax.axis_index("blk"), lax.axis_index("split")
    place = jnp.stack([chip // chips, (chip % chips) * cores + core]).astype(jnp.int32)

    def between(array, pairs):
        route = [(s * chips + c, t * chips + c) for s, t in pairs for c in range(chips)]
        return lax.ppermute(array, "blk", route)

    def swap(array, k):
        return between(array, [(part, part ^ k) for part in range(parts)])

    def chip_swap(array):
        return lax.ppermute(array, "blk", [(b, b ^ 1) for b in range(blocks)])

    def core_swap(array):
        return lax.ppermute(array, "split", [(c, c ^ 1) for c in range(cores)])

    borders = [(p, p + 1) for p in range(1, parts - 1, 2)]
    borders += [(t, s) for s, t in borders]
    near = all(s ^ t == 3 for s, t in borders)

    first, own_0, rank, facing, turned = in_order(place, embeddings, cluster_of, target_pos, parts)
    got_first = swap(first, 1)
    got_facing = [swap(facing[k - 2], k) for k in range(2, parts)]
    over_0 = chip_swap(own_0)
    beside_0 = core_swap(own_0)

    *held, own_1, border = pack(
        [got_first, own_0],
        [[(0, 0, slots)], [(1, half, half), (0, half, half)]],
        held=turned,
    )
    got_turned = [swap(held[k - 2], k) for k in range(2, parts)]
    over_1 = chip_swap(own_1)
    beside_1 = core_swap(own_1)

    (own_2,) = pack(got_facing, [[(i, 0, half) for i in range(parts - 2)]])
    over_2 = chip_swap(own_2)
    beside_2 = core_swap(own_2)
    passed = swap(own_2, 1)

    (border,) = after([border], [over_2])
    got_border = between(border, borders)
    if near:
        got_more = between(held[0], [(t ^ 1, t) for _, t in borders])

    (own_3,) = pack(got_turned, [[(i, 0, half) for i in range(parts - 2)]])
    over_3 = chip_swap(own_3)
    beside_3 = core_swap(own_3)

    across_0, across_1, across_2, across_3 = (
        core_swap(over) for over in (over_0, over_1, over_2, over_3)
    )

    def early(*three):
        return [(b, 0, n) for b, n in zip(three, (slots, slots, rest))]

    mine = early(own_0, own_1, own_2) + [(own_3, 0, rest)]
    others = early(beside_0, beside_1, beside_2)
    others += early(over_0, over_1, over_2) + early(across_0, across_1, across_2)
    (own_a,) = meet(mine, mine + others, own=True)
    visit_u = [(got_first, slots, half), (passed, 0, rest), (first, 0, half)]
    visit_v = [(got_border, 0, slots)]
    if near:
        visit_v += [(got_more, 0, half), (turned[1], 0, half)]
    else:
        visit_v += [(between(own_3, borders), 0, rest)]
    quarter = early(own_0, own_1, own_2) + others
    before_u, u_before = meet(quarter, visit_u, visits=True)
    before_v, v_before = meet(quarter, visit_v, visits=True)
    late = [(b, 0, rest) for b in (own_3, beside_3, over_3, across_3)]
    (own_b,) = meet(mine, late[1:])
    last, visit_last = meet(late, visit_u + visit_v, visits=True)
    found = pl.pallas_call(
        functools.partial(route_kernel, parts, members, half, near),
        out_shape=jax.ShapeDtypeStruct((parts * members, 1, 2 * slots), jnp.float32),
        in_specs=[SCALARS] + [WHOLE] * 8,
        out_specs=WHOLE,
        compiler_params=grant(8),
        name="route",
    )(place, own_a, own_b, before_u, before_v, last, u_before, v_before, visit_last)
    got = lax.all_to_all(found, ("blk", "split"), split_axis=0, concat_axis=0, tiled=True)
    return in_data_order(got, rank, parts, members).reshape(rows)


def solution(mesh):
    spec = P(("groups", "blk", "split"))
    return jax.shard_map(
        body,
        mesh=mesh,
        in_specs=(P(("groups", "blk", "split"), None), spec, spec),
        out_specs=spec,
        check_vma=False,
    )
```

time: 129 us -> 99 us (0.77)
  waiting for transfers between devices: 53.7 us -> 30.9 us
  Pallas kernels: 37.3 us -> 26 us
  starting transfers between devices: 21.8 us -> 28.3 us
  local copies, waits for them, and re-layouts: 4.48 us -> 2.79 us
    ppermute x4, waiting for transfers between devices: 25.3 us -> 4.24 us  [chip_swap(): return lax.ppermute(array, 'blk', [(b, b ^ 1) for b in range(blocks)])]
    pallas_call x3 -> x11, Pallas kernels: 36 us -> 24.6 us  [the longest x5 20.2 us: meet(): pl.pallas_call(functools.partial(meet_kernel, plan_left, plan_right, len(...]
    ppermute x5 -> x8, starting transfers between devices: 15.5 us -> 22 us  [between(): return lax.ppermute(array, 'blk', route)]
    ppermute x5 -> x8, waiting for transfers between devices: 28.3 us -> 26.6 us  [between(): return lax.ppermute(array, 'blk', route)]
    unnamed x16 -> x7, local copies, waits for them, and re-layouts: 4.39 us -> 2.79 us
  transfers between devices with their start and end apart: 17 -> 20, of which waited for: 6 -> 4; matrix products, arithmetic and copies ran while one was open for 0% -> 0% of each run, Pallas kernels for 10% -> 16%
where the time goes in v2:
time: 99 us; the launch traced here: 98.8 us
  waiting for transfers between devices  30.9 us (31%)
  starting transfers between devices  28.3 us (29%)
  Pallas kernels  26 us (26%)
  blocking collectives  10.6 us (11%)
  local copies, waits for them, and re-layouts  2.79 us (3%)
    ppermute x8, waiting for transfers between devices, between(): return lax.ppermute(array, 'blk', route)  26.6 us
    ppermute x8, starting transfers between devices, between(): return lax.ppermute(array, 'blk', route)  22 us
    pallas_call x5, Pallas kernels, meet(): pl.pallas_call(functools.partial(meet_kernel, plan_left, plan_right, len(...  20.2 us
    all_to_all x1, blocking collectives, body(): lax.all_to_all(found, ('blk', 'split'), split_axis=0, concat_axis=0, tile...  10.6 us
    ppermute x4, starting transfers between devices, chip_swap(): return lax.ppermute(array, 'blk', [(b, b ^ 1) for b in range(blocks)])  5.2 us
    ppermute x4, waiting for transfers between devices, chip_swap(): return lax.ppermute(array, 'blk', [(b, b ^ 1) for b in range(blocks)])  4.24 us
    pallas_call x1, Pallas kernels, in_order(): pl.pallas_call(functools.partial(order_kernel, parts), out_shape=outs, in...  3.79 us
    unnamed x7, local copies, waits for them, and re-layouts  2.79 us
  transfers between devices with their start and end apart: 20, of which 4 were waited for; matrix products, arithmetic and copies ran while one was open for 0% of the time, Pallas kernels for 16%

profile of v2, /device:TPU:0, one launch (start us, length us, event | category | flops | bytes accessed | tf_op | source)
XLA Modules:
  0.0 98.8 jit_solution(13953725414689131426)
XLA Ops:
  0.0 0.1 pad_add_fusion.place_ref
  0.1 0.0 copy-start
  0.1 1.4 %copy-done = bf16[1024,768]{1,0:T(8,128)(2,1)S(1)} copy-done((bf16[1024,768]{1,0:T(8,128)(2,1)S(1)}, bf16[1024,768]{1,0:T(8,128)(2,1)}, u32[]{:S(2)}) %copy-start) | copy-done | bytes 1572888
  1.5 0.0 copy-start.1
  1.5 0.7 copy-done.1
  2.2 0.0 copy-start.2
  2.2 0.7 copy-done.2
  2.9 3.8 %order.1 = (bf16[392,768]{1,0:T(8,128)(2,1)S(1)}, bf16[264,768]{1,0:T(8,128)(2,1)S(1)}, s32[1,1024]{1,0:T(1,128)S(1)}, bf16[136,768]{1,0:T(8,128)(2,1)S(1)}, bf1...) custom-call(s32[2]{0:T(128)S(1)} %pad_add_fusion.place_ref, ...), custom_call_target="tpu_custom_call" | custom-call | tf_op jit(solution)/shard_map/order/pallas_call | solution.py:96
  6.7 3.1 %collective-permute-start = (bf16[392,768]{1,0:T(8,128)(2,1)S(1)}, bf16[392,768]{1,0:T(8,128)(2,1)S(1)}, u32[]{:S(2)}, u32[]{:S(2)}) collective-permute-start(bf16[392,768]{1,0:T(8,128)(2,1)S(1)} %get-tuple-element.23.refs_14_.refs_6_), channel_id=1, source_target_pairs={{0,4},{2,6},{4,0},{6,2},{8,12},{10,14},{12,8},{14,10},{1,5},{3,7},... | collective-permute-start | bytes 1806344 | tf_op jit(solution)/shard_map/ppermute | solution.py:349
  9.8 1.5 %collective-permute-start.8 = (bf16[264,768]{1,0:T(8,128)(2,1)S(1)}, bf16[264,768]{1,0:T(8,128)(2,1)S(1)}, u32[]{:S(2)}, u32[]{:S(2)}) collective-permute-start(bf16[264,768]{1,0:T(8,128)(2,1)S(1)} %get-tuple-element.22.refs_1_.refs_0_), channel_id=1, source_target_pairs={{0,2},{2,0},{4,6},{6,4},{8,10},{10,8},{12,14},{14,12},{1,3},{3,1},... | collective-permute-start | bytes 1216520 | tf_op jit(solution)/shard_map/ppermute | solution.py:355
  11.3 0.0 collective-permute-start.5
  11.3 2.6 %collective-permute-start.1 = (bf16[136,768]{1,0:T(8,128)(2,1)S(1)}, bf16[136,768]{1,0:T(8,128)(2,1)S(1)}, u32[]{:S(2)}, u32[]{:S(2)}) collective-permute-start(bf16[136,768]{1,0:T(8,128)(2,1)S(1)} %get-tuple-element.27), channel_id=1, source_target_pairs={{0,8},{2,10},{4,12},{6,14},{8,0},{10,2},{12,4},{14,6},{1,9},{3,11}... | collective-permute-start | bytes 626696 | tf_op jit(solution)/shard_map/ppermute | solution.py:349
  13.9 0.2 collective-permute-start.2
  14.1 13.7 %collective-permute-done.refs_0_.refs_12_.refs_4_ = bf16[392,768]{1,0:T(8,128)(2,1)S(1)} collective-permute-done((bf16[392,768]{1,0:T(8,128)(2,1)S(1)}, bf16[392,768]{1,0:T(8,128)(2,1)S(1)}, u32[]{:S(2)}, u32[]{:S(2)}) %collective-permute-start) | collective-permute-done | bytes 602144 | tf_op jit(solution)/shard_map/ppermute | solution.py:349
  27.8 0.1 pack.3
  27.9 10.6 %collective-permute-start.4 = (bf16[136,768]{1,0:T(8,128)(2,1)S(1)}, bf16[136,768]{1,0:T(8,128)(2,1)S(1)}, u32[]{:S(2)}, u32[]{:S(2)}) collective-permute-start(bf16[136,768]{1,0:T(8,128)(2,1)S(1)} %get-tuple-element.30), channel_id=1, source_target_pairs={{0,12},{2,14},{4,8},{6,10},{8,4},{10,6},{12,0},{14,2},{1,13},{3,15... | collective-permute-start | bytes 626696 | tf_op jit(solution)/shard_map/ppermute | solution.py:349
  38.4 0.0 collective-permute-done.1.refs_0_
  38.4 0.0 collective-permute-done.2.refs_1_
  38.5 0.1 collective-permute-start.17
  38.6 1.6 %collective-permute-start.10 = (bf16[264,768]{1,0:T(8,128)(2,1)S(1)}, bf16[264,768]{1,0:T(8,128)(2,1)S(1)}, u32[]{:S(2)}, u32[]{:S(2)}) collective-permute-start(bf16[264,768]{1,0:T(8,128)(2,1)S(1)} %pack.4.refs_2_), channel_id=1, source_target_pairs={{0,2},{2,0},{4,6},{6,4},{8,10},{10,8},{12,14},{14,12},{1,3},{3,1},... | collective-permute-start | bytes 1216520 | tf_op jit(solution)/shard_map/ppermute | solution.py:355
  40.1 0.0 collective-permute-done.8.refs_7_.refs_6_
  40.1 0.0 collective-permute-start.7
  40.1 0.0 collective-permute-done.5.refs_4_.refs_3_
  40.2 0.6 collective-permute-start.9
  40.7 2.8 %collective-permute-done.4.refs_1_ = bf16[136,768]{1,0:T(8,128)(2,1)S(1)} collective-permute-done((bf16[136,768]{1,0:T(8,128)(2,1)S(1)}, bf16[136,768]{1,0:T(8,128)(2,1)S(1)}, u32[]{:S(2)}, u32[]{:S(2)}) %collective-permute-start.4) | collective-permute-done | bytes 208928 | tf_op jit(solution)/shard_map/ppermute | solution.py:349
  43.5 0.0 collective-permute-start.3
  43.5 10.1 %collective-permute-done.3.refs_0_ = bf16[136,768]{1,0:T(8,128)(2,1)S(1)} collective-permute-done((bf16[136,768]{1,0:T(8,128)(2,1)S(1)}, bf16[136,768]{1,0:T(8,128)(2,1)S(1)}, u32[]{:S(2)}, u32[]{:S(2)}) %collective-permute-start.3) | collective-permute-done | bytes 208928 | tf_op jit(solution)/shard_map/ppermute | solution.py:349
  53.6 0.0 collective-permute-start.11
  53.6 0.0 collective-permute-done.17.refs_13_.refs_5_
  53.7 0.6 collective-permute-start.6
  54.2 0.0 collective-permute-done.10.refs_9_.refs_8_.refs_1_
  54.2 0.1 collective-permute-start.13
  54.3 0.0 collective-permute-done.7.refs_6_.refs_5_
  54.3 1.5 %collective-permute-start.15 = (bf16[264,768]{1,0:T(8,128)(2,1)S(1)}, bf16[264,768]{1,0:T(8,128)(2,1)S(1)}, u32[]{:S(2)}, u32[]{:S(2)}) collective-permute-start(bf16[264,768]{1,0:T(8,128)(2,1)S(1)} %pack.5.refs_3_.refs_0_), channel_id=1, source_target_pairs={{0,2},{2,0},{4,6},{6,4},{8,10},{10,8},{12,14},{14,12},{1,3},{3,1},... | collective-permute-start | bytes 1216520 | tf_op jit(solution)/shard_map/ppermute | solution.py:355
  55.8 0.0 collective-permute-done.9.refs_8_.refs_7_
  55.8 0.2 collective-permute-start.12
  56.0 0.0 collective-permute-done.11.refs_10_.refs_9_
  56.0 0.7 collective-permute-start.18
  56.7 0.0 collective-permute-done.6.refs_5_.refs_4_
  56.7 4.8 %collective-permute-start.19 = (bf16[136,768]{1,0:T(8,128)(2,1)S(1)}, bf16[136,768]{1,0:T(8,128)(2,1)S(1)}, u32[]{:S(2)}, u32[]{:S(2)}) collective-permute-start(bf16[136,768]{1,0:T(8,128)(2,1)S(1)} %get-tuple-element.29), channel_id=1, source_target_pairs={{12,8},{14,10},{0,4},{2,6},{13,9},{15,11},{1,5},{3,7},{28,24},{30,... | collective-permute-start | bytes 626696 | tf_op jit(solution)/shard_map/ppermute | solution.py:349
  61.5 0.0 collective-permute-done.13.refs_12_.refs_11_
  61.5 0.3 collective-permute-start.14
  61.8 4.2 %collective-permute-done.15.refs_5_.refs_2_ = bf16[264,768]{1,0:T(8,128)(2,1)S(1)} collective-permute-done((bf16[264,768]{1,0:T(8,128)(2,1)S(1)}, bf16[264,768]{1,0:T(8,128)(2,1)S(1)}, u32[]{:S(2)}, u32[]{:S(2)}) %collective-permute-start.15) | collective-permute-done | bytes 405536 | tf_op jit(solution)/shard_map/ppermute | solution.py:355
  66.0 0.0 collective-permute-start.16
  66.1 0.0 collective-permute-done.12.refs_11_.refs_10_
  66.1 3.4 %meet.7 = (f32[1,3072]{1,0:T(1,128)S(1)}, f32[1,512]{1,0:T(1,128)S(1)}) custom-call(bf16[264,768]{1,0:T(8,128)(2,1)S(1)} %get-tuple-element.22.refs_1_.refs_0_, bf16[264,768]{1,0:T(8,128)(2,1)S(1)} %get-tuple-element.26.refs_1_, bf16[264,768]{1,0:T(8,128)(2,1)S(1)} %pack.4.refs_2_, bf16[264,768]{1,0:T(8,128)(2,1)S(1)} %collective-permute-done.5.refs_4_.refs_3_, ...), custom_call_target="tpu_custom_call" | custom-call | flops 2415919104 | tf_op jit(solution)/shard_map/meet/pallas_call | solution.py:241
  69.5 0.0 collective-permute-done.19.refs_13_.refs_8_
  69.5 0.0 collective-permute-done.18.refs_12_.refs_7_
  69.5 3.4 %meet.8 = (f32[1,3072]{1,0:T(1,128)S(1)}, f32[1,512]{1,0:T(1,128)S(1)}) custom-call(bf16[264,768]{1,0:T(8,128)(2,1)S(1)} %get-tuple-element.22.refs_1_.refs_0_, bf16[264,768]{1,0:T(8,128)(2,1)S(1)} %get-tuple-element.26.refs_1_, bf16[264,768]{1,0:T(8,128)(2,1)S(1)} %pack.4.refs_2_, bf16[264,768]{1,0:T(8,128)(2,1)S(1)} %collective-permute-done.5.refs_4_.refs_3_, ...), custom_call_target="tpu_custom_call" | custom-call | flops 2415919104 | tf_op jit(solution)/shard_map/meet/pallas_call | solution.py:241
  72.9 8.7 %meet.5.refs_0_ = f32[1,1024]{1,0:T(1,128)S(1)} custom-call(bf16[264,768]{1,0:T(8,128)(2,1)S(1)} %get-tuple-element.22.refs_1_.refs_0_, bf16[264,768]{1,0:T(8,128)(2,1)S(1)} %get-tuple-element.26.refs_1_, bf16[264,768]{1,0:T(8,128)(2,1)S(1)} %pack.4.refs_2_, bf16[264,768]{1,0:T(8,128)(2,1)S(1)} %pack.5.refs_3_.refs_0_, ...), custom_call_target="tpu_custom_call" | custom-call | flops 5234491392 | tf_op jit(solution)/shard_map/meet/pallas_call | solution.py:241
  81.7 0.0 collective-permute-done.14.refs_4_.refs_1_
  81.7 0.0 collective-permute-done.16.refs_6_.refs_3_
  81.7 2.0 %meet.6.refs_1_ = f32[1,1024]{1,0:T(1,128)S(1)} custom-call(bf16[264,768]{1,0:T(8,128)(2,1)S(1)} %get-tuple-element.22.refs_1_.refs_0_, bf16[264,768]{1,0:T(8,128)(2,1)S(1)} %get-tuple-element.26.refs_1_, bf16[264,768]{1,0:T(8,128)(2,1)S(1)} %pack.4.refs_2_, bf16[264,768]{1,0:T(8,128)(2,1)S(1)} %pack.5.refs_3_.refs_0_, ...), custom_call_target="tpu_custom_call" | custom-call | flops 1207959552 | tf_op jit(solution)/shard_map/meet/pallas_call | solution.py:241
  83.8 2.5 %meet.9 = (f32[1,1024]{1,0:T(1,128)S(1)}, f32[1,1024]{1,0:T(1,128)S(1)}) custom-call(bf16[264,768]{1,0:T(8,128)(2,1)S(1)} %pack.5.refs_3_.refs_0_, bf16[264,768]{1,0:T(8,128)(2,1)S(1)} %collective-permute-done.14.refs_4_.refs_1_, bf16[264,768]{1,0:T(8,128)(2,1)S(1)} %collective-permute-done.15.refs_5_.refs_2_, ...), custom_call_target="tpu_custom_call" | custom-call | flops 1610612736 | tf_op jit(solution)/shard_map/meet/pallas_call | solution.py:241
  86.3 0.6 route.1
  86.9 10.6 %all_to_all.5.got_ref = f32[16,1,512]{2,1,0:T(1,128)S(1)} all-to-all(f32[16,1,512]{2,1,0:T(1,128)S(1)} %route.1), channel_id=1, replica_groups=mesh['groups'=2,'blk'=8,'split'=2] {'blk','split'}, dimensions={0} | all-to-all | bytes 65536 | tf_op jit(solution)/shard_map/all_to_all | solution.py:424
  97.5 1.3 %back.1 = f32[1,1024]{1,0:T(1,128)} custom-call(f32[16,1,512]{2,1,0:T(1,128)S(1)} %all_to_all.5.got_ref, s32[1,1024]{1,0:T(1,128)S(1)} %get-tuple-element.38.rank_ref), custom_call_target="tpu_custom_call" | custom-call | tf_op jit(solution)/shard_map/back/pallas_call | solution.py:325
  (4 shorter events, 0.1 us)
Async XLA Ops:
  0.1 1.4 %copy-start = (bf16[1024,768]{1,0:T(8,128)(2,1)S(1)}, bf16[1024,768]{1,0:T(8,128)(2,1)}, u32[]{:S(2)}) copy-start(bf16[1024,768]{1,0:T(8,128)(2,1)} %rows_ref.1) | copy-start | bytes 4718596
  1.5 0.7 copy-start.1
  2.2 0.7 copy-start.2
  6.7 21.2 %collective-permute-start = (bf16[392,768]{1,0:T(8,128)(2,1)S(1)}, bf16[392,768]{1,0:T(8,128)(2,1)S(1)}, u32[]{:S(2)}, u32[]{:S(2)}) collective-permute-start(bf16[392,768]{1,0:T(8,128)(2,1)S(1)} %get-tuple-element.23.refs_14_.refs_6_), channel_id=1, source_target_pairs={{0,4},{2,6},{4,0},{6,2},{8,12},{10,14},{12,8},{14,10},{1,5},{3,7},... | collective-permute-start | bytes 1806344 | tf_op jit(solution)/shard_map/ppermute | solution.py:349
  9.8 30.4 %collective-permute-start.8 = (bf16[264,768]{1,0:T(8,128)(2,1)S(1)}, bf16[264,768]{1,0:T(8,128)(2,1)S(1)}, u32[]{:S(2)}, u32[]{:S(2)}) collective-permute-start(bf16[264,768]{1,0:T(8,128)(2,1)S(1)} %get-tuple-element.22.refs_1_.refs_0_), channel_id=1, source_target_pairs={{0,2},{2,0},{4,6},{6,4},{8,10},{10,8},{12,14},{14,12},{1,3},{3,1},... | collective-permute-start | bytes 1216520 | tf_op jit(solution)/shard_map/ppermute | solution.py:355
  11.3 28.9 %collective-permute-start.5 = (bf16[264,768]{1,0:T(8,128)(2,1)S(1)}, bf16[264,768]{1,0:T(8,128)(2,1)S(1)}, u32[]{:S(2)}, u32[]{:S(2)}) collective-permute-start(bf16[264,768]{1,0:T(8,128)(2,1)S(1)} %get-tuple-element.22.refs_1_.refs_0_), channel_id=1, source_target_pairs={{0,1},{1,0},{2,3},{3,2},{4,5},{5,4},{6,7},{7,6},{8,9},{9,8},{10,11... | collective-permute-start | bytes 1216520 | tf_op jit(solution)/shard_map/ppermute | solution.py:358
  11.3 27.2 %collective-permute-start.1 = (bf16[136,768]{1,0:T(8,128)(2,1)S(1)}, bf16[136,768]{1,0:T(8,128)(2,1)S(1)}, u32[]{:S(2)}, u32[]{:S(2)}) collective-permute-start(bf16[136,768]{1,0:T(8,128)(2,1)S(1)} %get-tuple-element.27), channel_id=1, source_target_pairs={{0,8},{2,10},{4,12},{6,14},{8,0},{10,2},{12,4},{14,6},{1,9},{3,11}... | collective-permute-start | bytes 626696 | tf_op jit(solution)/shard_map/ppermute | solution.py:349
  13.9 24.6 %collective-permute-start.2 = (bf16[136,768]{1,0:T(8,128)(2,1)S(1)}, bf16[136,768]{1,0:T(8,128)(2,1)S(1)}, u32[]{:S(2)}, u32[]{:S(2)}) collective-permute-start(bf16[136,768]{1,0:T(8,128)(2,1)S(1)} %get-tuple-element.28), channel_id=1, source_target_pairs={{0,12},{2,14},{4,8},{6,10},{8,4},{10,6},{12,0},{14,2},{1,13},{3,15... | collective-permute-start | bytes 626696 | tf_op jit(solution)/shard_map/ppermute | solution.py:349
  27.9 15.6 %collective-permute-start.4 = (bf16[136,768]{1,0:T(8,128)(2,1)S(1)}, bf16[136,768]{1,0:T(8,128)(2,1)S(1)}, u32[]{:S(2)}, u32[]{:S(2)}) collective-permute-start(bf16[136,768]{1,0:T(8,128)(2,1)S(1)} %get-tuple-element.30), channel_id=1, source_target_pairs={{0,12},{2,14},{4,8},{6,10},{8,4},{10,6},{12,0},{14,2},{1,13},{3,15... | collective-permute-start | bytes 626696 | tf_op jit(solution)/shard_map/ppermute | solution.py:349
  38.5 15.2 %collective-permute-start.17 = (bf16[264,768]{1,0:T(8,128)(2,1)S(1)}, bf16[264,768]{1,0:T(8,128)(2,1)S(1)}, u32[]{:S(2)}, u32[]{:S(2)}) collective-permute-start(bf16[264,768]{1,0:T(8,128)(2,1)S(1)} %pack.4.refs_2_), channel_id=1, source_target_pairs={{0,4},{2,6},{4,0},{6,2},{8,12},{10,14},{12,8},{14,10},{1,5},{3,7},... | collective-permute-start | bytes 1216520 | tf_op jit(solution)/shard_map/ppermute | solution.py:349
  38.6 15.7 %collective-permute-start.10 = (bf16[264,768]{1,0:T(8,128)(2,1)S(1)}, bf16[264,768]{1,0:T(8,128)(2,1)S(1)}, u32[]{:S(2)}, u32[]{:S(2)}) collective-permute-start(bf16[264,768]{1,0:T(8,128)(2,1)S(1)} %pack.4.refs_2_), channel_id=1, source_target_pairs={{0,2},{2,0},{4,6},{6,4},{8,10},{10,8},{12,14},{14,12},{1,3},{3,1},... | collective-permute-start | bytes 1216520 | tf_op jit(solution)/shard_map/ppermute | solution.py:355
  40.1 14.2 %collective-permute-start.7 = (bf16[264,768]{1,0:T(8,128)(2,1)S(1)}, bf16[264,768]{1,0:T(8,128)(2,1)S(1)}, u32[]{:S(2)}, u32[]{:S(2)}) collective-permute-start(bf16[264,768]{1,0:T(8,128)(2,1)S(1)} %pack.4.refs_2_), channel_id=1, source_target_pairs={{0,1},{1,0},{2,3},{3,2},{4,5},{5,4},{6,7},{7,6},{8,9},{9,8},{10,11... | collective-permute-start | bytes 1216520 | tf_op jit(solution)/shard_map/ppermute | solution.py:358
  40.2 15.7 %collective-permute-start.9 = (bf16[264,768]{1,0:T(8,128)(2,1)S(1)}, bf16[264,768]{1,0:T(8,128)(2,1)S(1)}, u32[]{:S(2)}, u32[]{:S(2)}) collective-permute-start(bf16[264,768]{1,0:T(8,128)(2,1)S(1)} %get-tuple-element.26.refs_1_), channel_id=1, source_target_pairs={{0,2},{2,0},{4,6},{6,4},{8,10},{10,8},{12,14},{14,12},{1,3},{3,1},... | collective-permute-start | bytes 1216520 | tf_op jit(solution)/shard_map/ppermute | solution.py:355
  43.5 10.1 %collective-permute-start.3 = (bf16[136,768]{1,0:T(8,128)(2,1)S(1)}, bf16[136,768]{1,0:T(8,128)(2,1)S(1)}, u32[]{:S(2)}, u32[]{:S(2)}) collective-permute-start(bf16[136,768]{1,0:T(8,128)(2,1)S(1)} %get-tuple-element.29), channel_id=1, source_target_pairs={{0,8},{2,10},{4,12},{6,14},{8,0},{10,2},{12,4},{14,6},{1,9},{3,11}... | collective-permute-start | bytes 626696 | tf_op jit(solution)/shard_map/ppermute | solution.py:349
  53.6 2.4 %collective-permute-start.11 = (bf16[264,768]{1,0:T(8,128)(2,1)S(1)}, bf16[264,768]{1,0:T(8,128)(2,1)S(1)}, u32[]{:S(2)}, u32[]{:S(2)}) collective-permute-start(bf16[264,768]{1,0:T(8,128)(2,1)S(1)} %collective-permute-done.8.refs_7_.refs_6_), channel_id=1, source_target_pairs={{0,1},{1,0},{2,3},{3,2},{4,5},{5,4},{6,7},{7,6},{8,9},{9,8},{10,11... | collective-permute-start | bytes 1216520 | tf_op jit(solution)/shard_map/ppermute | solution.py:358
  53.7 3.0 %collective-permute-start.6 = (bf16[264,768]{1,0:T(8,128)(2,1)S(1)}, bf16[264,768]{1,0:T(8,128)(2,1)S(1)}, u32[]{:S(2)}, u32[]{:S(2)}) collective-permute-start(bf16[264,768]{1,0:T(8,128)(2,1)S(1)} %get-tuple-element.26.refs_1_), channel_id=1, source_target_pairs={{0,1},{1,0},{2,3},{3,2},{4,5},{5,4},{6,7},{7,6},{8,9},{9,8},{10,11... | collective-permute-start | bytes 1216520 | tf_op jit(solution)/shard_map/ppermute | solution.py:358
  54.2 7.3 %collective-permute-start.13 = (bf16[264,768]{1,0:T(8,128)(2,1)S(1)}, bf16[264,768]{1,0:T(8,128)(2,1)S(1)}, u32[]{:S(2)}, u32[]{:S(2)}) collective-permute-start(bf16[264,768]{1,0:T(8,128)(2,1)S(1)} %collective-permute-done.10.refs_9_.refs_8_.refs_1_), channel_id=1, source_target_pairs={{0,1},{1,0},{2,3},{3,2},{4,5},{5,4},{6,7},{7,6},{8,9},{9,8},{10,11... | collective-permute-start | bytes 1216520 | tf_op jit(solution)/shard_map/ppermute | solution.py:358
  54.3 11.7 %collective-permute-start.15 = (bf16[264,768]{1,0:T(8,128)(2,1)S(1)}, bf16[264,768]{1,0:T(8,128)(2,1)S(1)}, u32[]{:S(2)}, u32[]{:S(2)}) collective-permute-start(bf16[264,768]{1,0:T(8,128)(2,1)S(1)} %pack.5.refs_3_.refs_0_), channel_id=1, source_target_pairs={{0,2},{2,0},{4,6},{6,4},{8,10},{10,8},{12,14},{14,12},{1,3},{3,1},... | collective-permute-start | bytes 1216520 | tf_op jit(solution)/shard_map/ppermute | solution.py:355
  55.8 10.2 %collective-permute-start.12 = (bf16[264,768]{1,0:T(8,128)(2,1)S(1)}, bf16[264,768]{1,0:T(8,128)(2,1)S(1)}, u32[]{:S(2)}, u32[]{:S(2)}) collective-permute-start(bf16[264,768]{1,0:T(8,128)(2,1)S(1)} %collective-permute-done.9.refs_8_.refs_7_), channel_id=1, source_target_pairs={{0,1},{1,0},{2,3},{3,2},{4,5},{5,4},{6,7},{7,6},{8,9},{9,8},{10,11... | collective-permute-start | bytes 1216520 | tf_op jit(solution)/shard_map/ppermute | solution.py:358
  56.0 13.5 %collective-permute-start.18 = (bf16[264,768]{1,0:T(8,128)(2,1)S(1)}, bf16[264,768]{1,0:T(8,128)(2,1)S(1)}, u32[]{:S(2)}, u32[]{:S(2)}) collective-permute-start(bf16[264,768]{1,0:T(8,128)(2,1)S(1)} %after.1), channel_id=1, source_target_pairs={{4,8},{6,10},{8,4},{10,6},{5,9},{7,11},{9,5},{11,7},{20,24},{22,26... | collective-permute-start | bytes 1216520 | tf_op jit(solution)/shard_map/ppermute | solution.py:349
  56.7 12.8 %collective-permute-start.19 = (bf16[136,768]{1,0:T(8,128)(2,1)S(1)}, bf16[136,768]{1,0:T(8,128)(2,1)S(1)}, u32[]{:S(2)}, u32[]{:S(2)}) collective-permute-start(bf16[136,768]{1,0:T(8,128)(2,1)S(1)} %get-tuple-element.29), channel_id=1, source_target_pairs={{12,8},{14,10},{0,4},{2,6},{13,9},{15,11},{1,5},{3,7},{28,24},{30,... | collective-permute-start | bytes 626696 | tf_op jit(solution)/shard_map/ppermute | solution.py:349
  61.5 20.2 %collective-permute-start.14 = (bf16[264,768]{1,0:T(8,128)(2,1)S(1)}, bf16[264,768]{1,0:T(8,128)(2,1)S(1)}, u32[]{:S(2)}, u32[]{:S(2)}) collective-permute-start(bf16[264,768]{1,0:T(8,128)(2,1)S(1)} %pack.5.refs_3_.refs_0_), channel_id=1, source_target_pairs={{0,1},{1,0},{2,3},{3,2},{4,5},{5,4},{6,7},{7,6},{8,9},{9,8},{10,11... | collective-permute-start | bytes 1216520 | tf_op jit(solution)/shard_map/ppermute | solution.py:358
  66.0 15.7 %collective-permute-start.16 = (bf16[264,768]{1,0:T(8,128)(2,1)S(1)}, bf16[264,768]{1,0:T(8,128)(2,1)S(1)}, u32[]{:S(2)}, u32[]{:S(2)}) collective-permute-start(bf16[264,768]{1,0:T(8,128)(2,1)S(1)} %collective-permute-done.15.refs_5_.refs_2_), channel_id=1, source_target_pairs={{0,1},{1,0},{2,3},{3,2},{4,5},{5,4},{6,7},{7,6},{8,9},{9,8},{10,11... | collective-permute-start | bytes 1216520 | tf_op jit(solution)/shard_map/ppermute | solution.py:358

commit v3 on v2

v3 whole, which is shorter than its diff:
```python
import functools

import jax
import jax.numpy as jnp
from jax import lax
from jax.experimental import pallas as pl
from jax.experimental.pallas import tpu as pltpu
from jax.sharding import PartitionSpec as P

MOST = 4096
FILL = -4.0
TAGS = 8
LANES = 128
MIB = 1024 * 1024
WHOLE = pl.BlockSpec(memory_space=pltpu.VMEM)
ANYWHERE = pl.BlockSpec(memory_space=pl.ANY)
REMAINS = pl.BlockSpec(memory_space=pltpu.HBM)
SCALARS = pl.BlockSpec(memory_space=pltpu.SMEM)


def grant(mib):
    return pltpu.CompilerParams(vmem_limit_bytes=mib * MIB)


def spread(row):
    return jnp.transpose(jnp.broadcast_to(row, (LANES, row.shape[1])))


def column_fold(scores):
    rows, columns = scores.shape
    return jnp.max(scores.reshape(rows // 8, 8, columns), axis=0)


def lane_fold(scores):
    best = scores[:, :LANES]
    for at in range(LANES, scores.shape[1], LANES):
        best = jnp.maximum(best, scores[:, at : at + LANES])
    return best


def order_kernel(parts, place_ref, rows_hbm, ids_hbm, pos_hbm, *refs):
    outs, rank_ref = refs[:parts], refs[parts]
    unit, pick, placed, tags, rows_ref, ids_ref, pos_ref, sems = refs[parts + 1 :]
    count, width = rows_ref.shape
    quart = count // parts // 4
    step = 256
    fetch_pos = pltpu.make_async_copy(pos_hbm, pos_ref, sems.at[0])
    fetch_rows = pltpu.make_async_copy(rows_hbm, rows_ref, sems.at[1])
    fetch_ids = pltpu.make_async_copy(ids_hbm, ids_ref, sems.at[2])
    fetch_pos.start()
    fetch_rows.start()
    fetch_ids.start()
    fetch_pos.wait()
    pos = pos_ref[...].astype(jnp.float32)
    below = jnp.zeros((8, count), jnp.float32)
    for at in range(0, count, step):
        other = spread(pos[:, at : at + step])[:, :1]
        below += jnp.sum(jnp.where(other < pos, 1.0, 0.0).reshape(step // 8, 8, count), axis=0)
    rank = jnp.sum(below, axis=0, keepdims=True).astype(jnp.int32)
    rank_ref[...] = rank
    for at in range(0, count, step):
        slot = lax.broadcasted_iota(jnp.int32, (step, count), 0) + at
        pick[at : at + step, :] = jnp.where(slot == rank, 1.0, 0.0).astype(jnp.bfloat16)
    fetch_rows.wait()
    fetch_ids.wait()
    values = rows_ref[...].astype(jnp.float32)
    total = jnp.sum(values * values, axis=1, keepdims=True)
    unit[...] = (values * lax.rsqrt(total + 1e-06)).astype(jnp.bfloat16)
    for at in range(0, count, step):
        placed[at : at + step, :] = jnp.dot(
            pick[at : at + step, :], unit[...], preferred_element_type=jnp.float32
        ).astype(jnp.bfloat16)
    ids = jnp.broadcast_to((ids_ref[...] + 1).astype(jnp.bfloat16), (16, count))
    sorted_ids = lax.dot_general(
        ids, pick[...], (((1,), (1,)), ((), ())), preferred_element_type=jnp.float32
    )
    for at in range(4 * parts):
        tags[at, :, :quart] = sorted_ids[:, at * quart : (at + 1) * quart]
    for k in range(parts):
        quarter = lax.bitwise_xor(place_ref[0], k)
        side = lax.rem(quarter, 2)
        for index, block in enumerate((3 - 3 * side, 2 - side, 3 * side, 1 + side)):
            which = 4 * quarter + block
            at = index * quart
            outs[k][at : at + quart, :] = placed[pl.ds(pl.multiple_of(which * quart, quart), quart), :]
            outs[k][4 * quart :, at : at + quart] = tags[which, :TAGS, :quart].astype(jnp.bfloat16)


def in_order(place, embeddings, ids, pos, parts):
    count, width = embeddings.shape
    slots = count // parts
    block = jax.ShapeDtypeStruct((slots + TAGS, width), jnp.bfloat16)
    outs = [block] * parts + [jax.ShapeDtypeStruct((1, count), jnp.int32)]
    *blocks, rank = pl.pallas_call(
        functools.partial(order_kernel, parts),
        out_shape=outs,
        in_specs=[SCALARS, REMAINS, REMAINS, REMAINS],
        out_specs=[WHOLE] * len(outs),
        scratch_shapes=[
            pltpu.VMEM((count, width), jnp.bfloat16),
            pltpu.VMEM((count, count), jnp.bfloat16),
            pltpu.VMEM((count, width), jnp.bfloat16),
            pltpu.VMEM((4 * parts, 16, max(slots // 4, LANES)), jnp.float32),
            pltpu.VMEM((count, width), jnp.bfloat16),
            pltpu.VMEM((1, count), jnp.int32),
            pltpu.VMEM((1, count), jnp.int32),
            pltpu.SemaphoreType.DMA((3,)),
        ],
        compiler_params=grant(24),
        name="order",
    )(place, embeddings, ids.reshape(1, count), pos.reshape(1, count))
    return blocks, rank


def pack_kernel(plan, inputs, *refs):
    given, outs = refs[:inputs], refs[-len(plan) :]
    for out, pieces in zip(outs, plan):
        at = 0
        for index, start, rows in pieces:
            ref = given[index]
            out[at : at + rows, :] = ref[start : start + rows, :]
            out[out.shape[0] - TAGS :, at : at + rows] = ref[
                ref.shape[0] - TAGS :, start : start + rows
            ]
            at += rows


def pack(blocks, plan, held=(), earlier=()):
    width = blocks[0].shape[1]
    plan = [list(pieces) for pieces in plan]
    outs = [
        jax.ShapeDtypeStruct((sum(p[2] for p in pieces) + TAGS, width), jnp.bfloat16)
        for pieces in plan
    ]
    kept = [jax.ShapeDtypeStruct(h.shape, h.dtype) for h in held]

    def kernel(*refs):
        given = refs[: len(blocks)]
        made = refs[len(blocks) + 2 * len(held) + len(earlier) :]
        pack_kernel(plan, len(given), *given, *made)

    return pl.pallas_call(
        kernel,
        out_shape=kept + outs,
        in_specs=[WHOLE] * len(blocks) + [ANYWHERE] * (len(held) + len(earlier)),
        out_specs=[ANYWHERE] * len(held) + [WHOLE] * len(outs),
        input_output_aliases={len(blocks) + i: i for i in range(len(held))},
        compiler_params=grant(8),
        name="pack",
    )(*blocks, *held, *earlier)


def after(held, earlier):
    return pl.pallas_call(
        lambda *refs: None,
        out_shape=[jax.ShapeDtypeStruct(h.shape, h.dtype) for h in held],
        in_specs=[ANYWHERE] * (len(held) + len(earlier)),
        out_specs=[ANYWHERE] * len(held),
        input_output_aliases={i: i for i in range(len(held))},
        compiler_params=grant(1),
        name="after",
    )(*held, *earlier)


def overlap(one, other):
    return jnp.logical_and(one[0] <= other[1], other[0] <= one[1])


def meet_kernel(lefts, rights, pairs, inputs, *refs):
    given = refs[:inputs]
    left_out, right_out, left, left_ids, right, right_ids, left_best, right_best = refs[inputs:]

    def ids_of(piece):
        ref, start, rows = given[piece[0]], piece[1], piece[2]
        return ref[ref.shape[0] - TAGS :, start : start + rows].astype(jnp.float32)

    def span(section):
        low, high = None, None
        for piece in section:
            ids = ids_of(piece)
            there = jnp.where(ids > 0.0, ids, 1e6)
            low = there if low is None else jnp.minimum(low, there)
            high = ids if high is None else jnp.maximum(high, ids)
        return jnp.min(low), jnp.max(high)

    tested = [(r, l) for r, l, _, test in pairs if test]
    right_span = {r: span(rights[r]) for r in sorted({r for r, _ in tested})}
    left_span = {l: span(lefts[l]) for l in sorted({l for _, l in tested})}
    wanted = {(r, l): overlap(right_span[r], left_span[l]) for r, l in tested}

    def place_of(sections):
        out, at = [], 0
        for section in sections:
            rows = sum(piece[2] for piece in section)
            out.append((at, rows))
            at += rows
        return out

    left_at, right_at = place_of(lefts), place_of(rights)

    def fill(buffer, section, at):
        for index, start, rows in section:
            buffer[at : at + rows, :] = given[index][start : start + rows, :]
            at += rows

    left_best[...] = jnp.full(left_best.shape, FILL, jnp.float32)
    right_best[...] = jnp.full(right_best.shape, FILL, jnp.float32)
    for section, (at, _) in zip(lefts, left_at):
        for piece in section:
            left_ids[:, at : at + piece[2]] = ids_of(piece)
            at += piece[2]
    for section, (at, _) in zip(rights, right_at):
        for piece in section:
            right_ids[at : at + piece[2], :] = spread(ids_of(piece)[:1, :])
            at += piece[2]
    for which, sections, places, buffer in ((1, lefts, left_at, left), (0, rights, right_at, right)):
        for number, section in enumerate(sections):
            uses = [p for p in pairs if p[which] == number]
            load = functools.partial(fill, buffer, section, places[number][0])
            if all(p[3] for p in uses):
                need = [wanted[p[0], p[1]] for p in uses]
                pl.when(functools.reduce(jnp.logical_or, need))(load)
            else:
                load()

    def score(r, l, diagonal):
        (row, rows), (column, columns) = right_at[r], left_at[l]
        step = rows
        while step * columns > 512 * 1024 and step % 32 == 0:
            step //= 2
        across = slice(column, column + columns)

        def turn(index, _):
            at = pl.multiple_of(row + index * step, 16)
            down = pl.ds(at, step)
            scores = lax.dot_general(
                right[down, :],
                left[across, :],
                (((1,), (1,)), ((), ())),
                preferred_element_type=jnp.float32,
            )
            scores = jnp.where(right_ids[down, :1] == left_ids[:1, across], scores, FILL)
            if diagonal:
                mine = lax.broadcasted_iota(jnp.int32, (step, columns), 0) + index * step
                theirs = lax.broadcasted_iota(jnp.int32, (step, columns), 1)
                scores = jnp.where(mine == theirs, FILL, scores)
            right_best[down, :] = jnp.maximum(right_best[down, :], lane_fold(scores))
            left_best[:, across] = jnp.maximum(left_best[:, across], column_fold(scores))
            return 0

        lax.fori_loop(0, rows // step, turn, 0)

    for r, l, diagonal, test in pairs:
        run = functools.partial(score, r, l, diagonal)
        if test:
            pl.when(wanted[r, l])(run)
        else:
            run()
    left_out[...] = jnp.max(left_best[...], axis=0, keepdims=True)
    right_out[...] = jnp.max(jnp.transpose(right_best[...]), axis=0, keepdims=True)


def meet(lefts, rights, pairs, earlier=()):
    blocks = []

    def plan(sections):
        out = []
        for section in sections:
            pieces = []
            for block, start, rows, _ in section:
                known = [i for i, b in enumerate(blocks) if b is block]
                if not known:
                    blocks.append(block)
                pieces.append((known[0] if known else len(blocks) - 1, start, rows))
            out.append(pieces)
        return out

    def goals(sections):
        return [(p[3], p[2]) for section in sections for p in section]

    plan_left, plan_right = plan(lefts), plan(rights)
    width = blocks[0].shape[1]
    count = sum(n for _, n in goals(lefts))
    total = sum(n for _, n in goals(rights))
    inputs = len(blocks)

    def kernel(*refs):
        meet_kernel(
            plan_left, plan_right, pairs, inputs, *refs[:inputs], *refs[inputs + len(earlier) :]
        )

    left_best, right_best = pl.pallas_call(
        kernel,
        out_shape=[
            jax.ShapeDtypeStruct((1, count), jnp.float32),
            jax.ShapeDtypeStruct((1, total), jnp.float32),
        ],
        in_specs=[WHOLE] * inputs + [ANYWHERE] * len(earlier),
        out_specs=[WHOLE] * 2,
        scratch_shapes=[
            pltpu.VMEM((count, width), jnp.bfloat16),
            pltpu.VMEM((TAGS, count), jnp.float32),
            pltpu.VMEM((total, width), jnp.bfloat16),
            pltpu.VMEM((total, LANES), jnp.float32),
            pltpu.VMEM((8, count), jnp.float32),
            pltpu.VMEM((total, LANES), jnp.float32),
        ],
        compiler_params=grant(24),
        cost_estimate=pl.CostEstimate(flops=0, bytes_accessed=0, transcendentals=0),
        name="meet",
    )(*blocks, *earlier)
    return [(left_best, goals(lefts)), (right_best, goals(rights))]


def route_kernel(plan, parts, members, half, near, place_ref, *refs):
    given, out_ref, gathered = refs[:-2], refs[-2], refs[-1]
    part, me = place_ref[0], place_ref[1]
    slots = 2 * half
    out_ref[...] = jnp.full(out_ref.shape, FILL, jnp.float32)
    gathered[...] = jnp.full(gathered.shape, FILL, jnp.float32)
    starts = {"u": members * parts * slots, "v": members * parts * slots + parts * half}
    for ref, pieces in zip(given, plan):
        at = 0
        for to, entries in pieces:
            gathered[:, to : to + entries] = jnp.maximum(
                gathered[:, to : to + entries], ref[:, at : at + entries]
            )
            at += entries
    for member in range(members):
        whose = lax.bitwise_xor(me, member)
        for k in range(parts):
            at = (member * parts + k) * slots
            source = lax.bitwise_xor(part, k) * members + whose
            out_ref[source, :, :slots] = gathered[:, at : at + slots]
    beyond = lax.rem(part + parts - 1 + 2 * lax.rem(part, 2), parts)
    if near:
        beyond = lax.bitwise_xor(part, 3)
    next_to = lax.bitwise_xor(part, 1)
    from_u = [next_to] + [lax.bitwise_xor(next_to, k) for k in range(2, parts)] + [part]
    from_v = [beyond, lax.bitwise_xor(beyond, 1)]
    from_v += [next_to, part] if near else [lax.bitwise_xor(beyond, k) for k in range(2, parts)]
    for kind, sources, lane in (("u", from_u, slots), ("v", from_v, slots + half)):
        for index, source in enumerate(sources):
            at = starts[kind] + index * half
            out_ref[source * members + me, :, lane : lane + half] = gathered[:, at : at + half]


def back_kernel(parts, members, got_ref, rank_ref, out_ref):
    slots = got_ref.shape[2] // 2
    half = slots // 2
    rows = []
    for part in range(parts):
        best = got_ref[part * members]
        for member in range(1, members):
            best = jnp.maximum(best, got_ref[part * members + member])
        rows.append(best)
    rank = rank_ref[...]
    nothing = jnp.full((1, half), FILL, jnp.float32)
    best = jnp.full((8, rank.shape[1]), FILL, jnp.float32)
    for part in range(parts):
        beyond = part + 1 if part % 2 else part - 1
        there = 0 <= beyond < parts
        faces = jnp.maximum(rows[part][:, :half], rows[part ^ 1][:, slots : slots + half])
        turned = jnp.maximum(
            rows[part][:, half:slots], rows[beyond][:, slots + half :] if there else nothing
        )
        near_u, far_u = faces[:, : half // 2], faces[:, half // 2 :]
        near_v, far_v = turned[:, : half // 2], turned[:, half // 2 :]
        order = [near_u, far_u, far_v, near_v] if part % 2 else [near_v, far_v, far_u, near_u]
        values = spread(jnp.concatenate(order, axis=1))[:, :1]
        slot = lax.broadcasted_iota(jnp.int32, (slots, rank.shape[1]), 0) + part * slots
        best = jnp.maximum(best, column_fold(jnp.where(slot == rank, values, FILL)))
    out_ref[...] = jnp.max(best, axis=0, keepdims=True)


def in_data_order(got, rank, parts, members):
    return pl.pallas_call(
        functools.partial(back_kernel, parts, members),
        out_shape=jax.ShapeDtypeStruct(rank.shape, jnp.float32),
        in_specs=[WHOLE, WHOLE],
        out_specs=WHOLE,
        compiler_params=grant(16),
        name="back",
    )(got, rank)


def body(embeddings, cluster_of, target_pos):
    blocks, cores = lax.axis_size("blk"), lax.axis_size("split")
    rows, width = embeddings.shape
    members = MOST // rows
    chips = members // cores
    parts = blocks // chips
    half = rows // parts // 2
    slots = 2 * half
    chip, core = lax.axis_index("blk"), lax.axis_index("split")
    place = jnp.stack([chip // chips, (chip % chips) * cores + core]).astype(jnp.int32)

    def between(array, pairs, name):
        route = [(s * chips + c, t * chips + c) for s, t in pairs for c in range(chips)]
        with jax.named_scope(name):
            return lax.ppermute(array, "blk", route)

    def swap(array, k, name):
        return between(array, [(part, part ^ k) for part in range(parts)], name)

    def chip_swap(array, name):
        with jax.named_scope(name):
            return lax.ppermute(array, "blk", [(b, b ^ 1) for b in range(blocks)])

    def core_swap(array, name):
        with jax.named_scope(name):
            return lax.ppermute(array, "split", [(c, c ^ 1) for c in range(cores)])

    borders = [(p, p + 1) for p in range(1, parts - 1, 2)]
    borders += [(t, s) for s, t in borders]
    near = all(s ^ t == 3 for s, t in borders)

    quart = half // 2
    middle = (parts + 2) // 2
    second, third = [1, *range(2, middle)], list(range(middle, parts))
    u_goal = members * parts * slots
    v_goal = u_goal + parts * half

    def sides(blocks, ks, member=0):
        out = []
        for side in (0, half):
            for m, block in enumerate(blocks, member):
                for i, k in enumerate(ks):
                    goal = (m * parts + k) * slots + side
                    out.append((block, i * slots + side, half, goal))
        return out[: len(out) // 2], out[len(out) // 2 :]

    def visits(pieces, goal):
        near_rows = [(b, at, quart, goal + i * half) for b, at, i in pieces]
        far_rows = [(b, at + quart, quart, goal + i * half + quart) for b, at, i in pieces]
        return near_rows, far_rows

    sent, rank = in_order(place, embeddings, cluster_of, target_pos, parts)
    own_0 = sent[0]
    got = [swap(sent[k], k, "rows_2") for k in second]
    over_0 = chip_swap(own_0, "over_0")
    beside_0 = core_swap(own_0, "beside_0")

    pieces = [(i, 0, slots) for i in range(len(second))]
    forward = [(len(second), 0, half)] + [(i, 0, half) for i in range(1, len(second))]
    *held, own_2, passing = pack(
        [*got, own_0], [pieces, forward], held=[sent[k] for k in third], earlier=[over_0]
    )
    got = [swap(b, k, "rows_3") for k, b in zip(third, held)]
    over_2 = chip_swap(own_2, "over_2")
    passed_2 = swap(passing, 1, "passed_2")
    across_0 = core_swap(over_0, "across_0")
    beside_2 = core_swap(own_2, "beside_2")
    left_0 = sides([own_0, beside_0, over_0, across_0], [0])
    mine_0, mine_2 = sides([own_0], [0]), sides([own_2], second)
    scores = meet(
        left_0,
        [*mine_0, *mine_2],
        [(0, 0, True, False), (0, 1, False, True), (1, 0, False, True), (1, 1, True, False)]
        + [(2, 0, False, False), (2, 1, False, True), (3, 0, False, True), (3, 1, False, False)],
    )

    last = len(third)
    border = [(last, half, half), (last + 1, half, half)]
    forward = [(i, 0, half) for i in range(last)]
    inputs = [*got, own_0, own_2]
    if near:
        inputs.append(sent[2])
        forward.append((last + 2, half, half))
    else:
        border += [(last + 1, i * slots + half, half) for i in range(1, len(second))]
        border += [(i, half, half) for i in range(last)]
    own_3, border, passing = pack(
        inputs,
        [[(i, 0, slots) for i in range(last)], border, forward],
        earlier=[over_2, passed_2, across_0, beside_2, scores[0][0]],
    )
    over_3 = chip_swap(own_3, "over_3")
    got_border = between(border, borders, "border")
    passed_3 = swap(passing, 1, "passed_3")
    across_2 = core_swap(over_2, "across_2")
    beside_3 = core_swap(own_3, "beside_3")
    left_2 = sides([own_2, beside_2, over_2, across_2], second)
    mine_3 = sides([own_3], third)
    visit_2 = [(passed_2, i * half, i) for i in range(len(second))]
    visit_2 = visits(visit_2 + [(sent[1], 0, parts - 1)], u_goal)
    visit_3 = visits([(passed_3, i * half, len(second) + i) for i in range(last)], u_goal)
    tested = [(r, l, False, True) for r in (4, 5) for l in (0, 1)]
    scores += meet(
        left_2,
        [*mine_2, *mine_3, *visit_2],
        [(0, 0, True, False), (0, 1, False, True), (1, 0, False, True), (1, 1, True, False)]
        + [(2, 0, False, False), (2, 1, False, True), (3, 0, False, True), (3, 1, False, False)]
        + tested,
    )
    scores += meet(
        left_0,
        [*mine_3, *visit_2],
        [(0, 0, False, False), (0, 1, False, True), (1, 0, False, True), (1, 1, False, False)]
        + [(r, l, False, True) for r in (2, 3) for l in (0, 1)],
    )

    visit_v = [(got_border, i * half, i) for i in range(got_border.shape[0] // half)]
    if near:
        visit_v += [(passed_3, last * half, 2), (sent[3], half, 3)]
    visit_v = visits(visit_v, v_goal)
    both = [left_0[0] + left_2[0], left_0[1] + left_2[1]]
    scores += meet(
        both, [*visit_3, *visit_v], [(r, l, False, True) for r in range(4) for l in (0, 1)]
    )
    (over_3,) = after([over_3], [best for best, _ in scores[2:6:2]])
    across_3 = core_swap(over_3, "across_3")
    left_3 = sides([own_3, beside_3, over_3, across_3], third)
    visit_u = [visit_2[0] + visit_3[0], visit_2[1] + visit_3[1]]
    scores += meet(
        left_3,
        [*mine_3, *visit_u, *visit_v],
        [(0, 0, True, False), (0, 1, False, True), (1, 0, False, True), (1, 1, True, False)]
        + [(r, l, False, True) for r in range(2, 6) for l in (0, 1)],
    )
    found = pl.pallas_call(
        functools.partial(
            route_kernel, [goals for _, goals in scores], parts, members, half, near
        ),
        out_shape=jax.ShapeDtypeStruct((parts * members, 1, 2 * slots), jnp.float32),
        in_specs=[SCALARS] + [WHOLE] * len(scores),
        out_specs=WHOLE,
        scratch_shapes=[pltpu.VMEM((1, v_goal + parts * half), jnp.float32)],
        compiler_params=grant(8),
        name="route",
    )(place, *[best for best, _ in scores])
    got = lax.all_to_all(found, ("blk", "split"), split_axis=0, concat_axis=0, tiled=True)
    return in_data_order(got, rank, parts, members).reshape(rows)


def solution(mesh):
    spec = P(("groups", "blk", "split"))
    return jax.shard_map(
        body,
        mesh=mesh,
        in_specs=(P(("groups", "blk", "split"), None), spec, spec),
        out_specs=spec,
        check_vma=False,
    )
```

time: 99 us -> 88.8 us (0.90); the launches traced: 98.8 us -> 87.4 us
  starting transfers between devices: 28.3 us -> 15.1 us
  blocking collectives: 10.6 us -> 16.1 us
  Pallas kernels: 26 us -> 20.6 us
  waiting for transfers between devices: 30.9 us -> 32.6 us
    ppermute x8 -> x6, starting transfers between devices: 22 us -> 10.9 us  [between(): return lax.ppermute(array, 'blk', route)]
    ppermute x4 -> x3, waiting for transfers between devices: 4.24 us -> 14.2 us  [chip_swap(): return lax.ppermute(array, 'blk', [(b, b ^ 1) for b in range(blocks)])]
    ppermute x8 -> x6, waiting for transfers between devices: 26.6 us -> 18.1 us  [between(): return lax.ppermute(array, 'blk', route)]
    pallas_call x6, Pallas kernels: 20.7 us -> 14.9 us  [the longest x5 14.2 us: meet(): pl.pallas_call(kernel, out_shape=[jax.ShapeDtypeStruct((1, count), jnp.fl...]
    all_to_all x1, blocking collectives: 10.6 us -> 16.1 us  [body(): lax.all_to_all(found, ('blk', 'split'), split_axis=0, concat_axis=0, tile...]
    ppermute x4 -> x3, starting transfers between devices: 5.2 us -> 3.67 us  [chip_swap(): return lax.ppermute(array, 'blk', [(b, b ^ 1) for b in range(blocks)])]
  transfers between devices with their start and end apart: 20 -> 15, of which waited for: 4 -> 7; matrix products, arithmetic and copies ran while one was open for 0% -> 0% of each run, Pallas kernels for 16% -> 14%
where the time goes in v3:
time: 88.8 us; the launch traced here: 87.4 us
  waiting for transfers between devices  32.6 us (37%)
  Pallas kernels  20.6 us (23%)
  blocking collectives  16.1 us (18%)
  starting transfers between devices  15.1 us (17%)
  local copies, waits for them, and re-layouts  2.81 us (3%)
    ppermute x6, waiting for transfers between devices, between(): return lax.ppermute(array, 'blk', route)  18.1 us
    all_to_all x1, blocking collectives, body(): lax.all_to_all(found, ('blk', 'split'), split_axis=0, concat_axis=0, tile...  16.1 us
    ppermute x3, waiting for transfers between devices, chip_swap(): return lax.ppermute(array, 'blk', [(b, b ^ 1) for b in range(blocks)])  14.2 us
    pallas_call x5, Pallas kernels, meet(): pl.pallas_call(kernel, out_shape=[jax.ShapeDtypeStruct((1, count), jnp.fl...  14.2 us
    ppermute x6, starting transfers between devices, between(): return lax.ppermute(array, 'blk', route)  10.9 us
    pallas_call x1, Pallas kernels, in_order(): pl.pallas_call(functools.partial(order_kernel, parts), out_shape=outs, in...  4.25 us
    ppermute x3, starting transfers between devices, chip_swap(): return lax.ppermute(array, 'blk', [(b, b ^ 1) for b in range(blocks)])  3.67 us
    unnamed x7, local copies, waits for them, and re-layouts  2.81 us
  transfers between devices with their start and end apart: 15, of which 7 were waited for; matrix products, arithmetic and copies ran while one was open for 0% of the time, Pallas kernels for 14%

profile of v3, /device:TPU:0, one launch (start us, length us, event | category | flops | bytes accessed | tf_op | source)
XLA Modules:
  0.0 87.4 jit_solution(15908253578330490619)
XLA Ops:
  0.0 0.1 pad_add_fusion.place_ref
  0.1 0.0 copy-start
  0.1 1.4 %copy-done = bf16[1024,768]{1,0:T(8,128)(2,1)S(1)} copy-done((bf16[1024,768]{1,0:T(8,128)(2,1)S(1)}, bf16[1024,768]{1,0:T(8,128)(2,1)}, u32[]{:S(2)}) %copy-start) | copy-done | bytes 1572888
  1.5 0.0 copy-start.1
  1.5 0.7 copy-done.1
  2.2 0.0 copy-start.2
  2.2 0.7 copy-done.2
  2.9 4.3 %order.1 = (bf16[264,768]{1,0:T(8,128)(2,1)S(1)}, bf16[264,768]{1,0:T(8,128)(2,1)S(1)}, bf16[264,768]{1,0:T(8,128)(2,1)S(1)}, bf16[264,768]{1,0:T(8,128)(2,1)S(1)}, s32[1,1024]{1,0:T(1,128)S(1)}) custom-call(s32[2]{0:T(128)S(1)} %pad_add_fusion.place_ref, bf16[1024,768]{1,0:T(8,128)(2,1)S(1)} %copy-done, s32[1,1024]{1,0:T(1,128)S(1)} %bitcast.5, ...), custom_call_target="tpu_custom_call" | custom-call | tf_op jit(solution)/shard_map/order/pallas_call | solution.py:94
  7.1 4.1 %collective-permute-start.4 = (bf16[264,768]{1,0:T(8,128)(2,1)S(1)}, bf16[264,768]{1,0:T(8,128)(2,1)S(1)}, u32[]{:S(2)}, u32[]{:S(2)}) collective-permute-start(bf16[264,768]{1,0:T(8,128)(2,1)S(1)} %get-tuple-element.28.refs_3_), channel_id=1, source_target_pairs={{0,8},{2,10},{4,12},{6,14},{8,0},{10,2},{12,4},{14,6},{1,9},{3,11}... | collective-permute-start | bytes 1216520 | tf_op jit(solution)/shard_map/rows_2/ppermute | solution.py:401
  11.2 1.6 %collective-permute-start.3 = (bf16[264,768]{1,0:T(8,128)(2,1)S(1)}, bf16[264,768]{1,0:T(8,128)(2,1)S(1)}, u32[]{:S(2)}, u32[]{:S(2)}) collective-permute-start(bf16[264,768]{1,0:T(8,128)(2,1)S(1)} %get-tuple-element.27.refs_6_.refs_5_), channel_id=1, source_target_pairs={{0,4},{2,6},{4,0},{6,2},{8,12},{10,14},{12,8},{14,10},{1,5},{3,7},... | collective-permute-start | bytes 1216520 | tf_op jit(solution)/shard_map/rows_2/ppermute | solution.py:401
  12.8 1.5 %collective-permute-start.1 = (bf16[264,768]{1,0:T(8,128)(2,1)S(1)}, bf16[264,768]{1,0:T(8,128)(2,1)S(1)}, u32[]{:S(2)}, u32[]{:S(2)}) collective-permute-start(bf16[264,768]{1,0:T(8,128)(2,1)S(1)} %get-tuple-element.26.refs_2_.refs_0_.refs_1_), channel_id=1, source_target_pairs={{0,2},{2,0},{4,6},{6,4},{8,10},{10,8},{12,14},{14,12},{1,3},{3,1},... | collective-permute-start | bytes 1216520 | tf_op jit(solution)/shard_map/over_0/ppermute | solution.py:408
  14.3 15.0 %collective-permute-done.4.refs_1_ = bf16[264,768]{1,0:T(8,128)(2,1)S(1)} collective-permute-done((bf16[264,768]{1,0:T(8,128)(2,1)S(1)}, bf16[264,768]{1,0:T(8,128)(2,1)S(1)}, u32[]{:S(2)}, u32[]{:S(2)}) %collective-permute-start.4) | collective-permute-done | bytes 405536 | tf_op jit(solution)/shard_map/rows_2/ppermute | solution.py:401
  29.4 0.2 collective-permute-done.3.refs_0_
  29.6 0.0 collective-permute-done.1.refs_4_.refs_2_
  29.6 0.1 pack.2
  29.7 1.6 %collective-permute-start.6 = (bf16[520,768]{1,0:T(8,128)(2,1)S(1)}, bf16[520,768]{1,0:T(8,128)(2,1)S(1)}, u32[]{:S(2)}, u32[]{:S(2)}) collective-permute-start(bf16[520,768]{1,0:T(8,128)(2,1)S(1)} %get-tuple-element.30.refs_4_.refs_2_.refs_0_), channel_id=1, source_target_pairs={{0,2},{2,0},{4,6},{6,4},{8,10},{10,8},{12,14},{14,12},{1,3},{3,1},... | collective-permute-start | bytes 2396168 | tf_op jit(solution)/shard_map/over_2/ppermute | solution.py:408
  31.3 0.0 collective-permute-start
  31.3 0.5 collective-permute-start.5
  31.8 3.2 %collective-permute-start.8 = (bf16[264,768]{1,0:T(8,128)(2,1)S(1)}, bf16[264,768]{1,0:T(8,128)(2,1)S(1)}, u32[]{:S(2)}, u32[]{:S(2)}) collective-permute-start(bf16[264,768]{1,0:T(8,128)(2,1)S(1)} %get-tuple-element.33), channel_id=1, source_target_pairs={{0,12},{2,14},{4,8},{6,10},{8,4},{10,6},{12,0},{14,2},{1,13},{3,15... | collective-permute-start | bytes 1216520 | tf_op jit(solution)/shard_map/rows_3/ppermute | solution.py:401
  35.0 0.0 collective-permute-start.2
  35.0 0.0 collective-permute-done.refs_1_
  35.0 0.0 collective-permute-start.9
  35.0 13.5 %collective-permute-done.6.refs_4_.refs_2_.refs_6_ = bf16[520,768]{1,0:T(8,128)(2,1)S(1)} collective-permute-done((bf16[520,768]{1,0:T(8,128)(2,1)S(1)}, bf16[520,768]{1,0:T(8,128)(2,1)S(1)}, u32[]{:S(2)}, u32[]{:S(2)}) %collective-permute-start.6) | collective-permute-done | bytes 798752 | tf_op jit(solution)/shard_map/over_2/ppermute | solution.py:408
  48.5 0.0 collective-permute-start.7
  48.5 0.0 collective-permute-done.2.refs_3_.refs_6_
  48.5 3.3 %meet.5 = (f32[1,1024]{1,0:T(1,128)S(1)}, f32[1,768]{1,0:T(1,128)S(1)}) custom-call(bf16[264,768]{1,0:T(8,128)(2,1)S(1)} %get-tuple-element.26.refs_2_.refs_0_.refs_1_, bf16[264,768]{1,0:T(8,128)(2,1)S(1)} %collective-permute-done.refs_1_, bf16[264,768]{1,0:T(8,128)(2,1)S(1)} %collective-permute-done.1.refs_4_.refs_2_, ...), custom_call_target="tpu_custom_call" | custom-call | tf_op jit(solution)/shard_map/meet/pallas_call | solution.py:292
  51.8 0.0 collective-permute-done.8.refs_0_
  51.8 1.9 %collective-permute-done.9.refs_5_.refs_4_ = bf16[264,768]{1,0:T(8,128)(2,1)S(1)} collective-permute-done((bf16[264,768]{1,0:T(8,128)(2,1)S(1)}, bf16[264,768]{1,0:T(8,128)(2,1)S(1)}, u32[]{:S(2)}, u32[]{:S(2)}) %collective-permute-start.9) | collective-permute-done | bytes 405536 | tf_op jit(solution)/shard_map/passed_2/ppermute | solution.py:401
  53.7 0.0 collective-permute-done.5.refs_7_.refs_1_.refs_5_
  53.7 0.1 pack.3
  53.8 0.5 collective-permute-start.13
  54.3 0.0 collective-permute-start.12
  54.3 1.4 %collective-permute-start.10 = (bf16[264,768]{1,0:T(8,128)(2,1)S(1)}, bf16[264,768]{1,0:T(8,128)(2,1)S(1)}, u32[]{:S(2)}, u32[]{:S(2)}) collective-permute-start(bf16[264,768]{1,0:T(8,128)(2,1)S(1)} %get-tuple-element.40), channel_id=1, source_target_pairs={{0,4},{2,6},{4,0},{6,2},{8,12},{10,14},{12,8},{14,10},{1,5},{3,7},... | collective-permute-start | bytes 1216520 | tf_op jit(solution)/shard_map/passed_3/ppermute | solution.py:401
  55.7 0.7 collective-permute-start.11
  56.4 2.1 %meet.7 = (f32[1,1024]{1,0:T(1,128)S(1)}, f32[1,640]{1,0:T(1,128)S(1)}) custom-call(bf16[264,768]{1,0:T(8,128)(2,1)S(1)} %get-tuple-element.26.refs_2_.refs_0_.refs_1_, bf16[264,768]{1,0:T(8,128)(2,1)S(1)} %collective-permute-done.refs_1_, bf16[264,768]{1,0:T(8,128)(2,1)S(1)} %collective-permute-done.1.refs_4_.refs_2_, ...), custom_call_target="tpu_custom_call" | custom-call | tf_op jit(solution)/shard_map/meet/pallas_call | solution.py:292
  58.5 0.0 collective-permute-done.7.refs_3_.refs_7_
  58.5 5.9 %meet.6 = (f32[1,2048]{1,0:T(1,128)S(1)}, f32[1,1152]{1,0:T(1,128)S(1)}) custom-call(bf16[520,768]{1,0:T(8,128)(2,1)S(1)} %get-tuple-element.30.refs_4_.refs_2_.refs_0_, bf16[520,768]{1,0:T(8,128)(2,1)S(1)} %collective-permute-done.5.refs_7_.refs_1_.refs_5_, bf16[520,768]{1,0:T(8,128)(2,1)S(1)} %collective-permute-done.6.refs_4_.refs_2_.refs_6_, ...), custom_call_target="tpu_custom_call" | custom-call | tf_op jit(solution)/shard_map/meet/pallas_call | solution.py:292
  64.4 0.8 collective-permute-done.13.refs_0_
  65.2 0.0 collective-permute-start.14
  65.2 0.9 %collective-permute-done.10.refs_8_.refs_6_ = bf16[264,768]{1,0:T(8,128)(2,1)S(1)} collective-permute-done((bf16[264,768]{1,0:T(8,128)(2,1)S(1)}, bf16[264,768]{1,0:T(8,128)(2,1)S(1)}, u32[]{:S(2)}, u32[]{:S(2)}) %collective-permute-start.10) | collective-permute-done | bytes 405536 | tf_op jit(solution)/shard_map/passed_3/ppermute | solution.py:401
  66.1 0.0 collective-permute-done.11.refs_9_.refs_7_
  66.1 0.5 meet.8
  66.6 0.0 collective-permute-done.12.refs_1_
  66.7 0.3 collective-permute-done.14.refs_3_
  66.9 2.4 %meet.9 = (f32[1,1024]{1,0:T(1,128)S(1)}, f32[1,1280]{1,0:T(1,128)S(1)}) custom-call(bf16[264,768]{1,0:T(8,128)(2,1)S(1)} %get-tuple-element.35.refs_4_.refs_0_, bf16[264,768]{1,0:T(8,128)(2,1)S(1)} %collective-permute-done.12.refs_1_, bf16[264,768]{1,0:T(8,128)(2,1)S(1)} %after.1.refs_2_, bf16[264,768]{1,0:T(8,128)(2,1)S(1)} %collective-permute-done.14.refs_3_, ...), custom_call_target="tpu_custom_call" | custom-call | tf_op jit(solution)/shard_map/meet/pallas_call | solution.py:292
  69.3 0.7 route.1
  70.0 16.1 %all_to_all.5.got_ref = f32[16,1,512]{2,1,0:T(1,128)S(1)} all-to-all(f32[16,1,512]{2,1,0:T(1,128)S(1)} %route.1), channel_id=1, replica_groups=mesh['groups'=2,'blk'=8,'split'=2] {'blk','split'}, dimensions={0} | all-to-all | bytes 65536 | tf_op jit(solution)/shard_map/all_to_all | solution.py:532
  86.1 1.3 %back.1 = f32[1,1024]{1,0:T(1,128)} custom-call(f32[16,1,512]{2,1,0:T(1,128)S(1)} %all_to_all.5.got_ref, s32[1,1024]{1,0:T(1,128)S(1)} %get-tuple-element.46.rank_ref), custom_call_target="tpu_custom_call" | custom-call | tf_op jit(solution)/shard_map/back/pallas_call | solution.py:377
  (2 shorter events, 0.0 us)
Async XLA Ops:
  0.1 1.4 %copy-start = (bf16[1024,768]{1,0:T(8,128)(2,1)S(1)}, bf16[1024,768]{1,0:T(8,128)(2,1)}, u32[]{:S(2)}) copy-start(bf16[1024,768]{1,0:T(8,128)(2,1)} %rows_hbm.1) | copy-start | bytes 4718596
  1.5 0.7 copy-start.1
  2.2 0.7 copy-start.2
  7.1 22.3 %collective-permute-start.4 = (bf16[264,768]{1,0:T(8,128)(2,1)S(1)}, bf16[264,768]{1,0:T(8,128)(2,1)S(1)}, u32[]{:S(2)}, u32[]{:S(2)}) collective-permute-start(bf16[264,768]{1,0:T(8,128)(2,1)S(1)} %get-tuple-element.28.refs_3_), channel_id=1, source_target_pairs={{0,8},{2,10},{4,12},{6,14},{8,0},{10,2},{12,4},{14,6},{1,9},{3,11}... | collective-permute-start | bytes 1216520 | tf_op jit(solution)/shard_map/rows_2/ppermute | solution.py:401
  11.2 18.4 %collective-permute-start.3 = (bf16[264,768]{1,0:T(8,128)(2,1)S(1)}, bf16[264,768]{1,0:T(8,128)(2,1)S(1)}, u32[]{:S(2)}, u32[]{:S(2)}) collective-permute-start(bf16[264,768]{1,0:T(8,128)(2,1)S(1)} %get-tuple-element.27.refs_6_.refs_5_), channel_id=1, source_target_pairs={{0,4},{2,6},{4,0},{6,2},{8,12},{10,14},{12,8},{14,10},{1,5},{3,7},... | collective-permute-start | bytes 1216520 | tf_op jit(solution)/shard_map/rows_2/ppermute | solution.py:401
  12.8 16.8 %collective-permute-start.1 = (bf16[264,768]{1,0:T(8,128)(2,1)S(1)}, bf16[264,768]{1,0:T(8,128)(2,1)S(1)}, u32[]{:S(2)}, u32[]{:S(2)}) collective-permute-start(bf16[264,768]{1,0:T(8,128)(2,1)S(1)} %get-tuple-element.26.refs_2_.refs_0_.refs_1_), channel_id=1, source_target_pairs={{0,2},{2,0},{4,6},{6,4},{8,10},{10,8},{12,14},{14,12},{1,3},{3,1},... | collective-permute-start | bytes 1216520 | tf_op jit(solution)/shard_map/over_0/ppermute | solution.py:408
  29.7 18.8 %collective-permute-start.6 = (bf16[520,768]{1,0:T(8,128)(2,1)S(1)}, bf16[520,768]{1,0:T(8,128)(2,1)S(1)}, u32[]{:S(2)}, u32[]{:S(2)}) collective-permute-start(bf16[520,768]{1,0:T(8,128)(2,1)S(1)} %get-tuple-element.30.refs_4_.refs_2_.refs_0_), channel_id=1, source_target_pairs={{0,2},{2,0},{4,6},{6,4},{8,10},{10,8},{12,14},{14,12},{1,3},{3,1},... | collective-permute-start | bytes 2396168 | tf_op jit(solution)/shard_map/over_2/ppermute | solution.py:408
  31.3 3.7 %collective-permute-start = (bf16[264,768]{1,0:T(8,128)(2,1)S(1)}, bf16[264,768]{1,0:T(8,128)(2,1)S(1)}, u32[]{:S(2)}, u32[]{:S(2)}) collective-permute-start(bf16[264,768]{1,0:T(8,128)(2,1)S(1)} %get-tuple-element.26.refs_2_.refs_0_.refs_1_), channel_id=1, source_target_pairs={{0,1},{1,0},{2,3},{3,2},{4,5},{5,4},{6,7},{7,6},{8,9},{9,8},{10,11... | collective-permute-start | bytes 1216520 | tf_op jit(solution)/shard_map/beside_0/ppermute | solution.py:412
  31.3 22.4 %collective-permute-start.5 = (bf16[520,768]{1,0:T(8,128)(2,1)S(1)}, bf16[520,768]{1,0:T(8,128)(2,1)S(1)}, u32[]{:S(2)}, u32[]{:S(2)}) collective-permute-start(bf16[520,768]{1,0:T(8,128)(2,1)S(1)} %get-tuple-element.30.refs_4_.refs_2_.refs_0_), channel_id=1, source_target_pairs={{0,1},{1,0},{2,3},{3,2},{4,5},{5,4},{6,7},{7,6},{8,9},{9,8},{10,11... | collective-permute-start | bytes 2396168 | tf_op jit(solution)/shard_map/beside_2/ppermute | solution.py:412
  31.8 19.9 %collective-permute-start.8 = (bf16[264,768]{1,0:T(8,128)(2,1)S(1)}, bf16[264,768]{1,0:T(8,128)(2,1)S(1)}, u32[]{:S(2)}, u32[]{:S(2)}) collective-permute-start(bf16[264,768]{1,0:T(8,128)(2,1)S(1)} %get-tuple-element.33), channel_id=1, source_target_pairs={{0,12},{2,14},{4,8},{6,10},{8,4},{10,6},{12,0},{14,2},{1,13},{3,15... | collective-permute-start | bytes 1216520 | tf_op jit(solution)/shard_map/rows_3/ppermute | solution.py:401
  35.0 13.5 %collective-permute-start.2 = (bf16[264,768]{1,0:T(8,128)(2,1)S(1)}, bf16[264,768]{1,0:T(8,128)(2,1)S(1)}, u32[]{:S(2)}, u32[]{:S(2)}) collective-permute-start(bf16[264,768]{1,0:T(8,128)(2,1)S(1)} %collective-permute-done.1.refs_4_.refs_2_), channel_id=1, source_target_pairs={{0,1},{1,0},{2,3},{3,2},{4,5},{5,4},{6,7},{7,6},{8,9},{9,8},{10,11... | collective-permute-start | bytes 1216520 | tf_op jit(solution)/shard_map/across_0/ppermute | solution.py:412
  35.0 18.7 %collective-permute-start.9 = (bf16[264,768]{1,0:T(8,128)(2,1)S(1)}, bf16[264,768]{1,0:T(8,128)(2,1)S(1)}, u32[]{:S(2)}, u32[]{:S(2)}) collective-permute-start(bf16[264,768]{1,0:T(8,128)(2,1)S(1)} %get-tuple-element.34), channel_id=1, source_target_pairs={{0,4},{2,6},{4,0},{6,2},{8,12},{10,14},{12,8},{14,10},{1,5},{3,7},... | collective-permute-start | bytes 1216520 | tf_op jit(solution)/shard_map/passed_2/ppermute | solution.py:401
  48.5 10.0 %collective-permute-start.7 = (bf16[520,768]{1,0:T(8,128)(2,1)S(1)}, bf16[520,768]{1,0:T(8,128)(2,1)S(1)}, u32[]{:S(2)}, u32[]{:S(2)}) collective-permute-start(bf16[520,768]{1,0:T(8,128)(2,1)S(1)} %collective-permute-done.6.refs_4_.refs_2_.refs_6_), channel_id=1, source_target_pairs={{0,1},{1,0},{2,3},{3,2},{4,5},{5,4},{6,7},{7,6},{8,9},{9,8},{10,11... | collective-permute-start | bytes 2396168 | tf_op jit(solution)/shard_map/across_2/ppermute | solution.py:412
  53.8 11.4 %collective-permute-start.13 = (bf16[264,768]{1,0:T(8,128)(2,1)S(1)}, bf16[264,768]{1,0:T(8,128)(2,1)S(1)}, u32[]{:S(2)}, u32[]{:S(2)}) collective-permute-start(bf16[264,768]{1,0:T(8,128)(2,1)S(1)} %get-tuple-element.35.refs_4_.refs_0_), channel_id=1, source_target_pairs={{0,2},{2,0},{4,6},{6,4},{8,10},{10,8},{12,14},{14,12},{1,3},{3,1},... | collective-permute-start | bytes 1216520 | tf_op jit(solution)/shard_map/over_3/ppermute | solution.py:408
  54.3 12.3 %collective-permute-start.12 = (bf16[264,768]{1,0:T(8,128)(2,1)S(1)}, bf16[264,768]{1,0:T(8,128)(2,1)S(1)}, u32[]{:S(2)}, u32[]{:S(2)}) collective-permute-start(bf16[264,768]{1,0:T(8,128)(2,1)S(1)} %get-tuple-element.35.refs_4_.refs_0_), channel_id=1, source_target_pairs={{0,1},{1,0},{2,3},{3,2},{4,5},{5,4},{6,7},{7,6},{8,9},{9,8},{10,11... | collective-permute-start | bytes 1216520 | tf_op jit(solution)/shard_map/beside_3/ppermute | solution.py:412
  54.3 11.8 %collective-permute-start.10 = (bf16[264,768]{1,0:T(8,128)(2,1)S(1)}, bf16[264,768]{1,0:T(8,128)(2,1)S(1)}, u32[]{:S(2)}, u32[]{:S(2)}) collective-permute-start(bf16[264,768]{1,0:T(8,128)(2,1)S(1)} %get-tuple-element.40), channel_id=1, source_target_pairs={{0,4},{2,6},{4,0},{6,2},{8,12},{10,14},{12,8},{14,10},{1,5},{3,7},... | collective-permute-start | bytes 1216520 | tf_op jit(solution)/shard_map/passed_3/ppermute | solution.py:401
  55.7 10.4 %collective-permute-start.11 = (bf16[264,768]{1,0:T(8,128)(2,1)S(1)}, bf16[264,768]{1,0:T(8,128)(2,1)S(1)}, u32[]{:S(2)}, u32[]{:S(2)}) collective-permute-start(bf16[264,768]{1,0:T(8,128)(2,1)S(1)} %get-tuple-element.41), channel_id=1, source_target_pairs={{4,8},{6,10},{8,4},{10,6},{5,9},{7,11},{9,5},{11,7},{20,24},{22,26... | collective-permute-start | bytes 1216520 | tf_op jit(solution)/shard_map/border/ppermute | solution.py:401
  65.2 1.7 %collective-permute-start.14 = (bf16[264,768]{1,0:T(8,128)(2,1)S(1)}, bf16[264,768]{1,0:T(8,128)(2,1)S(1)}, u32[]{:S(2)}, u32[]{:S(2)}) collective-permute-start(bf16[264,768]{1,0:T(8,128)(2,1)S(1)} %after.1.refs_2_), channel_id=1, source_target_pairs={{0,1},{1,0},{2,3},{3,2},{4,5},{5,4},{6,7},{7,6},{8,9},{9,8},{10,11... | collective-permute-start | bytes 1216520 | tf_op jit(solution)/shard_map/across_3/ppermute | solution.py:412

commit v4 on v3

--- a/solution.py
+++ b/solution.py
@@ -15,7 +15,6 @@
 WHOLE = pl.BlockSpec(memory_space=pltpu.VMEM)
 ANYWHERE = pl.BlockSpec(memory_space=pl.ANY)
 REMAINS = pl.BlockSpec(memory_space=pltpu.HBM)
-SCALARS = pl.BlockSpec(memory_space=pltpu.SMEM)
 
 
 def grant(mib):
@@ -38,20 +37,18 @@
     return best
 
 
-def order_kernel(parts, place_ref, rows_hbm, ids_hbm, pos_hbm, *refs):
+def order_kernel(parts, chips, rows_hbm, marks_hbm, *refs):
     outs, rank_ref = refs[:parts], refs[parts]
-    unit, pick, placed, tags, rows_ref, ids_ref, pos_ref, sems = refs[parts + 1 :]
+    unit, pick, placed, tags, rows_ref, marks_ref, sems = refs[parts + 1 :]
     count, width = rows_ref.shape
     quart = count // parts // 4
     step = 256
-    fetch_pos = pltpu.make_async_copy(pos_hbm, pos_ref, sems.at[0])
+    fetch_marks = pltpu.make_async_copy(marks_hbm, marks_ref, sems.at[0])
     fetch_rows = pltpu.make_async_copy(rows_hbm, rows_ref, sems.at[1])
-    fetch_ids = pltpu.make_async_copy(ids_hbm, ids_ref, sems.at[2])
-    fetch_pos.start()
+    fetch_marks.start()
     fetch_rows.start()
-    fetch_ids.start()
-    fetch_pos.wait()
-    pos = pos_ref[...].astype(jnp.float32)
+    fetch_marks.wait()
+    pos = marks_ref[1:2, :].astype(jnp.float32)
     below = jnp.zeros((8, count), jnp.float32)
     for at in range(0, count, step):
         other = spread(pos[:, at : at + step])[:, :1]
@@ -62,7 +59,6 @@
         slot = lax.broadcasted_iota(jnp.int32, (step, count), 0) + at
         pick[at : at + step, :] = jnp.where(slot == rank, 1.0, 0.0).astype(jnp.bfloat16)
     fetch_rows.wait()
-    fetch_ids.wait()
     values = rows_ref[...].astype(jnp.float32)
     total = jnp.sum(values * values, axis=1, keepdims=True)
     unit[...] = (values * lax.rsqrt(total + 1e-06)).astype(jnp.bfloat16)
@@ -70,14 +66,15 @@
         placed[at : at + step, :] = jnp.dot(
             pick[at : at + step, :], unit[...], preferred_element_type=jnp.float32
         ).astype(jnp.bfloat16)
-    ids = jnp.broadcast_to((ids_ref[...] + 1).astype(jnp.bfloat16), (16, count))
+    ids = jnp.broadcast_to((marks_ref[:1, :] + 1).astype(jnp.bfloat16), (16, count))
+    part = lax.axis_index("blk") // chips
     sorted_ids = lax.dot_general(
         ids, pick[...], (((1,), (1,)), ((), ())), preferred_element_type=jnp.float32
     )
     for at in range(4 * parts):
         tags[at, :, :quart] = sorted_ids[:, at * quart : (at + 1) * quart]
     for k in range(parts):
-        quarter = lax.bitwise_xor(place_ref[0], k)
+        quarter = lax.bitwise_xor(part, k)
         side = lax.rem(quarter, 2)
         for index, block in enumerate((3 - 3 * side, 2 - side, 3 * side, 1 + side)):
             which = 4 * quarter + block
@@ -86,15 +83,15 @@
             outs[k][4 * quart :, at : at + quart] = tags[which, :TAGS, :quart].astype(jnp.bfloat16)
 
 
-def in_order(place, embeddings, ids, pos, parts):
+def in_order(embeddings, ids, pos, parts, chips):
     count, width = embeddings.shape
     slots = count // parts
     block = jax.ShapeDtypeStruct((slots + TAGS, width), jnp.bfloat16)
     outs = [block] * parts + [jax.ShapeDtypeStruct((1, count), jnp.int32)]
     *blocks, rank = pl.pallas_call(
-        functools.partial(order_kernel, parts),
+        functools.partial(order_kernel, parts, chips),
         out_shape=outs,
-        in_specs=[SCALARS, REMAINS, REMAINS, REMAINS],
+        in_specs=[REMAINS, REMAINS],
         out_specs=[WHOLE] * len(outs),
         scratch_shapes=[
             pltpu.VMEM((count, width), jnp.bfloat16),
@@ -102,13 +99,12 @@
             pltpu.VMEM((count, width), jnp.bfloat16),
             pltpu.VMEM((4 * parts, 16, max(slots // 4, LANES)), jnp.float32),
             pltpu.VMEM((count, width), jnp.bfloat16),
-            pltpu.VMEM((1, count), jnp.int32),
-            pltpu.VMEM((1, count), jnp.int32),
-            pltpu.SemaphoreType.DMA((3,)),
+            pltpu.VMEM((2, count), jnp.int32),
+            pltpu.SemaphoreType.DMA((2,)),
         ],
         compiler_params=grant(24),
         name="order",
-    )(place, embeddings, ids.reshape(1, count), pos.reshape(1, count))
+    )(embeddings, jnp.stack([ids, pos]))
     return blocks, rank
 
 
@@ -162,6 +158,11 @@
     )(*held, *earlier)
 
 
+def padded(section):
+    rows = sum(piece[2] for piece in section)
+    return -(-rows // LANES) * LANES
+
+
 def overlap(one, other):
     return jnp.logical_and(one[0] <= other[1], other[0] <= one[1])
 
@@ -185,79 +186,86 @@
 
     tested = [(r, l) for r, l, _, test in pairs if test]
     right_span = {r: span(rights[r]) for r in sorted({r for r, _ in tested})}
-    left_span = {l: span(lefts[l]) for l in sorted({l for _, l in tested})}
+    left_span = {l: span(sum((lefts[i] for i in l), [])) for l in sorted({l for _, l in tested})}
     wanted = {(r, l): overlap(right_span[r], left_span[l]) for r, l in tested}
 
     def place_of(sections):
         out, at = [], 0
         for section in sections:
-            rows = sum(piece[2] for piece in section)
+            rows = padded(section)
             out.append((at, rows))
             at += rows
         return out
 
     left_at, right_at = place_of(lefts), place_of(rights)
 
-    def fill(buffer, section, at):
-        for index, start, rows in section:
-            buffer[at : at + rows, :] = given[index][start : start + rows, :]
+    def fill_left(number):
+        at = left_at[number][0]
+        for piece in lefts[number]:
+            index, start, rows = piece
+            left[at : at + rows, :] = given[index][start : start + rows, :]
+            left_ids[at : at + rows, :TAGS] = jnp.transpose(ids_of(piece))
+            at += rows
+
+    def fill_right(number):
+        at = right_at[number][0]
+        for piece in rights[number]:
+            index, start, rows = piece
+            right[at : at + rows, :] = given[index][start : start + rows, :]
+            right_ids[:, at : at + rows] = ids_of(piece)
             at += rows
 
     left_best[...] = jnp.full(left_best.shape, FILL, jnp.float32)
     right_best[...] = jnp.full(right_best.shape, FILL, jnp.float32)
-    for section, (at, _) in zip(lefts, left_at):
-        for piece in section:
-            left_ids[:, at : at + piece[2]] = ids_of(piece)
-            at += piece[2]
-    for section, (at, _) in zip(rights, right_at):
-        for piece in section:
-            right_ids[at : at + piece[2], :] = spread(ids_of(piece)[:1, :])
-            at += piece[2]
-    for which, sections, places, buffer in ((1, lefts, left_at, left), (0, rights, right_at, right)):
-        for number, section in enumerate(sections):
-            uses = [p for p in pairs if p[which] == number]
-            load = functools.partial(fill, buffer, section, places[number][0])
+    right_ids[...] = jnp.full(right_ids.shape, -1.0, jnp.float32)
+    for which, sections, fill in ((1, lefts, fill_left), (0, rights, fill_right)):
+        for number in range(len(sections)):
+            uses = [p for p in pairs if (number in p[1] if which else number == p[0])]
+            load = functools.partial(fill, number)
             if all(p[3] for p in uses):
                 need = [wanted[p[0], p[1]] for p in uses]
                 pl.when(functools.reduce(jnp.logical_or, need))(load)
             else:
                 load()
 
-    def score(r, l, diagonal):
-        (row, rows), (column, columns) = right_at[r], left_at[l]
+    def score(r, l, same):
+        (lane, lanes), row = right_at[r], left_at[l[0]][0]
+        rows = sum(left_at[i][1] for i in l)
         step = rows
-        while step * columns > 512 * 1024 and step % 32 == 0:
+        while step * lanes > 512 * 1024 and step % 32 == 0:
             step //= 2
-        across = slice(column, column + columns)
+        across = slice(lane, lane + lanes)
 
         def turn(index, _):
             at = pl.multiple_of(row + index * step, 16)
             down = pl.ds(at, step)
             scores = lax.dot_general(
-                right[down, :],
-                left[across, :],
+                left[down, :],
+                right[across, :],
                 (((1,), (1,)), ((), ())),
                 preferred_element_type=jnp.float32,
             )
-            scores = jnp.where(right_ids[down, :1] == left_ids[:1, across], scores, FILL)
-            if diagonal:
-                mine = lax.broadcasted_iota(jnp.int32, (step, columns), 0) + index * step
-                theirs = lax.broadcasted_iota(jnp.int32, (step, columns), 1)
-                scores = jnp.where(mine == theirs, FILL, scores)
-            right_best[down, :] = jnp.maximum(right_best[down, :], lane_fold(scores))
-            left_best[:, across] = jnp.maximum(left_best[:, across], column_fold(scores))
+            scores = jnp.where(left_ids[down, :1] == right_ids[:1, across], scores, FILL)
+            if same is not None:
+                first, count = same
+                theirs = lax.broadcasted_iota(jnp.int32, (step, lanes), 0) + index * step
+                mine = lax.broadcasted_iota(jnp.int32, (step, lanes), 1)
+                itself = jnp.logical_and(theirs + first == mine, theirs < count)
+                scores = jnp.where(itself, FILL, scores)
+            left_best[down, :] = jnp.maximum(left_best[down, :], lane_fold(scores))
+            right_best[:, across] = jnp.maximum(right_best[:, across], column_fold(scores))
             return 0
 
         lax.fori_loop(0, rows // step, turn, 0)
 
-    for r, l, diagonal, test in pairs:
-        run = functools.partial(score, r, l, diagonal)
+    for r, l, same, test in pairs:
+        run = functools.partial(score, r, l, same)
         if test:
             pl.when(wanted[r, l])(run)
         else:
             run()
-    left_out[...] = jnp.max(left_best[...], axis=0, keepdims=True)
-    right_out[...] = jnp.max(jnp.transpose(right_best[...]), axis=0, keepdims=True)
+    right_out[...] = jnp.max(right_best[...], axis=0, keepdims=True)
+    left_out[...] = jnp.max(jnp.transpose(left_best[...]), axis=0, keepdims=True)
 
 
 def meet(lefts, rights, pairs, earlier=()):
@@ -276,7 +284,11 @@
         return out
 
     def goals(sections):
-        return [(p[3], p[2]) for section in sections for p in section]
+        out = []
+        for section in sections:
+            out += [(p[3], p[2]) for p in section]
+            out.append((None, padded(section) - sum(p[2] for p in section)))
+        return out
 
     plan_left, plan_right = plan(lefts), plan(rights)
     width = blocks[0].shape[1]
@@ -299,22 +311,23 @@
         out_specs=[WHOLE] * 2,
         scratch_shapes=[
             pltpu.VMEM((count, width), jnp.bfloat16),
-            pltpu.VMEM((TAGS, count), jnp.float32),
+            pltpu.VMEM((count, LANES), jnp.float32),
             pltpu.VMEM((total, width), jnp.bfloat16),
-            pltpu.VMEM((total, LANES), jnp.float32),
-            pltpu.VMEM((8, count), jnp.float32),
-            pltpu.VMEM((total, LANES), jnp.float32),
+            pltpu.VMEM((TAGS, total), jnp.float32),
+            pltpu.VMEM((count, LANES), jnp.float32),
+            pltpu.VMEM((8, total), jnp.float32),
         ],
-        compiler_params=grant(24),
+        compiler_params=grant(28),
         cost_estimate=pl.CostEstimate(flops=0, bytes_accessed=0, transcendentals=0),
         name="meet",
     )(*blocks, *earlier)
     return [(left_best, goals(lefts)), (right_best, goals(rights))]
 
 
-def route_kernel(plan, parts, members, half, near, place_ref, *refs):
+def route_kernel(plan, parts, chips, cores, half, near, *refs):
     given, out_ref, gathered = refs[:-2], refs[-2], refs[-1]
-    part, me = place_ref[0], place_ref[1]
+    chip, members = lax.axis_index("blk"), chips * cores
+    part, me = chip // chips, lax.rem(chip, chips) * cores + lax.axis_index("split")
     slots = 2 * half
     out_ref[...] = jnp.full(out_ref.shape, FILL, jnp.float32)
     gathered[...] = jnp.full(gathered.shape, FILL, jnp.float32)
@@ -322,9 +335,10 @@
     for ref, pieces in zip(given, plan):
         at = 0
         for to, entries in pieces:
-            gathered[:, to : to + entries] = jnp.maximum(
-                gathered[:, to : to + entries], ref[:, at : at + entries]
-            )
+            if to is not None:
+                gathered[:, to : to + entries] = jnp.maximum(
+                    gathered[:, to : to + entries], ref[:, at : at + entries]
+                )
             at += entries
     for member in range(members):
         whose = lax.bitwise_xor(me, member)
@@ -392,9 +406,6 @@
     parts = blocks // chips
     half = rows // parts // 2
     slots = 2 * half
-    chip, core = lax.axis_index("blk"), lax.axis_index("split")
-    place = jnp.stack([chip // chips, (chip % chips) * cores + core]).astype(jnp.int32)
-
     def between(array, pairs, name):
         route = [(s * chips + c, t * chips + c) for s, t in pairs for c in range(chips)]
         with jax.named_scope(name):
@@ -430,12 +441,15 @@
                     out.append((block, i * slots + side, half, goal))
         return out[: len(out) // 2], out[len(out) // 2 :]
 
+    def whole(block, ks):
+        return [(block, i * slots, slots, k * slots) for i, k in enumerate(ks)]
+
     def visits(pieces, goal):
         near_rows = [(b, at, quart, goal + i * half) for b, at, i in pieces]
         far_rows = [(b, at + quart, quart, goal + i * half + quart) for b, at, i in pieces]
         return near_rows, far_rows
 
-    sent, rank = in_order(place, embeddings, cluster_of, target_pos, parts)
+    sent, rank = in_order(embeddings, cluster_of, target_pos, parts, chips)
     own_0 = sent[0]
     got = [swap(sent[k], k, "rows_2") for k in second]
     over_0 = chip_swap(own_0, "over_0")
@@ -452,12 +466,15 @@
     across_0 = core_swap(over_0, "across_0")
     beside_2 = core_swap(own_2, "beside_2")
     left_0 = sides([own_0, beside_0, over_0, across_0], [0])
-    mine_0, mine_2 = sides([own_0], [0]), sides([own_2], second)
+    here_2 = sides([own_2, beside_2], second)
+    mine_0, mine_2 = whole(own_0, [0]), sum(sides([own_2], second), [])
+    some = len(second) * half
     scores = meet(
-        left_0,
-        [*mine_0, *mine_2],
-        [(0, 0, True, False), (0, 1, False, True), (1, 0, False, True), (1, 1, True, False)]
-        + [(2, 0, False, False), (2, 1, False, True), (3, 0, False, True), (3, 1, False, False)],
+        [*left_0, *here_2],
+        [mine_0, mine_2],
+        [(0, (0,), (0, half), False), (0, (1,), (half, half), False)]
+        + [(1, (0, 1), None, False)]
+        + [(1, (2,), (0, some), False), (1, (3,), (some, some), False)],
     )
 
     last = len(third)
@@ -473,62 +490,54 @@
     own_3, border, passing = pack(
         inputs,
         [[(i, 0, slots) for i in range(last)], border, forward],
-        earlier=[over_2, passed_2, across_0, beside_2, scores[0][0]],
+        earlier=[scores[0][0]],
     )
     over_3 = chip_swap(own_3, "over_3")
     got_border = between(border, borders, "border")
     passed_3 = swap(passing, 1, "passed_3")
+    (over_2,) = after([over_2], [own_3, passed_2])
     across_2 = core_swap(over_2, "across_2")
     beside_3 = core_swap(own_3, "beside_3")
-    left_2 = sides([own_2, beside_2, over_2, across_2], second)
-    mine_3 = sides([own_3], third)
+    there_2 = sides([over_2, across_2], second, 2)
     visit_2 = [(passed_2, i * half, i) for i in range(len(second))]
     visit_2 = visits(visit_2 + [(sent[1], 0, parts - 1)], u_goal)
     visit_3 = visits([(passed_3, i * half, len(second) + i) for i in range(last)], u_goal)
-    tested = [(r, l, False, True) for r in (4, 5) for l in (0, 1)]
+    mine_3 = sum(sides([own_3], third), [])
+    lefts = [left_0[0], here_2[0], there_2[0], left_0[1], here_2[1], there_2[1]]
+    u_half, v_half = (0, 1, 2), (3, 4, 5)
     scores += meet(
-        left_2,
-        [*mine_2, *mine_3, *visit_2],
-        [(0, 0, True, False), (0, 1, False, True), (1, 0, False, True), (1, 1, True, False)]
-        + [(2, 0, False, False), (2, 1, False, True), (3, 0, False, True), (3, 1, False, False)]
-        + tested,
-    )
-    scores += meet(
-        left_0,
-        [*mine_3, *visit_2],
-        [(0, 0, False, False), (0, 1, False, True), (1, 0, False, True), (1, 1, False, False)]
-        + [(r, l, False, True) for r in (2, 3) for l in (0, 1)],
+        lefts,
+        [mine_2, mine_3, *visit_2],
+        [(0, (2,), None, False), (0, (5,), None, False), (1, u_half + v_half, None, False)]
+        + [(r, l, None, True) for r in (2, 3) for l in (u_half, v_half)],
     )
 
     visit_v = [(got_border, i * half, i) for i in range(got_border.shape[0] // half)]
     if near:
-        visit_v += [(passed_3, last * half, 2), (sent[3], half, 3)]
+        visit_v += [(passed_3, last * half, 2), (held[0], half, 3)]
     visit_v = visits(visit_v, v_goal)
-    both = [left_0[0] + left_2[0], left_0[1] + left_2[1]]
-    scores += meet(
-        both, [*visit_3, *visit_v], [(r, l, False, True) for r in range(4) for l in (0, 1)]
-    )
-    (over_3,) = after([over_3], [best for best, _ in scores[2:6:2]])
+    (over_3,) = after([over_3], [scores[2][0]])
     across_3 = core_swap(over_3, "across_3")
     left_3 = sides([own_3, beside_3, over_3, across_3], third)
-    visit_u = [visit_2[0] + visit_3[0], visit_2[1] + visit_3[1]]
+    some = last * half
     scores += meet(
-        left_3,
-        [*mine_3, *visit_u, *visit_v],
-        [(0, 0, True, False), (0, 1, False, True), (1, 0, False, True), (1, 1, True, False)]
-        + [(r, l, False, True) for r in range(2, 6) for l in (0, 1)],
+        [*lefts[:3], left_3[0], left_3[1], *lefts[3:]],
+        [mine_3, *visit_2, visit_3[0] + visit_3[1], *visit_v],
+        [(0, (3,), (0, some), False), (0, (4,), (some, some), False)]
+        + [(r, (l,), None, True) for r in (1, 2) for l in (3, 4)]
+        + [(r, l, None, True) for r in (3, 4, 5) for l in ((0, 1, 2, 3), (4, 5, 6, 7))],
     )
     found = pl.pallas_call(
         functools.partial(
-            route_kernel, [goals for _, goals in scores], parts, members, half, near
+            route_kernel, [goals for _, goals in scores], parts, chips, cores, half, near
         ),
         out_shape=jax.ShapeDtypeStruct((parts * members, 1, 2 * slots), jnp.float32),
-        in_specs=[SCALARS] + [WHOLE] * len(scores),
+        in_specs=[WHOLE] * len(scores),
         out_specs=WHOLE,
         scratch_shapes=[pltpu.VMEM((1, v_goal + parts * half), jnp.float32)],
         compiler_params=grant(8),
         name="route",
-    )(place, *[best for best, _ in scores])
+    )(*[best for best, _ in scores])
     got = lax.all_to_all(found, ("blk", "split"), split_axis=0, concat_axis=0, tiled=True)
     return in_data_order(got, rank, parts, members).reshape(rows)
 

time: 88.8 us -> 85.3 us (0.961); the launches traced: 87.4 us -> 84.8 us
  waiting for transfers between devices: 32.6 us -> 37.4 us
  Pallas kernels: 20.6 us -> 16.3 us
  blocking collectives: 16.1 us -> 13.9 us
  local copies, waits for them, and re-layouts: 2.81 us -> 1.4 us
    ppermute x6, waiting for transfers between devices: 18.1 us -> 32.2 us  [between(): return lax.ppermute(array, 'blk', route)]
    ppermute x3, waiting for transfers between devices: 14.2 us -> 3.98 us  [chip_swap(): return lax.ppermute(array, 'blk', [(b, b ^ 1) for b in range(blocks)])]
    pallas_call x5 -> x3, Pallas kernels: 14.2 us -> 11 us  [meet(): pl.pallas_call(kernel, out_shape=[jax.ShapeDtypeStruct((1, count), jnp.fl...]
    all_to_all x1, blocking collectives: 16.1 us -> 13.9 us  [body(): lax.all_to_all(found, ('blk', 'split'), split_axis=0, concat_axis=0, tile...]
    unnamed x7 -> x2, local copies, waits for them, and re-layouts: 2.81 us -> 1.4 us
    ppermute x6, waiting for transfers between devices: 0.3 us -> 1.23 us  [core_swap(): return lax.ppermute(array, 'split', [(c, c ^ 1) for c in range(cores)])]
  transfers between devices with their start and end apart: 15 -> 15, of which waited for: 7 -> 7; matrix products, arithmetic and copies ran while one was open for 0% -> 0% of each run, Pallas kernels for 14% -> 9%
where the time goes in v4:
time: 85.3 us; the launch traced here: 84.8 us
  waiting for transfers between devices  37.4 us (44%)
  Pallas kernels  16.3 us (19%)
  starting transfers between devices  15 us (18%)
  blocking collectives  13.9 us (16%)
  local copies, waits for them, and re-layouts  1.4 us (2%)
    ppermute x6, waiting for transfers between devices, between(): return lax.ppermute(array, 'blk', route)  32.2 us
    all_to_all x1, blocking collectives, body(): lax.all_to_all(found, ('blk', 'split'), split_axis=0, concat_axis=0, tile...  13.9 us
    pallas_call x3, Pallas kernels, meet(): pl.pallas_call(kernel, out_shape=[jax.ShapeDtypeStruct((1, count), jnp.fl...  11 us
    ppermute x6, starting transfers between devices, between(): return lax.ppermute(array, 'blk', route)  11 us
    ppermute x3, waiting for transfers between devices, chip_swap(): return lax.ppermute(array, 'blk', [(b, b ^ 1) for b in range(blocks)])  3.98 us
    pallas_call x1, Pallas kernels, in_order(): pl.pallas_call(functools.partial(order_kernel, parts, chips), out_shape=o...  3.7 us
    ppermute x3, starting transfers between devices, chip_swap(): return lax.ppermute(array, 'blk', [(b, b ^ 1) for b in range(blocks)])  3.65 us
  transfers between devices with their start and end apart: 15, of which 7 were waited for; matrix products, arithmetic and copies ran while one was open for 0% of the time, Pallas kernels for 9%

profile of v4, /device:TPU:0, one launch (start us, length us, event | category | flops | bytes accessed | tf_op | source)
XLA Modules:
  0.0 84.8 jit_solution(1071634321400238939)
XLA Ops:
  0.0 0.7 pad_add_fusion.marks_hbm
  0.7 0.0 copy-start
  0.7 1.4 %copy-done = bf16[1024,768]{1,0:T(8,128)(2,1)S(1)} copy-done((bf16[1024,768]{1,0:T(8,128)(2,1)S(1)}, bf16[1024,768]{1,0:T(8,128)(2,1)}, u32[]{:S(2)}) %copy-start) | copy-done | bytes 1572888
  2.1 3.7 %order.1 = (bf16[264,768]{1,0:T(8,128)(2,1)S(1)}, bf16[264,768]{1,0:T(8,128)(2,1)S(1)}, bf16[264,768]{1,0:T(8,128)(2,1)S(1)}, bf16[264,768]{1,0:T(8,128)(2,1)S(1)}, s32[1,1024]{1,0:T(1,128)S(1)}) custom-call(bf16[1024,768]{1,0:T(8,128)(2,1)S(1)} %copy-done, s32[2,1024]{1,0:T(2,128)S(1)} %pad_add_fusion.marks_hbm), custom_call_target="tpu_custom_call" | custom-call | tf_op jit(solution)/shard_map/order/pallas_call | solution.py:91
  5.8 4.1 %collective-permute-start.4 = (bf16[264,768]{1,0:T(8,128)(2,1)S(1)}, bf16[264,768]{1,0:T(8,128)(2,1)S(1)}, u32[]{:S(2)}, u32[]{:S(2)}) collective-permute-start(bf16[264,768]{1,0:T(8,128)(2,1)S(1)} %get-tuple-element.24.refs_3_), channel_id=1, source_target_pairs={{0,8},{2,10},{4,12},{6,14},{8,0},{10,2},{12,4},{14,6},{1,9},{3,11}... | collective-permute-start | bytes 1216520 | tf_op jit(solution)/shard_map/rows_2/ppermute | solution.py:412
  9.9 1.6 %collective-permute-start.3 = (bf16[264,768]{1,0:T(8,128)(2,1)S(1)}, bf16[264,768]{1,0:T(8,128)(2,1)S(1)}, u32[]{:S(2)}, u32[]{:S(2)}) collective-permute-start(bf16[264,768]{1,0:T(8,128)(2,1)S(1)} %get-tuple-element.23.refs_10_.refs_13_), channel_id=1, source_target_pairs={{0,4},{2,6},{4,0},{6,2},{8,12},{10,14},{12,8},{14,10},{1,5},{3,7},... | collective-permute-start | bytes 1216520 | tf_op jit(solution)/shard_map/rows_2/ppermute | solution.py:412
  11.5 1.5 %collective-permute-start.1 = (bf16[264,768]{1,0:T(8,128)(2,1)S(1)}, bf16[264,768]{1,0:T(8,128)(2,1)S(1)}, u32[]{:S(2)}, u32[]{:S(2)}) collective-permute-start(bf16[264,768]{1,0:T(8,128)(2,1)S(1)} %get-tuple-element.22.refs_2_.refs_0_.refs_1_), channel_id=1, source_target_pairs={{0,2},{2,0},{4,6},{6,4},{8,10},{10,8},{12,14},{14,12},{1,3},{3,1},... | collective-permute-start | bytes 1216520 | tf_op jit(solution)/shard_map/over_0/ppermute | solution.py:419
  13.0 0.0 collective-permute-start
  13.0 15.1 %collective-permute-done.4.refs_1_ = bf16[264,768]{1,0:T(8,128)(2,1)S(1)} collective-permute-done((bf16[264,768]{1,0:T(8,128)(2,1)S(1)}, bf16[264,768]{1,0:T(8,128)(2,1)S(1)}, u32[]{:S(2)}, u32[]{:S(2)}) %collective-permute-start.4) | collective-permute-done | bytes 405536 | tf_op jit(solution)/shard_map/rows_2/ppermute | solution.py:412
  28.1 0.2 collective-permute-done.3.refs_0_
  28.3 0.0 collective-permute-done.1.refs_4_.refs_2_
  28.3 0.1 pack.2
  28.4 0.1 collective-permute-start.5
  28.5 1.6 %collective-permute-start.6 = (bf16[520,768]{1,0:T(8,128)(2,1)S(1)}, bf16[520,768]{1,0:T(8,128)(2,1)S(1)}, u32[]{:S(2)}, u32[]{:S(2)}) collective-permute-start(bf16[520,768]{1,0:T(8,128)(2,1)S(1)} %get-tuple-element.26.refs_4_.refs_2_), channel_id=1, source_target_pairs={{0,2},{2,0},{4,6},{6,4},{8,10},{10,8},{12,14},{14,12},{1,3},{3,1},... | collective-permute-start | bytes 2396168 | tf_op jit(solution)/shard_map/over_2/ppermute | solution.py:419
  30.1 0.2 collective-permute-start.2
  30.3 3.2 %collective-permute-start.7 = (bf16[264,768]{1,0:T(8,128)(2,1)S(1)}, bf16[264,768]{1,0:T(8,128)(2,1)S(1)}, u32[]{:S(2)}, u32[]{:S(2)}) collective-permute-start(bf16[264,768]{1,0:T(8,128)(2,1)S(1)} %get-tuple-element.29.refs_16_), channel_id=1, source_target_pairs={{0,12},{2,14},{4,8},{6,10},{8,4},{10,6},{12,0},{14,2},{1,13},{3,15... | collective-permute-start | bytes 1216520 | tf_op jit(solution)/shard_map/rows_3/ppermute | solution.py:412
  33.5 0.0 collective-permute-done.refs_1_
  33.5 0.0 collective-permute-start.8
  33.5 0.0 collective-permute-done.2.refs_3_
  33.5 0.0 collective-permute-done.5.refs_5_
  33.5 2.5 %meet.3 = (f32[1,2048]{1,0:T(1,128)S(1)}, f32[1,768]{1,0:T(1,128)S(1)}) custom-call(bf16[264,768]{1,0:T(8,128)(2,1)S(1)} %get-tuple-element.22.refs_2_.refs_0_.refs_1_, bf16[264,768]{1,0:T(8,128)(2,1)S(1)} %collective-permute-done.refs_1_, bf16[264,768]{1,0:T(8,128)(2,1)S(1)} %collective-permute-done.1.refs_4_.refs_2_, ...), custom_call_target="tpu_custom_call" | custom-call | tf_op jit(solution)/shard_map/meet/pallas_call | solution.py:304
  35.9 8.4 %collective-permute-done.7.refs_0_ = bf16[264,768]{1,0:T(8,128)(2,1)S(1)} collective-permute-done((bf16[264,768]{1,0:T(8,128)(2,1)S(1)}, bf16[264,768]{1,0:T(8,128)(2,1)S(1)}, u32[]{:S(2)}, u32[]{:S(2)}) %collective-permute-start.7) | collective-permute-done | bytes 405536 | tf_op jit(solution)/shard_map/rows_3/ppermute | solution.py:412
  44.3 0.1 pack.3
  44.4 8.0 %collective-permute-done.8.refs_2_.refs_9_.refs_12_ = bf16[264,768]{1,0:T(8,128)(2,1)S(1)} collective-permute-done((bf16[264,768]{1,0:T(8,128)(2,1)S(1)}, bf16[264,768]{1,0:T(8,128)(2,1)S(1)}, u32[]{:S(2)}, u32[]{:S(2)}) %collective-permute-start.8) | collective-permute-done | bytes 405536 | tf_op jit(solution)/shard_map/passed_2/ppermute | solution.py:412
  52.5 0.0 collective-permute-done.6.refs_0_
  52.5 0.0 collective-permute-start.9
  52.5 0.5 collective-permute-start.11
  53.0 0.2 collective-permute-start.10
  53.2 1.4 %collective-permute-start.13 = (bf16[264,768]{1,0:T(8,128)(2,1)S(1)}, bf16[264,768]{1,0:T(8,128)(2,1)S(1)}, u32[]{:S(2)}, u32[]{:S(2)}) collective-permute-start(bf16[264,768]{1,0:T(8,128)(2,1)S(1)} %get-tuple-element.34), channel_id=1, source_target_pairs={{0,4},{2,6},{4,0},{6,2},{8,12},{10,14},{12,8},{14,10},{1,5},{3,7},... | collective-permute-start | bytes 1216520 | tf_op jit(solution)/shard_map/passed_3/ppermute | solution.py:412
  54.6 0.7 collective-permute-start.14
  55.2 0.0 collective-permute-done.9.refs_7_
  55.3 5.0 %meet.4 = (f32[1,3072]{1,0:T(1,128)S(1)}, f32[1,1280]{1,0:T(1,128)S(1)}) custom-call(bf16[264,768]{1,0:T(8,128)(2,1)S(1)} %get-tuple-element.22.refs_2_.refs_0_.refs_1_, bf16[264,768]{1,0:T(8,128)(2,1)S(1)} %collective-permute-done.refs_1_, bf16[264,768]{1,0:T(8,128)(2,1)S(1)} %collective-permute-done.1.refs_4_.refs_2_, ...), custom_call_target="tpu_custom_call" | custom-call | tf_op jit(solution)/shard_map/meet/pallas_call | solution.py:304
  60.3 4.0 %collective-permute-done.11.refs_0_ = bf16[264,768]{1,0:T(8,128)(2,1)S(1)} collective-permute-done((bf16[264,768]{1,0:T(8,128)(2,1)S(1)}, bf16[264,768]{1,0:T(8,128)(2,1)S(1)}, u32[]{:S(2)}, u32[]{:S(2)}) %collective-permute-start.11) | collective-permute-done | bytes 405536 | tf_op jit(solution)/shard_map/over_3/ppermute | solution.py:419
  64.3 0.0 collective-permute-start.12
  64.3 0.5 collective-permute-done.13.refs_14_
  64.8 0.0 collective-permute-done.14.refs_15_
  64.8 0.0 collective-permute-done.10.refs_9_
  64.8 1.2 %collective-permute-done.12.refs_11_ = bf16[264,768]{1,0:T(8,128)(2,1)S(1)} collective-permute-done((bf16[264,768]{1,0:T(8,128)(2,1)S(1)}, bf16[264,768]{1,0:T(8,128)(2,1)S(1)}, u32[]{:S(2)}, u32[]{:S(2)}) %collective-permute-start.12) | collective-permute-done | bytes 405536 | tf_op jit(solution)/shard_map/across_3/ppermute | solution.py:423
  66.0 3.5 %meet.5 = (f32[1,4096]{1,0:T(1,128)S(1)}, f32[1,1408]{1,0:T(1,128)S(1)}) custom-call(bf16[264,768]{1,0:T(8,128)(2,1)S(1)} %get-tuple-element.22.refs_2_.refs_0_.refs_1_, bf16[264,768]{1,0:T(8,128)(2,1)S(1)} %collective-permute-done.refs_1_, bf16[264,768]{1,0:T(8,128)(2,1)S(1)} %collective-permute-done.1.refs_4_.refs_2_, ...), custom_call_target="tpu_custom_call" | custom-call | tf_op jit(solution)/shard_map/meet/pallas_call | solution.py:304
  69.5 0.1 route.1
  69.6 13.9 %all_to_all.5.got_ref = f32[16,1,512]{2,1,0:T(1,128)S(1)} all-to-all(f32[16,1,512]{2,1,0:T(1,128)S(1)} %route.1), channel_id=1, replica_groups=mesh['groups'=2,'blk'=8,'split'=2] {'blk','split'}, dimensions={0} | all-to-all | bytes 65536 | tf_op jit(solution)/shard_map/all_to_all | solution.py:541
  83.5 1.3 %back.1 = f32[1,1024]{1,0:T(1,128)} custom-call(f32[16,1,512]{2,1,0:T(1,128)S(1)} %all_to_all.5.got_ref, s32[1,1024]{1,0:T(1,128)S(1)} %get-tuple-element.38.rank_ref), custom_call_target="tpu_custom_call" | custom-call | tf_op jit(solution)/shard_map/back/pallas_call | solution.py:391
  (2 shorter events, 0.0 us)
Async XLA Ops:
  0.7 1.4 %copy-start = (bf16[1024,768]{1,0:T(8,128)(2,1)S(1)}, bf16[1024,768]{1,0:T(8,128)(2,1)}, u32[]{:S(2)}) copy-start(bf16[1024,768]{1,0:T(8,128)(2,1)} %rows_hbm.1) | copy-start | bytes 4718596
  5.8 22.3 %collective-permute-start.4 = (bf16[264,768]{1,0:T(8,128)(2,1)S(1)}, bf16[264,768]{1,0:T(8,128)(2,1)S(1)}, u32[]{:S(2)}, u32[]{:S(2)}) collective-permute-start(bf16[264,768]{1,0:T(8,128)(2,1)S(1)} %get-tuple-element.24.refs_3_), channel_id=1, source_target_pairs={{0,8},{2,10},{4,12},{6,14},{8,0},{10,2},{12,4},{14,6},{1,9},{3,11}... | collective-permute-start | bytes 1216520 | tf_op jit(solution)/shard_map/rows_2/ppermute | solution.py:412
  9.9 18.4 %collective-permute-start.3 = (bf16[264,768]{1,0:T(8,128)(2,1)S(1)}, bf16[264,768]{1,0:T(8,128)(2,1)S(1)}, u32[]{:S(2)}, u32[]{:S(2)}) collective-permute-start(bf16[264,768]{1,0:T(8,128)(2,1)S(1)} %get-tuple-element.23.refs_10_.refs_13_), channel_id=1, source_target_pairs={{0,4},{2,6},{4,0},{6,2},{8,12},{10,14},{12,8},{14,10},{1,5},{3,7},... | collective-permute-start | bytes 1216520 | tf_op jit(solution)/shard_map/rows_2/ppermute | solution.py:412
  11.5 16.8 %collective-permute-start.1 = (bf16[264,768]{1,0:T(8,128)(2,1)S(1)}, bf16[264,768]{1,0:T(8,128)(2,1)S(1)}, u32[]{:S(2)}, u32[]{:S(2)}) collective-permute-start(bf16[264,768]{1,0:T(8,128)(2,1)S(1)} %get-tuple-element.22.refs_2_.refs_0_.refs_1_), channel_id=1, source_target_pairs={{0,2},{2,0},{4,6},{6,4},{8,10},{10,8},{12,14},{14,12},{1,3},{3,1},... | collective-permute-start | bytes 1216520 | tf_op jit(solution)/shard_map/over_0/ppermute | solution.py:419
  13.0 20.4 %collective-permute-start = (bf16[264,768]{1,0:T(8,128)(2,1)S(1)}, bf16[264,768]{1,0:T(8,128)(2,1)S(1)}, u32[]{:S(2)}, u32[]{:S(2)}) collective-permute-start(bf16[264,768]{1,0:T(8,128)(2,1)S(1)} %get-tuple-element.22.refs_2_.refs_0_.refs_1_), channel_id=1, source_target_pairs={{0,1},{1,0},{2,3},{3,2},{4,5},{5,4},{6,7},{7,6},{8,9},{9,8},{10,11... | collective-permute-start | bytes 1216520 | tf_op jit(solution)/shard_map/beside_0/ppermute | solution.py:423
  28.4 5.1 %collective-permute-start.5 = (bf16[520,768]{1,0:T(8,128)(2,1)S(1)}, bf16[520,768]{1,0:T(8,128)(2,1)S(1)}, u32[]{:S(2)}, u32[]{:S(2)}) collective-permute-start(bf16[520,768]{1,0:T(8,128)(2,1)S(1)} %get-tuple-element.26.refs_4_.refs_2_), channel_id=1, source_target_pairs={{0,1},{1,0},{2,3},{3,2},{4,5},{5,4},{6,7},{7,6},{8,9},{9,8},{10,11... | collective-permute-start | bytes 2396168 | tf_op jit(solution)/shard_map/beside_2/ppermute | solution.py:423
  28.5 24.0 %collective-permute-start.6 = (bf16[520,768]{1,0:T(8,128)(2,1)S(1)}, bf16[520,768]{1,0:T(8,128)(2,1)S(1)}, u32[]{:S(2)}, u32[]{:S(2)}) collective-permute-start(bf16[520,768]{1,0:T(8,128)(2,1)S(1)} %get-tuple-element.26.refs_4_.refs_2_), channel_id=1, source_target_pairs={{0,2},{2,0},{4,6},{6,4},{8,10},{10,8},{12,14},{14,12},{1,3},{3,1},... | collective-permute-start | bytes 2396168 | tf_op jit(solution)/shard_map/over_2/ppermute | solution.py:419
  30.1 3.4 %collective-permute-start.2 = (bf16[264,768]{1,0:T(8,128)(2,1)S(1)}, bf16[264,768]{1,0:T(8,128)(2,1)S(1)}, u32[]{:S(2)}, u32[]{:S(2)}) collective-permute-start(bf16[264,768]{1,0:T(8,128)(2,1)S(1)} %collective-permute-done.1.refs_4_.refs_2_), channel_id=1, source_target_pairs={{0,1},{1,0},{2,3},{3,2},{4,5},{5,4},{6,7},{7,6},{8,9},{9,8},{10,11... | collective-permute-start | bytes 1216520 | tf_op jit(solution)/shard_map/across_0/ppermute | solution.py:423
  30.3 14.1 %collective-permute-start.7 = (bf16[264,768]{1,0:T(8,128)(2,1)S(1)}, bf16[264,768]{1,0:T(8,128)(2,1)S(1)}, u32[]{:S(2)}, u32[]{:S(2)}) collective-permute-start(bf16[264,768]{1,0:T(8,128)(2,1)S(1)} %get-tuple-element.29.refs_16_), channel_id=1, source_target_pairs={{0,12},{2,14},{4,8},{6,10},{8,4},{10,6},{12,0},{14,2},{1,13},{3,15... | collective-permute-start | bytes 1216520 | tf_op jit(solution)/shard_map/rows_3/ppermute | solution.py:412
  33.5 19.0 %collective-permute-start.8 = (bf16[264,768]{1,0:T(8,128)(2,1)S(1)}, bf16[264,768]{1,0:T(8,128)(2,1)S(1)}, u32[]{:S(2)}, u32[]{:S(2)}) collective-permute-start(bf16[264,768]{1,0:T(8,128)(2,1)S(1)} %get-tuple-element.31), channel_id=1, source_target_pairs={{0,4},{2,6},{4,0},{6,2},{8,12},{10,14},{12,8},{14,10},{1,5},{3,7},... | collective-permute-start | bytes 1216520 | tf_op jit(solution)/shard_map/passed_2/ppermute | solution.py:412
  52.5 2.8 %collective-permute-start.9 = (bf16[520,768]{1,0:T(8,128)(2,1)S(1)}, bf16[520,768]{1,0:T(8,128)(2,1)S(1)}, u32[]{:S(2)}, u32[]{:S(2)}) collective-permute-start(bf16[520,768]{1,0:T(8,128)(2,1)S(1)} %after.2.refs_6_), channel_id=1, source_target_pairs={{0,1},{1,0},{2,3},{3,2},{4,5},{5,4},{6,7},{7,6},{8,9},{9,8},{10,11... | collective-permute-start | bytes 2396168 | tf_op jit(solution)/shard_map/across_2/ppermute | solution.py:423
  52.5 11.8 %collective-permute-start.11 = (bf16[264,768]{1,0:T(8,128)(2,1)S(1)}, bf16[264,768]{1,0:T(8,128)(2,1)S(1)}, u32[]{:S(2)}, u32[]{:S(2)}) collective-permute-start(bf16[264,768]{1,0:T(8,128)(2,1)S(1)} %get-tuple-element.30.refs_1_.refs_8_), channel_id=1, source_target_pairs={{0,2},{2,0},{4,6},{6,4},{8,10},{10,8},{12,14},{14,12},{1,3},{3,1},... | collective-permute-start | bytes 1216520 | tf_op jit(solution)/shard_map/over_3/ppermute | solution.py:419
  53.0 11.8 %collective-permute-start.10 = (bf16[264,768]{1,0:T(8,128)(2,1)S(1)}, bf16[264,768]{1,0:T(8,128)(2,1)S(1)}, u32[]{:S(2)}, u32[]{:S(2)}) collective-permute-start(bf16[264,768]{1,0:T(8,128)(2,1)S(1)} %get-tuple-element.30.refs_1_.refs_8_), channel_id=1, source_target_pairs={{0,1},{1,0},{2,3},{3,2},{4,5},{5,4},{6,7},{7,6},{8,9},{9,8},{10,11... | collective-permute-start | bytes 1216520 | tf_op jit(solution)/shard_map/beside_3/ppermute | solution.py:423
  53.2 11.6 %collective-permute-start.13 = (bf16[264,768]{1,0:T(8,128)(2,1)S(1)}, bf16[264,768]{1,0:T(8,128)(2,1)S(1)}, u32[]{:S(2)}, u32[]{:S(2)}) collective-permute-start(bf16[264,768]{1,0:T(8,128)(2,1)S(1)} %get-tuple-element.34), channel_id=1, source_target_pairs={{0,4},{2,6},{4,0},{6,2},{8,12},{10,14},{12,8},{14,10},{1,5},{3,7},... | collective-permute-start | bytes 1216520 | tf_op jit(solution)/shard_map/passed_3/ppermute | solution.py:412
  54.6 10.2 %collective-permute-start.14 = (bf16[264,768]{1,0:T(8,128)(2,1)S(1)}, bf16[264,768]{1,0:T(8,128)(2,1)S(1)}, u32[]{:S(2)}, u32[]{:S(2)}) collective-permute-start(bf16[264,768]{1,0:T(8,128)(2,1)S(1)} %get-tuple-element.35), channel_id=1, source_target_pairs={{4,8},{6,10},{8,4},{10,6},{5,9},{7,11},{9,5},{11,7},{20,24},{22,26... | collective-permute-start | bytes 1216520 | tf_op jit(solution)/shard_map/border/ppermute | solution.py:412
  64.3 1.7 %collective-permute-start.12 = (bf16[264,768]{1,0:T(8,128)(2,1)S(1)}, bf16[264,768]{1,0:T(8,128)(2,1)S(1)}, u32[]{:S(2)}, u32[]{:S(2)}) collective-permute-start(bf16[264,768]{1,0:T(8,128)(2,1)S(1)} %after.3.refs_10_), channel_id=1, source_target_pairs={{0,1},{1,0},{2,3},{3,2},{4,5},{5,4},{6,7},{7,6},{8,9},{9,8},{10,11... | collective-permute-start | bytes 1216520 | tf_op jit(solution)/shard_map/across_3/ppermute | solution.py:423

commit v5 on v4

--- a/solution.py
+++ b/solution.py
@@ -37,18 +37,20 @@
     return best
 
 
-def order_kernel(parts, chips, rows_hbm, marks_hbm, *refs):
+def order_kernel(parts, chips, rows_hbm, ids_hbm, pos_hbm, *refs):
     outs, rank_ref = refs[:parts], refs[parts]
-    unit, pick, placed, tags, rows_ref, marks_ref, sems = refs[parts + 1 :]
+    unit, pick, placed, tags, rows_ref, ids_ref, pos_ref, sems = refs[parts + 1 :]
     count, width = rows_ref.shape
     quart = count // parts // 4
     step = 256
-    fetch_marks = pltpu.make_async_copy(marks_hbm, marks_ref, sems.at[0])
+    fetch_pos = pltpu.make_async_copy(pos_hbm, pos_ref, sems.at[0])
     fetch_rows = pltpu.make_async_copy(rows_hbm, rows_ref, sems.at[1])
-    fetch_marks.start()
+    fetch_ids = pltpu.make_async_copy(ids_hbm, ids_ref, sems.at[2])
+    fetch_pos.start()
     fetch_rows.start()
-    fetch_marks.wait()
-    pos = marks_ref[1:2, :].astype(jnp.float32)
+    fetch_ids.start()
+    fetch_pos.wait()
+    pos = pos_ref[...].astype(jnp.float32)
     below = jnp.zeros((8, count), jnp.float32)
     for at in range(0, count, step):
         other = spread(pos[:, at : at + step])[:, :1]
@@ -59,6 +61,7 @@
         slot = lax.broadcasted_iota(jnp.int32, (step, count), 0) + at
         pick[at : at + step, :] = jnp.where(slot == rank, 1.0, 0.0).astype(jnp.bfloat16)
     fetch_rows.wait()
+    fetch_ids.wait()
     values = rows_ref[...].astype(jnp.float32)
     total = jnp.sum(values * values, axis=1, keepdims=True)
     unit[...] = (values * lax.rsqrt(total + 1e-06)).astype(jnp.bfloat16)
@@ -66,7 +69,7 @@
         placed[at : at + step, :] = jnp.dot(
             pick[at : at + step, :], unit[...], preferred_element_type=jnp.float32
         ).astype(jnp.bfloat16)
-    ids = jnp.broadcast_to((marks_ref[:1, :] + 1).astype(jnp.bfloat16), (16, count))
+    ids = jnp.broadcast_to((ids_ref[...] + 1).astype(jnp.bfloat16), (16, count))
     part = lax.axis_index("blk") // chips
     sorted_ids = lax.dot_general(
         ids, pick[...], (((1,), (1,)), ((), ())), preferred_element_type=jnp.float32
@@ -80,18 +83,19 @@
             which = 4 * quarter + block
             at = index * quart
             outs[k][at : at + quart, :] = placed[pl.ds(pl.multiple_of(which * quart, quart), quart), :]
-            outs[k][4 * quart :, at : at + quart] = tags[which, :TAGS, :quart].astype(jnp.bfloat16)
-
-
-def in_order(embeddings, ids, pos, parts, chips):
+            outs[k][outs[k].shape[0] - TAGS :, at : at + quart] = tags[which, :TAGS, :quart].astype(jnp.bfloat16)
+
+
+def in_order(embeddings, ids, pos, tag_rows, chips):
+    parts = len(tag_rows)
     count, width = embeddings.shape
     slots = count // parts
-    block = jax.ShapeDtypeStruct((slots + TAGS, width), jnp.bfloat16)
-    outs = [block] * parts + [jax.ShapeDtypeStruct((1, count), jnp.int32)]
+    outs = [pltpu.VMEM((slots + tags, width), jnp.bfloat16) for tags in tag_rows]
+    outs.append(jax.ShapeDtypeStruct((1, count), jnp.int32))
     *blocks, rank = pl.pallas_call(
         functools.partial(order_kernel, parts, chips),
         out_shape=outs,
-        in_specs=[REMAINS, REMAINS],
+        in_specs=[REMAINS, REMAINS, REMAINS],
         out_specs=[WHOLE] * len(outs),
         scratch_shapes=[
             pltpu.VMEM((count, width), jnp.bfloat16),
@@ -99,12 +103,13 @@
             pltpu.VMEM((count, width), jnp.bfloat16),
             pltpu.VMEM((4 * parts, 16, max(slots // 4, LANES)), jnp.float32),
             pltpu.VMEM((count, width), jnp.bfloat16),
-            pltpu.VMEM((2, count), jnp.int32),
-            pltpu.SemaphoreType.DMA((2,)),
+            pltpu.VMEM((1, count), jnp.int32),
+            pltpu.VMEM((1, count), jnp.int32),
+            pltpu.SemaphoreType.DMA((3,)),
         ],
         compiler_params=grant(24),
         name="order",
-    )(embeddings, jnp.stack([ids, pos]))
+    )(*[pltpu.with_memory_space_constraint(x, pltpu.HBM) for x in (embeddings, ids.reshape(1, count), pos.reshape(1, count))])
     return blocks, rank
 
 
@@ -449,25 +454,38 @@
         far_rows = [(b, at + quart, quart, goal + i * half + quart) for b, at, i in pieces]
         return near_rows, far_rows
 
-    sent, rank = in_order(embeddings, cluster_of, target_pos, parts, chips)
+    sent, rank = in_order(
+        embeddings, cluster_of, target_pos, [TAGS if k < middle else 2 * TAGS for k in range(parts)], chips
+    )
     own_0 = sent[0]
     got = [swap(sent[k], k, "rows_2") for k in second]
     over_0 = chip_swap(own_0, "over_0")
     beside_0 = core_swap(own_0, "beside_0")
 
-    pieces = [(i, 0, slots) for i in range(len(second))]
-    forward = [(len(second), 0, half)] + [(i, 0, half) for i in range(1, len(second))]
-    *held, own_2, passing = pack(
-        [*got, own_0], [pieces, forward], held=[sent[k] for k in third], earlier=[over_0]
-    )
-    got = [swap(b, k, "rows_3") for k, b in zip(third, held)]
-    over_2 = chip_swap(own_2, "over_2")
+    def joined(got):
+        if len(got) == 1:
+            return got[0]
+        return pack(got, [[(i, 0, slots) for i in range(len(got))]])[0]
+
+    own_1, own_2 = got[0], joined(got[1:])
+    forward = [(len(second) - 1, 0, half)] + [(i, 0, half) for i in range(len(second) - 1)]
+    *held, passing = pack(
+        [*got[1:], own_0], [forward], held=[sent[k] for k in third], earlier=[over_0]
+    )
+    got_3 = [swap(b, k, "rows_3") for k, b in zip(third, held)]
+    over_1, over_2 = chip_swap(own_1, "over_1"), chip_swap(own_2, "over_2")
     passed_2 = swap(passing, 1, "passed_2")
     across_0 = core_swap(over_0, "across_0")
-    beside_2 = core_swap(own_2, "beside_2")
+    beside_1, beside_2 = core_swap(own_1, "beside_1"), core_swap(own_2, "beside_2")
+
+    def pair(member, block_1, block_2):
+        return [
+            a + b for a, b in zip(sides([block_1], [1], member), sides([block_2], second[1:], member))
+        ]
+
     left_0 = sides([own_0, beside_0, over_0, across_0], [0])
-    here_2 = sides([own_2, beside_2], second)
-    mine_0, mine_2 = whole(own_0, [0]), sum(sides([own_2], second), [])
+    mine_0, mine_2 = whole(own_0, [0]), sum(pair(0, own_1, own_2), [])
+    here_2 = [a + b for a, b in zip(pair(0, own_1, own_2), pair(1, beside_1, beside_2))]
     some = len(second) * half
     scores = meet(
         [*left_0, *here_2],
@@ -478,37 +496,37 @@
     )
 
     last = len(third)
+    own_3 = joined(got_3)
     border = [(last, half, half), (last + 1, half, half)]
     forward = [(i, 0, half) for i in range(last)]
-    inputs = [*got, own_0, own_2]
+    inputs = [*got_3, own_0, own_1]
     if near:
         inputs.append(sent[2])
         forward.append((last + 2, half, half))
     else:
-        border += [(last + 1, i * slots + half, half) for i in range(1, len(second))]
+        border += [(last + 1 + i, half, half) for i in range(1, len(second))]
         border += [(i, half, half) for i in range(last)]
+        inputs += got[1:]
     own_3, border, passing = pack(
-        inputs,
-        [[(i, 0, slots) for i in range(last)], border, forward],
-        earlier=[scores[0][0]],
+        inputs, [border, forward], held=[own_3], earlier=[scores[0][0]]
     )
     over_3 = chip_swap(own_3, "over_3")
     got_border = between(border, borders, "border")
     passed_3 = swap(passing, 1, "passed_3")
-    (over_2,) = after([over_2], [own_3, passed_2])
-    across_2 = core_swap(over_2, "across_2")
+    over_1, over_2 = after([over_1, over_2], [own_3, passed_2])
+    across_1, across_2 = core_swap(over_1, "across_1"), core_swap(over_2, "across_2")
     beside_3 = core_swap(own_3, "beside_3")
-    there_2 = sides([over_2, across_2], second, 2)
+    there_2 = [a + b for a, b in zip(pair(2, over_1, over_2), pair(3, across_1, across_2))]
     visit_2 = [(passed_2, i * half, i) for i in range(len(second))]
     visit_2 = visits(visit_2 + [(sent[1], 0, parts - 1)], u_goal)
     visit_3 = visits([(passed_3, i * half, len(second) + i) for i in range(last)], u_goal)
     mine_3 = sum(sides([own_3], third), [])
-    lefts = [left_0[0], here_2[0], there_2[0], left_0[1], here_2[1], there_2[1]]
+    lefts = [left_0[0], here_2[0], there_2[0], there_2[1], left_0[1], here_2[1]]
     u_half, v_half = (0, 1, 2), (3, 4, 5)
     scores += meet(
         lefts,
         [mine_2, mine_3, *visit_2],
-        [(0, (2,), None, False), (0, (5,), None, False), (1, u_half + v_half, None, False)]
+        [(0, (2, 3), None, False), (1, u_half + v_half, None, False)]
         + [(r, l, None, True) for r in (2, 3) for l in (u_half, v_half)],
     )
 
@@ -516,7 +534,7 @@
     if near:
         visit_v += [(passed_3, last * half, 2), (held[0], half, 3)]
     visit_v = visits(visit_v, v_goal)
-    (over_3,) = after([over_3], [scores[2][0]])
+    (over_3,) = after([over_3], [scores[2][0], got_border, passed_3])
     across_3 = core_swap(over_3, "across_3")
     left_3 = sides([own_3, beside_3, over_3, across_3], third)
     some = last * half

time: 85.3 us -> 83.1 us (0.974)
  starting transfers between devices: 15 us -> 17.3 us
  Pallas kernels: 16.3 us -> 14.2 us
  local copies, waits for them, and re-layouts: 1.4 us -> 0.03 us
    ppermute x6, waiting for transfers between devices: 32.2 us -> 27.5 us  [between(): return lax.ppermute(array, 'blk', route)]
    ppermute x3 -> x4, waiting for transfers between devices: 3.98 us -> 8.21 us  [chip_swap(): return lax.ppermute(array, 'blk', [(b, b ^ 1) for b in range(blocks)])]
    pallas_call x3, Pallas kernels: 11 us -> 8.4 us  [meet(): pl.pallas_call(kernel, out_shape=[jax.ShapeDtypeStruct((1, count), jnp.fl...]
    ppermute x3 -> x4, starting transfers between devices: 3.65 us -> 5.19 us  [chip_swap(): return lax.ppermute(array, 'blk', [(b, b ^ 1) for b in range(blocks)])]
    unnamed x2 -> x1, local copies, waits for them, and re-layouts: 1.4 us -> 0.03 us
    ppermute x6 -> x8, waiting for transfers between devices: 1.23 us -> 1.77 us  [core_swap(): return lax.ppermute(array, 'split', [(c, c ^ 1) for c in range(cores)])]
  transfers between devices with their start and end apart: 15 -> 18, of which waited for: 7 -> 6; matrix products, arithmetic and copies ran while one was open for 0% -> 0% of each run, Pallas kernels for 9% -> 8%
where the time goes in v5:
time: 83.1 us; the launch traced here: 82.7 us
  waiting for transfers between devices  37.5 us (45%)
  starting transfers between devices  17.3 us (21%)
  Pallas kernels  14.2 us (17%)
  blocking collectives  13.6 us (16%)
    ppermute x6, waiting for transfers between devices, between(): return lax.ppermute(array, 'blk', route)  27.5 us
    all_to_all x1, blocking collectives, body(): lax.all_to_all(found, ('blk', 'split'), split_axis=0, concat_axis=0, tile...  13.6 us
    ppermute x6, starting transfers between devices, between(): return lax.ppermute(array, 'blk', route)  11.2 us
    pallas_call x3, Pallas kernels, meet(): pl.pallas_call(kernel, out_shape=[jax.ShapeDtypeStruct((1, count), jnp.fl...  8.4 us
    ppermute x4, waiting for transfers between devices, chip_swap(): return lax.ppermute(array, 'blk', [(b, b ^ 1) for b in range(blocks)])  8.21 us
    ppermute x4, starting transfers between devices, chip_swap(): return lax.ppermute(array, 'blk', [(b, b ^ 1) for b in range(blocks)])  5.19 us
    pallas_call x1, Pallas kernels, in_order(): pl.pallas_call(functools.partial(order_kernel, parts, chips), out_shape=o...  4.28 us
    ppermute x8, waiting for transfers between devices, core_swap(): return lax.ppermute(array, 'split', [(c, c ^ 1) for c in range(cores)])  1.77 us
  transfers between devices with their start and end apart: 18, of which 6 were waited for; matrix products, arithmetic and copies ran while one was open for 0% of the time, Pallas kernels for 8%

profile of v5, /device:TPU:0, one launch (start us, length us, event | category | flops | bytes accessed | tf_op | source)
XLA Modules:
  0.0 82.7 jit_solution(7033998616334008258)
XLA Ops:
  0.0 4.3 %order.1 = (bf16[264,768]{1,0:T(8,128)(2,1)S(1)}, bf16[264,768]{1,0:T(8,128)(2,1)S(1)}, bf16[264,768]{1,0:T(8,128)(2,1)S(1)}, bf16[272,768]{1,0:T(8,128)(2,1)S(1)}, s32[1,1024]{1,0:T(1,128)S(1)}) custom-call(bf16[1024,768]{1,0:T(8,128)(2,1)} %rows_hbm.1, s32[1,1024]{1,0:T(1,128)} %bitcast.3, s32[1,1024]{1,0:T(1,128)} %bitcast.4), custom_call_target="tpu_custom_call" | custom-call | tf_op jit(solution)/shard_map/order/pallas_call | solution.py:95
  4.3 4.1 %collective-permute-start.4 = (bf16[264,768]{1,0:T(8,128)(2,1)S(1)}, bf16[264,768]{1,0:T(8,128)(2,1)S(1)}, u32[]{:S(2)}, u32[]{:S(2)}) collective-permute-start(bf16[264,768]{1,0:T(8,128)(2,1)S(1)} %get-tuple-element.25.refs_3_), channel_id=1, source_target_pairs={{0,8},{2,10},{4,12},{6,14},{8,0},{10,2},{12,4},{14,6},{1,9},{3,11}... | collective-permute-start | bytes 1216520 | tf_op jit(solution)/shard_map/rows_2/ppermute | solution.py:417
  8.4 1.6 %collective-permute-start.3 = (bf16[264,768]{1,0:T(8,128)(2,1)S(1)}, bf16[264,768]{1,0:T(8,128)(2,1)S(1)}, u32[]{:S(2)}, u32[]{:S(2)}) collective-permute-start(bf16[264,768]{1,0:T(8,128)(2,1)S(1)} %get-tuple-element.24.refs_14_.refs_17_), channel_id=1, source_target_pairs={{0,4},{2,6},{4,0},{6,2},{8,12},{10,14},{12,8},{14,10},{1,5},{3,7},... | collective-permute-start | bytes 1216520 | tf_op jit(solution)/shard_map/rows_2/ppermute | solution.py:417
  10.0 1.5 %collective-permute-start.1 = (bf16[264,768]{1,0:T(8,128)(2,1)S(1)}, bf16[264,768]{1,0:T(8,128)(2,1)S(1)}, u32[]{:S(2)}, u32[]{:S(2)}) collective-permute-start(bf16[264,768]{1,0:T(8,128)(2,1)S(1)} %get-tuple-element.23.refs_0_.refs_1_), channel_id=1, source_target_pairs={{0,2},{2,0},{4,6},{6,4},{8,10},{10,8},{12,14},{14,12},{1,3},{3,1},... | collective-permute-start | bytes 1216520 | tf_op jit(solution)/shard_map/over_0/ppermute | solution.py:424
  11.5 0.0 collective-permute-start
  11.5 15.1 %collective-permute-done.4.refs_5_.refs_0_ = bf16[264,768]{1,0:T(8,128)(2,1)S(1)} collective-permute-done((bf16[264,768]{1,0:T(8,128)(2,1)S(1)}, bf16[264,768]{1,0:T(8,128)(2,1)S(1)}, u32[]{:S(2)}, u32[]{:S(2)}) %collective-permute-start.4) | collective-permute-done | bytes 405536 | tf_op jit(solution)/shard_map/rows_2/ppermute | solution.py:417
  26.6 0.0 collective-permute-start.6
  26.6 0.2 collective-permute-done.3.refs_4_.refs_2_
  26.8 0.3 collective-permute-start.5
  27.1 0.0 collective-permute-done.1.refs_2_.refs_3_
  27.1 3.5 %collective-permute-start.9 = (bf16[272,768]{1,0:T(8,128)(2,1)S(1)}, bf16[272,768]{1,0:T(8,128)(2,1)S(1)}, u32[]{:S(2)}, u32[]{:S(2)}) collective-permute-start(bf16[272,768]{1,0:T(8,128)(2,1)S(1)} %get-tuple-element.29.refs_20_), channel_id=1, source_target_pairs={{0,12},{2,14},{4,8},{6,10},{8,4},{10,6},{12,0},{14,2},{1,13},{3,15... | collective-permute-start | bytes 1253384 | tf_op jit(solution)/shard_map/rows_3/ppermute | solution.py:417
  30.6 0.0 collective-permute-start.2
  30.6 0.0 collective-permute-done.refs_1_
  30.6 1.5 %collective-permute-start.8 = (bf16[264,768]{1,0:T(8,128)(2,1)S(1)}, bf16[264,768]{1,0:T(8,128)(2,1)S(1)}, u32[]{:S(2)}, u32[]{:S(2)}) collective-permute-start(bf16[264,768]{1,0:T(8,128)(2,1)S(1)} %collective-permute-done.4.refs_5_.refs_0_), channel_id=1, source_target_pairs={{0,2},{2,0},{4,6},{6,4},{8,10},{10,8},{12,14},{14,12},{1,3},{3,1},... | collective-permute-start | bytes 1216520 | tf_op jit(solution)/shard_map/over_2/ppermute | solution.py:424
  32.1 0.0 collective-permute-done.6.refs_7_
  32.1 0.5 collective-permute-start.7
  32.6 0.0 collective-permute-done.5.refs_6_
  32.7 0.0 collective-permute-start.10
  32.7 0.0 collective-permute-done.2.refs_3_
  32.7 2.5 %meet.3 = (f32[1,2048]{1,0:T(1,128)S(1)}, f32[1,768]{1,0:T(1,128)S(1)}) custom-call(bf16[264,768]{1,0:T(8,128)(2,1)S(1)} %get-tuple-element.23.refs_0_.refs_1_, bf16[264,768]{1,0:T(8,128)(2,1)S(1)} %collective-permute-done.refs_1_, bf16[264,768]{1,0:T(8,128)(2,1)S(1)} %collective-permute-done.1.refs_2_.refs_3_, ...), custom_call_target="tpu_custom_call" | custom-call | tf_op jit(solution)/shard_map/meet/pallas_call | solution.py:309
  35.1 6.4 %collective-permute-done.9.refs_0_ = bf16[272,768]{1,0:T(8,128)(2,1)S(1)} collective-permute-done((bf16[272,768]{1,0:T(8,128)(2,1)S(1)}, bf16[272,768]{1,0:T(8,128)(2,1)S(1)}, u32[]{:S(2)}, u32[]{:S(2)}) %collective-permute-start.9) | collective-permute-done | bytes 417824 | tf_op jit(solution)/shard_map/rows_3/ppermute | solution.py:417
  41.6 0.1 pack.3
  41.6 1.6 %collective-permute-start.14 = (bf16[272,768]{1,0:T(8,128)(2,1)S(1)}, bf16[272,768]{1,0:T(8,128)(2,1)S(1)}, u32[]{:S(2)}, u32[]{:S(2)}) collective-permute-start(bf16[272,768]{1,0:T(8,128)(2,1)S(1)} %get-tuple-element.30.refs_2_.refs_12_), channel_id=1, source_target_pairs={{0,2},{2,0},{4,6},{6,4},{8,10},{10,8},{12,14},{14,12},{1,3},{3,1},... | collective-permute-start | bytes 1253384 | tf_op jit(solution)/shard_map/over_3/ppermute | solution.py:424
  43.3 0.0 collective-permute-done.8.refs_1_
  43.3 8.2 %collective-permute-done.7.refs_0_ = bf16[264,768]{1,0:T(8,128)(2,1)S(1)} collective-permute-done((bf16[264,768]{1,0:T(8,128)(2,1)S(1)}, bf16[264,768]{1,0:T(8,128)(2,1)S(1)}, u32[]{:S(2)}, u32[]{:S(2)}) %collective-permute-start.7) | collective-permute-done | bytes 405536 | tf_op jit(solution)/shard_map/over_1/ppermute | solution.py:424
  51.5 0.0 collective-permute-done.10.refs_3_.refs_13_.refs_16_
  51.5 0.0 collective-permute-start.11
  51.5 0.5 collective-permute-start.12
  52.0 0.7 collective-permute-start.15
  52.7 1.4 %collective-permute-start.16 = (bf16[264,768]{1,0:T(8,128)(2,1)S(1)}, bf16[264,768]{1,0:T(8,128)(2,1)S(1)}, u32[]{:S(2)}, u32[]{:S(2)}) collective-permute-start(bf16[264,768]{1,0:T(8,128)(2,1)S(1)} %get-tuple-element.37), channel_id=1, source_target_pairs={{0,4},{2,6},{4,0},{6,2},{8,12},{10,14},{12,8},{14,10},{1,5},{3,7},... | collective-permute-start | bytes 1216520 | tf_op jit(solution)/shard_map/passed_3/ppermute | solution.py:417
  54.1 0.0 collective-permute-done.11.refs_10_
  54.1 0.0 collective-permute-start.13
  54.1 0.0 collective-permute-done.12.refs_11_
  54.1 4.2 %meet.4 = (f32[1,3072]{1,0:T(1,128)S(1)}, f32[1,1280]{1,0:T(1,128)S(1)}) custom-call(bf16[264,768]{1,0:T(8,128)(2,1)S(1)} %get-tuple-element.23.refs_0_.refs_1_, bf16[264,768]{1,0:T(8,128)(2,1)S(1)} %collective-permute-done.refs_1_, bf16[264,768]{1,0:T(8,128)(2,1)S(1)} %collective-permute-done.1.refs_2_.refs_3_, ...), custom_call_target="tpu_custom_call" | custom-call | tf_op jit(solution)/shard_map/meet/pallas_call | solution.py:309
  58.2 0.0 collective-permute-done.15.refs_2_.refs_19_
  58.3 5.8 %collective-permute-done.16.refs_3_.refs_18_ = bf16[264,768]{1,0:T(8,128)(2,1)S(1)} collective-permute-done((bf16[264,768]{1,0:T(8,128)(2,1)S(1)}, bf16[264,768]{1,0:T(8,128)(2,1)S(1)}, u32[]{:S(2)}, u32[]{:S(2)}) %collective-permute-start.16) | collective-permute-done | bytes 405536 | tf_op jit(solution)/shard_map/passed_3/ppermute | solution.py:417
  64.1 0.0 collective-permute-done.14.refs_0_
  64.1 0.0 collective-permute-start.17
  64.1 0.0 collective-permute-done.13.refs_13_
  64.1 1.8 %collective-permute-done.17.refs_15_ = bf16[272,768]{1,0:T(8,128)(2,1)S(1)} collective-permute-done((bf16[272,768]{1,0:T(8,128)(2,1)S(1)}, bf16[272,768]{1,0:T(8,128)(2,1)S(1)}, u32[]{:S(2)}, u32[]{:S(2)}) %collective-permute-start.17) | collective-permute-done | bytes 417824 | tf_op jit(solution)/shard_map/across_3/ppermute | solution.py:428
  65.9 1.8 %meet.5 = (f32[1,4096]{1,0:T(1,128)S(1)}, f32[1,1408]{1,0:T(1,128)S(1)}) custom-call(bf16[264,768]{1,0:T(8,128)(2,1)S(1)} %get-tuple-element.23.refs_0_.refs_1_, bf16[264,768]{1,0:T(8,128)(2,1)S(1)} %collective-permute-done.refs_1_, bf16[264,768]{1,0:T(8,128)(2,1)S(1)} %collective-permute-done.1.refs_2_.refs_3_, ...), custom_call_target="tpu_custom_call" | custom-call | tf_op jit(solution)/shard_map/meet/pallas_call | solution.py:309
  67.6 0.1 route.1
  67.8 13.6 %all_to_all.5.got_ref = f32[16,1,512]{2,1,0:T(1,128)S(1)} all-to-all(f32[16,1,512]{2,1,0:T(1,128)S(1)} %route.1), channel_id=1, replica_groups=mesh['groups'=2,'blk'=8,'split'=2] {'blk','split'}, dimensions={0} | all-to-all | bytes 65536 | tf_op jit(solution)/shard_map/all_to_all | solution.py:559
  81.4 1.3 %back.1 = f32[1,1024]{1,0:T(1,128)} custom-call(f32[16,1,512]{2,1,0:T(1,128)S(1)} %all_to_all.5.got_ref, s32[1,1024]{1,0:T(1,128)S(1)} %get-tuple-element.40.rank_ref), custom_call_target="tpu_custom_call" | custom-call | tf_op jit(solution)/shard_map/back/pallas_call | solution.py:396
  (4 shorter events, 0.1 us)
Async XLA Ops:
  4.3 22.3 %collective-permute-start.4 = (bf16[264,768]{1,0:T(8,128)(2,1)S(1)}, bf16[264,768]{1,0:T(8,128)(2,1)S(1)}, u32[]{:S(2)}, u32[]{:S(2)}) collective-permute-start(bf16[264,768]{1,0:T(8,128)(2,1)S(1)} %get-tuple-element.25.refs_3_), channel_id=1, source_target_pairs={{0,8},{2,10},{4,12},{6,14},{8,0},{10,2},{12,4},{14,6},{1,9},{3,11}... | collective-permute-start | bytes 1216520 | tf_op jit(solution)/shard_map/rows_2/ppermute | solution.py:417
  8.4 18.4 %collective-permute-start.3 = (bf16[264,768]{1,0:T(8,128)(2,1)S(1)}, bf16[264,768]{1,0:T(8,128)(2,1)S(1)}, u32[]{:S(2)}, u32[]{:S(2)}) collective-permute-start(bf16[264,768]{1,0:T(8,128)(2,1)S(1)} %get-tuple-element.24.refs_14_.refs_17_), channel_id=1, source_target_pairs={{0,4},{2,6},{4,0},{6,2},{8,12},{10,14},{12,8},{14,10},{1,5},{3,7},... | collective-permute-start | bytes 1216520 | tf_op jit(solution)/shard_map/rows_2/ppermute | solution.py:417
  10.0 17.1 %collective-permute-start.1 = (bf16[264,768]{1,0:T(8,128)(2,1)S(1)}, bf16[264,768]{1,0:T(8,128)(2,1)S(1)}, u32[]{:S(2)}, u32[]{:S(2)}) collective-permute-start(bf16[264,768]{1,0:T(8,128)(2,1)S(1)} %get-tuple-element.23.refs_0_.refs_1_), channel_id=1, source_target_pairs={{0,2},{2,0},{4,6},{6,4},{8,10},{10,8},{12,14},{14,12},{1,3},{3,1},... | collective-permute-start | bytes 1216520 | tf_op jit(solution)/shard_map/over_0/ppermute | solution.py:424
  11.5 19.1 %collective-permute-start = (bf16[264,768]{1,0:T(8,128)(2,1)S(1)}, bf16[264,768]{1,0:T(8,128)(2,1)S(1)}, u32[]{:S(2)}, u32[]{:S(2)}) collective-permute-start(bf16[264,768]{1,0:T(8,128)(2,1)S(1)} %get-tuple-element.23.refs_0_.refs_1_), channel_id=1, source_target_pairs={{0,1},{1,0},{2,3},{3,2},{4,5},{5,4},{6,7},{7,6},{8,9},{9,8},{10,11... | collective-permute-start | bytes 1216520 | tf_op jit(solution)/shard_map/beside_0/ppermute | solution.py:428
  26.6 5.6 %collective-permute-start.6 = (bf16[264,768]{1,0:T(8,128)(2,1)S(1)}, bf16[264,768]{1,0:T(8,128)(2,1)S(1)}, u32[]{:S(2)}, u32[]{:S(2)}) collective-permute-start(bf16[264,768]{1,0:T(8,128)(2,1)S(1)} %collective-permute-done.4.refs_5_.refs_0_), channel_id=1, source_target_pairs={{0,1},{1,0},{2,3},{3,2},{4,5},{5,4},{6,7},{7,6},{8,9},{9,8},{10,11... | collective-permute-start | bytes 1216520 | tf_op jit(solution)/shard_map/beside_2/ppermute | solution.py:428
  26.8 5.9 %collective-permute-start.5 = (bf16[264,768]{1,0:T(8,128)(2,1)S(1)}, bf16[264,768]{1,0:T(8,128)(2,1)S(1)}, u32[]{:S(2)}, u32[]{:S(2)}) collective-permute-start(bf16[264,768]{1,0:T(8,128)(2,1)S(1)} %collective-permute-done.3.refs_4_.refs_2_), channel_id=1, source_target_pairs={{0,1},{1,0},{2,3},{3,2},{4,5},{5,4},{6,7},{7,6},{8,9},{9,8},{10,11... | collective-permute-start | bytes 1216520 | tf_op jit(solution)/shard_map/beside_1/ppermute | solution.py:428
  27.1 14.4 %collective-permute-start.9 = (bf16[272,768]{1,0:T(8,128)(2,1)S(1)}, bf16[272,768]{1,0:T(8,128)(2,1)S(1)}, u32[]{:S(2)}, u32[]{:S(2)}) collective-permute-start(bf16[272,768]{1,0:T(8,128)(2,1)S(1)} %get-tuple-element.29.refs_20_), channel_id=1, source_target_pairs={{0,12},{2,14},{4,8},{6,10},{8,4},{10,6},{12,0},{14,2},{1,13},{3,15... | collective-permute-start | bytes 1253384 | tf_op jit(solution)/shard_map/rows_3/ppermute | solution.py:417
  30.6 2.0 %collective-permute-start.2 = (bf16[264,768]{1,0:T(8,128)(2,1)S(1)}, bf16[264,768]{1,0:T(8,128)(2,1)S(1)}, u32[]{:S(2)}, u32[]{:S(2)}) collective-permute-start(bf16[264,768]{1,0:T(8,128)(2,1)S(1)} %collective-permute-done.1.refs_2_.refs_3_), channel_id=1, source_target_pairs={{0,1},{1,0},{2,3},{3,2},{4,5},{5,4},{6,7},{7,6},{8,9},{9,8},{10,11... | collective-permute-start | bytes 1216520 | tf_op jit(solution)/shard_map/across_0/ppermute | solution.py:428
  30.6 12.7 %collective-permute-start.8 = (bf16[264,768]{1,0:T(8,128)(2,1)S(1)}, bf16[264,768]{1,0:T(8,128)(2,1)S(1)}, u32[]{:S(2)}, u32[]{:S(2)}) collective-permute-start(bf16[264,768]{1,0:T(8,128)(2,1)S(1)} %collective-permute-done.4.refs_5_.refs_0_), channel_id=1, source_target_pairs={{0,2},{2,0},{4,6},{6,4},{8,10},{10,8},{12,14},{14,12},{1,3},{3,1},... | collective-permute-start | bytes 1216520 | tf_op jit(solution)/shard_map/over_2/ppermute | solution.py:424
  32.1 19.3 %collective-permute-start.7 = (bf16[264,768]{1,0:T(8,128)(2,1)S(1)}, bf16[264,768]{1,0:T(8,128)(2,1)S(1)}, u32[]{:S(2)}, u32[]{:S(2)}) collective-permute-start(bf16[264,768]{1,0:T(8,128)(2,1)S(1)} %collective-permute-done.3.refs_4_.refs_2_), channel_id=1, source_target_pairs={{0,2},{2,0},{4,6},{6,4},{8,10},{10,8},{12,14},{14,12},{1,3},{3,1},... | collective-permute-start | bytes 1216520 | tf_op jit(solution)/shard_map/over_1/ppermute | solution.py:424
  32.7 18.8 %collective-permute-start.10 = (bf16[264,768]{1,0:T(8,128)(2,1)S(1)}, bf16[264,768]{1,0:T(8,128)(2,1)S(1)}, u32[]{:S(2)}, u32[]{:S(2)}) collective-permute-start(bf16[264,768]{1,0:T(8,128)(2,1)S(1)} %get-tuple-element.31), channel_id=1, source_target_pairs={{0,4},{2,6},{4,0},{6,2},{8,12},{10,14},{12,8},{14,10},{1,5},{3,7},... | collective-permute-start | bytes 1216520 | tf_op jit(solution)/shard_map/passed_2/ppermute | solution.py:417
  41.6 22.5 %collective-permute-start.14 = (bf16[272,768]{1,0:T(8,128)(2,1)S(1)}, bf16[272,768]{1,0:T(8,128)(2,1)S(1)}, u32[]{:S(2)}, u32[]{:S(2)}) collective-permute-start(bf16[272,768]{1,0:T(8,128)(2,1)S(1)} %get-tuple-element.30.refs_2_.refs_12_), channel_id=1, source_target_pairs={{0,2},{2,0},{4,6},{6,4},{8,10},{10,8},{12,14},{14,12},{1,3},{3,1},... | collective-permute-start | bytes 1253384 | tf_op jit(solution)/shard_map/over_3/ppermute | solution.py:424
  51.5 2.6 %collective-permute-start.11 = (bf16[264,768]{1,0:T(8,128)(2,1)S(1)}, bf16[264,768]{1,0:T(8,128)(2,1)S(1)}, u32[]{:S(2)}, u32[]{:S(2)}) collective-permute-start(bf16[264,768]{1,0:T(8,128)(2,1)S(1)} %get-tuple-element.32.refs_8_), channel_id=1, source_target_pairs={{0,1},{1,0},{2,3},{3,2},{4,5},{5,4},{6,7},{7,6},{8,9},{9,8},{10,11... | collective-permute-start | bytes 1216520 | tf_op jit(solution)/shard_map/across_1/ppermute | solution.py:428
  51.5 2.6 %collective-permute-start.12 = (bf16[264,768]{1,0:T(8,128)(2,1)S(1)}, bf16[264,768]{1,0:T(8,128)(2,1)S(1)}, u32[]{:S(2)}, u32[]{:S(2)}) collective-permute-start(bf16[264,768]{1,0:T(8,128)(2,1)S(1)} %get-tuple-element.33.refs_9_), channel_id=1, source_target_pairs={{0,1},{1,0},{2,3},{3,2},{4,5},{5,4},{6,7},{7,6},{8,9},{9,8},{10,11... | collective-permute-start | bytes 1216520 | tf_op jit(solution)/shard_map/across_2/ppermute | solution.py:428
  52.0 6.2 %collective-permute-start.15 = (bf16[264,768]{1,0:T(8,128)(2,1)S(1)}, bf16[264,768]{1,0:T(8,128)(2,1)S(1)}, u32[]{:S(2)}, u32[]{:S(2)}) collective-permute-start(bf16[264,768]{1,0:T(8,128)(2,1)S(1)} %get-tuple-element.36), channel_id=1, source_target_pairs={{4,8},{6,10},{8,4},{10,6},{5,9},{7,11},{9,5},{11,7},{20,24},{22,26... | collective-permute-start | bytes 1216520 | tf_op jit(solution)/shard_map/border/ppermute | solution.py:417
  52.7 11.4 %collective-permute-start.16 = (bf16[264,768]{1,0:T(8,128)(2,1)S(1)}, bf16[264,768]{1,0:T(8,128)(2,1)S(1)}, u32[]{:S(2)}, u32[]{:S(2)}) collective-permute-start(bf16[264,768]{1,0:T(8,128)(2,1)S(1)} %get-tuple-element.37), channel_id=1, source_target_pairs={{0,4},{2,6},{4,0},{6,2},{8,12},{10,14},{12,8},{14,10},{1,5},{3,7},... | collective-permute-start | bytes 1216520 | tf_op jit(solution)/shard_map/passed_3/ppermute | solution.py:417
  54.1 10.0 %collective-permute-start.13 = (bf16[272,768]{1,0:T(8,128)(2,1)S(1)}, bf16[272,768]{1,0:T(8,128)(2,1)S(1)}, u32[]{:S(2)}, u32[]{:S(2)}) collective-permute-start(bf16[272,768]{1,0:T(8,128)(2,1)S(1)} %get-tuple-element.30.refs_2_.refs_12_), channel_id=1, source_target_pairs={{0,1},{1,0},{2,3},{3,2},{4,5},{5,4},{6,7},{7,6},{8,9},{9,8},{10,11... | collective-permute-start | bytes 1253384 | tf_op jit(solution)/shard_map/beside_3/ppermute | solution.py:428
  64.1 1.8 %collective-permute-start.17 = (bf16[272,768]{1,0:T(8,128)(2,1)S(1)}, bf16[272,768]{1,0:T(8,128)(2,1)S(1)}, u32[]{:S(2)}, u32[]{:S(2)}) collective-permute-start(bf16[272,768]{1,0:T(8,128)(2,1)S(1)} %after.3.refs_14_), channel_id=1, source_target_pairs={{0,1},{1,0},{2,3},{3,2},{4,5},{5,4},{6,7},{7,6},{8,9},{9,8},{10,11... | collective-permute-start | bytes 1253384 | tf_op jit(solution)/shard_map/across_3/ppermute | solution.py:428

commit v6 on v5

--- a/solution.py
+++ b/solution.py
@@ -65,10 +65,9 @@
     values = rows_ref[...].astype(jnp.float32)
     total = jnp.sum(values * values, axis=1, keepdims=True)
     unit[...] = (values * lax.rsqrt(total + 1e-06)).astype(jnp.bfloat16)
-    for at in range(0, count, step):
-        placed[at : at + step, :] = jnp.dot(
-            pick[at : at + step, :], unit[...], preferred_element_type=jnp.float32
-        ).astype(jnp.bfloat16)
+    placed[...] = jnp.dot(pick[...], unit[...], preferred_element_type=jnp.float32).astype(
+        jnp.bfloat16
+    )
     ids = jnp.broadcast_to((ids_ref[...] + 1).astype(jnp.bfloat16), (16, count))
     part = lax.axis_index("blk") // chips
     sorted_ids = lax.dot_general(
@@ -126,11 +125,13 @@
             at += rows
 
 
-def pack(blocks, plan, held=(), earlier=()):
+def pack(blocks, plan, held=(), earlier=(), spare=0):
     width = blocks[0].shape[1]
     plan = [list(pieces) for pieces in plan]
     outs = [
-        jax.ShapeDtypeStruct((sum(p[2] for p in pieces) + TAGS, width), jnp.bfloat16)
+        jax.ShapeDtypeStruct(
+            (sum(p[2] for p in pieces) + TAGS + spare, width), jnp.bfloat16
+        )
         for pieces in plan
     ]
     kept = [jax.ShapeDtypeStruct(h.shape, h.dtype) for h in held]
@@ -508,7 +509,7 @@
         border += [(i, half, half) for i in range(last)]
         inputs += got[1:]
     own_3, border, passing = pack(
-        inputs, [border, forward], held=[own_3], earlier=[scores[0][0]]
+        inputs, [border, forward], held=[own_3], earlier=[scores[0][0]], spare=TAGS
     )
     over_3 = chip_swap(own_3, "over_3")
     got_border = between(border, borders, "border")
@@ -530,7 +531,7 @@
         + [(r, l, None, True) for r in (2, 3) for l in (u_half, v_half)],
     )
 
-    visit_v = [(got_border, i * half, i) for i in range(got_border.shape[0] // half)]
+    visit_v = [(got_border, i * half, i) for i in range(2 if near else parts)]
     if near:
         visit_v += [(passed_3, last * half, 2), (held[0], half, 3)]
     visit_v = visits(visit_v, v_goal)

time: 83.1 us -> 82.5 us (level)
  waiting for transfers between devices: 37.5 us -> 26.9 us
  starting transfers between devices: 17.3 us -> 25.5 us
  Pallas kernels: 14.2 us -> 16.7 us
    ppermute x6, starting transfers between devices: 11.2 us -> 19.4 us  [between(): return lax.ppermute(array, 'blk', route)]
    ppermute x4, waiting for transfers between devices: 8.21 us -> 1.47 us  [chip_swap(): return lax.ppermute(array, 'blk', [(b, b ^ 1) for b in range(blocks)])]
    ppermute x6, waiting for transfers between devices: 27.5 us -> 22 us  [between(): return lax.ppermute(array, 'blk', route)]
    pallas_call x3, Pallas kernels: 8.4 us -> 11 us  [meet(): pl.pallas_call(kernel, out_shape=[jax.ShapeDtypeStruct((1, count), jnp.fl...]
    ppermute x8, waiting for transfers between devices: 1.77 us -> 3.44 us  [core_swap(): return lax.ppermute(array, 'split', [(c, c ^ 1) for c in range(cores)])]
  transfers between devices with their start and end apart: 18 -> 18, of which waited for: 6 -> 8; matrix products, arithmetic and copies ran while one was open for 0% -> 0% of each run, Pallas kernels for 8% -> 9%
where the time goes in v6:
time: 82.5 us; the launch traced here: 82.8 us
  waiting for transfers between devices  26.9 us (33%)
  starting transfers between devices  25.5 us (31%)
  Pallas kernels  16.7 us (20%)
  blocking collectives  13.6 us (16%)
    ppermute x6, waiting for transfers between devices, between(): return lax.ppermute(array, 'blk', route)  22 us
    ppermute x6, starting transfers between devices, between(): return lax.ppermute(array, 'blk', route)  19.4 us
    all_to_all x1, blocking collectives, body(): lax.all_to_all(found, ('blk', 'split'), split_axis=0, concat_axis=0, tile...  13.6 us
    pallas_call x3, Pallas kernels, meet(): pl.pallas_call(kernel, out_shape=[jax.ShapeDtypeStruct((1, count), jnp.fl...  11 us
    ppermute x4, starting transfers between devices, chip_swap(): return lax.ppermute(array, 'blk', [(b, b ^ 1) for b in range(blocks)])  5.06 us
    pallas_call x1, Pallas kernels, in_order(): pl.pallas_call(functools.partial(order_kernel, parts, chips), out_shape=o...  4.2 us
    ppermute x8, waiting for transfers between devices, core_swap(): return lax.ppermute(array, 'split', [(c, c ^ 1) for c in range(cores)])  3.44 us
  transfers between devices with their start and end apart: 18, of which 8 were waited for; matrix products, arithmetic and copies ran while one was open for 0% of the time, Pallas kernels for 9%

profile of v6, /device:TPU:0, one launch (start us, length us, event | category | flops | bytes accessed | tf_op | source)
XLA Modules:
  0.0 82.8 jit_solution(10905544896345981515)
XLA Ops:
  0.0 4.2 %order.1 = (bf16[264,768]{1,0:T(8,128)(2,1)S(1)}, bf16[264,768]{1,0:T(8,128)(2,1)S(1)}, bf16[264,768]{1,0:T(8,128)(2,1)S(1)}, bf16[272,768]{1,0:T(8,128)(2,1)S(1)}, s32[1,1024]{1,0:T(1,128)S(1)}) custom-call(bf16[1024,768]{1,0:T(8,128)(2,1)} %rows_hbm.1, s32[1,1024]{1,0:T(1,128)} %bitcast.3, s32[1,1024]{1,0:T(1,128)} %bitcast.4), custom_call_target="tpu_custom_call" | custom-call | tf_op jit(solution)/shard_map/order/pallas_call | solution.py:94
  4.2 4.1 %collective-permute-start.4 = (bf16[264,768]{1,0:T(8,128)(2,1)S(1)}, bf16[264,768]{1,0:T(8,128)(2,1)S(1)}, u32[]{:S(2)}, u32[]{:S(2)}) collective-permute-start(bf16[264,768]{1,0:T(8,128)(2,1)S(1)} %get-tuple-element.25.refs_3_), channel_id=1, source_target_pairs={{0,8},{2,10},{4,12},{6,14},{8,0},{10,2},{12,4},{14,6},{1,9},{3,11}... | collective-permute-start | bytes 1216520 | tf_op jit(solution)/shard_map/rows_2/ppermute | solution.py:418
  8.3 1.6 %collective-permute-start.3 = (bf16[264,768]{1,0:T(8,128)(2,1)S(1)}, bf16[264,768]{1,0:T(8,128)(2,1)S(1)}, u32[]{:S(2)}, u32[]{:S(2)}) collective-permute-start(bf16[264,768]{1,0:T(8,128)(2,1)S(1)} %get-tuple-element.24.refs_14_.refs_17_), channel_id=1, source_target_pairs={{0,4},{2,6},{4,0},{6,2},{8,12},{10,14},{12,8},{14,10},{1,5},{3,7},... | collective-permute-start | bytes 1216520 | tf_op jit(solution)/shard_map/rows_2/ppermute | solution.py:418
  9.9 1.5 %collective-permute-start.1 = (bf16[264,768]{1,0:T(8,128)(2,1)S(1)}, bf16[264,768]{1,0:T(8,128)(2,1)S(1)}, u32[]{:S(2)}, u32[]{:S(2)}) collective-permute-start(bf16[264,768]{1,0:T(8,128)(2,1)S(1)} %get-tuple-element.23.refs_0_.refs_1_), channel_id=1, source_target_pairs={{0,2},{2,0},{4,6},{6,4},{8,10},{10,8},{12,14},{14,12},{1,3},{3,1},... | collective-permute-start | bytes 1216520 | tf_op jit(solution)/shard_map/over_0/ppermute | solution.py:425
  11.4 0.0 collective-permute-start
  11.4 15.1 %collective-permute-done.4.refs_5_.refs_0_ = bf16[264,768]{1,0:T(8,128)(2,1)S(1)} collective-permute-done((bf16[264,768]{1,0:T(8,128)(2,1)S(1)}, bf16[264,768]{1,0:T(8,128)(2,1)S(1)}, u32[]{:S(2)}, u32[]{:S(2)}) %collective-permute-start.4) | collective-permute-done | bytes 405536 | tf_op jit(solution)/shard_map/rows_2/ppermute | solution.py:418
  26.5 0.0 collective-permute-start.6
  26.5 0.2 collective-permute-done.3.refs_4_.refs_2_
  26.7 0.3 collective-permute-start.5
  27.0 0.0 collective-permute-done.1.refs_2_.refs_3_
  27.0 3.5 %collective-permute-start.9 = (bf16[272,768]{1,0:T(8,128)(2,1)S(1)}, bf16[272,768]{1,0:T(8,128)(2,1)S(1)}, u32[]{:S(2)}, u32[]{:S(2)}) collective-permute-start(bf16[272,768]{1,0:T(8,128)(2,1)S(1)} %get-tuple-element.29.refs_20_), channel_id=1, source_target_pairs={{0,12},{2,14},{4,8},{6,10},{8,4},{10,6},{12,0},{14,2},{1,13},{3,15... | collective-permute-start | bytes 1253384 | tf_op jit(solution)/shard_map/rows_3/ppermute | solution.py:418
  30.5 0.0 collective-permute-start.2
  30.5 0.0 collective-permute-done.refs_1_
  30.5 1.5 %collective-permute-start.8 = (bf16[264,768]{1,0:T(8,128)(2,1)S(1)}, bf16[264,768]{1,0:T(8,128)(2,1)S(1)}, u32[]{:S(2)}, u32[]{:S(2)}) collective-permute-start(bf16[264,768]{1,0:T(8,128)(2,1)S(1)} %collective-permute-done.4.refs_5_.refs_0_), channel_id=1, source_target_pairs={{0,2},{2,0},{4,6},{6,4},{8,10},{10,8},{12,14},{14,12},{1,3},{3,1},... | collective-permute-start | bytes 1216520 | tf_op jit(solution)/shard_map/over_2/ppermute | solution.py:425
  32.1 0.0 collective-permute-done.6.refs_7_
  32.1 0.5 collective-permute-start.7
  32.6 0.0 collective-permute-done.5.refs_6_
  32.6 0.0 collective-permute-start.10
  32.6 0.0 collective-permute-done.2.refs_3_
  32.6 2.5 %meet.3 = (f32[1,2048]{1,0:T(1,128)S(1)}, f32[1,768]{1,0:T(1,128)S(1)}) custom-call(bf16[264,768]{1,0:T(8,128)(2,1)S(1)} %get-tuple-element.23.refs_0_.refs_1_, bf16[264,768]{1,0:T(8,128)(2,1)S(1)} %collective-permute-done.refs_1_, bf16[264,768]{1,0:T(8,128)(2,1)S(1)} %collective-permute-done.1.refs_2_.refs_3_, ...), custom_call_target="tpu_custom_call" | custom-call | tf_op jit(solution)/shard_map/meet/pallas_call | solution.py:310
  35.1 6.4 %collective-permute-done.9.refs_0_ = bf16[272,768]{1,0:T(8,128)(2,1)S(1)} collective-permute-done((bf16[272,768]{1,0:T(8,128)(2,1)S(1)}, bf16[272,768]{1,0:T(8,128)(2,1)S(1)}, u32[]{:S(2)}, u32[]{:S(2)}) %collective-permute-start.9) | collective-permute-done | bytes 417824 | tf_op jit(solution)/shard_map/rows_3/ppermute | solution.py:418
  41.5 0.1 pack.3
  41.6 0.7 collective-permute-start.15
  42.3 9.6 %collective-permute-start.16 = (bf16[272,768]{1,0:T(8,128)(2,1)S(1)}, bf16[272,768]{1,0:T(8,128)(2,1)S(1)}, u32[]{:S(2)}, u32[]{:S(2)}) collective-permute-start(bf16[272,768]{1,0:T(8,128)(2,1)S(1)} %get-tuple-element.37), channel_id=1, source_target_pairs={{0,4},{2,6},{4,0},{6,2},{8,12},{10,14},{12,8},{14,10},{1,5},{3,7},... | collective-permute-start | bytes 1253384 | tf_op jit(solution)/shard_map/passed_3/ppermute | solution.py:418
  51.8 0.0 collective-permute-done.8.refs_1_
  51.8 1.5 %collective-permute-start.14 = (bf16[272,768]{1,0:T(8,128)(2,1)S(1)}, bf16[272,768]{1,0:T(8,128)(2,1)S(1)}, u32[]{:S(2)}, u32[]{:S(2)}) collective-permute-start(bf16[272,768]{1,0:T(8,128)(2,1)S(1)} %get-tuple-element.30.refs_2_.refs_12_), channel_id=1, source_target_pairs={{0,2},{2,0},{4,6},{6,4},{8,10},{10,8},{12,14},{14,12},{1,3},{3,1},... | collective-permute-start | bytes 1253384 | tf_op jit(solution)/shard_map/over_3/ppermute | solution.py:425
  53.3 0.0 collective-permute-done.7.refs_0_
  53.3 0.0 collective-permute-done.10.refs_3_.refs_13_.refs_16_
  53.3 0.0 collective-permute-start.11
  53.3 0.5 collective-permute-start.12
  53.9 1.2 %collective-permute-done.11.refs_10_ = bf16[264,768]{1,0:T(8,128)(2,1)S(1)} collective-permute-done((bf16[264,768]{1,0:T(8,128)(2,1)S(1)}, bf16[264,768]{1,0:T(8,128)(2,1)S(1)}, u32[]{:S(2)}, u32[]{:S(2)}) %collective-permute-start.11) | collective-permute-done | bytes 405536 | tf_op jit(solution)/shard_map/across_1/ppermute | solution.py:429
  55.1 0.1 collective-permute-start.13
  55.2 0.4 collective-permute-done.12.refs_11_
  55.7 5.0 %meet.4 = (f32[1,3072]{1,0:T(1,128)S(1)}, f32[1,1280]{1,0:T(1,128)S(1)}) custom-call(bf16[264,768]{1,0:T(8,128)(2,1)S(1)} %get-tuple-element.23.refs_0_.refs_1_, bf16[264,768]{1,0:T(8,128)(2,1)S(1)} %collective-permute-done.refs_1_, bf16[264,768]{1,0:T(8,128)(2,1)S(1)} %collective-permute-done.1.refs_2_.refs_3_, ...), custom_call_target="tpu_custom_call" | custom-call | tf_op jit(solution)/shard_map/meet/pallas_call | solution.py:310
  60.7 0.0 collective-permute-done.15.refs_2_.refs_19_
  60.7 0.4 collective-permute-done.16.refs_3_.refs_18_
  61.1 1.5 %collective-permute-done.14.refs_0_ = bf16[272,768]{1,0:T(8,128)(2,1)S(1)} collective-permute-done((bf16[272,768]{1,0:T(8,128)(2,1)S(1)}, bf16[272,768]{1,0:T(8,128)(2,1)S(1)}, u32[]{:S(2)}, u32[]{:S(2)}) %collective-permute-start.14) | collective-permute-done | bytes 417824 | tf_op jit(solution)/shard_map/over_3/ppermute | solution.py:425
  62.5 0.0 collective-permute-start.17
  62.5 0.0 collective-permute-done.13.refs_13_
  62.5 1.8 %collective-permute-done.17.refs_15_ = bf16[272,768]{1,0:T(8,128)(2,1)S(1)} collective-permute-done((bf16[272,768]{1,0:T(8,128)(2,1)S(1)}, bf16[272,768]{1,0:T(8,128)(2,1)S(1)}, u32[]{:S(2)}, u32[]{:S(2)}) %collective-permute-start.17) | collective-permute-done | bytes 417824 | tf_op jit(solution)/shard_map/across_3/ppermute | solution.py:429
  64.3 3.5 %meet.5 = (f32[1,4096]{1,0:T(1,128)S(1)}, f32[1,1408]{1,0:T(1,128)S(1)}) custom-call(bf16[264,768]{1,0:T(8,128)(2,1)S(1)} %get-tuple-element.23.refs_0_.refs_1_, bf16[264,768]{1,0:T(8,128)(2,1)S(1)} %collective-permute-done.refs_1_, bf16[264,768]{1,0:T(8,128)(2,1)S(1)} %collective-permute-done.1.refs_2_.refs_3_, ...), custom_call_target="tpu_custom_call" | custom-call | tf_op jit(solution)/shard_map/meet/pallas_call | solution.py:310
  67.8 0.1 route.1
  67.9 13.6 %all_to_all.5.got_ref = f32[16,1,512]{2,1,0:T(1,128)S(1)} all-to-all(f32[16,1,512]{2,1,0:T(1,128)S(1)} %route.1), channel_id=1, replica_groups=mesh['groups'=2,'blk'=8,'split'=2] {'blk','split'}, dimensions={0} | all-to-all | bytes 65536 | tf_op jit(solution)/shard_map/all_to_all | solution.py:560
  81.5 1.3 %back.1 = f32[1,1024]{1,0:T(1,128)} custom-call(f32[16,1,512]{2,1,0:T(1,128)S(1)} %all_to_all.5.got_ref, s32[1,1024]{1,0:T(1,128)S(1)} %get-tuple-element.40.rank_ref), custom_call_target="tpu_custom_call" | custom-call | tf_op jit(solution)/shard_map/back/pallas_call | solution.py:397
  (4 shorter events, 0.1 us)
Async XLA Ops:
  4.2 22.3 %collective-permute-start.4 = (bf16[264,768]{1,0:T(8,128)(2,1)S(1)}, bf16[264,768]{1,0:T(8,128)(2,1)S(1)}, u32[]{:S(2)}, u32[]{:S(2)}) collective-permute-start(bf16[264,768]{1,0:T(8,128)(2,1)S(1)} %get-tuple-element.25.refs_3_), channel_id=1, source_target_pairs={{0,8},{2,10},{4,12},{6,14},{8,0},{10,2},{12,4},{14,6},{1,9},{3,11}... | collective-permute-start | bytes 1216520 | tf_op jit(solution)/shard_map/rows_2/ppermute | solution.py:418
  8.3 18.3 %collective-permute-start.3 = (bf16[264,768]{1,0:T(8,128)(2,1)S(1)}, bf16[264,768]{1,0:T(8,128)(2,1)S(1)}, u32[]{:S(2)}, u32[]{:S(2)}) collective-permute-start(bf16[264,768]{1,0:T(8,128)(2,1)S(1)} %get-tuple-element.24.refs_14_.refs_17_), channel_id=1, source_target_pairs={{0,4},{2,6},{4,0},{6,2},{8,12},{10,14},{12,8},{14,10},{1,5},{3,7},... | collective-permute-start | bytes 1216520 | tf_op jit(solution)/shard_map/rows_2/ppermute | solution.py:418
  9.9 17.1 %collective-permute-start.1 = (bf16[264,768]{1,0:T(8,128)(2,1)S(1)}, bf16[264,768]{1,0:T(8,128)(2,1)S(1)}, u32[]{:S(2)}, u32[]{:S(2)}) collective-permute-start(bf16[264,768]{1,0:T(8,128)(2,1)S(1)} %get-tuple-element.23.refs_0_.refs_1_), channel_id=1, source_target_pairs={{0,2},{2,0},{4,6},{6,4},{8,10},{10,8},{12,14},{14,12},{1,3},{3,1},... | collective-permute-start | bytes 1216520 | tf_op jit(solution)/shard_map/over_0/ppermute | solution.py:425
  11.4 19.1 %collective-permute-start = (bf16[264,768]{1,0:T(8,128)(2,1)S(1)}, bf16[264,768]{1,0:T(8,128)(2,1)S(1)}, u32[]{:S(2)}, u32[]{:S(2)}) collective-permute-start(bf16[264,768]{1,0:T(8,128)(2,1)S(1)} %get-tuple-element.23.refs_0_.refs_1_), channel_id=1, source_target_pairs={{0,1},{1,0},{2,3},{3,2},{4,5},{5,4},{6,7},{7,6},{8,9},{9,8},{10,11... | collective-permute-start | bytes 1216520 | tf_op jit(solution)/shard_map/beside_0/ppermute | solution.py:429
  26.5 5.6 %collective-permute-start.6 = (bf16[264,768]{1,0:T(8,128)(2,1)S(1)}, bf16[264,768]{1,0:T(8,128)(2,1)S(1)}, u32[]{:S(2)}, u32[]{:S(2)}) collective-permute-start(bf16[264,768]{1,0:T(8,128)(2,1)S(1)} %collective-permute-done.4.refs_5_.refs_0_), channel_id=1, source_target_pairs={{0,1},{1,0},{2,3},{3,2},{4,5},{5,4},{6,7},{7,6},{8,9},{9,8},{10,11... | collective-permute-start | bytes 1216520 | tf_op jit(solution)/shard_map/beside_2/ppermute | solution.py:429
  26.7 5.9 %collective-permute-start.5 = (bf16[264,768]{1,0:T(8,128)(2,1)S(1)}, bf16[264,768]{1,0:T(8,128)(2,1)S(1)}, u32[]{:S(2)}, u32[]{:S(2)}) collective-permute-start(bf16[264,768]{1,0:T(8,128)(2,1)S(1)} %collective-permute-done.3.refs_4_.refs_2_), channel_id=1, source_target_pairs={{0,1},{1,0},{2,3},{3,2},{4,5},{5,4},{6,7},{7,6},{8,9},{9,8},{10,11... | collective-permute-start | bytes 1216520 | tf_op jit(solution)/shard_map/beside_1/ppermute | solution.py:429
  27.0 14.4 %collective-permute-start.9 = (bf16[272,768]{1,0:T(8,128)(2,1)S(1)}, bf16[272,768]{1,0:T(8,128)(2,1)S(1)}, u32[]{:S(2)}, u32[]{:S(2)}) collective-permute-start(bf16[272,768]{1,0:T(8,128)(2,1)S(1)} %get-tuple-element.29.refs_20_), channel_id=1, source_target_pairs={{0,12},{2,14},{4,8},{6,10},{8,4},{10,6},{12,0},{14,2},{1,13},{3,15... | collective-permute-start | bytes 1253384 | tf_op jit(solution)/shard_map/rows_3/ppermute | solution.py:418
  30.5 2.0 %collective-permute-start.2 = (bf16[264,768]{1,0:T(8,128)(2,1)S(1)}, bf16[264,768]{1,0:T(8,128)(2,1)S(1)}, u32[]{:S(2)}, u32[]{:S(2)}) collective-permute-start(bf16[264,768]{1,0:T(8,128)(2,1)S(1)} %collective-permute-done.1.refs_2_.refs_3_), channel_id=1, source_target_pairs={{0,1},{1,0},{2,3},{3,2},{4,5},{5,4},{6,7},{7,6},{8,9},{9,8},{10,11... | collective-permute-start | bytes 1216520 | tf_op jit(solution)/shard_map/across_0/ppermute | solution.py:429
  30.5 21.3 %collective-permute-start.8 = (bf16[264,768]{1,0:T(8,128)(2,1)S(1)}, bf16[264,768]{1,0:T(8,128)(2,1)S(1)}, u32[]{:S(2)}, u32[]{:S(2)}) collective-permute-start(bf16[264,768]{1,0:T(8,128)(2,1)S(1)} %collective-permute-done.4.refs_5_.refs_0_), channel_id=1, source_target_pairs={{0,2},{2,0},{4,6},{6,4},{8,10},{10,8},{12,14},{14,12},{1,3},{3,1},... | collective-permute-start | bytes 1216520 | tf_op jit(solution)/shard_map/over_2/ppermute | solution.py:425
  32.1 21.3 %collective-permute-start.7 = (bf16[264,768]{1,0:T(8,128)(2,1)S(1)}, bf16[264,768]{1,0:T(8,128)(2,1)S(1)}, u32[]{:S(2)}, u32[]{:S(2)}) collective-permute-start(bf16[264,768]{1,0:T(8,128)(2,1)S(1)} %collective-permute-done.3.refs_4_.refs_2_), channel_id=1, source_target_pairs={{0,2},{2,0},{4,6},{6,4},{8,10},{10,8},{12,14},{14,12},{1,3},{3,1},... | collective-permute-start | bytes 1216520 | tf_op jit(solution)/shard_map/over_1/ppermute | solution.py:425
  32.6 20.8 %collective-permute-start.10 = (bf16[264,768]{1,0:T(8,128)(2,1)S(1)}, bf16[264,768]{1,0:T(8,128)(2,1)S(1)}, u32[]{:S(2)}, u32[]{:S(2)}) collective-permute-start(bf16[264,768]{1,0:T(8,128)(2,1)S(1)} %get-tuple-element.31), channel_id=1, source_target_pairs={{0,4},{2,6},{4,0},{6,2},{8,12},{10,14},{12,8},{14,10},{1,5},{3,7},... | collective-permute-start | bytes 1216520 | tf_op jit(solution)/shard_map/passed_2/ppermute | solution.py:418
  41.6 19.1 %collective-permute-start.15 = (bf16[272,768]{1,0:T(8,128)(2,1)S(1)}, bf16[272,768]{1,0:T(8,128)(2,1)S(1)}, u32[]{:S(2)}, u32[]{:S(2)}) collective-permute-start(bf16[272,768]{1,0:T(8,128)(2,1)S(1)} %get-tuple-element.36), channel_id=1, source_target_pairs={{4,8},{6,10},{8,4},{10,6},{5,9},{7,11},{9,5},{11,7},{20,24},{22,26... | collective-permute-start | bytes 1253384 | tf_op jit(solution)/shard_map/border/ppermute | solution.py:418
  42.3 18.8 %collective-permute-start.16 = (bf16[272,768]{1,0:T(8,128)(2,1)S(1)}, bf16[272,768]{1,0:T(8,128)(2,1)S(1)}, u32[]{:S(2)}, u32[]{:S(2)}) collective-permute-start(bf16[272,768]{1,0:T(8,128)(2,1)S(1)} %get-tuple-element.37), channel_id=1, source_target_pairs={{0,4},{2,6},{4,0},{6,2},{8,12},{10,14},{12,8},{14,10},{1,5},{3,7},... | collective-permute-start | bytes 1253384 | tf_op jit(solution)/shard_map/passed_3/ppermute | solution.py:418
  51.8 10.7 %collective-permute-start.14 = (bf16[272,768]{1,0:T(8,128)(2,1)S(1)}, bf16[272,768]{1,0:T(8,128)(2,1)S(1)}, u32[]{:S(2)}, u32[]{:S(2)}) collective-permute-start(bf16[272,768]{1,0:T(8,128)(2,1)S(1)} %get-tuple-element.30.refs_2_.refs_12_), channel_id=1, source_target_pairs={{0,2},{2,0},{4,6},{6,4},{8,10},{10,8},{12,14},{14,12},{1,3},{3,1},... | collective-permute-start | bytes 1253384 | tf_op jit(solution)/shard_map/over_3/ppermute | solution.py:425
  53.3 1.7 %collective-permute-start.11 = (bf16[264,768]{1,0:T(8,128)(2,1)S(1)}, bf16[264,768]{1,0:T(8,128)(2,1)S(1)}, u32[]{:S(2)}, u32[]{:S(2)}) collective-permute-start(bf16[264,768]{1,0:T(8,128)(2,1)S(1)} %get-tuple-element.32.refs_8_), channel_id=1, source_target_pairs={{0,1},{1,0},{2,3},{3,2},{4,5},{5,4},{6,7},{7,6},{8,9},{9,8},{10,11... | collective-permute-start | bytes 1216520 | tf_op jit(solution)/shard_map/across_1/ppermute | solution.py:429
  53.3 2.3 %collective-permute-start.12 = (bf16[264,768]{1,0:T(8,128)(2,1)S(1)}, bf16[264,768]{1,0:T(8,128)(2,1)S(1)}, u32[]{:S(2)}, u32[]{:S(2)}) collective-permute-start(bf16[264,768]{1,0:T(8,128)(2,1)S(1)} %get-tuple-element.33.refs_9_), channel_id=1, source_target_pairs={{0,1},{1,0},{2,3},{3,2},{4,5},{5,4},{6,7},{7,6},{8,9},{9,8},{10,11... | collective-permute-start | bytes 1216520 | tf_op jit(solution)/shard_map/across_2/ppermute | solution.py:429
  55.1 7.5 %collective-permute-start.13 = (bf16[272,768]{1,0:T(8,128)(2,1)S(1)}, bf16[272,768]{1,0:T(8,128)(2,1)S(1)}, u32[]{:S(2)}, u32[]{:S(2)}) collective-permute-start(bf16[272,768]{1,0:T(8,128)(2,1)S(1)} %get-tuple-element.30.refs_2_.refs_12_), channel_id=1, source_target_pairs={{0,1},{1,0},{2,3},{3,2},{4,5},{5,4},{6,7},{7,6},{8,9},{9,8},{10,11... | collective-permute-start | bytes 1253384 | tf_op jit(solution)/shard_map/beside_3/ppermute | solution.py:429
  62.5 1.8 %collective-permute-start.17 = (bf16[272,768]{1,0:T(8,128)(2,1)S(1)}, bf16[272,768]{1,0:T(8,128)(2,1)S(1)}, u32[]{:S(2)}, u32[]{:S(2)}) collective-permute-start(bf16[272,768]{1,0:T(8,128)(2,1)S(1)} %after.3.refs_14_), channel_id=1, source_target_pairs={{0,1},{1,0},{2,3},{3,2},{4,5},{5,4},{6,7},{7,6},{8,9},{9,8},{10,11... | collective-permute-start | bytes 1253384 | tf_op jit(solution)/shard_map/across_3/ppermute | solution.py:429

commit v7 on v6

--- a/solution.py
+++ b/solution.py
@@ -173,15 +173,16 @@
     return jnp.logical_and(one[0] <= other[1], other[0] <= one[1])
 
 
-def meet_kernel(lefts, rights, pairs, inputs, *refs):
-    given = refs[:inputs]
-    left_out, right_out, left, left_ids, right, right_ids, left_best, right_best = refs[inputs:]
+def meet_kernel(table, fresh, rights, pairs, inputs, first, last, *refs):
+    given, outs = refs[:inputs], refs[inputs:]
+    left, left_ids, left_best, right_out = outs[:4]
+    right, right_ids, right_best = outs[5:] if last else outs[4:]
 
     def ids_of(piece):
         ref, start, rows = given[piece[0]], piece[1], piece[2]
         return ref[ref.shape[0] - TAGS :, start : start + rows].astype(jnp.float32)
 
-    def span(section):
+    def span_right(section):
         low, high = None, None
         for piece in section:
             ids = ids_of(piece)
@@ -190,28 +191,30 @@
             high = ids if high is None else jnp.maximum(high, ids)
         return jnp.min(low), jnp.max(high)
 
-    tested = [(r, l) for r, l, _, test in pairs if test]
-    right_span = {r: span(rights[r]) for r in sorted({r for r, _ in tested})}
-    left_span = {l: span(sum((lefts[i] for i in l), [])) for l in sorted({l for _, l in tested})}
-    wanted = {(r, l): overlap(right_span[r], left_span[l]) for r, l in tested}
-
-    def place_of(sections):
-        out, at = [], 0
-        for section in sections:
-            rows = padded(section)
-            out.append((at, rows))
-            at += rows
-        return out
-
-    left_at, right_at = place_of(lefts), place_of(rights)
-
-    def fill_left(number):
-        at = left_at[number][0]
-        for piece in lefts[number]:
+    def span_left(sections):
+        at, rows = table[sections[0]][0], sum(table[l][1] for l in sections)
+        ids = left_ids[at : at + rows, :TAGS]
+        return jnp.min(ids), jnp.max(ids)
+
+    if first:
+        left_best[...] = jnp.full(left_best.shape, FILL, jnp.float32)
+    for number, section in fresh.items():
+        at = table[number][0]
+        for piece in section:
             index, start, rows = piece
             left[at : at + rows, :] = given[index][start : start + rows, :]
             left_ids[at : at + rows, :TAGS] = jnp.transpose(ids_of(piece))
             at += rows
+
+    tested = [(r, l) for r, l, _, test in pairs if test]
+    right_span = {r: span_right(rights[r[0]]) for r in sorted({r for r, _ in tested})}
+    left_span = {l: span_left(l) for l in sorted({l for _, l in tested})}
+    wanted = {(r, l): overlap(right_span[r], left_span[l]) for r, l in tested}
+
+    right_at, at = [], 0
+    for section in rights:
+        right_at.append((at, padded(section)))
+        at += padded(section)
 
     def fill_right(number):
         at = right_at[number][0]
@@ -221,22 +224,20 @@
             right_ids[:, at : at + rows] = ids_of(piece)
             at += rows
 
-    left_best[...] = jnp.full(left_best.shape, FILL, jnp.float32)
     right_best[...] = jnp.full(right_best.shape, FILL, jnp.float32)
     right_ids[...] = jnp.full(right_ids.shape, -1.0, jnp.float32)
-    for which, sections, fill in ((1, lefts, fill_left), (0, rights, fill_right)):
-        for number in range(len(sections)):
-            uses = [p for p in pairs if (number in p[1] if which else number == p[0])]
-            load = functools.partial(fill, number)
-            if all(p[3] for p in uses):
-                need = [wanted[p[0], p[1]] for p in uses]
-                pl.when(functools.reduce(jnp.logical_or, need))(load)
-            else:
-                load()
+    for number in range(len(rights)):
+        uses = [p for p in pairs if number in p[0]]
+        load = functools.partial(fill_right, number)
+        if all(p[3] for p in uses):
+            pl.when(functools.reduce(jnp.logical_or, [wanted[p[0], p[1]] for p in uses]))(load)
+        else:
+            load()
 
     def score(r, l, same):
-        (lane, lanes), row = right_at[r], left_at[l[0]][0]
-        rows = sum(left_at[i][1] for i in l)
+        lane, row = right_at[r[0]][0], table[l[0]][0]
+        lanes = sum(right_at[i][1] for i in r)
+        rows = sum(table[i][1] for i in l)
         step = rows
         while step * lanes > 512 * 1024 and step % 32 == 0:
             step //= 2
@@ -253,11 +254,11 @@
             )
             scores = jnp.where(left_ids[down, :1] == right_ids[:1, across], scores, FILL)
             if same is not None:
-                first, count = same
-                theirs = lax.broadcasted_iota(jnp.int32, (step, lanes), 0) + index * step
-                mine = lax.broadcasted_iota(jnp.int32, (step, lanes), 1)
-                itself = jnp.logical_and(theirs + first == mine, theirs < count)
-                scores = jnp.where(itself, FILL, scores)
+                skip, start, count = same
+                theirs = lax.broadcasted_iota(jnp.int32, (step, lanes), 0) + (index * step - skip)
+                mine = lax.broadcasted_iota(jnp.int32, (step, lanes), 1) - start
+                inside = jnp.logical_and(mine >= 0, mine < count)
+                scores = jnp.where(jnp.logical_and(theirs == mine, inside), FILL, scores)
             left_best[down, :] = jnp.maximum(left_best[down, :], lane_fold(scores))
             right_best[:, across] = jnp.maximum(right_best[:, across], column_fold(scores))
             return 0
@@ -271,63 +272,68 @@
         else:
             run()
     right_out[...] = jnp.max(right_best[...], axis=0, keepdims=True)
-    left_out[...] = jnp.max(jnp.transpose(left_best[...]), axis=0, keepdims=True)
-
-
-def meet(lefts, rights, pairs, earlier=()):
+    if last:
+        outs[4][...] = jnp.max(jnp.transpose(left_best[...]), axis=0, keepdims=True)
+
+
+def meet(table, state, fresh, rights, pairs, last=False, earlier=()):
     blocks = []
 
-    def plan(sections):
-        out = []
-        for section in sections:
-            pieces = []
-            for block, start, rows, _ in section:
-                known = [i for i, b in enumerate(blocks) if b is block]
-                if not known:
-                    blocks.append(block)
-                pieces.append((known[0] if known else len(blocks) - 1, start, rows))
-            out.append(pieces)
-        return out
-
-    def goals(sections):
-        out = []
-        for section in sections:
-            out += [(p[3], p[2]) for p in section]
-            out.append((None, padded(section) - sum(p[2] for p in section)))
-        return out
-
-    plan_left, plan_right = plan(lefts), plan(rights)
+    def plan(section):
+        pieces = []
+        for block, start, rows, _ in section:
+            known = [i for i, b in enumerate(blocks) if b is block]
+            if not known:
+                blocks.append(block)
+            pieces.append((known[0] if known else len(blocks) - 1, start, rows))
+        return pieces
+
+    def goals(section):
+        filler = padded(section) - sum(p[2] for p in section)
+        return [(p[3], p[2]) for p in section] + [(None, filler)]
+
+    plan_left = {number: plan(section) for number, section in fresh.items()}
+    plan_right = [plan(section) for section in rights]
     width = blocks[0].shape[1]
-    count = sum(n for _, n in goals(lefts))
-    total = sum(n for _, n in goals(rights))
-    inputs = len(blocks)
+    count = sum(rows for _, rows in table)
+    total = sum(padded(section) for section in rights)
+    inputs, first = len(blocks), not state
+    unread = len(state) + len(earlier)
 
     def kernel(*refs):
         meet_kernel(
-            plan_left, plan_right, pairs, inputs, *refs[:inputs], *refs[inputs + len(earlier) :]
+            table, plan_left, plan_right, pairs, inputs, first, last,
+            *refs[:inputs], *refs[inputs + unread :]
         )
 
-    left_best, right_best = pl.pallas_call(
+    outs = [
+        pltpu.VMEM((count, width), jnp.bfloat16),
+        pltpu.VMEM((count, LANES), jnp.float32),
+        pltpu.VMEM((count, LANES), jnp.float32),
+        jax.ShapeDtypeStruct((1, total), jnp.float32),
+    ]
+    if last:
+        outs.append(jax.ShapeDtypeStruct((1, count), jnp.float32))
+    *state, right_best = pl.pallas_call(
         kernel,
-        out_shape=[
-            jax.ShapeDtypeStruct((1, count), jnp.float32),
-            jax.ShapeDtypeStruct((1, total), jnp.float32),
-        ],
-        in_specs=[WHOLE] * inputs + [ANYWHERE] * len(earlier),
-        out_specs=[WHOLE] * 2,
+        out_shape=outs,
+        in_specs=[WHOLE] * (inputs + len(state)) + [ANYWHERE] * len(earlier),
+        out_specs=[WHOLE] * len(outs),
+        input_output_aliases={inputs + i: i for i in range(len(state))},
         scratch_shapes=[
-            pltpu.VMEM((count, width), jnp.bfloat16),
-            pltpu.VMEM((count, LANES), jnp.float32),
             pltpu.VMEM((total, width), jnp.bfloat16),
             pltpu.VMEM((TAGS, total), jnp.float32),
-            pltpu.VMEM((count, LANES), jnp.float32),
             pltpu.VMEM((8, total), jnp.float32),
         ],
-        compiler_params=grant(28),
+        compiler_params=grant(24),
         cost_estimate=pl.CostEstimate(flops=0, bytes_accessed=0, transcendentals=0),
         name="meet",
-    )(*blocks, *earlier)
-    return [(left_best, goals(lefts)), (right_best, goals(rights))]
+    )(*blocks, *state, *earlier)
+    found = []
+    if last:
+        left_best, right_best = right_best, state.pop()
+        found = [(left_best, None)]
+    return state, [*found, (right_best, sum((goals(section) for section in rights), []))]
 
 
 def route_kernel(plan, parts, chips, cores, half, near, *refs):
@@ -487,13 +493,17 @@
     left_0 = sides([own_0, beside_0, over_0, across_0], [0])
     mine_0, mine_2 = whole(own_0, [0]), sum(pair(0, own_1, own_2), [])
     here_2 = [a + b for a, b in zip(pair(0, own_1, own_2), pair(1, beside_1, beside_2))]
-    some = len(second) * half
-    scores = meet(
-        [*left_0, *here_2],
+    sizes = [len(third) * members, members, 2 * len(second), 2 * len(second)]
+    sizes += [sizes[3], sizes[1], sizes[2], sizes[0]]
+    table = [(sum(sizes[:i]) * half, size * half) for i, size in enumerate(sizes)]
+    some, mates = len(second) * half, members * half
+    state, scores = meet(
+        table,
+        [],
+        {1: left_0[0], 2: here_2[0], 5: left_0[1], 6: here_2[1]},
         [mine_0, mine_2],
-        [(0, (0,), (0, half), False), (0, (1,), (half, half), False)]
-        + [(1, (0, 1), None, False)]
-        + [(1, (2,), (0, some), False), (1, (3,), (some, some), False)],
+        [((0,), (1,), (0, 0, half), False), ((0,), (5,), (0, half, half), False)]
+        + [((1,), (1, 2), (mates, 0, some), False), ((1,), (5, 6), (mates, some, some), False)],
     )
 
     last = len(third)
@@ -518,34 +528,41 @@
     across_1, across_2 = core_swap(over_1, "across_1"), core_swap(over_2, "across_2")
     beside_3 = core_swap(own_3, "beside_3")
     there_2 = [a + b for a, b in zip(pair(2, over_1, over_2), pair(3, across_1, across_2))]
-    visit_2 = [(passed_2, i * half, i) for i in range(len(second))]
-    visit_2 = visits(visit_2 + [(sent[1], 0, parts - 1)], u_goal)
-    visit_3 = visits([(passed_3, i * half, len(second) + i) for i in range(last)], u_goal)
+    visit_2 = [(passed_2, i * half, half, u_goal + i * half) for i in range(len(second))]
+    visit_3 = [(sent[1], 0, half, u_goal + (parts - 1) * half)]
+    visit_3 += [(passed_3, i * half, half, u_goal + (len(second) + i) * half) for i in range(last)]
     mine_3 = sum(sides([own_3], third), [])
-    lefts = [left_0[0], here_2[0], there_2[0], there_2[1], left_0[1], here_2[1]]
-    u_half, v_half = (0, 1, 2), (3, 4, 5)
-    scores += meet(
-        lefts,
-        [mine_2, mine_3, *visit_2],
-        [(0, (2, 3), None, False), (1, u_half + v_half, None, False)]
-        + [(r, l, None, True) for r in (2, 3) for l in (u_half, v_half)],
-    )
+    state, more_scores = meet(
+        table,
+        state,
+        {3: there_2[0], 4: there_2[1]},
+        [mine_2, mine_3, visit_2],
+        [((0,), (3, 4), None, False), ((1,), (1, 2, 3, 4, 5, 6), None, False)]
+        + [((2,), l, None, True) for l in ((1, 2, 3), (4, 5, 6))],
+    )
+    scores += more_scores
 
     visit_v = [(got_border, i * half, i) for i in range(2 if near else parts)]
     if near:
         visit_v += [(passed_3, last * half, 2), (held[0], half, 3)]
     visit_v = visits(visit_v, v_goal)
-    (over_3,) = after([over_3], [scores[2][0], got_border, passed_3])
+    (over_3,) = after([over_3], [scores[1][0], got_border, passed_3])
     across_3 = core_swap(over_3, "across_3")
     left_3 = sides([own_3, beside_3, over_3, across_3], third)
     some = last * half
-    scores += meet(
-        [*lefts[:3], left_3[0], left_3[1], *lefts[3:]],
-        [mine_3, *visit_2, visit_3[0] + visit_3[1], *visit_v],
-        [(0, (3,), (0, some), False), (0, (4,), (some, some), False)]
-        + [(r, (l,), None, True) for r in (1, 2) for l in (3, 4)]
-        + [(r, l, None, True) for r in (3, 4, 5) for l in ((0, 1, 2, 3), (4, 5, 6, 7))],
-    )
+    _, more_scores = meet(
+        table,
+        state,
+        {0: left_3[0], 7: left_3[1]},
+        [mine_3, visit_2, visit_3, *visit_v],
+        [((0, 1, 2), (0,), (0, 0, some), False), ((0, 1, 2), (7,), (0, some, some), False)]
+        + [((2,), l, None, True) for l in ((1, 2, 3), (4, 5, 6))]
+        + [((r,), l, None, True) for r in (3, 4) for l in ((0, 1, 2, 3), (4, 5, 6, 7))],
+        last=True,
+    )
+    rows_in = [left_3[0], left_0[0], here_2[0], there_2[0], there_2[1], left_0[1], here_2[1], left_3[1]]
+    everywhere = [(p[3], p[2]) for section in rows_in for p in section]
+    scores += [(best, goals or everywhere) for best, goals in more_scores]
     found = pl.pallas_call(
         functools.partial(
             route_kernel, [goals for _, goals in scores], parts, chips, cores, half, near

time: 82.5 us -> 82.3 us (level)
  waiting for transfers between devices: 26.9 us -> 29.5 us
  starting transfers between devices: 25.5 us -> 23.7 us
  blocking collectives: 13.6 us -> 12.5 us
    ppermute x6, waiting for transfers between devices: 22 us -> 24.6 us  [between(): return lax.ppermute(array, 'blk', route)]
    ppermute x6, starting transfers between devices: 19.4 us -> 17.8 us  [between(): return lax.ppermute(array, 'blk', route)]
    all_to_all x1, blocking collectives: 13.6 us -> 12.5 us  [body(): lax.all_to_all(found, ('blk', 'split'), split_axis=0, concat_axis=0, tile...]
  transfers between devices with their start and end apart: 18 -> 18, of which waited for: 8 -> 8; matrix products, arithmetic and copies ran while one was open for 0% -> 0% of each run, Pallas kernels for 9% -> 8%
where the time goes in v7:
time: 82.3 us
  waiting for transfers between devices  29.5 us (36%)
  starting transfers between devices  23.7 us (29%)
  Pallas kernels  16.4 us (20%)
  blocking collectives  12.5 us (15%)
    ppermute x6, waiting for transfers between devices, between(): return lax.ppermute(array, 'blk', route)  24.6 us
    ppermute x6, starting transfers between devices, between(): return lax.ppermute(array, 'blk', route)  17.8 us
    all_to_all x1, blocking collectives, body(): lax.all_to_all(found, ('blk', 'split'), split_axis=0, concat_axis=0, tile...  12.5 us
    pallas_call x3, Pallas kernels, meet(): pl.pallas_call(kernel, out_shape=outs, in_specs=[WHOLE] * (inputs + len(s...  10.7 us
    ppermute x4, starting transfers between devices, chip_swap(): return lax.ppermute(array, 'blk', [(b, b ^ 1) for b in range(blocks)])  5.06 us
    pallas_call x1, Pallas kernels, in_order(): pl.pallas_call(functools.partial(order_kernel, parts, chips), out_shape=o...  4.2 us
    ppermute x8, waiting for transfers between devices, core_swap(): return lax.ppermute(array, 'split', [(c, c ^ 1) for c in range(cores)])  3.44 us
  transfers between devices with their start and end apart: 18, of which 8 were waited for; matrix products, arithmetic and copies ran while one was open for 0% of the time, Pallas kernels for 8%

profile of v7, /device:TPU:0, one launch (start us, length us, event | category | flops | bytes accessed | tf_op | source)
XLA Modules:
  0.0 82.3 jit_solution(5588287390259488934)
XLA Ops:
  0.0 4.2 %order.1 = (bf16[264,768]{1,0:T(8,128)(2,1)S(1)}, bf16[264,768]{1,0:T(8,128)(2,1)S(1)}, bf16[264,768]{1,0:T(8,128)(2,1)S(1)}, bf16[272,768]{1,0:T(8,128)(2,1)S(1)}, s32[1,1024]{1,0:T(1,128)S(1)}) custom-call(bf16[1024,768]{1,0:T(8,128)(2,1)} %rows_hbm.1, s32[1,1024]{1,0:T(1,128)} %bitcast.3, s32[1,1024]{1,0:T(1,128)} %bitcast.4), custom_call_target="tpu_custom_call" | custom-call | tf_op jit(solution)/shard_map/order/pallas_call | solution.py:94
  4.2 3.1 %collective-permute-start.3 = (bf16[264,768]{1,0:T(8,128)(2,1)S(1)}, bf16[264,768]{1,0:T(8,128)(2,1)S(1)}, u32[]{:S(2)}, u32[]{:S(2)}) collective-permute-start(bf16[264,768]{1,0:T(8,128)(2,1)S(1)} %get-tuple-element.28.refs_5_), channel_id=1, source_target_pairs={{0,4},{2,6},{4,0},{6,2},{8,12},{10,14},{12,8},{14,10},{1,5},{3,7},... | collective-permute-start | bytes 1216520 | tf_op jit(solution)/shard_map/rows_2/ppermute | solution.py:424
  7.3 2.6 %collective-permute-start.4 = (bf16[264,768]{1,0:T(8,128)(2,1)S(1)}, bf16[264,768]{1,0:T(8,128)(2,1)S(1)}, u32[]{:S(2)}, u32[]{:S(2)}) collective-permute-start(bf16[264,768]{1,0:T(8,128)(2,1)S(1)} %get-tuple-element.29.refs_3_), channel_id=1, source_target_pairs={{0,8},{2,10},{4,12},{6,14},{8,0},{10,2},{12,4},{14,6},{1,9},{3,11}... | collective-permute-start | bytes 1216520 | tf_op jit(solution)/shard_map/rows_2/ppermute | solution.py:424
  9.9 1.5 %collective-permute-start.1 = (bf16[264,768]{1,0:T(8,128)(2,1)S(1)}, bf16[264,768]{1,0:T(8,128)(2,1)S(1)}, u32[]{:S(2)}, u32[]{:S(2)}) collective-permute-start(bf16[264,768]{1,0:T(8,128)(2,1)S(1)} %get-tuple-element.27.refs_0_.refs_1_), channel_id=1, source_target_pairs={{0,2},{2,0},{4,6},{6,4},{8,10},{10,8},{12,14},{14,12},{1,3},{3,1},... | collective-permute-start | bytes 1216520 | tf_op jit(solution)/shard_map/over_0/ppermute | solution.py:431
  11.4 0.0 collective-permute-start
  11.4 13.8 %collective-permute-done.3.refs_4_.refs_2_ = bf16[264,768]{1,0:T(8,128)(2,1)S(1)} collective-permute-done((bf16[264,768]{1,0:T(8,128)(2,1)S(1)}, bf16[264,768]{1,0:T(8,128)(2,1)S(1)}, u32[]{:S(2)}, u32[]{:S(2)}) %collective-permute-start.3) | collective-permute-done | bytes 405536 | tf_op jit(solution)/shard_map/rows_2/ppermute | solution.py:424
  25.2 0.0 collective-permute-start.5
  25.2 2.5 %collective-permute-done.4.refs_5_.refs_0_ = bf16[264,768]{1,0:T(8,128)(2,1)S(1)} collective-permute-done((bf16[264,768]{1,0:T(8,128)(2,1)S(1)}, bf16[264,768]{1,0:T(8,128)(2,1)S(1)}, u32[]{:S(2)}, u32[]{:S(2)}) %collective-permute-start.4) | collective-permute-done | bytes 405536 | tf_op jit(solution)/shard_map/rows_2/ppermute | solution.py:424
  27.8 0.0 collective-permute-start.6
  27.8 0.0 collective-permute-done.1.refs_2_.refs_3_
  27.8 2.5 %collective-permute-start.9 = (bf16[272,768]{1,0:T(8,128)(2,1)S(1)}, bf16[272,768]{1,0:T(8,128)(2,1)S(1)}, u32[]{:S(2)}, u32[]{:S(2)}) collective-permute-start(bf16[272,768]{1,0:T(8,128)(2,1)S(1)} %get-tuple-element.32.refs_8_), channel_id=1, source_target_pairs={{0,12},{2,14},{4,8},{6,10},{8,4},{10,6},{12,0},{14,2},{1,13},{3,15... | collective-permute-start | bytes 1253384 | tf_op jit(solution)/shard_map/rows_3/ppermute | solution.py:424
  30.3 0.2 collective-permute-start.2
  30.6 0.0 collective-permute-done.refs_1_
  30.6 1.5 %collective-permute-start.7 = (bf16[264,768]{1,0:T(8,128)(2,1)S(1)}, bf16[264,768]{1,0:T(8,128)(2,1)S(1)}, u32[]{:S(2)}, u32[]{:S(2)}) collective-permute-start(bf16[264,768]{1,0:T(8,128)(2,1)S(1)} %collective-permute-done.3.refs_4_.refs_2_), channel_id=1, source_target_pairs={{0,2},{2,0},{4,6},{6,4},{8,10},{10,8},{12,14},{14,12},{1,3},{3,1},... | collective-permute-start | bytes 1216520 | tf_op jit(solution)/shard_map/over_1/ppermute | solution.py:431
  32.1 0.0 collective-permute-done.5.refs_6_
  32.1 0.5 collective-permute-start.8
  32.6 0.0 collective-permute-done.6.refs_7_
  32.6 0.0 collective-permute-start.10
  32.6 0.0 collective-permute-done.2.refs_3_
  32.6 2.4 %meet.3 = (bf16[4096,768]{1,0:T(8,128)(2,1)S(1)}, f32[4096,128]{1,0:T(8,128)S(1)}, f32[4096,128]{1,0:T(8,128)S(1)}, f32[1,768]{1,0:T(1,128)S(1)}) custom-call(bf16[264,768]{1,0:T(8,128)(2,1)S(1)} %get-tuple-element.27.refs_0_.refs_1_, bf16[264,768]{1,0:T(8,128)(2,1)S(1)} %collective-permute-done.refs_1_, ...), custom_call_target="tpu_custom_call" | custom-call | tf_op jit(solution)/shard_map/meet/pallas_call | solution.py:317
  35.0 7.2 %collective-permute-done.9.refs_0_ = bf16[272,768]{1,0:T(8,128)(2,1)S(1)} collective-permute-done((bf16[272,768]{1,0:T(8,128)(2,1)S(1)}, bf16[272,768]{1,0:T(8,128)(2,1)S(1)}, u32[]{:S(2)}, u32[]{:S(2)}) %collective-permute-start.9) | collective-permute-done | bytes 417824 | tf_op jit(solution)/shard_map/rows_3/ppermute | solution.py:424
  42.2 0.1 pack.3
  42.3 0.7 collective-permute-start.15
  43.0 8.9 %collective-permute-start.16 = (bf16[272,768]{1,0:T(8,128)(2,1)S(1)}, bf16[272,768]{1,0:T(8,128)(2,1)S(1)}, u32[]{:S(2)}, u32[]{:S(2)}) collective-permute-start(bf16[272,768]{1,0:T(8,128)(2,1)S(1)} %get-tuple-element.42), channel_id=1, source_target_pairs={{0,4},{2,6},{4,0},{6,2},{8,12},{10,14},{12,8},{14,10},{1,5},{3,7},... | collective-permute-start | bytes 1253384 | tf_op jit(solution)/shard_map/passed_3/ppermute | solution.py:424
  51.9 0.0 collective-permute-done.7.refs_0_
  51.9 1.5 %collective-permute-start.14 = (bf16[272,768]{1,0:T(8,128)(2,1)S(1)}, bf16[272,768]{1,0:T(8,128)(2,1)S(1)}, u32[]{:S(2)}, u32[]{:S(2)}) collective-permute-start(bf16[272,768]{1,0:T(8,128)(2,1)S(1)} %get-tuple-element.33.refs_2_.refs_6_.refs_0_), channel_id=1, source_target_pairs={{0,2},{2,0},{4,6},{6,4},{8,10},{10,8},{12,14},{14,12},{1,3},{3,1},... | collective-permute-start | bytes 1253384 | tf_op jit(solution)/shard_map/over_3/ppermute | solution.py:431
  53.4 0.0 collective-permute-done.8.refs_1_
  53.4 0.0 collective-permute-done.10.refs_3_.refs_7_.refs_4_
  53.4 0.0 collective-permute-start.11
  53.4 0.5 collective-permute-start.12
  53.9 1.2 %collective-permute-done.11.refs_2_ = bf16[264,768]{1,0:T(8,128)(2,1)S(1)} collective-permute-done((bf16[264,768]{1,0:T(8,128)(2,1)S(1)}, bf16[264,768]{1,0:T(8,128)(2,1)S(1)}, u32[]{:S(2)}, u32[]{:S(2)}) %collective-permute-start.11) | collective-permute-done | bytes 405536 | tf_op jit(solution)/shard_map/across_1/ppermute | solution.py:435
  55.1 0.1 collective-permute-start.13
  55.3 0.4 collective-permute-done.12.refs_3_
  55.7 4.3 %meet.4 = (bf16[4096,768]{1,0:T(8,128)(2,1)S(1)}, f32[4096,128]{1,0:T(8,128)S(1)}, f32[4096,128]{1,0:T(8,128)S(1)}, f32[1,1024]{1,0:T(1,128)S(1)}) custom-call(bf16[264,768]{1,0:T(8,128)(2,1)S(1)} %get-tuple-element.35.refs_0_, bf16[264,768]{1,0:T(8,128)(2,1)S(1)} %get-tuple-element.36.refs_1_, ...), custom_call_target="tpu_custom_call", output_to_operand_aliasing={{0}: (8, {}), {1}: (9, {}), {2}: (10, {})} | custom-call | tf_op jit(solution)/shard_map/meet/pallas_call | solution.py:317
  60.0 0.0 collective-permute-done.15.refs_2_.refs_7_
  60.0 1.1 %collective-permute-done.16.refs_3_.refs_6_ = bf16[272,768]{1,0:T(8,128)(2,1)S(1)} collective-permute-done((bf16[272,768]{1,0:T(8,128)(2,1)S(1)}, bf16[272,768]{1,0:T(8,128)(2,1)S(1)}, u32[]{:S(2)}, u32[]{:S(2)}) %collective-permute-start.16) | collective-permute-done | bytes 417824 | tf_op jit(solution)/shard_map/passed_3/ppermute | solution.py:424
  61.1 1.5 %collective-permute-done.14.refs_0_ = bf16[272,768]{1,0:T(8,128)(2,1)S(1)} collective-permute-done((bf16[272,768]{1,0:T(8,128)(2,1)S(1)}, bf16[272,768]{1,0:T(8,128)(2,1)S(1)}, u32[]{:S(2)}, u32[]{:S(2)}) %collective-permute-start.14) | collective-permute-done | bytes 417824 | tf_op jit(solution)/shard_map/over_3/ppermute | solution.py:431
  62.6 0.0 collective-permute-start.17
  62.6 0.0 collective-permute-done.13.refs_1_
  62.6 1.8 %collective-permute-done.17.refs_3_ = bf16[272,768]{1,0:T(8,128)(2,1)S(1)} collective-permute-done((bf16[272,768]{1,0:T(8,128)(2,1)S(1)}, bf16[272,768]{1,0:T(8,128)(2,1)S(1)}, u32[]{:S(2)}, u32[]{:S(2)}) %collective-permute-start.17) | collective-permute-done | bytes 417824 | tf_op jit(solution)/shard_map/across_3/ppermute | solution.py:435
  64.3 4.0 %meet.5 = (bf16[4096,768]{1,0:T(8,128)(2,1)S(1)}, f32[4096,128]{1,0:T(8,128)S(1)}, f32[4096,128]{1,0:T(8,128)S(1)}, f32[1,1280]{1,0:T(1,128)S(1)}, f32[1,4096]{1,0:T(1,128)S(1)}) custom-call(bf16[272,768]{1,0:T(8,128)(2,1)S(1)} %get-tuple-element.33.refs_2_.refs_6_.refs_0_, ...), custom_call_target="tpu_custom_call", output_to_operand_aliasing={{0}: (9, {}), {1}: (10, {}), {2}: (11, {})} | custom-call | tf_op jit(solution)/shard_map/meet/pallas_call | solution.py:317
  68.3 0.1 route.1
  68.4 12.5 %all_to_all.5.got_ref = f32[16,1,512]{2,1,0:T(1,128)S(1)} all-to-all(f32[16,1,512]{2,1,0:T(1,128)S(1)} %route.1), channel_id=1, replica_groups=mesh['groups'=2,'blk'=8,'split'=2] {'blk','split'}, dimensions={0} | all-to-all | bytes 65536 | tf_op jit(solution)/shard_map/all_to_all | solution.py:577
  80.9 1.3 %back.1 = f32[1,1024]{1,0:T(1,128)} custom-call(f32[16,1,512]{2,1,0:T(1,128)S(1)} %all_to_all.5.got_ref, s32[1,1024]{1,0:T(1,128)S(1)} %get-tuple-element.48.rank_ref), custom_call_target="tpu_custom_call" | custom-call | tf_op jit(solution)/shard_map/back/pallas_call | solution.py:403
  (4 shorter events, 0.1 us)
Async XLA Ops:
  4.2 21.0 %collective-permute-start.3 = (bf16[264,768]{1,0:T(8,128)(2,1)S(1)}, bf16[264,768]{1,0:T(8,128)(2,1)S(1)}, u32[]{:S(2)}, u32[]{:S(2)}) collective-permute-start(bf16[264,768]{1,0:T(8,128)(2,1)S(1)} %get-tuple-element.28.refs_5_), channel_id=1, source_target_pairs={{0,4},{2,6},{4,0},{6,2},{8,12},{10,14},{12,8},{14,10},{1,5},{3,7},... | collective-permute-start | bytes 1216520 | tf_op jit(solution)/shard_map/rows_2/ppermute | solution.py:424
  7.3 20.5 %collective-permute-start.4 = (bf16[264,768]{1,0:T(8,128)(2,1)S(1)}, bf16[264,768]{1,0:T(8,128)(2,1)S(1)}, u32[]{:S(2)}, u32[]{:S(2)}) collective-permute-start(bf16[264,768]{1,0:T(8,128)(2,1)S(1)} %get-tuple-element.29.refs_3_), channel_id=1, source_target_pairs={{0,8},{2,10},{4,12},{6,14},{8,0},{10,2},{12,4},{14,6},{1,9},{3,11}... | collective-permute-start | bytes 1216520 | tf_op jit(solution)/shard_map/rows_2/ppermute | solution.py:424
  9.9 17.9 %collective-permute-start.1 = (bf16[264,768]{1,0:T(8,128)(2,1)S(1)}, bf16[264,768]{1,0:T(8,128)(2,1)S(1)}, u32[]{:S(2)}, u32[]{:S(2)}) collective-permute-start(bf16[264,768]{1,0:T(8,128)(2,1)S(1)} %get-tuple-element.27.refs_0_.refs_1_), channel_id=1, source_target_pairs={{0,2},{2,0},{4,6},{6,4},{8,10},{10,8},{12,14},{14,12},{1,3},{3,1},... | collective-permute-start | bytes 1216520 | tf_op jit(solution)/shard_map/over_0/ppermute | solution.py:431
  11.4 19.2 %collective-permute-start = (bf16[264,768]{1,0:T(8,128)(2,1)S(1)}, bf16[264,768]{1,0:T(8,128)(2,1)S(1)}, u32[]{:S(2)}, u32[]{:S(2)}) collective-permute-start(bf16[264,768]{1,0:T(8,128)(2,1)S(1)} %get-tuple-element.27.refs_0_.refs_1_), channel_id=1, source_target_pairs={{0,1},{1,0},{2,3},{3,2},{4,5},{5,4},{6,7},{7,6},{8,9},{9,8},{10,11... | collective-permute-start | bytes 1216520 | tf_op jit(solution)/shard_map/beside_0/ppermute | solution.py:435
  25.2 6.9 %collective-permute-start.5 = (bf16[264,768]{1,0:T(8,128)(2,1)S(1)}, bf16[264,768]{1,0:T(8,128)(2,1)S(1)}, u32[]{:S(2)}, u32[]{:S(2)}) collective-permute-start(bf16[264,768]{1,0:T(8,128)(2,1)S(1)} %collective-permute-done.3.refs_4_.refs_2_), channel_id=1, source_target_pairs={{0,1},{1,0},{2,3},{3,2},{4,5},{5,4},{6,7},{7,6},{8,9},{9,8},{10,11... | collective-permute-start | bytes 1216520 | tf_op jit(solution)/shard_map/beside_1/ppermute | solution.py:435
  27.8 4.8 %collective-permute-start.6 = (bf16[264,768]{1,0:T(8,128)(2,1)S(1)}, bf16[264,768]{1,0:T(8,128)(2,1)S(1)}, u32[]{:S(2)}, u32[]{:S(2)}) collective-permute-start(bf16[264,768]{1,0:T(8,128)(2,1)S(1)} %collective-permute-done.4.refs_5_.refs_0_), channel_id=1, source_target_pairs={{0,1},{1,0},{2,3},{3,2},{4,5},{5,4},{6,7},{7,6},{8,9},{9,8},{10,11... | collective-permute-start | bytes 1216520 | tf_op jit(solution)/shard_map/beside_2/ppermute | solution.py:435
  27.8 14.4 %collective-permute-start.9 = (bf16[272,768]{1,0:T(8,128)(2,1)S(1)}, bf16[272,768]{1,0:T(8,128)(2,1)S(1)}, u32[]{:S(2)}, u32[]{:S(2)}) collective-permute-start(bf16[272,768]{1,0:T(8,128)(2,1)S(1)} %get-tuple-element.32.refs_8_), channel_id=1, source_target_pairs={{0,12},{2,14},{4,8},{6,10},{8,4},{10,6},{12,0},{14,2},{1,13},{3,15... | collective-permute-start | bytes 1253384 | tf_op jit(solution)/shard_map/rows_3/ppermute | solution.py:424
  30.3 2.3 %collective-permute-start.2 = (bf16[264,768]{1,0:T(8,128)(2,1)S(1)}, bf16[264,768]{1,0:T(8,128)(2,1)S(1)}, u32[]{:S(2)}, u32[]{:S(2)}) collective-permute-start(bf16[264,768]{1,0:T(8,128)(2,1)S(1)} %collective-permute-done.1.refs_2_.refs_3_), channel_id=1, source_target_pairs={{0,1},{1,0},{2,3},{3,2},{4,5},{5,4},{6,7},{7,6},{8,9},{9,8},{10,11... | collective-permute-start | bytes 1216520 | tf_op jit(solution)/shard_map/across_0/ppermute | solution.py:435
  30.6 21.3 %collective-permute-start.7 = (bf16[264,768]{1,0:T(8,128)(2,1)S(1)}, bf16[264,768]{1,0:T(8,128)(2,1)S(1)}, u32[]{:S(2)}, u32[]{:S(2)}) collective-permute-start(bf16[264,768]{1,0:T(8,128)(2,1)S(1)} %collective-permute-done.3.refs_4_.refs_2_), channel_id=1, source_target_pairs={{0,2},{2,0},{4,6},{6,4},{8,10},{10,8},{12,14},{14,12},{1,3},{3,1},... | collective-permute-start | bytes 1216520 | tf_op jit(solution)/shard_map/over_1/ppermute | solution.py:431
  32.1 21.3 %collective-permute-start.8 = (bf16[264,768]{1,0:T(8,128)(2,1)S(1)}, bf16[264,768]{1,0:T(8,128)(2,1)S(1)}, u32[]{:S(2)}, u32[]{:S(2)}) collective-permute-start(bf16[264,768]{1,0:T(8,128)(2,1)S(1)} %collective-permute-done.4.refs_5_.refs_0_), channel_id=1, source_target_pairs={{0,2},{2,0},{4,6},{6,4},{8,10},{10,8},{12,14},{14,12},{1,3},{3,1},... | collective-permute-start | bytes 1216520 | tf_op jit(solution)/shard_map/over_2/ppermute | solution.py:431
  32.6 20.8 %collective-permute-start.10 = (bf16[264,768]{1,0:T(8,128)(2,1)S(1)}, bf16[264,768]{1,0:T(8,128)(2,1)S(1)}, u32[]{:S(2)}, u32[]{:S(2)}) collective-permute-start(bf16[264,768]{1,0:T(8,128)(2,1)S(1)} %get-tuple-element.34), channel_id=1, source_target_pairs={{0,4},{2,6},{4,0},{6,2},{8,12},{10,14},{12,8},{14,10},{1,5},{3,7},... | collective-permute-start | bytes 1216520 | tf_op jit(solution)/shard_map/passed_2/ppermute | solution.py:424
  42.3 17.7 %collective-permute-start.15 = (bf16[272,768]{1,0:T(8,128)(2,1)S(1)}, bf16[272,768]{1,0:T(8,128)(2,1)S(1)}, u32[]{:S(2)}, u32[]{:S(2)}) collective-permute-start(bf16[272,768]{1,0:T(8,128)(2,1)S(1)} %get-tuple-element.41), channel_id=1, source_target_pairs={{4,8},{6,10},{8,4},{10,6},{5,9},{7,11},{9,5},{11,7},{20,24},{22,26... | collective-permute-start | bytes 1253384 | tf_op jit(solution)/shard_map/border/ppermute | solution.py:424
  43.0 18.1 %collective-permute-start.16 = (bf16[272,768]{1,0:T(8,128)(2,1)S(1)}, bf16[272,768]{1,0:T(8,128)(2,1)S(1)}, u32[]{:S(2)}, u32[]{:S(2)}) collective-permute-start(bf16[272,768]{1,0:T(8,128)(2,1)S(1)} %get-tuple-element.42), channel_id=1, source_target_pairs={{0,4},{2,6},{4,0},{6,2},{8,12},{10,14},{12,8},{14,10},{1,5},{3,7},... | collective-permute-start | bytes 1253384 | tf_op jit(solution)/shard_map/passed_3/ppermute | solution.py:424
  51.9 10.7 %collective-permute-start.14 = (bf16[272,768]{1,0:T(8,128)(2,1)S(1)}, bf16[272,768]{1,0:T(8,128)(2,1)S(1)}, u32[]{:S(2)}, u32[]{:S(2)}) collective-permute-start(bf16[272,768]{1,0:T(8,128)(2,1)S(1)} %get-tuple-element.33.refs_2_.refs_6_.refs_0_), channel_id=1, source_target_pairs={{0,2},{2,0},{4,6},{6,4},{8,10},{10,8},{12,14},{14,12},{1,3},{3,1},... | collective-permute-start | bytes 1253384 | tf_op jit(solution)/shard_map/over_3/ppermute | solution.py:431
  53.4 1.7 %collective-permute-start.11 = (bf16[264,768]{1,0:T(8,128)(2,1)S(1)}, bf16[264,768]{1,0:T(8,128)(2,1)S(1)}, u32[]{:S(2)}, u32[]{:S(2)}) collective-permute-start(bf16[264,768]{1,0:T(8,128)(2,1)S(1)} %get-tuple-element.35.refs_0_), channel_id=1, source_target_pairs={{0,1},{1,0},{2,3},{3,2},{4,5},{5,4},{6,7},{7,6},{8,9},{9,8},{10,11... | collective-permute-start | bytes 1216520 | tf_op jit(solution)/shard_map/across_1/ppermute | solution.py:435
  53.4 2.3 %collective-permute-start.12 = (bf16[264,768]{1,0:T(8,128)(2,1)S(1)}, bf16[264,768]{1,0:T(8,128)(2,1)S(1)}, u32[]{:S(2)}, u32[]{:S(2)}) collective-permute-start(bf16[264,768]{1,0:T(8,128)(2,1)S(1)} %get-tuple-element.36.refs_1_), channel_id=1, source_target_pairs={{0,1},{1,0},{2,3},{3,2},{4,5},{5,4},{6,7},{7,6},{8,9},{9,8},{10,11... | collective-permute-start | bytes 1216520 | tf_op jit(solution)/shard_map/across_2/ppermute | solution.py:435
  55.1 7.5 %collective-permute-start.13 = (bf16[272,768]{1,0:T(8,128)(2,1)S(1)}, bf16[272,768]{1,0:T(8,128)(2,1)S(1)}, u32[]{:S(2)}, u32[]{:S(2)}) collective-permute-start(bf16[272,768]{1,0:T(8,128)(2,1)S(1)} %get-tuple-element.33.refs_2_.refs_6_.refs_0_), channel_id=1, source_target_pairs={{0,1},{1,0},{2,3},{3,2},{4,5},{5,4},{6,7},{7,6},{8,9},{9,8},{10,11... | collective-permute-start | bytes 1253384 | tf_op jit(solution)/shard_map/beside_3/ppermute | solution.py:435
  62.6 1.8 %collective-permute-start.17 = (bf16[272,768]{1,0:T(8,128)(2,1)S(1)}, bf16[272,768]{1,0:T(8,128)(2,1)S(1)}, u32[]{:S(2)}, u32[]{:S(2)}) collective-permute-start(bf16[272,768]{1,0:T(8,128)(2,1)S(1)} %after.3.refs_2_), channel_id=1, source_target_pairs={{0,1},{1,0},{2,3},{3,2},{4,5},{5,4},{6,7},{7,6},{8,9},{9,8},{10,11... | collective-permute-start | bytes 1253384 | tf_op jit(solution)/shard_map/across_3/ppermute | solution.py:435

commit v8 on v7

--- a/solution.py
+++ b/solution.py
@@ -37,11 +37,32 @@
     return best
 
 
-def order_kernel(parts, chips, rows_hbm, ids_hbm, pos_hbm, *refs):
-    outs, rank_ref = refs[:parts], refs[parts]
-    unit, pick, placed, tags, rows_ref, ids_ref, pos_ref, sems = refs[parts + 1 :]
-    count, width = rows_ref.shape
-    quart = count // parts // 4
+def place_blocks(ks, chips, parts, rank, ids, unit, pick, outs):
+    count = unit.shape[0]
+    slots = count // parts
+    quart = slots // 4
+    part = lax.axis_index("blk") // chips
+    for j, k in enumerate(ks):
+        quarter = lax.bitwise_xor(part, k)
+        side = lax.rem(quarter, 2)
+        for index, block in enumerate((3 - 3 * side, 2 - side, 3 * side, 1 + side)):
+            slot = lax.broadcasted_iota(jnp.int32, (quart, count), 0) + (4 * quarter + block) * quart
+            at = j * slots + index * quart
+            pick[at : at + quart, :] = jnp.where(slot == rank, 1.0, 0.0).astype(jnp.bfloat16)
+    rows = jnp.dot(pick[...], unit[...], preferred_element_type=jnp.float32).astype(jnp.bfloat16)
+    marks = jnp.broadcast_to((ids + 1).astype(jnp.bfloat16), (16, count))
+    tags = lax.dot_general(
+        marks, pick[...], (((1,), (1,)), ((), ())), preferred_element_type=jnp.float32
+    ).astype(jnp.bfloat16)
+    for j, out in enumerate(outs):
+        out[:slots, :] = rows[j * slots : (j + 1) * slots, :]
+        out[out.shape[0] - TAGS :, :slots] = tags[:TAGS, j * slots : (j + 1) * slots]
+
+
+def order_kernel(ks, chips, parts, rows_hbm, ids_hbm, pos_hbm, *refs):
+    outs = refs[: len(ks)]
+    unit, rank_ref, ids_ref, pick, rows_ref, pos_ref, sems = refs[len(ks) :]
+    count = unit.shape[0]
     step = 256
     fetch_pos = pltpu.make_async_copy(pos_hbm, pos_ref, sems.at[0])
     fetch_rows = pltpu.make_async_copy(rows_hbm, rows_ref, sems.at[1])
@@ -57,59 +78,55 @@
         below += jnp.sum(jnp.where(other < pos, 1.0, 0.0).reshape(step // 8, 8, count), axis=0)
     rank = jnp.sum(below, axis=0, keepdims=True).astype(jnp.int32)
     rank_ref[...] = rank
-    for at in range(0, count, step):
-        slot = lax.broadcasted_iota(jnp.int32, (step, count), 0) + at
-        pick[at : at + step, :] = jnp.where(slot == rank, 1.0, 0.0).astype(jnp.bfloat16)
     fetch_rows.wait()
     fetch_ids.wait()
     values = rows_ref[...].astype(jnp.float32)
     total = jnp.sum(values * values, axis=1, keepdims=True)
     unit[...] = (values * lax.rsqrt(total + 1e-06)).astype(jnp.bfloat16)
-    placed[...] = jnp.dot(pick[...], unit[...], preferred_element_type=jnp.float32).astype(
-        jnp.bfloat16
-    )
-    ids = jnp.broadcast_to((ids_ref[...] + 1).astype(jnp.bfloat16), (16, count))
-    part = lax.axis_index("blk") // chips
-    sorted_ids = lax.dot_general(
-        ids, pick[...], (((1,), (1,)), ((), ())), preferred_element_type=jnp.float32
-    )
-    for at in range(4 * parts):
-        tags[at, :, :quart] = sorted_ids[:, at * quart : (at + 1) * quart]
-    for k in range(parts):
-        quarter = lax.bitwise_xor(part, k)
-        side = lax.rem(quarter, 2)
-        for index, block in enumerate((3 - 3 * side, 2 - side, 3 * side, 1 + side)):
-            which = 4 * quarter + block
-            at = index * quart
-            outs[k][at : at + quart, :] = placed[pl.ds(pl.multiple_of(which * quart, quart), quart), :]
-            outs[k][outs[k].shape[0] - TAGS :, at : at + quart] = tags[which, :TAGS, :quart].astype(jnp.bfloat16)
-
-
-def in_order(embeddings, ids, pos, tag_rows, chips):
+    place_blocks(ks, chips, parts, rank, ids_ref[...], unit, pick, outs)
+
+
+def rest_kernel(ks, chips, parts, unit, rank_ref, ids_ref, *refs):
+    place_blocks(ks, chips, parts, rank_ref[...], ids_ref[...], unit, refs[-1], refs[:-1])
+
+
+def in_order(embeddings, ids, pos, tag_rows, chips, soon):
     parts = len(tag_rows)
     count, width = embeddings.shape
     slots = count // parts
-    outs = [pltpu.VMEM((slots + tags, width), jnp.bfloat16) for tags in tag_rows]
-    outs.append(jax.ShapeDtypeStruct((1, count), jnp.int32))
-    *blocks, rank = pl.pallas_call(
-        functools.partial(order_kernel, parts, chips),
-        out_shape=outs,
-        in_specs=[REMAINS, REMAINS, REMAINS],
-        out_specs=[WHOLE] * len(outs),
+    others = [k for k in range(parts) if k not in soon]
+
+    def blocks(ks):
+        return [pltpu.VMEM((slots + tag_rows[k], width), jnp.bfloat16) for k in ks]
+
+    given = [embeddings, ids.reshape(1, count), pos.reshape(1, count)]
+    row = pltpu.VMEM((1, count), jnp.int32)
+    *early, unit, rank, marks = pl.pallas_call(
+        functools.partial(order_kernel, soon, chips, parts),
+        out_shape=[*blocks(soon), pltpu.VMEM((count, width), jnp.bfloat16), row, row],
+        in_specs=[REMAINS] * 3,
+        out_specs=[WHOLE] * (len(soon) + 3),
         scratch_shapes=[
+            pltpu.VMEM((len(soon) * slots, count), jnp.bfloat16),
             pltpu.VMEM((count, width), jnp.bfloat16),
-            pltpu.VMEM((count, count), jnp.bfloat16),
-            pltpu.VMEM((count, width), jnp.bfloat16),
-            pltpu.VMEM((4 * parts, 16, max(slots // 4, LANES)), jnp.float32),
-            pltpu.VMEM((count, width), jnp.bfloat16),
-            pltpu.VMEM((1, count), jnp.int32),
             pltpu.VMEM((1, count), jnp.int32),
             pltpu.SemaphoreType.DMA((3,)),
         ],
         compiler_params=grant(24),
         name="order",
-    )(*[pltpu.with_memory_space_constraint(x, pltpu.HBM) for x in (embeddings, ids.reshape(1, count), pos.reshape(1, count))])
-    return blocks, rank
+    )(*[pltpu.with_memory_space_constraint(x, pltpu.HBM) for x in given])
+    late = pl.pallas_call(
+        functools.partial(rest_kernel, others, chips, parts),
+        out_shape=blocks(others),
+        in_specs=[WHOLE] * 3,
+        out_specs=[WHOLE] * len(others),
+        scratch_shapes=[pltpu.VMEM((len(others) * slots, count), jnp.bfloat16)],
+        compiler_params=grant(24),
+        cost_estimate=pl.CostEstimate(flops=0, bytes_accessed=0, transcendentals=0),
+        name="rest",
+    )(unit, rank, marks)
+    found = dict(zip(soon + others, early + list(late)))
+    return [found[k] for k in range(parts)], rank
 
 
 def pack_kernel(plan, inputs, *refs):
@@ -461,9 +478,8 @@
         far_rows = [(b, at + quart, quart, goal + i * half + quart) for b, at, i in pieces]
         return near_rows, far_rows
 
-    sent, rank = in_order(
-        embeddings, cluster_of, target_pos, [TAGS if k < middle else 2 * TAGS for k in range(parts)], chips
-    )
+    tag_rows = [TAGS if k < middle else 2 * TAGS for k in range(parts)]
+    sent, rank = in_order(embeddings, cluster_of, target_pos, tag_rows, chips, second)
     own_0 = sent[0]
     got = [swap(sent[k], k, "rows_2") for k in second]
     over_0 = chip_swap(own_0, "over_0")

time: 82.3 us -> 79 us (0.960)
  starting transfers between devices: 23.7 us -> 20.5 us
  blocking collectives: 12.5 us -> 10.1 us
  waiting for transfers between devices: 29.5 us -> 31.1 us
    ppermute x4, waiting for transfers between devices: 1.47 us -> 7.91 us  [chip_swap(): return lax.ppermute(array, 'blk', [(b, b ^ 1) for b in range(blocks)])]
    ppermute x6, waiting for transfers between devices: 24.6 us -> 19.8 us  [between(): return lax.ppermute(array, 'blk', route)]
    ppermute x6, starting transfers between devices: 17.8 us -> 14.2 us  [between(): return lax.ppermute(array, 'blk', route)]
    all_to_all x1, blocking collectives: 12.5 us -> 10.1 us  [body(): lax.all_to_all(found, ('blk', 'split'), split_axis=0, concat_axis=0, tile...]
    pallas_call x1 -> x2, Pallas kernels: 4.2 us -> 4.2 us  [the longest x1 2.95 us: in_order(): pl.pallas_call(functools.partial(order_kernel, soon, chips, parts), out_s...]
  transfers between devices with their start and end apart: 18 -> 18, of which waited for: 8 -> 9; matrix products, arithmetic and copies ran while one was open for 0% -> 0% of each run, Pallas kernels for 8% -> 9%
where the time goes in v8:
time: 79 us; the launch traced here: 78.2 us
  waiting for transfers between devices  31.1 us (39%)
  starting transfers between devices  20.5 us (26%)
  Pallas kernels  16.4 us (21%)
  blocking collectives  10.1 us (13%)
    ppermute x6, waiting for transfers between devices, between(): return lax.ppermute(array, 'blk', route)  19.8 us
    ppermute x6, starting transfers between devices, between(): return lax.ppermute(array, 'blk', route)  14.2 us
    pallas_call x3, Pallas kernels, meet(): pl.pallas_call(kernel, out_shape=outs, in_specs=[WHOLE] * (inputs + len(s...  10.7 us
    all_to_all x1, blocking collectives, body(): lax.all_to_all(found, ('blk', 'split'), split_axis=0, concat_axis=0, tile...  10.1 us
    ppermute x4, waiting for transfers between devices, chip_swap(): return lax.ppermute(array, 'blk', [(b, b ^ 1) for b in range(blocks)])  7.91 us
    ppermute x4, starting transfers between devices, chip_swap(): return lax.ppermute(array, 'blk', [(b, b ^ 1) for b in range(blocks)])  5.63 us
    ppermute x8, waiting for transfers between devices, core_swap(): return lax.ppermute(array, 'split', [(c, c ^ 1) for c in range(cores)])  3.44 us
    pallas_call x1, Pallas kernels, in_order(): pl.pallas_call(functools.partial(order_kernel, soon, chips, parts), out_s...  2.95 us
  transfers between devices with their start and end apart: 18, of which 9 were waited for; matrix products, arithmetic and copies ran while one was open for 0% of the time, Pallas kernels for 9%

profile of v8, /device:TPU:0, one launch (start us, length us, event | category | flops | bytes accessed | tf_op | source)
XLA Modules:
  0.0 78.2 jit_solution(11142444705835885145)
XLA Ops:
  0.0 3.0 %order.1 = (bf16[264,768]{1,0:T(8,128)(2,1)S(1)}, bf16[264,768]{1,0:T(8,128)(2,1)S(1)}, bf16[1024,768]{1,0:T(8,128)(2,1)S(1)}, s32[1,1024]{1,0:T(1,128)S(1)}, s32[1,1024]{1,0:T(1,128)S(1)}) custom-call(bf16[1024,768]{1,0:T(8,128)(2,1)} %rows_hbm.1, s32[1,1024]{1,0:T(1,128)} %bitcast.3, s32[1,1024]{1,0:T(1,128)} %bitcast.4), custom_call_target="tpu_custom_call" | custom-call | tf_op jit(solution)/shard_map/order/pallas_call | solution.py:104
  3.0 1.3 %rest.1 = (bf16[264,768]{1,0:T(8,128)(2,1)S(1)}, bf16[272,768]{1,0:T(8,128)(2,1)S(1)}) custom-call(bf16[1024,768]{1,0:T(8,128)(2,1)S(1)} %get-tuple-element.29.unit, s32[1,1024]{1,0:T(1,128)S(1)} %get-tuple-element.30.rank_ref, s32[1,1024]{1,0:T(1,128)S(1)} %get-tuple-element.31.ids_ref), custom_call_target="tpu_custom_call" | custom-call | tf_op jit(solution)/shard_map/rest/pallas_call | solution.py:118
  4.2 3.0 %collective-permute-start.1 = (bf16[264,768]{1,0:T(8,128)(2,1)S(1)}, bf16[264,768]{1,0:T(8,128)(2,1)S(1)}, u32[]{:S(2)}, u32[]{:S(2)}) collective-permute-start(bf16[264,768]{1,0:T(8,128)(2,1)S(1)} %get-tuple-element.32.refs_0_.refs_1_), channel_id=1, source_target_pairs={{0,2},{2,0},{4,6},{6,4},{8,10},{10,8},{12,14},{14,12},{1,3},{3,1},... | collective-permute-start | bytes 1216520 | tf_op jit(solution)/shard_map/over_0/ppermute | solution.py:448
  7.3 1.6 %collective-permute-start.3 = (bf16[264,768]{1,0:T(8,128)(2,1)S(1)}, bf16[264,768]{1,0:T(8,128)(2,1)S(1)}, u32[]{:S(2)}, u32[]{:S(2)}) collective-permute-start(bf16[264,768]{1,0:T(8,128)(2,1)S(1)} %get-tuple-element.33.refs_5_), channel_id=1, source_target_pairs={{0,4},{2,6},{4,0},{6,2},{8,12},{10,14},{12,8},{14,10},{1,5},{3,7},... | collective-permute-start | bytes 1216520 | tf_op jit(solution)/shard_map/rows_2/ppermute | solution.py:441
  8.8 2.6 %collective-permute-start.4 = (bf16[264,768]{1,0:T(8,128)(2,1)S(1)}, bf16[264,768]{1,0:T(8,128)(2,1)S(1)}, u32[]{:S(2)}, u32[]{:S(2)}) collective-permute-start(bf16[264,768]{1,0:T(8,128)(2,1)S(1)} %get-tuple-element.34.refs_3_), channel_id=1, source_target_pairs={{0,8},{2,10},{4,12},{6,14},{8,0},{10,2},{12,4},{14,6},{1,9},{3,11}... | collective-permute-start | bytes 1216520 | tf_op jit(solution)/shard_map/rows_2/ppermute | solution.py:441
  11.4 0.0 collective-permute-start
  11.4 5.2 %collective-permute-done.1.refs_2_.refs_3_ = bf16[264,768]{1,0:T(8,128)(2,1)S(1)} collective-permute-done((bf16[264,768]{1,0:T(8,128)(2,1)S(1)}, bf16[264,768]{1,0:T(8,128)(2,1)S(1)}, u32[]{:S(2)}, u32[]{:S(2)}) %collective-permute-start.1) | collective-permute-done | bytes 405536 | tf_op jit(solution)/shard_map/over_0/ppermute | solution.py:448
  16.6 0.0 collective-permute-start.2
  16.6 10.0 %collective-permute-done.3.refs_4_.refs_2_ = bf16[264,768]{1,0:T(8,128)(2,1)S(1)} collective-permute-done((bf16[264,768]{1,0:T(8,128)(2,1)S(1)}, bf16[264,768]{1,0:T(8,128)(2,1)S(1)}, u32[]{:S(2)}, u32[]{:S(2)}) %collective-permute-start.3) | collective-permute-done | bytes 405536 | tf_op jit(solution)/shard_map/rows_2/ppermute | solution.py:441
  26.7 0.0 collective-permute-start.5
  26.7 2.3 %collective-permute-done.4.refs_5_.refs_0_ = bf16[264,768]{1,0:T(8,128)(2,1)S(1)} collective-permute-done((bf16[264,768]{1,0:T(8,128)(2,1)S(1)}, bf16[264,768]{1,0:T(8,128)(2,1)S(1)}, u32[]{:S(2)}, u32[]{:S(2)}) %collective-permute-start.4) | collective-permute-done | bytes 405536 | tf_op jit(solution)/shard_map/rows_2/ppermute | solution.py:441
  29.0 2.5 %collective-permute-start.9 = (bf16[272,768]{1,0:T(8,128)(2,1)S(1)}, bf16[272,768]{1,0:T(8,128)(2,1)S(1)}, u32[]{:S(2)}, u32[]{:S(2)}) collective-permute-start(bf16[272,768]{1,0:T(8,128)(2,1)S(1)} %get-tuple-element.37.refs_8_), channel_id=1, source_target_pairs={{0,12},{2,14},{4,8},{6,10},{8,4},{10,6},{12,0},{14,2},{1,13},{3,15... | collective-permute-start | bytes 1253384 | tf_op jit(solution)/shard_map/rows_3/ppermute | solution.py:441
  31.6 0.0 collective-permute-start.6
  31.6 0.0 collective-permute-done.refs_1_
  31.6 0.5 collective-permute-start.7
  32.1 0.0 collective-permute-done.2.refs_3_
  32.1 0.0 collective-permute-start.10
  32.1 0.0 collective-permute-done.5.refs_6_
  32.1 1.6 %collective-permute-start.8 = (bf16[264,768]{1,0:T(8,128)(2,1)S(1)}, bf16[264,768]{1,0:T(8,128)(2,1)S(1)}, u32[]{:S(2)}, u32[]{:S(2)}) collective-permute-start(bf16[264,768]{1,0:T(8,128)(2,1)S(1)} %collective-permute-done.4.refs_5_.refs_0_), channel_id=1, source_target_pairs={{0,2},{2,0},{4,6},{6,4},{8,10},{10,8},{12,14},{14,12},{1,3},{3,1},... | collective-permute-start | bytes 1216520 | tf_op jit(solution)/shard_map/over_2/ppermute | solution.py:448
  33.7 0.0 collective-permute-done.6.refs_7_
  33.7 2.4 %meet.3 = (bf16[4096,768]{1,0:T(8,128)(2,1)S(1)}, f32[4096,128]{1,0:T(8,128)S(1)}, f32[4096,128]{1,0:T(8,128)S(1)}, f32[1,768]{1,0:T(1,128)S(1)}) custom-call(bf16[264,768]{1,0:T(8,128)(2,1)S(1)} %get-tuple-element.32.refs_0_.refs_1_, bf16[264,768]{1,0:T(8,128)(2,1)S(1)} %collective-permute-done.refs_1_, ...), custom_call_target="tpu_custom_call" | custom-call | tf_op jit(solution)/shard_map/meet/pallas_call | solution.py:334
  36.1 7.4 %collective-permute-done.9.refs_0_ = bf16[272,768]{1,0:T(8,128)(2,1)S(1)} collective-permute-done((bf16[272,768]{1,0:T(8,128)(2,1)S(1)}, bf16[272,768]{1,0:T(8,128)(2,1)S(1)}, u32[]{:S(2)}, u32[]{:S(2)}) %collective-permute-start.9) | collective-permute-done | bytes 417824 | tf_op jit(solution)/shard_map/rows_3/ppermute | solution.py:441
  43.6 0.1 pack.3
  43.6 0.7 collective-permute-start.15
  44.3 6.8 %collective-permute-start.16 = (bf16[272,768]{1,0:T(8,128)(2,1)S(1)}, bf16[272,768]{1,0:T(8,128)(2,1)S(1)}, u32[]{:S(2)}, u32[]{:S(2)}) collective-permute-start(bf16[272,768]{1,0:T(8,128)(2,1)S(1)} %get-tuple-element.47), channel_id=1, source_target_pairs={{0,4},{2,6},{4,0},{6,2},{8,12},{10,14},{12,8},{14,10},{1,5},{3,7},... | collective-permute-start | bytes 1253384 | tf_op jit(solution)/shard_map/passed_3/ppermute | solution.py:441
  51.2 0.0 collective-permute-done.7.refs_0_
  51.2 0.5 collective-permute-start.14
  51.7 0.0 collective-permute-done.10.refs_3_.refs_7_.refs_4_
  51.7 0.8 collective-permute-done.8.refs_1_
  52.5 0.0 collective-permute-start.11
  52.5 0.5 collective-permute-start.12
  53.0 1.2 %collective-permute-done.11.refs_2_ = bf16[264,768]{1,0:T(8,128)(2,1)S(1)} collective-permute-done((bf16[264,768]{1,0:T(8,128)(2,1)S(1)}, bf16[264,768]{1,0:T(8,128)(2,1)S(1)}, u32[]{:S(2)}, u32[]{:S(2)}) %collective-permute-start.11) | collective-permute-done | bytes 405536 | tf_op jit(solution)/shard_map/across_1/ppermute | solution.py:452
  54.2 0.1 collective-permute-start.13
  54.3 0.4 collective-permute-done.12.refs_3_
  54.8 4.3 %meet.4 = (bf16[4096,768]{1,0:T(8,128)(2,1)S(1)}, f32[4096,128]{1,0:T(8,128)S(1)}, f32[4096,128]{1,0:T(8,128)S(1)}, f32[1,1024]{1,0:T(1,128)S(1)}) custom-call(bf16[264,768]{1,0:T(8,128)(2,1)S(1)} %get-tuple-element.40.refs_0_, bf16[264,768]{1,0:T(8,128)(2,1)S(1)} %get-tuple-element.41.refs_1_, ...), custom_call_target="tpu_custom_call", output_to_operand_aliasing={{0}: (8, {}), {1}: (9, {}), {2}: (10, {})} | custom-call | tf_op jit(solution)/shard_map/meet/pallas_call | solution.py:334
  59.1 0.0 collective-permute-done.15.refs_2_.refs_7_
  59.1 0.0 collective-permute-done.16.refs_3_.refs_6_
  59.1 1.9 %collective-permute-done.14.refs_0_ = bf16[272,768]{1,0:T(8,128)(2,1)S(1)} collective-permute-done((bf16[272,768]{1,0:T(8,128)(2,1)S(1)}, bf16[272,768]{1,0:T(8,128)(2,1)S(1)}, u32[]{:S(2)}, u32[]{:S(2)}) %collective-permute-start.14) | collective-permute-done | bytes 417824 | tf_op jit(solution)/shard_map/over_3/ppermute | solution.py:448
  61.0 0.0 collective-permute-start.17
  61.0 0.0 collective-permute-done.13.refs_1_
  61.0 1.8 %collective-permute-done.17.refs_3_ = bf16[272,768]{1,0:T(8,128)(2,1)S(1)} collective-permute-done((bf16[272,768]{1,0:T(8,128)(2,1)S(1)}, bf16[272,768]{1,0:T(8,128)(2,1)S(1)}, u32[]{:S(2)}, u32[]{:S(2)}) %collective-permute-start.17) | collective-permute-done | bytes 417824 | tf_op jit(solution)/shard_map/across_3/ppermute | solution.py:452
  62.8 4.0 %meet.5 = (bf16[4096,768]{1,0:T(8,128)(2,1)S(1)}, f32[4096,128]{1,0:T(8,128)S(1)}, f32[4096,128]{1,0:T(8,128)S(1)}, f32[1,1280]{1,0:T(1,128)S(1)}, f32[1,4096]{1,0:T(1,128)S(1)}) custom-call(bf16[272,768]{1,0:T(8,128)(2,1)S(1)} %get-tuple-element.38.refs_2_.refs_6_.refs_0_, ...), custom_call_target="tpu_custom_call", output_to_operand_aliasing={{0}: (9, {}), {1}: (10, {}), {2}: (11, {})} | custom-call | tf_op jit(solution)/shard_map/meet/pallas_call | solution.py:334
  66.8 0.1 route.1
  66.9 10.1 %all_to_all.5.got_ref = f32[16,1,512]{2,1,0:T(1,128)S(1)} all-to-all(f32[16,1,512]{2,1,0:T(1,128)S(1)} %route.1), channel_id=1, replica_groups=mesh['groups'=2,'blk'=8,'split'=2] {'blk','split'}, dimensions={0} | all-to-all | bytes 65536 | tf_op jit(solution)/shard_map/all_to_all | solution.py:593
  76.9 1.3 %back.1 = f32[1,1024]{1,0:T(1,128)} custom-call(f32[16,1,512]{2,1,0:T(1,128)S(1)} %all_to_all.5.got_ref, s32[1,1024]{1,0:T(1,128)S(1)} %get-tuple-element.30.rank_ref), custom_call_target="tpu_custom_call" | custom-call | tf_op jit(solution)/shard_map/back/pallas_call | solution.py:420
  (4 shorter events, 0.1 us)
Async XLA Ops:
  4.2 12.4 %collective-permute-start.1 = (bf16[264,768]{1,0:T(8,128)(2,1)S(1)}, bf16[264,768]{1,0:T(8,128)(2,1)S(1)}, u32[]{:S(2)}, u32[]{:S(2)}) collective-permute-start(bf16[264,768]{1,0:T(8,128)(2,1)S(1)} %get-tuple-element.32.refs_0_.refs_1_), channel_id=1, source_target_pairs={{0,2},{2,0},{4,6},{6,4},{8,10},{10,8},{12,14},{14,12},{1,3},{3,1},... | collective-permute-start | bytes 1216520 | tf_op jit(solution)/shard_map/over_0/ppermute | solution.py:448
  7.3 19.4 %collective-permute-start.3 = (bf16[264,768]{1,0:T(8,128)(2,1)S(1)}, bf16[264,768]{1,0:T(8,128)(2,1)S(1)}, u32[]{:S(2)}, u32[]{:S(2)}) collective-permute-start(bf16[264,768]{1,0:T(8,128)(2,1)S(1)} %get-tuple-element.33.refs_5_), channel_id=1, source_target_pairs={{0,4},{2,6},{4,0},{6,2},{8,12},{10,14},{12,8},{14,10},{1,5},{3,7},... | collective-permute-start | bytes 1216520 | tf_op jit(solution)/shard_map/rows_2/ppermute | solution.py:441
  8.8 20.2 %collective-permute-start.4 = (bf16[264,768]{1,0:T(8,128)(2,1)S(1)}, bf16[264,768]{1,0:T(8,128)(2,1)S(1)}, u32[]{:S(2)}, u32[]{:S(2)}) collective-permute-start(bf16[264,768]{1,0:T(8,128)(2,1)S(1)} %get-tuple-element.34.refs_3_), channel_id=1, source_target_pairs={{0,8},{2,10},{4,12},{6,14},{8,0},{10,2},{12,4},{14,6},{1,9},{3,11}... | collective-permute-start | bytes 1216520 | tf_op jit(solution)/shard_map/rows_2/ppermute | solution.py:441
  11.4 20.2 %collective-permute-start = (bf16[264,768]{1,0:T(8,128)(2,1)S(1)}, bf16[264,768]{1,0:T(8,128)(2,1)S(1)}, u32[]{:S(2)}, u32[]{:S(2)}) collective-permute-start(bf16[264,768]{1,0:T(8,128)(2,1)S(1)} %get-tuple-element.32.refs_0_.refs_1_), channel_id=1, source_target_pairs={{0,1},{1,0},{2,3},{3,2},{4,5},{5,4},{6,7},{7,6},{8,9},{9,8},{10,11... | collective-permute-start | bytes 1216520 | tf_op jit(solution)/shard_map/beside_0/ppermute | solution.py:452
  16.6 15.5 %collective-permute-start.2 = (bf16[264,768]{1,0:T(8,128)(2,1)S(1)}, bf16[264,768]{1,0:T(8,128)(2,1)S(1)}, u32[]{:S(2)}, u32[]{:S(2)}) collective-permute-start(bf16[264,768]{1,0:T(8,128)(2,1)S(1)} %collective-permute-done.1.refs_2_.refs_3_), channel_id=1, source_target_pairs={{0,1},{1,0},{2,3},{3,2},{4,5},{5,4},{6,7},{7,6},{8,9},{9,8},{10,11... | collective-permute-start | bytes 1216520 | tf_op jit(solution)/shard_map/across_0/ppermute | solution.py:452
  26.7 5.4 %collective-permute-start.5 = (bf16[264,768]{1,0:T(8,128)(2,1)S(1)}, bf16[264,768]{1,0:T(8,128)(2,1)S(1)}, u32[]{:S(2)}, u32[]{:S(2)}) collective-permute-start(bf16[264,768]{1,0:T(8,128)(2,1)S(1)} %collective-permute-done.3.refs_4_.refs_2_), channel_id=1, source_target_pairs={{0,1},{1,0},{2,3},{3,2},{4,5},{5,4},{6,7},{7,6},{8,9},{9,8},{10,11... | collective-permute-start | bytes 1216520 | tf_op jit(solution)/shard_map/beside_1/ppermute | solution.py:452
  29.0 14.5 %collective-permute-start.9 = (bf16[272,768]{1,0:T(8,128)(2,1)S(1)}, bf16[272,768]{1,0:T(8,128)(2,1)S(1)}, u32[]{:S(2)}, u32[]{:S(2)}) collective-permute-start(bf16[272,768]{1,0:T(8,128)(2,1)S(1)} %get-tuple-element.37.refs_8_), channel_id=1, source_target_pairs={{0,12},{2,14},{4,8},{6,10},{8,4},{10,6},{12,0},{14,2},{1,13},{3,15... | collective-permute-start | bytes 1253384 | tf_op jit(solution)/shard_map/rows_3/ppermute | solution.py:441
  31.6 2.1 %collective-permute-start.6 = (bf16[264,768]{1,0:T(8,128)(2,1)S(1)}, bf16[264,768]{1,0:T(8,128)(2,1)S(1)}, u32[]{:S(2)}, u32[]{:S(2)}) collective-permute-start(bf16[264,768]{1,0:T(8,128)(2,1)S(1)} %collective-permute-done.4.refs_5_.refs_0_), channel_id=1, source_target_pairs={{0,1},{1,0},{2,3},{3,2},{4,5},{5,4},{6,7},{7,6},{8,9},{9,8},{10,11... | collective-permute-start | bytes 1216520 | tf_op jit(solution)/shard_map/beside_2/ppermute | solution.py:452
  31.6 19.6 %collective-permute-start.7 = (bf16[264,768]{1,0:T(8,128)(2,1)S(1)}, bf16[264,768]{1,0:T(8,128)(2,1)S(1)}, u32[]{:S(2)}, u32[]{:S(2)}) collective-permute-start(bf16[264,768]{1,0:T(8,128)(2,1)S(1)} %collective-permute-done.3.refs_4_.refs_2_), channel_id=1, source_target_pairs={{0,2},{2,0},{4,6},{6,4},{8,10},{10,8},{12,14},{14,12},{1,3},{3,1},... | collective-permute-start | bytes 1216520 | tf_op jit(solution)/shard_map/over_1/ppermute | solution.py:448
  32.1 19.6 %collective-permute-start.10 = (bf16[264,768]{1,0:T(8,128)(2,1)S(1)}, bf16[264,768]{1,0:T(8,128)(2,1)S(1)}, u32[]{:S(2)}, u32[]{:S(2)}) collective-permute-start(bf16[264,768]{1,0:T(8,128)(2,1)S(1)} %get-tuple-element.39), channel_id=1, source_target_pairs={{0,4},{2,6},{4,0},{6,2},{8,12},{10,14},{12,8},{14,10},{1,5},{3,7},... | collective-permute-start | bytes 1216520 | tf_op jit(solution)/shard_map/passed_2/ppermute | solution.py:441
  32.1 20.3 %collective-permute-start.8 = (bf16[264,768]{1,0:T(8,128)(2,1)S(1)}, bf16[264,768]{1,0:T(8,128)(2,1)S(1)}, u32[]{:S(2)}, u32[]{:S(2)}) collective-permute-start(bf16[264,768]{1,0:T(8,128)(2,1)S(1)} %collective-permute-done.4.refs_5_.refs_0_), channel_id=1, source_target_pairs={{0,2},{2,0},{4,6},{6,4},{8,10},{10,8},{12,14},{14,12},{1,3},{3,1},... | collective-permute-start | bytes 1216520 | tf_op jit(solution)/shard_map/over_2/ppermute | solution.py:448
  43.6 15.5 %collective-permute-start.15 = (bf16[272,768]{1,0:T(8,128)(2,1)S(1)}, bf16[272,768]{1,0:T(8,128)(2,1)S(1)}, u32[]{:S(2)}, u32[]{:S(2)}) collective-permute-start(bf16[272,768]{1,0:T(8,128)(2,1)S(1)} %get-tuple-element.46), channel_id=1, source_target_pairs={{4,8},{6,10},{8,4},{10,6},{5,9},{7,11},{9,5},{11,7},{20,24},{22,26... | collective-permute-start | bytes 1253384 | tf_op jit(solution)/shard_map/border/ppermute | solution.py:441
  44.3 14.8 %collective-permute-start.16 = (bf16[272,768]{1,0:T(8,128)(2,1)S(1)}, bf16[272,768]{1,0:T(8,128)(2,1)S(1)}, u32[]{:S(2)}, u32[]{:S(2)}) collective-permute-start(bf16[272,768]{1,0:T(8,128)(2,1)S(1)} %get-tuple-element.47), channel_id=1, source_target_pairs={{0,4},{2,6},{4,0},{6,2},{8,12},{10,14},{12,8},{14,10},{1,5},{3,7},... | collective-permute-start | bytes 1253384 | tf_op jit(solution)/shard_map/passed_3/ppermute | solution.py:441
  51.2 9.9 %collective-permute-start.14 = (bf16[272,768]{1,0:T(8,128)(2,1)S(1)}, bf16[272,768]{1,0:T(8,128)(2,1)S(1)}, u32[]{:S(2)}, u32[]{:S(2)}) collective-permute-start(bf16[272,768]{1,0:T(8,128)(2,1)S(1)} %get-tuple-element.38.refs_2_.refs_6_.refs_0_), channel_id=1, source_target_pairs={{0,2},{2,0},{4,6},{6,4},{8,10},{10,8},{12,14},{14,12},{1,3},{3,1},... | collective-permute-start | bytes 1253384 | tf_op jit(solution)/shard_map/over_3/ppermute | solution.py:448
  52.5 1.7 %collective-permute-start.11 = (bf16[264,768]{1,0:T(8,128)(2,1)S(1)}, bf16[264,768]{1,0:T(8,128)(2,1)S(1)}, u32[]{:S(2)}, u32[]{:S(2)}) collective-permute-start(bf16[264,768]{1,0:T(8,128)(2,1)S(1)} %get-tuple-element.40.refs_0_), channel_id=1, source_target_pairs={{0,1},{1,0},{2,3},{3,2},{4,5},{5,4},{6,7},{7,6},{8,9},{9,8},{10,11... | collective-permute-start | bytes 1216520 | tf_op jit(solution)/shard_map/across_1/ppermute | solution.py:452
  52.5 2.3 %collective-permute-start.12 = (bf16[264,768]{1,0:T(8,128)(2,1)S(1)}, bf16[264,768]{1,0:T(8,128)(2,1)S(1)}, u32[]{:S(2)}, u32[]{:S(2)}) collective-permute-start(bf16[264,768]{1,0:T(8,128)(2,1)S(1)} %get-tuple-element.41.refs_1_), channel_id=1, source_target_pairs={{0,1},{1,0},{2,3},{3,2},{4,5},{5,4},{6,7},{7,6},{8,9},{9,8},{10,11... | collective-permute-start | bytes 1216520 | tf_op jit(solution)/shard_map/across_2/ppermute | solution.py:452
  54.2 6.8 %collective-permute-start.13 = (bf16[272,768]{1,0:T(8,128)(2,1)S(1)}, bf16[272,768]{1,0:T(8,128)(2,1)S(1)}, u32[]{:S(2)}, u32[]{:S(2)}) collective-permute-start(bf16[272,768]{1,0:T(8,128)(2,1)S(1)} %get-tuple-element.38.refs_2_.refs_6_.refs_0_), channel_id=1, source_target_pairs={{0,1},{1,0},{2,3},{3,2},{4,5},{5,4},{6,7},{7,6},{8,9},{9,8},{10,11... | collective-permute-start | bytes 1253384 | tf_op jit(solution)/shard_map/beside_3/ppermute | solution.py:452
  61.0 1.8 %collective-permute-start.17 = (bf16[272,768]{1,0:T(8,128)(2,1)S(1)}, bf16[272,768]{1,0:T(8,128)(2,1)S(1)}, u32[]{:S(2)}, u32[]{:S(2)}) collective-permute-start(bf16[272,768]{1,0:T(8,128)(2,1)S(1)} %after.3.refs_2_), channel_id=1, source_target_pairs={{0,1},{1,0},{2,3},{3,2},{4,5},{5,4},{6,7},{7,6},{8,9},{9,8},{10,11... | collective-permute-start | bytes 1253384 | tf_op jit(solution)/shard_map/across_3/ppermute | solution.py:452

commit v9 on v8

--- a/solution.py
+++ b/solution.py
@@ -209,9 +209,8 @@
         return jnp.min(low), jnp.max(high)
 
     def span_left(sections):
-        at, rows = table[sections[0]][0], sum(table[l][1] for l in sections)
-        ids = left_ids[at : at + rows, :TAGS]
-        return jnp.min(ids), jnp.max(ids)
+        lows, highs = zip(*[section_span[l] for l in sections])
+        return functools.reduce(jnp.minimum, lows), functools.reduce(jnp.maximum, highs)
 
     if first:
         left_best[...] = jnp.full(left_best.shape, FILL, jnp.float32)
@@ -225,6 +224,11 @@
 
     tested = [(r, l) for r, l, _, test in pairs if test]
     right_span = {r: span_right(rights[r[0]]) for r in sorted({r for r, _ in tested})}
+    section_span = {}
+    for l in sorted({i for _, group in tested for i in group}):
+        at, rows = table[l]
+        ids = left_ids[at : at + rows, :TAGS]
+        section_span[l] = jnp.min(ids), jnp.max(ids)
     left_span = {l: span_left(l) for l in sorted({l for _, l in tested})}
     wanted = {(r, l): overlap(right_span[r], left_span[l]) for r, l in tested}
 
@@ -479,7 +483,7 @@
         return near_rows, far_rows
 
     tag_rows = [TAGS if k < middle else 2 * TAGS for k in range(parts)]
-    sent, rank = in_order(embeddings, cluster_of, target_pos, tag_rows, chips, second)
+    sent, rank = in_order(embeddings, cluster_of, target_pos, tag_rows, chips, [*second, *third])
     own_0 = sent[0]
     got = [swap(sent[k], k, "rows_2") for k in second]
     over_0 = chip_swap(own_0, "over_0")

time: 79 us -> 79.8 us (1.010); the launches traced: 78.2 us -> 80.3 us
  blocking collectives: 10.1 us -> 12.4 us
    all_to_all x1, blocking collectives: 10.1 us -> 12.4 us  [body(): lax.all_to_all(found, ('blk', 'split'), split_axis=0, concat_axis=0, tile...]
  transfers between devices with their start and end apart: 18 -> 18, of which waited for: 9 -> 9; matrix products, arithmetic and copies ran while one was open for 0% -> 0% of each run, Pallas kernels for 9% -> 8%
where the time goes in v9:
time: 79.8 us; the launch traced here: 80.3 us
  waiting for transfers between devices  31.2 us (39%)
  starting transfers between devices  20.5 us (26%)
  Pallas kernels  16.1 us (20%)
  blocking collectives  12.4 us (16%)
    ppermute x6, waiting for transfers between devices, between(): return lax.ppermute(array, 'blk', route)  19.8 us
    ppermute x6, starting transfers between devices, between(): return lax.ppermute(array, 'blk', route)  14.2 us
    all_to_all x1, blocking collectives, body(): lax.all_to_all(found, ('blk', 'split'), split_axis=0, concat_axis=0, tile...  12.4 us
    pallas_call x3, Pallas kernels, meet(): pl.pallas_call(kernel, out_shape=outs, in_specs=[WHOLE] * (inputs + len(s...  10.4 us
    ppermute x4, waiting for transfers between devices, chip_swap(): return lax.ppermute(array, 'blk', [(b, b ^ 1) for b in range(blocks)])  8.01 us
    ppermute x4, starting transfers between devices, chip_swap(): return lax.ppermute(array, 'blk', [(b, b ^ 1) for b in range(blocks)])  5.66 us
    pallas_call x1, Pallas kernels, in_order(): pl.pallas_call(functools.partial(order_kernel, soon, chips, parts), out_s...  3.45 us
    ppermute x8, waiting for transfers between devices, core_swap(): return lax.ppermute(array, 'split', [(c, c ^ 1) for c in range(cores)])  3.44 us
  transfers between devices with their start and end apart: 18, of which 9 were waited for; matrix products, arithmetic and copies ran while one was open for 0% of the time, Pallas kernels for 8%

profile of v9, /device:TPU:0, one launch (start us, length us, event | category | flops | bytes accessed | tf_op | source)
XLA Modules:
  0.0 80.3 jit_solution(17280932650858582707)
XLA Ops:
  0.0 3.4 %order.1 = (bf16[264,768]{1,0:T(8,128)(2,1)S(1)}, bf16[264,768]{1,0:T(8,128)(2,1)S(1)}, bf16[272,768]{1,0:T(8,128)(2,1)S(1)}, bf16[1024,768]{1,0:T(8,128)(2,1)S(...) custom-call(bf16[1024,768]{1,0:T(8,128)(2,1)} %rows_hbm.1, s32[1,1024]{1,0:T(1,128)} %bitcast.3, s32[1,1024]{1,0:T(1,128)} %bitcast.4), custom_call_target="tpu_custom_call" | custom-call | tf_op jit(solution)/shard_map/order/pallas_call | solution.py:104
  3.5 0.7 rest.1.refs_0_.refs_1_
  4.2 3.0 %collective-permute-start.1 = (bf16[264,768]{1,0:T(8,128)(2,1)S(1)}, bf16[264,768]{1,0:T(8,128)(2,1)S(1)}, u32[]{:S(2)}, u32[]{:S(2)}) collective-permute-start(bf16[264,768]{1,0:T(8,128)(2,1)S(1)} %rest.1.refs_0_.refs_1_), channel_id=1, source_target_pairs={{0,2},{2,0},{4,6},{6,4},{8,10},{10,8},{12,14},{14,12},{1,3},{3,1},... | collective-permute-start | bytes 1216520 | tf_op jit(solution)/shard_map/over_0/ppermute | solution.py:452
  7.2 1.6 %collective-permute-start.3 = (bf16[264,768]{1,0:T(8,128)(2,1)S(1)}, bf16[264,768]{1,0:T(8,128)(2,1)S(1)}, u32[]{:S(2)}, u32[]{:S(2)}) collective-permute-start(bf16[264,768]{1,0:T(8,128)(2,1)S(1)} %get-tuple-element.31.refs_5_), channel_id=1, source_target_pairs={{0,4},{2,6},{4,0},{6,2},{8,12},{10,14},{12,8},{14,10},{1,5},{3,7},... | collective-permute-start | bytes 1216520 | tf_op jit(solution)/shard_map/rows_2/ppermute | solution.py:445
  8.8 2.6 %collective-permute-start.4 = (bf16[264,768]{1,0:T(8,128)(2,1)S(1)}, bf16[264,768]{1,0:T(8,128)(2,1)S(1)}, u32[]{:S(2)}, u32[]{:S(2)}) collective-permute-start(bf16[264,768]{1,0:T(8,128)(2,1)S(1)} %get-tuple-element.32.refs_3_), channel_id=1, source_target_pairs={{0,8},{2,10},{4,12},{6,14},{8,0},{10,2},{12,4},{14,6},{1,9},{3,11}... | collective-permute-start | bytes 1216520 | tf_op jit(solution)/shard_map/rows_2/ppermute | solution.py:445
  11.4 0.0 collective-permute-start
  11.4 5.2 %collective-permute-done.1.refs_2_.refs_3_ = bf16[264,768]{1,0:T(8,128)(2,1)S(1)} collective-permute-done((bf16[264,768]{1,0:T(8,128)(2,1)S(1)}, bf16[264,768]{1,0:T(8,128)(2,1)S(1)}, u32[]{:S(2)}, u32[]{:S(2)}) %collective-permute-start.1) | collective-permute-done | bytes 405536 | tf_op jit(solution)/shard_map/over_0/ppermute | solution.py:452
  16.6 0.0 collective-permute-start.2
  16.6 10.0 %collective-permute-done.3.refs_4_.refs_2_ = bf16[264,768]{1,0:T(8,128)(2,1)S(1)} collective-permute-done((bf16[264,768]{1,0:T(8,128)(2,1)S(1)}, bf16[264,768]{1,0:T(8,128)(2,1)S(1)}, u32[]{:S(2)}, u32[]{:S(2)}) %collective-permute-start.3) | collective-permute-done | bytes 405536 | tf_op jit(solution)/shard_map/rows_2/ppermute | solution.py:445
  26.6 0.0 collective-permute-start.5
  26.6 2.3 %collective-permute-done.4.refs_5_.refs_0_ = bf16[264,768]{1,0:T(8,128)(2,1)S(1)} collective-permute-done((bf16[264,768]{1,0:T(8,128)(2,1)S(1)}, bf16[264,768]{1,0:T(8,128)(2,1)S(1)}, u32[]{:S(2)}, u32[]{:S(2)}) %collective-permute-start.4) | collective-permute-done | bytes 405536 | tf_op jit(solution)/shard_map/rows_2/ppermute | solution.py:445
  29.0 2.5 %collective-permute-start.9 = (bf16[272,768]{1,0:T(8,128)(2,1)S(1)}, bf16[272,768]{1,0:T(8,128)(2,1)S(1)}, u32[]{:S(2)}, u32[]{:S(2)}) collective-permute-start(bf16[272,768]{1,0:T(8,128)(2,1)S(1)} %get-tuple-element.35.refs_8_), channel_id=1, source_target_pairs={{0,12},{2,14},{4,8},{6,10},{8,4},{10,6},{12,0},{14,2},{1,13},{3,15... | collective-permute-start | bytes 1253384 | tf_op jit(solution)/shard_map/rows_3/ppermute | solution.py:445
  31.5 0.0 collective-permute-start.6
  31.5 0.0 collective-permute-done.refs_1_
  31.5 0.5 collective-permute-start.7
  32.1 0.0 collective-permute-done.2.refs_3_
  32.1 0.0 collective-permute-start.10
  32.1 0.0 collective-permute-done.5.refs_6_
  32.1 1.6 %collective-permute-start.8 = (bf16[264,768]{1,0:T(8,128)(2,1)S(1)}, bf16[264,768]{1,0:T(8,128)(2,1)S(1)}, u32[]{:S(2)}, u32[]{:S(2)}) collective-permute-start(bf16[264,768]{1,0:T(8,128)(2,1)S(1)} %collective-permute-done.4.refs_5_.refs_0_), channel_id=1, source_target_pairs={{0,2},{2,0},{4,6},{6,4},{8,10},{10,8},{12,14},{14,12},{1,3},{3,1},... | collective-permute-start | bytes 1216520 | tf_op jit(solution)/shard_map/over_2/ppermute | solution.py:452
  33.6 0.0 collective-permute-done.6.refs_7_
  33.6 2.4 %meet.3 = (bf16[4096,768]{1,0:T(8,128)(2,1)S(1)}, f32[4096,128]{1,0:T(8,128)S(1)}, f32[4096,128]{1,0:T(8,128)S(1)}, f32[1,768]{1,0:T(1,128)S(1)}) custom-call(bf16[264,768]{1,0:T(8,128)(2,1)S(1)} %rest.1.refs_0_.refs_1_, bf16[264,768]{1,0:T(8,128)(2,1)S(1)} %collective-permute-done.refs_1_, bf16[264,768]{1,0:T(8,128)(2,1)S(1)} %collective-permute-done.1.refs_2_.refs_3_, ...), custom_call_target="tpu_custom_call" | custom-call | tf_op jit(solution)/shard_map/meet/pallas_call | solution.py:338
  36.1 7.4 %collective-permute-done.9.refs_0_ = bf16[272,768]{1,0:T(8,128)(2,1)S(1)} collective-permute-done((bf16[272,768]{1,0:T(8,128)(2,1)S(1)}, bf16[272,768]{1,0:T(8,128)(2,1)S(1)}, u32[]{:S(2)}, u32[]{:S(2)}) %collective-permute-start.9) | collective-permute-done | bytes 417824 | tf_op jit(solution)/shard_map/rows_3/ppermute | solution.py:445
  43.5 0.1 pack.3
  43.6 0.7 collective-permute-start.15
  44.3 6.8 %collective-permute-start.16 = (bf16[272,768]{1,0:T(8,128)(2,1)S(1)}, bf16[272,768]{1,0:T(8,128)(2,1)S(1)}, u32[]{:S(2)}, u32[]{:S(2)}) collective-permute-start(bf16[272,768]{1,0:T(8,128)(2,1)S(1)} %get-tuple-element.45), channel_id=1, source_target_pairs={{0,4},{2,6},{4,0},{6,2},{8,12},{10,14},{12,8},{14,10},{1,5},{3,7},... | collective-permute-start | bytes 1253384 | tf_op jit(solution)/shard_map/passed_3/ppermute | solution.py:445
  51.1 0.0 collective-permute-done.7.refs_0_
  51.1 0.5 collective-permute-start.14
  51.6 0.0 collective-permute-done.10.refs_3_.refs_7_.refs_4_
  51.6 0.8 collective-permute-done.8.refs_1_
  52.4 0.0 collective-permute-start.11
  52.4 0.5 collective-permute-start.12
  52.9 1.2 %collective-permute-done.11.refs_2_ = bf16[264,768]{1,0:T(8,128)(2,1)S(1)} collective-permute-done((bf16[264,768]{1,0:T(8,128)(2,1)S(1)}, bf16[264,768]{1,0:T(8,128)(2,1)S(1)}, u32[]{:S(2)}, u32[]{:S(2)}) %collective-permute-start.11) | collective-permute-done | bytes 405536 | tf_op jit(solution)/shard_map/across_1/ppermute | solution.py:456
  54.1 0.1 collective-permute-start.13
  54.3 0.4 collective-permute-done.12.refs_3_
  54.7 4.2 %meet.4 = (bf16[4096,768]{1,0:T(8,128)(2,1)S(1)}, f32[4096,128]{1,0:T(8,128)S(1)}, f32[4096,128]{1,0:T(8,128)S(1)}, f32[1,1024]{1,0:T(1,128)S(1)}) custom-call(bf16[264,768]{1,0:T(8,128)(2,1)S(1)} %get-tuple-element.38.refs_0_, bf16[264,768]{1,0:T(8,128)(2,1)S(1)} %get-tuple-element.39.refs_1_, ...), custom_call_target="tpu_custom_call", output_to_operand_aliasing={{0}: (8, {}), {1}: (9, {}), {2}: (10, {})} | custom-call | tf_op jit(solution)/shard_map/meet/pallas_call | solution.py:338
  58.9 0.0 collective-permute-done.15.refs_2_.refs_7_
  58.9 0.0 collective-permute-done.16.refs_3_.refs_6_
  58.9 2.0 %collective-permute-done.14.refs_0_ = bf16[272,768]{1,0:T(8,128)(2,1)S(1)} collective-permute-done((bf16[272,768]{1,0:T(8,128)(2,1)S(1)}, bf16[272,768]{1,0:T(8,128)(2,1)S(1)}, u32[]{:S(2)}, u32[]{:S(2)}) %collective-permute-start.14) | collective-permute-done | bytes 417824 | tf_op jit(solution)/shard_map/over_3/ppermute | solution.py:452
  61.0 0.0 collective-permute-start.17
  61.0 0.0 collective-permute-done.13.refs_1_
  61.0 1.8 %collective-permute-done.17.refs_3_ = bf16[272,768]{1,0:T(8,128)(2,1)S(1)} collective-permute-done((bf16[272,768]{1,0:T(8,128)(2,1)S(1)}, bf16[272,768]{1,0:T(8,128)(2,1)S(1)}, u32[]{:S(2)}, u32[]{:S(2)}) %collective-permute-start.17) | collective-permute-done | bytes 417824 | tf_op jit(solution)/shard_map/across_3/ppermute | solution.py:456
  62.7 3.8 %meet.5 = (bf16[4096,768]{1,0:T(8,128)(2,1)S(1)}, f32[4096,128]{1,0:T(8,128)S(1)}, f32[4096,128]{1,0:T(8,128)S(1)}, f32[1,1280]{1,0:T(1,128)S(1)}, f32[1,4096]{1,0:T(1,128)S(1)}) custom-call(bf16[272,768]{1,0:T(8,128)(2,1)S(1)} %get-tuple-element.36.refs_2_.refs_6_.refs_0_, ...), custom_call_target="tpu_custom_call", output_to_operand_aliasing={{0}: (9, {}), {1}: (10, {}), {2}: (11, {})} | custom-call | tf_op jit(solution)/shard_map/meet/pallas_call | solution.py:338
  66.5 0.1 route.1
  66.6 12.4 %all_to_all.5.got_ref = f32[16,1,512]{2,1,0:T(1,128)S(1)} all-to-all(f32[16,1,512]{2,1,0:T(1,128)S(1)} %route.1), channel_id=1, replica_groups=mesh['groups'=2,'blk'=8,'split'=2] {'blk','split'}, dimensions={0} | all-to-all | bytes 65536 | tf_op jit(solution)/shard_map/all_to_all | solution.py:597
  79.0 1.3 %back.1 = f32[1,1024]{1,0:T(1,128)} custom-call(f32[16,1,512]{2,1,0:T(1,128)S(1)} %all_to_all.5.got_ref, s32[1,1024]{1,0:T(1,128)S(1)} %get-tuple-element.29.rank_ref), custom_call_target="tpu_custom_call" | custom-call | tf_op jit(solution)/shard_map/back/pallas_call | solution.py:424
  (4 shorter events, 0.1 us)
Async XLA Ops:
  4.2 12.4 %collective-permute-start.1 = (bf16[264,768]{1,0:T(8,128)(2,1)S(1)}, bf16[264,768]{1,0:T(8,128)(2,1)S(1)}, u32[]{:S(2)}, u32[]{:S(2)}) collective-permute-start(bf16[264,768]{1,0:T(8,128)(2,1)S(1)} %rest.1.refs_0_.refs_1_), channel_id=1, source_target_pairs={{0,2},{2,0},{4,6},{6,4},{8,10},{10,8},{12,14},{14,12},{1,3},{3,1},... | collective-permute-start | bytes 1216520 | tf_op jit(solution)/shard_map/over_0/ppermute | solution.py:452
  7.2 19.4 %collective-permute-start.3 = (bf16[264,768]{1,0:T(8,128)(2,1)S(1)}, bf16[264,768]{1,0:T(8,128)(2,1)S(1)}, u32[]{:S(2)}, u32[]{:S(2)}) collective-permute-start(bf16[264,768]{1,0:T(8,128)(2,1)S(1)} %get-tuple-element.31.refs_5_), channel_id=1, source_target_pairs={{0,4},{2,6},{4,0},{6,2},{8,12},{10,14},{12,8},{14,10},{1,5},{3,7},... | collective-permute-start | bytes 1216520 | tf_op jit(solution)/shard_map/rows_2/ppermute | solution.py:445
  8.8 20.2 %collective-permute-start.4 = (bf16[264,768]{1,0:T(8,128)(2,1)S(1)}, bf16[264,768]{1,0:T(8,128)(2,1)S(1)}, u32[]{:S(2)}, u32[]{:S(2)}) collective-permute-start(bf16[264,768]{1,0:T(8,128)(2,1)S(1)} %get-tuple-element.32.refs_3_), channel_id=1, source_target_pairs={{0,8},{2,10},{4,12},{6,14},{8,0},{10,2},{12,4},{14,6},{1,9},{3,11}... | collective-permute-start | bytes 1216520 | tf_op jit(solution)/shard_map/rows_2/ppermute | solution.py:445
  11.4 20.2 %collective-permute-start = (bf16[264,768]{1,0:T(8,128)(2,1)S(1)}, bf16[264,768]{1,0:T(8,128)(2,1)S(1)}, u32[]{:S(2)}, u32[]{:S(2)}) collective-permute-start(bf16[264,768]{1,0:T(8,128)(2,1)S(1)} %rest.1.refs_0_.refs_1_), channel_id=1, source_target_pairs={{0,1},{1,0},{2,3},{3,2},{4,5},{5,4},{6,7},{7,6},{8,9},{9,8},{10,11... | collective-permute-start | bytes 1216520 | tf_op jit(solution)/shard_map/beside_0/ppermute | solution.py:456
  16.6 15.5 %collective-permute-start.2 = (bf16[264,768]{1,0:T(8,128)(2,1)S(1)}, bf16[264,768]{1,0:T(8,128)(2,1)S(1)}, u32[]{:S(2)}, u32[]{:S(2)}) collective-permute-start(bf16[264,768]{1,0:T(8,128)(2,1)S(1)} %collective-permute-done.1.refs_2_.refs_3_), channel_id=1, source_target_pairs={{0,1},{1,0},{2,3},{3,2},{4,5},{5,4},{6,7},{7,6},{8,9},{9,8},{10,11... | collective-permute-start | bytes 1216520 | tf_op jit(solution)/shard_map/across_0/ppermute | solution.py:456
  26.6 5.4 %collective-permute-start.5 = (bf16[264,768]{1,0:T(8,128)(2,1)S(1)}, bf16[264,768]{1,0:T(8,128)(2,1)S(1)}, u32[]{:S(2)}, u32[]{:S(2)}) collective-permute-start(bf16[264,768]{1,0:T(8,128)(2,1)S(1)} %collective-permute-done.3.refs_4_.refs_2_), channel_id=1, source_target_pairs={{0,1},{1,0},{2,3},{3,2},{4,5},{5,4},{6,7},{7,6},{8,9},{9,8},{10,11... | collective-permute-start | bytes 1216520 | tf_op jit(solution)/shard_map/beside_1/ppermute | solution.py:456
  29.0 14.5 %collective-permute-start.9 = (bf16[272,768]{1,0:T(8,128)(2,1)S(1)}, bf16[272,768]{1,0:T(8,128)(2,1)S(1)}, u32[]{:S(2)}, u32[]{:S(2)}) collective-permute-start(bf16[272,768]{1,0:T(8,128)(2,1)S(1)} %get-tuple-element.35.refs_8_), channel_id=1, source_target_pairs={{0,12},{2,14},{4,8},{6,10},{8,4},{10,6},{12,0},{14,2},{1,13},{3,15... | collective-permute-start | bytes 1253384 | tf_op jit(solution)/shard_map/rows_3/ppermute | solution.py:445
  31.5 2.1 %collective-permute-start.6 = (bf16[264,768]{1,0:T(8,128)(2,1)S(1)}, bf16[264,768]{1,0:T(8,128)(2,1)S(1)}, u32[]{:S(2)}, u32[]{:S(2)}) collective-permute-start(bf16[264,768]{1,0:T(8,128)(2,1)S(1)} %collective-permute-done.4.refs_5_.refs_0_), channel_id=1, source_target_pairs={{0,1},{1,0},{2,3},{3,2},{4,5},{5,4},{6,7},{7,6},{8,9},{9,8},{10,11... | collective-permute-start | bytes 1216520 | tf_op jit(solution)/shard_map/beside_2/ppermute | solution.py:456
  31.5 19.6 %collective-permute-start.7 = (bf16[264,768]{1,0:T(8,128)(2,1)S(1)}, bf16[264,768]{1,0:T(8,128)(2,1)S(1)}, u32[]{:S(2)}, u32[]{:S(2)}) collective-permute-start(bf16[264,768]{1,0:T(8,128)(2,1)S(1)} %collective-permute-done.3.refs_4_.refs_2_), channel_id=1, source_target_pairs={{0,2},{2,0},{4,6},{6,4},{8,10},{10,8},{12,14},{14,12},{1,3},{3,1},... | collective-permute-start | bytes 1216520 | tf_op jit(solution)/shard_map/over_1/ppermute | solution.py:452
  32.1 19.6 %collective-permute-start.10 = (bf16[264,768]{1,0:T(8,128)(2,1)S(1)}, bf16[264,768]{1,0:T(8,128)(2,1)S(1)}, u32[]{:S(2)}, u32[]{:S(2)}) collective-permute-start(bf16[264,768]{1,0:T(8,128)(2,1)S(1)} %get-tuple-element.37), channel_id=1, source_target_pairs={{0,4},{2,6},{4,0},{6,2},{8,12},{10,14},{12,8},{14,10},{1,5},{3,7},... | collective-permute-start | bytes 1216520 | tf_op jit(solution)/shard_map/passed_2/ppermute | solution.py:445
  32.1 20.3 %collective-permute-start.8 = (bf16[264,768]{1,0:T(8,128)(2,1)S(1)}, bf16[264,768]{1,0:T(8,128)(2,1)S(1)}, u32[]{:S(2)}, u32[]{:S(2)}) collective-permute-start(bf16[264,768]{1,0:T(8,128)(2,1)S(1)} %collective-permute-done.4.refs_5_.refs_0_), channel_id=1, source_target_pairs={{0,2},{2,0},{4,6},{6,4},{8,10},{10,8},{12,14},{14,12},{1,3},{3,1},... | collective-permute-start | bytes 1216520 | tf_op jit(solution)/shard_map/over_2/ppermute | solution.py:452
  43.6 15.4 %collective-permute-start.15 = (bf16[272,768]{1,0:T(8,128)(2,1)S(1)}, bf16[272,768]{1,0:T(8,128)(2,1)S(1)}, u32[]{:S(2)}, u32[]{:S(2)}) collective-permute-start(bf16[272,768]{1,0:T(8,128)(2,1)S(1)} %get-tuple-element.44), channel_id=1, source_target_pairs={{4,8},{6,10},{8,4},{10,6},{5,9},{7,11},{9,5},{11,7},{20,24},{22,26... | collective-permute-start | bytes 1253384 | tf_op jit(solution)/shard_map/border/ppermute | solution.py:445
  44.3 14.7 %collective-permute-start.16 = (bf16[272,768]{1,0:T(8,128)(2,1)S(1)}, bf16[272,768]{1,0:T(8,128)(2,1)S(1)}, u32[]{:S(2)}, u32[]{:S(2)}) collective-permute-start(bf16[272,768]{1,0:T(8,128)(2,1)S(1)} %get-tuple-element.45), channel_id=1, source_target_pairs={{0,4},{2,6},{4,0},{6,2},{8,12},{10,14},{12,8},{14,10},{1,5},{3,7},... | collective-permute-start | bytes 1253384 | tf_op jit(solution)/shard_map/passed_3/ppermute | solution.py:445
  51.1 9.9 %collective-permute-start.14 = (bf16[272,768]{1,0:T(8,128)(2,1)S(1)}, bf16[272,768]{1,0:T(8,128)(2,1)S(1)}, u32[]{:S(2)}, u32[]{:S(2)}) collective-permute-start(bf16[272,768]{1,0:T(8,128)(2,1)S(1)} %get-tuple-element.36.refs_2_.refs_6_.refs_0_), channel_id=1, source_target_pairs={{0,2},{2,0},{4,6},{6,4},{8,10},{10,8},{12,14},{14,12},{1,3},{3,1},... | collective-permute-start | bytes 1253384 | tf_op jit(solution)/shard_map/over_3/ppermute | solution.py:452
  52.4 1.7 %collective-permute-start.11 = (bf16[264,768]{1,0:T(8,128)(2,1)S(1)}, bf16[264,768]{1,0:T(8,128)(2,1)S(1)}, u32[]{:S(2)}, u32[]{:S(2)}) collective-permute-start(bf16[264,768]{1,0:T(8,128)(2,1)S(1)} %get-tuple-element.38.refs_0_), channel_id=1, source_target_pairs={{0,1},{1,0},{2,3},{3,2},{4,5},{5,4},{6,7},{7,6},{8,9},{9,8},{10,11... | collective-permute-start | bytes 1216520 | tf_op jit(solution)/shard_map/across_1/ppermute | solution.py:456
  52.4 2.3 %collective-permute-start.12 = (bf16[264,768]{1,0:T(8,128)(2,1)S(1)}, bf16[264,768]{1,0:T(8,128)(2,1)S(1)}, u32[]{:S(2)}, u32[]{:S(2)}) collective-permute-start(bf16[264,768]{1,0:T(8,128)(2,1)S(1)} %get-tuple-element.39.refs_1_), channel_id=1, source_target_pairs={{0,1},{1,0},{2,3},{3,2},{4,5},{5,4},{6,7},{7,6},{8,9},{9,8},{10,11... | collective-permute-start | bytes 1216520 | tf_op jit(solution)/shard_map/across_2/ppermute | solution.py:456
  54.1 6.8 %collective-permute-start.13 = (bf16[272,768]{1,0:T(8,128)(2,1)S(1)}, bf16[272,768]{1,0:T(8,128)(2,1)S(1)}, u32[]{:S(2)}, u32[]{:S(2)}) collective-permute-start(bf16[272,768]{1,0:T(8,128)(2,1)S(1)} %get-tuple-element.36.refs_2_.refs_6_.refs_0_), channel_id=1, source_target_pairs={{0,1},{1,0},{2,3},{3,2},{4,5},{5,4},{6,7},{7,6},{8,9},{9,8},{10,11... | collective-permute-start | bytes 1253384 | tf_op jit(solution)/shard_map/beside_3/ppermute | solution.py:456
  61.0 1.8 %collective-permute-start.17 = (bf16[272,768]{1,0:T(8,128)(2,1)S(1)}, bf16[272,768]{1,0:T(8,128)(2,1)S(1)}, u32[]{:S(2)}, u32[]{:S(2)}) collective-permute-start(bf16[272,768]{1,0:T(8,128)(2,1)S(1)} %after.3.refs_2_), channel_id=1, source_target_pairs={{0,1},{1,0},{2,3},{3,2},{4,5},{5,4},{6,7},{7,6},{8,9},{9,8},{10,11... | collective-permute-start | bytes 1253384 | tf_op jit(solution)/shard_map/across_3/ppermute | solution.py:456

commit v10 on v9

--- a/solution.py
+++ b/solution.py
@@ -265,7 +265,7 @@
         across = slice(lane, lane + lanes)
 
         def turn(index, _):
-            at = pl.multiple_of(row + index * step, 16)
+            at = row if rows == step else pl.multiple_of(row + index * step, 16)
             down = pl.ds(at, step)
             scores = lax.dot_general(
                 left[down, :],
@@ -284,7 +284,10 @@
             right_best[:, across] = jnp.maximum(right_best[:, across], column_fold(scores))
             return 0
 
-        lax.fori_loop(0, rows // step, turn, 0)
+        if rows == step:
+            turn(0, 0)
+        else:
+            lax.fori_loop(0, rows // step, turn, 0)
 
     for r, l, same, test in pairs:
         run = functools.partial(score, r, l, same)

time: 79.8 us -> 79.1 us (level); the launches traced: 80.3 us -> 78.1 us
  blocking collectives: 12.4 us -> 9.21 us
  Pallas kernels: 16.1 us -> 17.8 us
  waiting for transfers between devices: 31.2 us -> 30.3 us
    all_to_all x1, blocking collectives: 12.4 us -> 9.21 us  [body(): lax.all_to_all(found, ('blk', 'split'), split_axis=0, concat_axis=0, tile...]
    pallas_call x3, Pallas kernels: 10.4 us -> 12.2 us  [meet(): pl.pallas_call(kernel, out_shape=outs, in_specs=[WHOLE] * (inputs + len(s...]
    ppermute x4, waiting for transfers between devices: 8.01 us -> 7.13 us  [chip_swap(): return lax.ppermute(array, 'blk', [(b, b ^ 1) for b in range(blocks)])]
  transfers between devices with their start and end apart: 18 -> 18, of which waited for: 9 -> 9; matrix products, arithmetic and copies ran while one was open for 0% -> 0% of each run, Pallas kernels for 8% -> 10%
where the time goes in v10:
time: 79.1 us; the launch traced here: 78.1 us
  waiting for transfers between devices  30.3 us (38%)
  starting transfers between devices  20.5 us (26%)
  Pallas kernels  17.8 us (23%)
  blocking collectives  9.21 us (12%)
    ppermute x6, waiting for transfers between devices, between(): return lax.ppermute(array, 'blk', route)  19.8 us
    ppermute x6, starting transfers between devices, between(): return lax.ppermute(array, 'blk', route)  14.2 us
    pallas_call x3, Pallas kernels, meet(): pl.pallas_call(kernel, out_shape=outs, in_specs=[WHOLE] * (inputs + len(s...  12.2 us
    all_to_all x1, blocking collectives, body(): lax.all_to_all(found, ('blk', 'split'), split_axis=0, concat_axis=0, tile...  9.21 us
    ppermute x4, waiting for transfers between devices, chip_swap(): return lax.ppermute(array, 'blk', [(b, b ^ 1) for b in range(blocks)])  7.13 us
    ppermute x4, starting transfers between devices, chip_swap(): return lax.ppermute(array, 'blk', [(b, b ^ 1) for b in range(blocks)])  5.66 us
    pallas_call x1, Pallas kernels, in_order(): pl.pallas_call(functools.partial(order_kernel, soon, chips, parts), out_s...  3.45 us
    ppermute x8, waiting for transfers between devices, core_swap(): return lax.ppermute(array, 'split', [(c, c ^ 1) for c in range(cores)])  3.44 us
  transfers between devices with their start and end apart: 18, of which 9 were waited for; matrix products, arithmetic and copies ran while one was open for 0% of the time, Pallas kernels for 10%

profile of v10, /device:TPU:0, one launch (start us, length us, event | category | flops | bytes accessed | tf_op | source)
XLA Modules:
  0.0 78.1 jit_solution(17280932650858582707)
XLA Ops:
  0.0 3.4 %order.1 = (bf16[264,768]{1,0:T(8,128)(2,1)S(1)}, bf16[264,768]{1,0:T(8,128)(2,1)S(1)}, bf16[272,768]{1,0:T(8,128)(2,1)S(1)}, bf16[1024,768]{1,0:T(8,128)(2,1)S(...) custom-call(bf16[1024,768]{1,0:T(8,128)(2,1)} %rows_hbm.1, s32[1,1024]{1,0:T(1,128)} %bitcast.3, s32[1,1024]{1,0:T(1,128)} %bitcast.4), custom_call_target="tpu_custom_call" | custom-call | tf_op jit(solution)/shard_map/order/pallas_call | solution.py:104
  3.5 0.7 rest.1.refs_0_.refs_1_
  4.2 3.0 %collective-permute-start.1 = (bf16[264,768]{1,0:T(8,128)(2,1)S(1)}, bf16[264,768]{1,0:T(8,128)(2,1)S(1)}, u32[]{:S(2)}, u32[]{:S(2)}) collective-permute-start(bf16[264,768]{1,0:T(8,128)(2,1)S(1)} %rest.1.refs_0_.refs_1_), channel_id=1, source_target_pairs={{0,2},{2,0},{4,6},{6,4},{8,10},{10,8},{12,14},{14,12},{1,3},{3,1},... | collective-permute-start | bytes 1216520 | tf_op jit(solution)/shard_map/over_0/ppermute | solution.py:455
  7.2 1.6 %collective-permute-start.3 = (bf16[264,768]{1,0:T(8,128)(2,1)S(1)}, bf16[264,768]{1,0:T(8,128)(2,1)S(1)}, u32[]{:S(2)}, u32[]{:S(2)}) collective-permute-start(bf16[264,768]{1,0:T(8,128)(2,1)S(1)} %get-tuple-element.31.refs_5_), channel_id=1, source_target_pairs={{0,4},{2,6},{4,0},{6,2},{8,12},{10,14},{12,8},{14,10},{1,5},{3,7},... | collective-permute-start | bytes 1216520 | tf_op jit(solution)/shard_map/rows_2/ppermute | solution.py:448
  8.8 2.6 %collective-permute-start.4 = (bf16[264,768]{1,0:T(8,128)(2,1)S(1)}, bf16[264,768]{1,0:T(8,128)(2,1)S(1)}, u32[]{:S(2)}, u32[]{:S(2)}) collective-permute-start(bf16[264,768]{1,0:T(8,128)(2,1)S(1)} %get-tuple-element.32.refs_3_), channel_id=1, source_target_pairs={{0,8},{2,10},{4,12},{6,14},{8,0},{10,2},{12,4},{14,6},{1,9},{3,11}... | collective-permute-start | bytes 1216520 | tf_op jit(solution)/shard_map/rows_2/ppermute | solution.py:448
  11.4 0.0 collective-permute-start
  11.4 5.2 %collective-permute-done.1.refs_2_.refs_3_ = bf16[264,768]{1,0:T(8,128)(2,1)S(1)} collective-permute-done((bf16[264,768]{1,0:T(8,128)(2,1)S(1)}, bf16[264,768]{1,0:T(8,128)(2,1)S(1)}, u32[]{:S(2)}, u32[]{:S(2)}) %collective-permute-start.1) | collective-permute-done | bytes 405536 | tf_op jit(solution)/shard_map/over_0/ppermute | solution.py:455
  16.6 0.0 collective-permute-start.2
  16.6 10.0 %collective-permute-done.3.refs_4_.refs_2_ = bf16[264,768]{1,0:T(8,128)(2,1)S(1)} collective-permute-done((bf16[264,768]{1,0:T(8,128)(2,1)S(1)}, bf16[264,768]{1,0:T(8,128)(2,1)S(1)}, u32[]{:S(2)}, u32[]{:S(2)}) %collective-permute-start.3) | collective-permute-done | bytes 405536 | tf_op jit(solution)/shard_map/rows_2/ppermute | solution.py:448
  26.6 0.0 collective-permute-start.5
  26.6 2.3 %collective-permute-done.4.refs_5_.refs_0_ = bf16[264,768]{1,0:T(8,128)(2,1)S(1)} collective-permute-done((bf16[264,768]{1,0:T(8,128)(2,1)S(1)}, bf16[264,768]{1,0:T(8,128)(2,1)S(1)}, u32[]{:S(2)}, u32[]{:S(2)}) %collective-permute-start.4) | collective-permute-done | bytes 405536 | tf_op jit(solution)/shard_map/rows_2/ppermute | solution.py:448
  29.0 2.5 %collective-permute-start.9 = (bf16[272,768]{1,0:T(8,128)(2,1)S(1)}, bf16[272,768]{1,0:T(8,128)(2,1)S(1)}, u32[]{:S(2)}, u32[]{:S(2)}) collective-permute-start(bf16[272,768]{1,0:T(8,128)(2,1)S(1)} %get-tuple-element.35.refs_8_), channel_id=1, source_target_pairs={{0,12},{2,14},{4,8},{6,10},{8,4},{10,6},{12,0},{14,2},{1,13},{3,15... | collective-permute-start | bytes 1253384 | tf_op jit(solution)/shard_map/rows_3/ppermute | solution.py:448
  31.5 0.0 collective-permute-start.6
  31.5 0.0 collective-permute-done.refs_1_
  31.5 0.5 collective-permute-start.7
  32.1 0.0 collective-permute-done.2.refs_3_
  32.1 0.0 collective-permute-start.10
  32.1 0.0 collective-permute-done.5.refs_6_
  32.1 1.6 %collective-permute-start.8 = (bf16[264,768]{1,0:T(8,128)(2,1)S(1)}, bf16[264,768]{1,0:T(8,128)(2,1)S(1)}, u32[]{:S(2)}, u32[]{:S(2)}) collective-permute-start(bf16[264,768]{1,0:T(8,128)(2,1)S(1)} %collective-permute-done.4.refs_5_.refs_0_), channel_id=1, source_target_pairs={{0,2},{2,0},{4,6},{6,4},{8,10},{10,8},{12,14},{14,12},{1,3},{3,1},... | collective-permute-start | bytes 1216520 | tf_op jit(solution)/shard_map/over_2/ppermute | solution.py:455
  33.6 0.0 collective-permute-done.6.refs_7_
  33.6 2.4 %meet.3 = (bf16[4096,768]{1,0:T(8,128)(2,1)S(1)}, f32[4096,128]{1,0:T(8,128)S(1)}, f32[4096,128]{1,0:T(8,128)S(1)}, f32[1,768]{1,0:T(1,128)S(1)}) custom-call(bf16[264,768]{1,0:T(8,128)(2,1)S(1)} %rest.1.refs_0_.refs_1_, bf16[264,768]{1,0:T(8,128)(2,1)S(1)} %collective-permute-done.refs_1_, bf16[264,768]{1,0:T(8,128)(2,1)S(1)} %collective-permute-done.1.refs_2_.refs_3_, ...), custom_call_target="tpu_custom_call" | custom-call | tf_op jit(solution)/shard_map/meet/pallas_call | solution.py:341
  36.1 7.4 %collective-permute-done.9.refs_0_ = bf16[272,768]{1,0:T(8,128)(2,1)S(1)} collective-permute-done((bf16[272,768]{1,0:T(8,128)(2,1)S(1)}, bf16[272,768]{1,0:T(8,128)(2,1)S(1)}, u32[]{:S(2)}, u32[]{:S(2)}) %collective-permute-start.9) | collective-permute-done | bytes 417824 | tf_op jit(solution)/shard_map/rows_3/ppermute | solution.py:448
  43.5 0.1 pack.3
  43.6 0.7 collective-permute-start.15
  44.3 6.8 %collective-permute-start.16 = (bf16[272,768]{1,0:T(8,128)(2,1)S(1)}, bf16[272,768]{1,0:T(8,128)(2,1)S(1)}, u32[]{:S(2)}, u32[]{:S(2)}) collective-permute-start(bf16[272,768]{1,0:T(8,128)(2,1)S(1)} %get-tuple-element.45), channel_id=1, source_target_pairs={{0,4},{2,6},{4,0},{6,2},{8,12},{10,14},{12,8},{14,10},{1,5},{3,7},... | collective-permute-start | bytes 1253384 | tf_op jit(solution)/shard_map/passed_3/ppermute | solution.py:448
  51.1 0.0 collective-permute-done.7.refs_0_
  51.1 0.5 collective-permute-start.14
  51.6 0.0 collective-permute-done.10.refs_3_.refs_7_.refs_4_
  51.6 0.8 collective-permute-done.8.refs_1_
  52.4 0.0 collective-permute-start.11
  52.4 0.5 collective-permute-start.12
  52.9 1.2 %collective-permute-done.11.refs_2_ = bf16[264,768]{1,0:T(8,128)(2,1)S(1)} collective-permute-done((bf16[264,768]{1,0:T(8,128)(2,1)S(1)}, bf16[264,768]{1,0:T(8,128)(2,1)S(1)}, u32[]{:S(2)}, u32[]{:S(2)}) %collective-permute-start.11) | collective-permute-done | bytes 405536 | tf_op jit(solution)/shard_map/across_1/ppermute | solution.py:459
  54.1 0.1 collective-permute-start.13
  54.3 0.4 collective-permute-done.12.refs_3_
  54.7 5.1 %meet.4 = (bf16[4096,768]{1,0:T(8,128)(2,1)S(1)}, f32[4096,128]{1,0:T(8,128)S(1)}, f32[4096,128]{1,0:T(8,128)S(1)}, f32[1,1024]{1,0:T(1,128)S(1)}) custom-call(bf16[264,768]{1,0:T(8,128)(2,1)S(1)} %get-tuple-element.38.refs_0_, bf16[264,768]{1,0:T(8,128)(2,1)S(1)} %get-tuple-element.39.refs_1_, ...), custom_call_target="tpu_custom_call", output_to_operand_aliasing={{0}: (8, {}), {1}: (9, {}), {2}: (10, {})} | custom-call | tf_op jit(solution)/shard_map/meet/pallas_call | solution.py:341
  59.8 0.0 collective-permute-done.15.refs_2_.refs_7_
  59.8 0.0 collective-permute-done.16.refs_3_.refs_6_
  59.8 1.1 %collective-permute-done.14.refs_0_ = bf16[272,768]{1,0:T(8,128)(2,1)S(1)} collective-permute-done((bf16[272,768]{1,0:T(8,128)(2,1)S(1)}, bf16[272,768]{1,0:T(8,128)(2,1)S(1)}, u32[]{:S(2)}, u32[]{:S(2)}) %collective-permute-start.14) | collective-permute-done | bytes 417824 | tf_op jit(solution)/shard_map/over_3/ppermute | solution.py:455
  61.0 0.0 collective-permute-start.17
  61.0 0.0 collective-permute-done.13.refs_1_
  61.0 1.8 %collective-permute-done.17.refs_3_ = bf16[272,768]{1,0:T(8,128)(2,1)S(1)} collective-permute-done((bf16[272,768]{1,0:T(8,128)(2,1)S(1)}, bf16[272,768]{1,0:T(8,128)(2,1)S(1)}, u32[]{:S(2)}, u32[]{:S(2)}) %collective-permute-start.17) | collective-permute-done | bytes 417824 | tf_op jit(solution)/shard_map/across_3/ppermute | solution.py:459
  62.7 4.7 %meet.5 = (bf16[4096,768]{1,0:T(8,128)(2,1)S(1)}, f32[4096,128]{1,0:T(8,128)S(1)}, f32[4096,128]{1,0:T(8,128)S(1)}, f32[1,1280]{1,0:T(1,128)S(1)}, f32[1,4096]{1,0:T(1,128)S(1)}) custom-call(bf16[272,768]{1,0:T(8,128)(2,1)S(1)} %get-tuple-element.36.refs_2_.refs_6_.refs_0_, ...), custom_call_target="tpu_custom_call", output_to_operand_aliasing={{0}: (9, {}), {1}: (10, {}), {2}: (11, {})} | custom-call | tf_op jit(solution)/shard_map/meet/pallas_call | solution.py:341
  67.4 0.1 route.1
  67.5 9.2 %all_to_all.5.got_ref = f32[16,1,512]{2,1,0:T(1,128)S(1)} all-to-all(f32[16,1,512]{2,1,0:T(1,128)S(1)} %route.1), channel_id=1, replica_groups=mesh['groups'=2,'blk'=8,'split'=2] {'blk','split'}, dimensions={0} | all-to-all | bytes 65536 | tf_op jit(solution)/shard_map/all_to_all | solution.py:600
  76.7 1.3 %back.1 = f32[1,1024]{1,0:T(1,128)} custom-call(f32[16,1,512]{2,1,0:T(1,128)S(1)} %all_to_all.5.got_ref, s32[1,1024]{1,0:T(1,128)S(1)} %get-tuple-element.29.rank_ref), custom_call_target="tpu_custom_call" | custom-call | tf_op jit(solution)/shard_map/back/pallas_call | solution.py:427
  (4 shorter events, 0.1 us)
Async XLA Ops:
  4.2 12.4 %collective-permute-start.1 = (bf16[264,768]{1,0:T(8,128)(2,1)S(1)}, bf16[264,768]{1,0:T(8,128)(2,1)S(1)}, u32[]{:S(2)}, u32[]{:S(2)}) collective-permute-start(bf16[264,768]{1,0:T(8,128)(2,1)S(1)} %rest.1.refs_0_.refs_1_), channel_id=1, source_target_pairs={{0,2},{2,0},{4,6},{6,4},{8,10},{10,8},{12,14},{14,12},{1,3},{3,1},... | collective-permute-start | bytes 1216520 | tf_op jit(solution)/shard_map/over_0/ppermute | solution.py:455
  7.2 19.4 %collective-permute-start.3 = (bf16[264,768]{1,0:T(8,128)(2,1)S(1)}, bf16[264,768]{1,0:T(8,128)(2,1)S(1)}, u32[]{:S(2)}, u32[]{:S(2)}) collective-permute-start(bf16[264,768]{1,0:T(8,128)(2,1)S(1)} %get-tuple-element.31.refs_5_), channel_id=1, source_target_pairs={{0,4},{2,6},{4,0},{6,2},{8,12},{10,14},{12,8},{14,10},{1,5},{3,7},... | collective-permute-start | bytes 1216520 | tf_op jit(solution)/shard_map/rows_2/ppermute | solution.py:448
  8.8 20.2 %collective-permute-start.4 = (bf16[264,768]{1,0:T(8,128)(2,1)S(1)}, bf16[264,768]{1,0:T(8,128)(2,1)S(1)}, u32[]{:S(2)}, u32[]{:S(2)}) collective-permute-start(bf16[264,768]{1,0:T(8,128)(2,1)S(1)} %get-tuple-element.32.refs_3_), channel_id=1, source_target_pairs={{0,8},{2,10},{4,12},{6,14},{8,0},{10,2},{12,4},{14,6},{1,9},{3,11}... | collective-permute-start | bytes 1216520 | tf_op jit(solution)/shard_map/rows_2/ppermute | solution.py:448
  11.4 20.2 %collective-permute-start = (bf16[264,768]{1,0:T(8,128)(2,1)S(1)}, bf16[264,768]{1,0:T(8,128)(2,1)S(1)}, u32[]{:S(2)}, u32[]{:S(2)}) collective-permute-start(bf16[264,768]{1,0:T(8,128)(2,1)S(1)} %rest.1.refs_0_.refs_1_), channel_id=1, source_target_pairs={{0,1},{1,0},{2,3},{3,2},{4,5},{5,4},{6,7},{7,6},{8,9},{9,8},{10,11... | collective-permute-start | bytes 1216520 | tf_op jit(solution)/shard_map/beside_0/ppermute | solution.py:459
  16.6 15.5 %collective-permute-start.2 = (bf16[264,768]{1,0:T(8,128)(2,1)S(1)}, bf16[264,768]{1,0:T(8,128)(2,1)S(1)}, u32[]{:S(2)}, u32[]{:S(2)}) collective-permute-start(bf16[264,768]{1,0:T(8,128)(2,1)S(1)} %collective-permute-done.1.refs_2_.refs_3_), channel_id=1, source_target_pairs={{0,1},{1,0},{2,3},{3,2},{4,5},{5,4},{6,7},{7,6},{8,9},{9,8},{10,11... | collective-permute-start | bytes 1216520 | tf_op jit(solution)/shard_map/across_0/ppermute | solution.py:459
  26.6 5.4 %collective-permute-start.5 = (bf16[264,768]{1,0:T(8,128)(2,1)S(1)}, bf16[264,768]{1,0:T(8,128)(2,1)S(1)}, u32[]{:S(2)}, u32[]{:S(2)}) collective-permute-start(bf16[264,768]{1,0:T(8,128)(2,1)S(1)} %collective-permute-done.3.refs_4_.refs_2_), channel_id=1, source_target_pairs={{0,1},{1,0},{2,3},{3,2},{4,5},{5,4},{6,7},{7,6},{8,9},{9,8},{10,11... | collective-permute-start | bytes 1216520 | tf_op jit(solution)/shard_map/beside_1/ppermute | solution.py:459
  29.0 14.5 %collective-permute-start.9 = (bf16[272,768]{1,0:T(8,128)(2,1)S(1)}, bf16[272,768]{1,0:T(8,128)(2,1)S(1)}, u32[]{:S(2)}, u32[]{:S(2)}) collective-permute-start(bf16[272,768]{1,0:T(8,128)(2,1)S(1)} %get-tuple-element.35.refs_8_), channel_id=1, source_target_pairs={{0,12},{2,14},{4,8},{6,10},{8,4},{10,6},{12,0},{14,2},{1,13},{3,15... | collective-permute-start | bytes 1253384 | tf_op jit(solution)/shard_map/rows_3/ppermute | solution.py:448
  31.5 2.1 %collective-permute-start.6 = (bf16[264,768]{1,0:T(8,128)(2,1)S(1)}, bf16[264,768]{1,0:T(8,128)(2,1)S(1)}, u32[]{:S(2)}, u32[]{:S(2)}) collective-permute-start(bf16[264,768]{1,0:T(8,128)(2,1)S(1)} %collective-permute-done.4.refs_5_.refs_0_), channel_id=1, source_target_pairs={{0,1},{1,0},{2,3},{3,2},{4,5},{5,4},{6,7},{7,6},{8,9},{9,8},{10,11... | collective-permute-start | bytes 1216520 | tf_op jit(solution)/shard_map/beside_2/ppermute | solution.py:459
  31.5 19.6 %collective-permute-start.7 = (bf16[264,768]{1,0:T(8,128)(2,1)S(1)}, bf16[264,768]{1,0:T(8,128)(2,1)S(1)}, u32[]{:S(2)}, u32[]{:S(2)}) collective-permute-start(bf16[264,768]{1,0:T(8,128)(2,1)S(1)} %collective-permute-done.3.refs_4_.refs_2_), channel_id=1, source_target_pairs={{0,2},{2,0},{4,6},{6,4},{8,10},{10,8},{12,14},{14,12},{1,3},{3,1},... | collective-permute-start | bytes 1216520 | tf_op jit(solution)/shard_map/over_1/ppermute | solution.py:455
  32.1 19.6 %collective-permute-start.10 = (bf16[264,768]{1,0:T(8,128)(2,1)S(1)}, bf16[264,768]{1,0:T(8,128)(2,1)S(1)}, u32[]{:S(2)}, u32[]{:S(2)}) collective-permute-start(bf16[264,768]{1,0:T(8,128)(2,1)S(1)} %get-tuple-element.37), channel_id=1, source_target_pairs={{0,4},{2,6},{4,0},{6,2},{8,12},{10,14},{12,8},{14,10},{1,5},{3,7},... | collective-permute-start | bytes 1216520 | tf_op jit(solution)/shard_map/passed_2/ppermute | solution.py:448
  32.1 20.3 %collective-permute-start.8 = (bf16[264,768]{1,0:T(8,128)(2,1)S(1)}, bf16[264,768]{1,0:T(8,128)(2,1)S(1)}, u32[]{:S(2)}, u32[]{:S(2)}) collective-permute-start(bf16[264,768]{1,0:T(8,128)(2,1)S(1)} %collective-permute-done.4.refs_5_.refs_0_), channel_id=1, source_target_pairs={{0,2},{2,0},{4,6},{6,4},{8,10},{10,8},{12,14},{14,12},{1,3},{3,1},... | collective-permute-start | bytes 1216520 | tf_op jit(solution)/shard_map/over_2/ppermute | solution.py:455
  43.6 16.2 %collective-permute-start.15 = (bf16[272,768]{1,0:T(8,128)(2,1)S(1)}, bf16[272,768]{1,0:T(8,128)(2,1)S(1)}, u32[]{:S(2)}, u32[]{:S(2)}) collective-permute-start(bf16[272,768]{1,0:T(8,128)(2,1)S(1)} %get-tuple-element.44), channel_id=1, source_target_pairs={{4,8},{6,10},{8,4},{10,6},{5,9},{7,11},{9,5},{11,7},{20,24},{22,26... | collective-permute-start | bytes 1253384 | tf_op jit(solution)/shard_map/border/ppermute | solution.py:448
  44.3 15.6 %collective-permute-start.16 = (bf16[272,768]{1,0:T(8,128)(2,1)S(1)}, bf16[272,768]{1,0:T(8,128)(2,1)S(1)}, u32[]{:S(2)}, u32[]{:S(2)}) collective-permute-start(bf16[272,768]{1,0:T(8,128)(2,1)S(1)} %get-tuple-element.45), channel_id=1, source_target_pairs={{0,4},{2,6},{4,0},{6,2},{8,12},{10,14},{12,8},{14,10},{1,5},{3,7},... | collective-permute-start | bytes 1253384 | tf_op jit(solution)/shard_map/passed_3/ppermute | solution.py:448
  51.1 9.9 %collective-permute-start.14 = (bf16[272,768]{1,0:T(8,128)(2,1)S(1)}, bf16[272,768]{1,0:T(8,128)(2,1)S(1)}, u32[]{:S(2)}, u32[]{:S(2)}) collective-permute-start(bf16[272,768]{1,0:T(8,128)(2,1)S(1)} %get-tuple-element.36.refs_2_.refs_6_.refs_0_), channel_id=1, source_target_pairs={{0,2},{2,0},{4,6},{6,4},{8,10},{10,8},{12,14},{14,12},{1,3},{3,1},... | collective-permute-start | bytes 1253384 | tf_op jit(solution)/shard_map/over_3/ppermute | solution.py:455
  52.4 1.7 %collective-permute-start.11 = (bf16[264,768]{1,0:T(8,128)(2,1)S(1)}, bf16[264,768]{1,0:T(8,128)(2,1)S(1)}, u32[]{:S(2)}, u32[]{:S(2)}) collective-permute-start(bf16[264,768]{1,0:T(8,128)(2,1)S(1)} %get-tuple-element.38.refs_0_), channel_id=1, source_target_pairs={{0,1},{1,0},{2,3},{3,2},{4,5},{5,4},{6,7},{7,6},{8,9},{9,8},{10,11... | collective-permute-start | bytes 1216520 | tf_op jit(solution)/shard_map/across_1/ppermute | solution.py:459
  52.4 2.3 %collective-permute-start.12 = (bf16[264,768]{1,0:T(8,128)(2,1)S(1)}, bf16[264,768]{1,0:T(8,128)(2,1)S(1)}, u32[]{:S(2)}, u32[]{:S(2)}) collective-permute-start(bf16[264,768]{1,0:T(8,128)(2,1)S(1)} %get-tuple-element.39.refs_1_), channel_id=1, source_target_pairs={{0,1},{1,0},{2,3},{3,2},{4,5},{5,4},{6,7},{7,6},{8,9},{9,8},{10,11... | collective-permute-start | bytes 1216520 | tf_op jit(solution)/shard_map/across_2/ppermute | solution.py:459
  54.1 6.8 %collective-permute-start.13 = (bf16[272,768]{1,0:T(8,128)(2,1)S(1)}, bf16[272,768]{1,0:T(8,128)(2,1)S(1)}, u32[]{:S(2)}, u32[]{:S(2)}) collective-permute-start(bf16[272,768]{1,0:T(8,128)(2,1)S(1)} %get-tuple-element.36.refs_2_.refs_6_.refs_0_), channel_id=1, source_target_pairs={{0,1},{1,0},{2,3},{3,2},{4,5},{5,4},{6,7},{7,6},{8,9},{9,8},{10,11... | collective-permute-start | bytes 1253384 | tf_op jit(solution)/shard_map/beside_3/ppermute | solution.py:459
  61.0 1.8 %collective-permute-start.17 = (bf16[272,768]{1,0:T(8,128)(2,1)S(1)}, bf16[272,768]{1,0:T(8,128)(2,1)S(1)}, u32[]{:S(2)}, u32[]{:S(2)}) collective-permute-start(bf16[272,768]{1,0:T(8,128)(2,1)S(1)} %after.3.refs_2_), channel_id=1, source_target_pairs={{0,1},{1,0},{2,3},{3,2},{4,5},{5,4},{6,7},{7,6},{8,9},{9,8},{10,11... | collective-permute-start | bytes 1253384 | tf_op jit(solution)/shard_map/across_3/ppermute | solution.py:459
